TPU v7x, 32 devices: a whole 2x2x4 slice. The times are simulated.
32 devices in a mesh: gz: 16 (over z, y, x), gy: 2 (over core).
Axes of the slice: x: 2, y: 2, z: 4, core: 2. Of those that a mesh axis runs over, the one named last changes fastest.
Arguments:
- scalar: float32 [32, 128, 1024], P('gz', 'gy'), as said below
- bin_index: int32 [32, 128, 1024], P('gz', 'gy'), may hold values from 0 to 255, as said below
- color_table: bfloat16 [3, 257], replicated, may hold values from 0.099609375 to 1
- opacity_table: bfloat16 [257], replicated, may hold values from 0.00049972534 to 0.019897461
- light_dir: float32 [3], replicated, may hold values from -4 to 4
- view_order: int32 [16], replicated, may hold values from 0 to 15, each once
Outputs:
- image_rgba: float32 [4, 2, 64, 1024], P(None, 'gy', 'gz')
Inputs may be any that keep to these rules, and one draw needn't show every extreme that they name: bin_index is the floor of 256 scalar in every cell, except that fraction may reach 1. scalar lies between bin_index / 256 and (bin_index + 1) / 256. `view_order`: each brick position appears once.
All inputs are finite; a program needn't handle non-finite values.
Results may differ from a plain program's by a relative error of at most 0.0003.
Values sent between devices are 32-bit elements; how exact they have to be, the bound alone decides.
No kernel may reach another device: no remote copies, remote signals or barrier semaphores. Data moves between devices by JAX's collectives and lax.ppermute only.
A program may use at most 64 MiB of HBM per device.

v0:
```python
import jax
import jax.numpy as jnp
from jax import lax
from jax.sharding import PartitionSpec as P


def extended(x, sides, width):
    for axis, dim in sides:
        devices, length = (lax.axis_size(axis), x.shape[dim])
        up = [(i, (i + 1) % devices) for i in range(devices - 1)]
        down = [(j, i) for i, j in up]
        last = lax.slice_in_dim(x, length - width, length, axis=dim)
        initial = lax.slice_in_dim(x, 0, width, axis=dim)
        before = lax.ppermute(last, axis, up)
        after = lax.ppermute(initial, axis, down)
        x = jnp.concatenate([before, x, after], axis=dim)
    return x


def shading_from(field, row_padded, light_dir):
    next_slice = jnp.concatenate([field[1:], field[-1:]], axis=0)
    behind = jnp.concatenate([field[:1], field[:-1]], axis=0)
    grad_depth = next_slice - behind
    grad_rows = row_padded[:, 2:] - row_padded[:, :-2]
    col_padded = jnp.pad(field, ((0, 0), (0, 0), (1, 1)))
    grad_cols = col_padded[:, :, 2:] - col_padded[:, :, :-2]
    facing = grad_depth * light_dir[0] + grad_rows * light_dir[1] + grad_cols * light_dir[2]
    squared = grad_depth * grad_depth + grad_rows * grad_rows + grad_cols * grad_cols
    return 0.25 + 0.75 * facing * facing / (squared + 1.0)


def blend_emission(lower, upper, fraction, shading):
    blended = (1.0 - fraction) * lower + fraction * upper
    opacity = blended[3]
    emitted = opacity * shading * blended[:3]
    return (emitted, jnp.log1p(-opacity))


def shards(scalar, bin_index, color_table, opacity_table, light_dir, view_order):
    depth_count, row_count, col_count = scalar.shape
    bricks = lax.axis_size("gz")
    tile_rows = row_count // bricks
    band_rows = 16
    band_count = row_count // band_rows
    block_count = depth_count * band_count
    block_cells = band_rows * col_count
    bin_count = color_table.shape[1] - 1
    stacked = jnp.concatenate(
        [
            color_table[:, :-1],
            opacity_table[None, :-1],
            color_table[:, 1:],
            opacity_table[None, 1:],
        ],
        axis=0,
    )
    fraction = scalar * bin_count - bin_index.astype(jnp.float32)
    row_padded = extended(scalar, (("gy", 1),), 1)
    shading = shading_from(scalar, row_padded, light_dir)
    levels = lax.broadcasted_iota(jnp.int32, (bin_count, 1), 0)

    def lookup(pieces):
        codes_block, fraction_block, shading_block = pieces
        onehot = (levels == codes_block[None, :]).astype(jnp.bfloat16)
        looked_up = jnp.dot(stacked, onehot, preferred_element_type=jnp.float32)
        return blend_emission(looked_up[:4], looked_up[4:], fraction_block, shading_block)

    def as_blocks(values):
        return values.reshape(block_count, block_cells)

    emitted, log_keep = lax.map(
        lookup, (as_blocks(bin_index), as_blocks(fraction), as_blocks(shading))
    )
    emitted = emitted.reshape(depth_count, band_count, 3, block_cells)
    log_keep = log_keep.reshape(depth_count, band_count, block_cells)
    passed = jnp.cumsum(log_keep, axis=0) - log_keep
    brick_color = jnp.sum(emitted * jnp.exp(passed)[:, :, None, :], axis=0)
    brick_keep = jnp.sum(log_keep, axis=0)
    color_part = jnp.transpose(brick_color, (1, 0, 2)).reshape(3, bricks, tile_rows, col_count)
    keep_part = brick_keep.reshape(1, bricks, tile_rows, col_count)
    earlier = (view_order[None, :] < view_order[:, None]).astype(jnp.float32)
    color_in, keep_in = (
        lax.all_to_all(color_part, "gz", split_axis=1, concat_axis=1, tiled=True),
        lax.all_to_all(keep_part, "gz", split_axis=1, concat_axis=1, tiled=True),
    )
    before = jnp.einsum("ji,cirw->cjrw", earlier, keep_in, precision=lax.Precision.HIGHEST)
    color_sum = jnp.sum(color_in * jnp.exp(before), axis=1, keepdims=True)
    coverage = 1.0 - jnp.exp(jnp.sum(keep_in, axis=1, keepdims=True))
    return jnp.concatenate([color_sum, coverage], axis=0)


def solution(mesh):
    in_specs = (P("gz", "gy", None), P("gz", "gy", None), P(), P(), P(), P())
    out_specs = P(None, "gy", "gz", None)
    return jax.shard_map(shards, mesh=mesh, in_specs=in_specs, out_specs=out_specs, check_vma=False)
```

profile of v0, /device:TPU:0, one launch (start us, length us, event | category | flops | bytes accessed | tf_op | source)
XLA Modules:
  0.0 111.8 jit_solution(15383587480228910581)
XLA Ops:
  0.0 1.0 fusion.19
  1.0 1.3 %collective-permute-start = (f32[2,1,1024]{2,1,0:T(1,128)S(1)}, f32[2,1,1024]{2,1,0:T(1,128)S(1)}, u32[]{:S(2)}, u32[]{:S(2)}) collective-permute-start(f32[2,1,1024]{2,1,0:T(1,128)S(1)} %get-tuple-element.88), channel_id=1, source_target_pairs={{1,0},{3,2},{5,4},{7,6},{9,8},{11,10},{13,12},{15,14},{17,16},{19,... | collective-permute-start | bytes 24584 | tf_op jit(solution)/shard_map/ppermute | solution.py:15
  2.3 3.0 %collective-permute-start.1 = (f32[2,1,1024]{2,1,0:T(1,128)S(1)}, f32[2,1,1024]{2,1,0:T(1,128)S(1)}, u32[]{:S(2)}, u32[]{:S(2)}) collective-permute-start(f32[2,1,1024]{2,1,0:T(1,128)S(1)} %get-tuple-element.89), channel_id=1, source_target_pairs={{0,1},{2,3},{4,5},{6,7},{8,9},{10,11},{12,13},{14,15},{16,17},{18,... | collective-permute-start | bytes 24584 | tf_op jit(solution)/shard_map/ppermute | solution.py:14
  5.3 1.8 %fusion.18 = (f32[1,64,1024]{2,1,0:T(8,128)S(1)}, f32[1,64,1024]{2,1,0:T(8,128)}) fusion(f32[2,64,1024]{2,1,0:T(8,128)} %param.8), kind=kLoop, calls=%fused_computation.41 | loop fusion | bytes 1048576 | tf_op jit(solution)/shard_map/slice | solution.py:21
  7.1 0.8 fusion.21
  7.9 1.4 %fusion.22 = (f32[1]{0:T(128)}, f32[1]{0:T(128)}, f32[1]{0:T(128)}) fusion(f32[3]{0:T(128)} %param.12), kind=kLoop, calls=%fused_computation.45 | loop fusion | bytes 24 | tf_op jit(solution)/shard_map/slice | solution.py:27
  9.4 0.8 fusion.20
  10.2 1.9 %reshape.58 = s32[8,16384]{1,0:T(8,128)} reshape(s32[2,64,1024]{2,1,0:T(8,128)} %param.9) | data formatting | bytes 1048576 | tf_op jit(solution)/shard_map/reshape | solution.py:69
  12.2 4.4 %fusion.10 = (f32[2,64,1024]{2,1,0:T(8,128)}, f32[2,64,1024]{2,1,0:T(8,128)}) fusion(f32[2,64,1024]{2,1,0:T(8,128)S(1)} %copy-done, f32[2,1,1024]{2,1,0:T(1,128)S(1)} %collective-permute-done.1, f32[2,1,1024]{2,1,0:T(1,128)S(1)} %collective-permute-done, f32[1,64,1024]{2,1,0:T(8,128)} %get-tuple-element.87, f32[1,64,1024]{2,1,0:T(8,128)S(1)} %get-tuple-element.86, ...), kind=kLoop, calls=%fused_computation.26 | loop fusion | flops 3276800 | bytes 2637836 | tf_op jit(solution)/shard_map/add | solution.py:29
  16.6 1.1 %reshape.59 = f32[8,16384]{1,0:T(8,128)S(1)} reshape(f32[2,64,1024]{2,1,0:T(8,128)} %get-tuple-element.84) | data formatting | bytes 1048576 | tf_op jit(solution)/shard_map/reshape | solution.py:69
  17.7 1.1 %reshape.57 = f32[8,16384]{1,0:T(8,128)S(1)} reshape(f32[2,64,1024]{2,1,0:T(8,128)} %get-tuple-element.85) | data formatting | bytes 1048576 | tf_op jit(solution)/shard_map/reshape | solution.py:69
  18.9 49.3 %while.13 = (s32[]{:T(128)}, f32[8,3,16384]{2,1,0:T(4,128)S(1)}, f32[8,16384]{1,0:T(8,128)}, f32[8,16384]{1,0:T(8,128)S(1)}, s32[8,16384]{1,0:T(8,128)}, /*index...) while((s32[]{:T(128)}, f32[8,3,16384]{2,1,0:T(4,128)S(1)}, ...), condition=%wide.region_1.2_spmd.clone, body=%wide.region_0.1_spmd.clone.sunk | while | flops 71598080 | bytes 2822265 | solution.py:71
  18.9 1.1 constant_dynamic-slice_fusion.4
  20.1 2.6 %convolution_bitcast_fusion.2 = f32[8,16384]{1,0:T(8,128)S(1)} fusion(bf16[8,256]{1,0:T(8,128)(2,1)S(1)} %get-tuple-element.171, s32[16384]{0:T(1024)S(1)} %bitcast.52), kind=kOutput, calls=%fused_computation.1.clone.1 | convolution fusion | flops 71303168 | bytes 593920 | tf_op jit(solution)/shard_map/while/body/eval_jaxpr/dot_general | solution.py:65
  23.0 1.9 %dynamic_update_slice.14 = f32[8,16384]{1,0:T(8,128)} dynamic-update-slice(f32[8,16384]{1,0:T(8,128)} %get-tuple-element.159, f32[1,16384]{1,0:T(1,128)S(1)} %get-tuple-element.147, s32[]{:T(128)S(6)} %copy.24, s32[]{:T(128)} %constant.8.clone.1..sunk) | dynamic-update-slice | bytes 131076 | tf_op jit(solution)/shard_map/while/body/jit(dynamic_update_index_in_dim)/dynamic_update_slice | solution.py:71
  25.1 1.1 constant_dynamic-slice_fusion.4
  26.3 2.6 %convolution_bitcast_fusion.2 = f32[8,16384]{1,0:T(8,128)S(1)} fusion(bf16[8,256]{1,0:T(8,128)(2,1)S(1)} %get-tuple-element.171, s32[16384]{0:T(1024)S(1)} %bitcast.52), kind=kOutput, calls=%fused_computation.1.clone.1 | convolution fusion | flops 71303168 | bytes 593920 | tf_op jit(solution)/shard_map/while/body/eval_jaxpr/dot_general | solution.py:65
  29.2 1.9 %dynamic_update_slice.14 = f32[8,16384]{1,0:T(8,128)} dynamic-update-slice(f32[8,16384]{1,0:T(8,128)} %get-tuple-element.159, f32[1,16384]{1,0:T(1,128)S(1)} %get-tuple-element.147, s32[]{:T(128)S(6)} %copy.24, s32[]{:T(128)} %constant.8.clone.1..sunk) | dynamic-update-slice | bytes 131076 | tf_op jit(solution)/shard_map/while/body/jit(dynamic_update_index_in_dim)/dynamic_update_slice | solution.py:71
  31.2 1.1 constant_dynamic-slice_fusion.4
  32.4 2.6 %convolution_bitcast_fusion.2 = f32[8,16384]{1,0:T(8,128)S(1)} fusion(bf16[8,256]{1,0:T(8,128)(2,1)S(1)} %get-tuple-element.171, s32[16384]{0:T(1024)S(1)} %bitcast.52), kind=kOutput, calls=%fused_computation.1.clone.1 | convolution fusion | flops 71303168 | bytes 593920 | tf_op jit(solution)/shard_map/while/body/eval_jaxpr/dot_general | solution.py:65
  35.3 1.9 %dynamic_update_slice.14 = f32[8,16384]{1,0:T(8,128)} dynamic-update-slice(f32[8,16384]{1,0:T(8,128)} %get-tuple-element.159, f32[1,16384]{1,0:T(1,128)S(1)} %get-tuple-element.147, s32[]{:T(128)S(6)} %copy.24, s32[]{:T(128)} %constant.8.clone.1..sunk) | dynamic-update-slice | bytes 131076 | tf_op jit(solution)/shard_map/while/body/jit(dynamic_update_index_in_dim)/dynamic_update_slice | solution.py:71
  37.4 1.1 constant_dynamic-slice_fusion.4
  38.6 2.6 %convolution_bitcast_fusion.2 = f32[8,16384]{1,0:T(8,128)S(1)} fusion(bf16[8,256]{1,0:T(8,128)(2,1)S(1)} %get-tuple-element.171, s32[16384]{0:T(1024)S(1)} %bitcast.52), kind=kOutput, calls=%fused_computation.1.clone.1 | convolution fusion | flops 71303168 | bytes 593920 | tf_op jit(solution)/shard_map/while/body/eval_jaxpr/dot_general | solution.py:65
  41.5 1.9 %dynamic_update_slice.14 = f32[8,16384]{1,0:T(8,128)} dynamic-update-slice(f32[8,16384]{1,0:T(8,128)} %get-tuple-element.159, f32[1,16384]{1,0:T(1,128)S(1)} %get-tuple-element.147, s32[]{:T(128)S(6)} %copy.24, s32[]{:T(128)} %constant.8.clone.1..sunk) | dynamic-update-slice | bytes 131076 | tf_op jit(solution)/shard_map/while/body/jit(dynamic_update_index_in_dim)/dynamic_update_slice | solution.py:71
  43.6 1.1 constant_dynamic-slice_fusion.4
  44.7 2.6 %convolution_bitcast_fusion.2 = f32[8,16384]{1,0:T(8,128)S(1)} fusion(bf16[8,256]{1,0:T(8,128)(2,1)S(1)} %get-tuple-element.171, s32[16384]{0:T(1024)S(1)} %bitcast.52), kind=kOutput, calls=%fused_computation.1.clone.1 | convolution fusion | flops 71303168 | bytes 593920 | tf_op jit(solution)/shard_map/while/body/eval_jaxpr/dot_general | solution.py:65
  47.7 1.9 %dynamic_update_slice.14 = f32[8,16384]{1,0:T(8,128)} dynamic-update-slice(f32[8,16384]{1,0:T(8,128)} %get-tuple-element.159, f32[1,16384]{1,0:T(1,128)S(1)} %get-tuple-element.147, s32[]{:T(128)S(6)} %copy.24, s32[]{:T(128)} %constant.8.clone.1..sunk) | dynamic-update-slice | bytes 131076 | tf_op jit(solution)/shard_map/while/body/jit(dynamic_update_index_in_dim)/dynamic_update_slice | solution.py:71
  49.7 1.1 constant_dynamic-slice_fusion.4
  50.9 2.6 %convolution_bitcast_fusion.2 = f32[8,16384]{1,0:T(8,128)S(1)} fusion(bf16[8,256]{1,0:T(8,128)(2,1)S(1)} %get-tuple-element.171, s32[16384]{0:T(1024)S(1)} %bitcast.52), kind=kOutput, calls=%fused_computation.1.clone.1 | convolution fusion | flops 71303168 | bytes 593920 | tf_op jit(solution)/shard_map/while/body/eval_jaxpr/dot_general | solution.py:65
  53.8 1.9 %dynamic_update_slice.14 = f32[8,16384]{1,0:T(8,128)} dynamic-update-slice(f32[8,16384]{1,0:T(8,128)} %get-tuple-element.159, f32[1,16384]{1,0:T(1,128)S(1)} %get-tuple-element.147, s32[]{:T(128)S(6)} %copy.24, s32[]{:T(128)} %constant.8.clone.1..sunk) | dynamic-update-slice | bytes 131076 | tf_op jit(solution)/shard_map/while/body/jit(dynamic_update_index_in_dim)/dynamic_update_slice | solution.py:71
  55.9 1.1 constant_dynamic-slice_fusion.4
  57.1 2.6 %convolution_bitcast_fusion.2 = f32[8,16384]{1,0:T(8,128)S(1)} fusion(bf16[8,256]{1,0:T(8,128)(2,1)S(1)} %get-tuple-element.171, s32[16384]{0:T(1024)S(1)} %bitcast.52), kind=kOutput, calls=%fused_computation.1.clone.1 | convolution fusion | flops 71303168 | bytes 593920 | tf_op jit(solution)/shard_map/while/body/eval_jaxpr/dot_general | solution.py:65
  60.0 1.9 %dynamic_update_slice.14 = f32[8,16384]{1,0:T(8,128)} dynamic-update-slice(f32[8,16384]{1,0:T(8,128)} %get-tuple-element.159, f32[1,16384]{1,0:T(1,128)S(1)} %get-tuple-element.147, s32[]{:T(128)S(6)} %copy.24, s32[]{:T(128)} %constant.8.clone.1..sunk) | dynamic-update-slice | bytes 131076 | tf_op jit(solution)/shard_map/while/body/jit(dynamic_update_index_in_dim)/dynamic_update_slice | solution.py:71
  62.0 1.1 constant_dynamic-slice_fusion.4
  63.2 2.6 %convolution_bitcast_fusion.2 = f32[8,16384]{1,0:T(8,128)S(1)} fusion(bf16[8,256]{1,0:T(8,128)(2,1)S(1)} %get-tuple-element.171, s32[16384]{0:T(1024)S(1)} %bitcast.52), kind=kOutput, calls=%fused_computation.1.clone.1 | convolution fusion | flops 71303168 | bytes 593920 | tf_op jit(solution)/shard_map/while/body/eval_jaxpr/dot_general | solution.py:65
  66.2 1.9 %dynamic_update_slice.14 = f32[8,16384]{1,0:T(8,128)} dynamic-update-slice(f32[8,16384]{1,0:T(8,128)} %get-tuple-element.159, f32[1,16384]{1,0:T(1,128)S(1)} %get-tuple-element.147, s32[]{:T(128)S(6)} %copy.24, s32[]{:T(128)} %constant.8.clone.1..sunk) | dynamic-update-slice | bytes 131076 | tf_op jit(solution)/shard_map/while/body/jit(dynamic_update_index_in_dim)/dynamic_update_slice | solution.py:71
  68.2 1.2 %reduce_window_sum.13 = f32[2,4,16384]{2,1,0:T(4,128)S(1)} reshape(f32[8,16384]{1,0:T(8,128)} %get-tuple-element.49) | data formatting | bytes 1048576 | tf_op jit(solution)/shard_map/jit(cumsum)/reduce_window_sum | solution.py:76
  69.6 0.9 reshape.62
  70.5 8.3 %all-to-all-start.1 = ((f32[1,16,4,1024]{3,2,0,1:T(4,128)}), f32[1,16,4,1024]{3,2,0,1:T(4,128)S(1)}, u32[]{:S(2)}, u32[]{:S(2)}) async-start(f32[1,16,4,1024]{3,2,0,1:T(4,128)} %bitcast.5), calls=%async_computation.1 | async-start | bytes 524288 | tf_op jit(solution)/shard_map/all_to_all | solution.py:84
  79.0 1.1 multiply_reduce_fusion
  80.0 0.5 copy.10
  80.6 0.7 reshape.61
  81.2 0.9 copy.11
  82.2 6.1 %all-to-all-done.1 = f32[1,16,4,1024]{3,2,0,1:T(4,128)S(1)} async-done(((f32[1,16,4,1024]{3,2,0,1:T(4,128)}), f32[1,16,4,1024]{3,2,0,1:T(4,128)S(1)}, u32[]{:S(2)}, u32[]{:S(2)}) %all-to-all-start.1) | async-done | bytes 262176 | tf_op jit(solution)/shard_map/all_to_all | solution.py:84
  88.2 3.6 %all-to-all-start = ((f32[3,16,4,1024]{3,2,0,1:T(4,128)}), f32[3,16,4,1024]{3,2,0,1:T(4,128)S(1)}, u32[]{:S(2)}, u32[]{:S(2)}) async-start(f32[3,16,4,1024]{3,2,0,1:T(4,128)} %copy.11), calls=%async_computation | async-start | bytes 1572864 | tf_op jit(solution)/shard_map/all_to_all | solution.py:83
  91.9 0.4 fusion.7
  92.6 18.3 %all-to-all-done = f32[3,16,4,1024]{3,2,0,1:T(4,128)S(1)} async-done(((f32[3,16,4,1024]{3,2,0,1:T(4,128)}), f32[3,16,4,1024]{3,2,0,1:T(4,128)S(1)}, u32[]{:S(2)}, u32[]{:S(2)}) %all-to-all-start) | async-done | bytes 786464 | tf_op jit(solution)/shard_map/all_to_all | solution.py:83
  111.1 0.6 pad_maximum_fusion.2
  (51 shorter events, 5.2 us)
Async XLA Ops:
  0.0 12.2 %copy-start = (f32[2,64,1024]{2,1,0:T(8,128)S(1)}, f32[2,64,1024]{2,1,0:T(8,128)}, u32[]{:S(2)}) copy-start(f32[2,64,1024]{2,1,0:T(8,128)} %param.8) | copy-start | bytes 1572868
  0.0 12.2 %copy-start.1 = (s32[2,64,1024]{2,1,0:T(8,128)S(1)}, s32[2,64,1024]{2,1,0:T(8,128)}, u32[]{:S(2)}) copy-start(s32[2,64,1024]{2,1,0:T(8,128)} %param.9) | copy-start | bytes 1572868
  1.0 11.2 %collective-permute-start = (f32[2,1,1024]{2,1,0:T(1,128)S(1)}, f32[2,1,1024]{2,1,0:T(1,128)S(1)}, u32[]{:S(2)}, u32[]{:S(2)}) collective-permute-start(f32[2,1,1024]{2,1,0:T(1,128)S(1)} %get-tuple-element.88), channel_id=1, source_target_pairs={{1,0},{3,2},{5,4},{7,6},{9,8},{11,10},{13,12},{15,14},{17,16},{19,... | collective-permute-start | bytes 24584 | tf_op jit(solution)/shard_map/ppermute | solution.py:15
  2.3 9.9 %collective-permute-start.1 = (f32[2,1,1024]{2,1,0:T(1,128)S(1)}, f32[2,1,1024]{2,1,0:T(1,128)S(1)}, u32[]{:S(2)}, u32[]{:S(2)}) collective-permute-start(f32[2,1,1024]{2,1,0:T(1,128)S(1)} %get-tuple-element.89), channel_id=1, source_target_pairs={{0,1},{2,3},{4,5},{6,7},{8,9},{10,11},{12,13},{14,15},{16,17},{18,... | collective-permute-start | bytes 24584 | tf_op jit(solution)/shard_map/ppermute | solution.py:14
  70.5 17.7 %all-to-all-start.1 = ((f32[1,16,4,1024]{3,2,0,1:T(4,128)}), f32[1,16,4,1024]{3,2,0,1:T(4,128)S(1)}, u32[]{:S(2)}, u32[]{:S(2)}) async-start(f32[1,16,4,1024]{3,2,0,1:T(4,128)} %bitcast.5), calls=%async_computation.1 | async-start | bytes 524288 | tf_op jit(solution)/shard_map/all_to_all | solution.py:84
  80.6 11.3 %copy-start.2 = (s32[16]{0:T(128)S(1)}, s32[16]{0:T(128)}, u32[]{:S(2)}) copy-start(s32[16]{0:T(128)} %param.13) | copy-start | bytes 196
  88.2 22.6 %all-to-all-start = ((f32[3,16,4,1024]{3,2,0,1:T(4,128)}), f32[3,16,4,1024]{3,2,0,1:T(4,128)S(1)}, u32[]{:S(2)}, u32[]{:S(2)}) async-start(f32[3,16,4,1024]{3,2,0,1:T(4,128)} %copy.11), calls=%async_computation | async-start | bytes 1572864 | tf_op jit(solution)/shard_map/all_to_all | solution.py:83
where the time goes:
time: 113 us; the launch traced here: 112 us
  local copies, waits for them, and re-layouts  38.7 us (34%)
  waiting for transfers between devices  24.4 us (22%)
  matrix products  20.8 us (18%)
  starting transfers between devices  16.2 us (14%)
  other arithmetic  11.1 us (10%)
    dot_general x8, matrix products, lookup(): looked_up = jnp.dot(stacked, onehot, preferred_element_type=jnp.float32)  20.4 us
    all_to_all x1, waiting for transfers between devices, shards(): lax.all_to_all(color_part, 'gz', split_axis=1, concat_axis=1, tiled=True)  18.3 us
    dynamic_update_slice x8, local copies, waits for them, and re-layouts, shards(): lax.map(lookup, (as_blocks(bin_index), as_blocks(fraction), as_blocks(sha...  15.5 us
    dynamic_slice x8, local copies, waits for them, and re-layouts, shards(): lax.map(lookup, (as_blocks(bin_index), as_blocks(fraction), as_blocks(sha...  8.75 us
    all_to_all x1, starting transfers between devices, shards(): lax.all_to_all(keep_part, 'gz', split_axis=1, concat_axis=1, tiled=True)  8.31 us
    all_to_all x1, waiting for transfers between devices, shards(): lax.all_to_all(keep_part, 'gz', split_axis=1, concat_axis=1, tiled=True)  6.06 us
    add x1, other arithmetic, shading_from(): return 0.25 + 0.75 * facing * facing / (squared + 1.0)  4.41 us
    reshape x3, local copies, waits for them, and re-layouts, as_blocks(): return values.reshape(block_count, block_cells)  4.21 us
  transfers between devices with their start and end apart: 4, of which 2 were waited for; matrix products, arithmetic and copies ran while one was open for 10% of the time, Pallas kernels for 0%

commit v1 on v0

v1 whole, which is shorter than its diff:
```python
import jax
import jax.numpy as jnp
from jax import lax
from jax.experimental import pallas as pl
from jax.experimental.pallas import tpu as pltpu
from jax.sharding import PartitionSpec as P

SUB, LANES = 8, 128


def pack_kernel(field_ref, out_ref):
    depth, rows, cols = field_ref.shape
    chunks = cols // LANES
    for k in range(depth):
        for j in range(rows // SUB):
            for c in range(chunks):
                tile = field_ref[k, j * SUB:(j + 1) * SUB, c * LANES:(c + 1) * LANES]
                base = (j * SUB * depth + k) * chunks + c
                out_ref[pl.ds(base, SUB, stride=depth * chunks), :] = tile


def packed(field):
    depth, rows, cols = field.shape
    shape = (rows * depth * (cols // LANES), LANES)
    return pl.pallas_call(
        pack_kernel,
        out_shape=jax.ShapeDtypeStruct(shape, field.dtype),
        in_specs=[pl.BlockSpec(memory_space=pltpu.VMEM)],
        out_specs=pl.BlockSpec(memory_space=pltpu.VMEM),
        compiler_params=pltpu.CompilerParams(vmem_limit_bytes=16 << 20),
        name="pack_rows",
    )(field)


def shared(x, axis, shift):
    return pltpu.roll(x, shift % x.shape[axis], axis)


def composite_kernel(order_ref, light_ref, color_ref, opacity_ref, tile_ref, up_ref, down_ref,
                     out_ref, brick_at, staged):
    bricks, rows, depth, chunks, _ = tile_ref.shape
    bins = color_ref.shape[1] - 1
    halves = bins // LANES
    shape = (chunks, LANES)

    def place(b, carry):
        brick_at[order_ref[b]] = b
        return carry

    lax.fori_loop(0, bricks, place, 0)

    table = jnp.concatenate(
        [color_ref[...].astype(jnp.float32), opacity_ref[...].astype(jnp.float32)], axis=0)
    lower = table[:, :bins]
    slope = table[:, 1:] - lower

    def spread(values, channel, half):
        row = values[channel:channel + 1, half * LANES:(half + 1) * LANES]
        return jnp.broadcast_to(row, shape)

    lows = [[spread(lower, c, h) for h in range(halves)] for c in range(4)]
    slopes = [[spread(slope, c, h) for h in range(halves)] for c in range(4)]
    light = [light_ref[i] for i in range(3)]
    lane = lax.broadcasted_iota(jnp.int32, shape, 1)
    chunk = lax.broadcasted_iota(jnp.int32, shape, 0)
    at_first, at_last = lane == 0, lane == LANES - 1
    at_left = at_first & (chunk == 0)
    at_right = at_last & (chunk == chunks - 1)

    def pick(tables, low_bits, upper_half):
        found = [jnp.take_along_axis(t, low_bits, axis=1, mode="promise_in_bounds") for t in tables]
        result = found[0]
        for h in range(1, halves):
            result = jnp.where(upper_half[h - 1], found[h], result)
        return result

    def column_gradient(x):
        right = shared(x, 1, -1)
        right = jnp.where(at_last, shared(right, 0, -1), right)
        right = jnp.where(at_right, 0.0, right)
        left = shared(x, 1, 1)
        left = jnp.where(at_first, shared(left, 0, 1), left)
        left = jnp.where(at_left, 0.0, left)
        return right - left

    def step(position, carry):
        colors, keeps = carry
        b = brick_at[position]
        colors, keeps = list(colors), list(keeps)
        for r in range(rows):
            field = [tile_ref[b, r, k] for k in range(depth)]
            depth_gradient = {}
            for k in range(depth):
                ends = (min(k + 1, depth - 1), max(k - 1, 0))
                if ends not in depth_gradient:
                    depth_gradient[ends] = field[ends[0]] - field[ends[1]]
                dz = depth_gradient[ends]
                above = tile_ref[b, r - 1, k] if r > 0 else up_ref[b, k]
                below = tile_ref[b, r + 1, k] if r + 1 < rows else down_ref[b, k]
                dy = below - above
                x = field[k]
                dx = column_gradient(x)
                facing = dz * light[0] + dy * light[1] + dx * light[2]
                squared = dz * dz + dy * dy + dx * dx
                shading = 0.25 + 0.75 * facing * facing / (squared + 1.0)
                scaled = x * float(bins)
                index = jnp.minimum(scaled.astype(jnp.int32), bins - 1)
                fraction = scaled - index.astype(jnp.float32)
                low_bits = index & (LANES - 1)
                upper_half = [index >= h * LANES for h in range(1, halves)]
                blend = [
                    pick(lows[c], low_bits, upper_half)
                    + fraction * pick(slopes[c], low_bits, upper_half)
                    for c in range(4)
                ]
                weight = keeps[r] * blend[3] * shading
                for c in range(3):
                    colors[c * rows + r] = colors[c * rows + r] + weight * blend[c]
                keeps[r] = keeps[r] - keeps[r] * blend[3]
        return tuple(colors), tuple(keeps)

    zero, one = jnp.zeros(shape, jnp.float32), jnp.ones(shape, jnp.float32)
    colors, keeps = lax.fori_loop(0, bricks, step, ((zero,) * (3 * rows), (one,) * rows))
    for i, value in enumerate(list(colors) + [1.0 - k for k in keeps]):
        staged[i * chunks:(i + 1) * chunks, :] = value
    for c in range(4):
        for q in range(chunks):
            out_ref[c, 0, :, q * LANES:(q + 1) * LANES] = staged[
                pl.ds(c * rows * chunks + q, rows, stride=chunks), :]


def composite(view_order, light_dir, color_table, opacity_table, tiles, up, down):
    bricks, rows, depth, chunks, lanes = tiles.shape
    vmem = pl.BlockSpec(memory_space=pltpu.VMEM)
    smem = pl.BlockSpec(memory_space=pltpu.SMEM)
    return pl.pallas_call(
        composite_kernel,
        out_shape=jax.ShapeDtypeStruct((4, 1, rows, chunks * lanes), jnp.float32),
        in_specs=[smem, smem, vmem, vmem, vmem, vmem, vmem],
        out_specs=vmem,
        scratch_shapes=[
            pltpu.SMEM((bricks,), jnp.int32),
            pltpu.VMEM((4 * rows * chunks, lanes), jnp.float32),
        ],
        compiler_params=pltpu.CompilerParams(vmem_limit_bytes=32 << 20),
        name="composite_bricks",
    )(view_order, light_dir, color_table, opacity_table[None, :], tiles, up, down)


def shards(scalar, bin_index, color_table, opacity_table, light_dir, view_order):
    depth, rows, cols = scalar.shape
    bricks, bands = lax.axis_size("gz"), lax.axis_size("gy")
    tile_rows = rows // bricks
    chunks = cols // LANES
    sent = packed(scalar).reshape(bricks, tile_rows, depth, chunks, LANES)
    tiles = lax.all_to_all(sent, "gz", split_axis=0, concat_axis=0, tiled=True)
    along = [t * bands + g for g in range(bands) for t in range(bricks)]
    ahead = list(zip(along[:-1], along[1:]))
    back = [(j, i) for i, j in ahead]
    up = lax.ppermute(tiles[:, -1], ("gz", "gy"), ahead)
    down = lax.ppermute(tiles[:, 0], ("gz", "gy"), back)
    return composite(view_order, light_dir, color_table, opacity_table, tiles, up, down)


def solution(mesh):
    in_specs = (P("gz", "gy", None), P("gz", "gy", None), P(), P(), P(), P())
    out_specs = P(None, "gy", "gz", None)
    return jax.shard_map(shards, mesh=mesh, in_specs=in_specs, out_specs=out_specs, check_vma=False)
```

time: 113 us -> 41.4 us (0.37)
  the two profiles are of different devices: /device:TPU:0 before, /device:TPU:6 now
where the time goes in v1:
time: 41.4 us; the launch traced here: 41.2 us
  blocking collectives  20.3 us (49%)
  waiting for transfers between devices  6.71 us (16%)
  starting transfers between devices  6.54 us (16%)
  Pallas kernels  6.48 us (16%)
  local copies, waits for them, and re-layouts  1.09 us (3%)
    all_to_all x1, blocking collectives, shards(): tiles = lax.all_to_all(sent, 'gz', split_axis=0, concat_axis=0, tiled=True)  20.3 us
    pallas_call x1, Pallas kernels, composite(): pl.pallas_call(composite_kernel, out_shape=jax.ShapeDtypeStruct((4, 1, ro...  6.33 us
    ppermute x1, waiting for transfers between devices, shards(): down = lax.ppermute(tiles[:, 0], ('gz', 'gy'), back)  6.17 us
    ppermute x1, starting transfers between devices, shards(): up = lax.ppermute(tiles[:, -1], ('gz', 'gy'), ahead)  4.62 us
    ppermute x1, starting transfers between devices, shards(): down = lax.ppermute(tiles[:, 0], ('gz', 'gy'), back)  1.92 us
    unnamed x10, local copies, waits for them, and re-layouts  1.06 us
  transfers between devices with their start and end apart: 2, of which 2 were waited for; matrix products, arithmetic and copies ran while one was open for 0% of the time, Pallas kernels for 0%

profile of v1, /device:TPU:6, one launch (start us, length us, event | category | flops | bytes accessed | tf_op | source)
XLA Modules:
  0.0 41.2 jit_solution(6128425570468562683)
XLA Ops:
  0.0 0.0 copy-start
  0.0 1.0 %copy-done = f32[2,64,1024]{2,1,0:T(8,128)S(1)} copy-done((f32[2,64,1024]{2,1,0:T(8,128)S(1)}, f32[2,64,1024]{2,1,0:T(8,128)}, u32[]{:S(2)}) %copy-start) | copy-done | bytes 524312
  1.0 0.1 pack_rows.1
  1.2 20.3 %all_to_all.5.tile_ref = f32[16,4,2,8,128]{4,3,2,1,0:T(8,128)S(1)} all-to-all(f32[16,4,2,8,128]{4,3,2,1,0:T(8,128)S(1)} %bitcast.9), channel_id=1, replica_groups=mesh['gz'=16,'gy'=2] {'gz'}, dimensions={0} | all-to-all | bytes 1048576 | tf_op jit(solution)/shard_map/all_to_all | solution.py:156
  21.5 0.0 copy-start.4
  21.5 0.0 copy-start.1
  21.5 4.6 %collective-permute-start = (f32[16,2,8,128]{3,2,1,0:T(8,128)S(1)}, f32[16,2,8,128]{3,2,1,0:T(8,128)S(1)}, u32[]{:S(2)}, u32[]{:S(2)}) collective-permute-start(f32[16,2,8,128]{3,2,1,0:T(8,128)S(1)} %get-tuple-element.6), channel_id=1, source_target_pairs={{0,2},{2,4},{4,6},{6,8},{8,10},{10,12},{12,14},{14,16},{16,18},{18... | collective-permute-start | bytes 393224 | tf_op jit(solution)/shard_map/ppermute | solution.py:160
  26.1 0.0 copy-start.2
  26.1 0.0 copy-start.3
  26.2 1.9 %collective-permute-start.1 = (f32[16,2,8,128]{3,2,1,0:T(8,128)S(1)}, f32[16,2,8,128]{3,2,1,0:T(8,128)S(1)}, u32[]{:S(2)}, u32[]{:S(2)}) collective-permute-start(f32[16,2,8,128]{3,2,1,0:T(8,128)S(1)} %get-tuple-element.5), channel_id=1, source_target_pairs={{2,0},{4,2},{6,4},{8,6},{10,8},{12,10},{14,12},{16,14},{18,16},{20... | collective-permute-start | bytes 393224 | tf_op jit(solution)/shard_map/ppermute | solution.py:161
  28.1 0.0 copy-done.4
  28.1 0.5 %collective-permute-done.up_ref = f32[16,2,8,128]{3,2,1,0:T(8,128)S(1)} collective-permute-done((f32[16,2,8,128]{3,2,1,0:T(8,128)S(1)}, f32[16,2,8,128]{3,2,1,0:T(8,128)S(1)}, u32[]{:S(2)}, u32[]{:S(2)}) %collective-permute-start) | collective-permute-done | bytes 131104 | tf_op jit(solution)/shard_map/ppermute | solution.py:160
  28.6 6.2 %collective-permute-done.1.down_ref = f32[16,2,8,128]{3,2,1,0:T(8,128)S(1)} collective-permute-done((f32[16,2,8,128]{3,2,1,0:T(8,128)S(1)}, f32[16,2,8,128]{3,2,1,0:T(8,128)S(1)}, u32[]{:S(2)}, u32[]{:S(2)}) %collective-permute-start.1) | collective-permute-done | bytes 131104 | tf_op jit(solution)/shard_map/ppermute | solution.py:161
  34.8 0.0 copy-done.1
  34.8 0.0 copy-done.2
  34.8 0.0 copy-done.3
  34.8 6.3 %composite_bricks.1 = f32[4,1,4,1024]{3,2,1,0:T(4,128)} custom-call(s32[16]{0:T(128)S(1)} %copy-done.2, f32[3]{0:T(128)S(1)} %copy-done.3, bf16[3,257]{1,0:T(4,128)(2,1)S(1)} %copy-done.1, bf16[1,257]{1,0:T(2,128)(2,1)S(1)} %broadcast_in_dim.3.opacity_ref, f32[16,4,2,8,128]{4,3,2,1,0:T(8,128)S(1)} %all_to_all.5.tile_ref, ...), custom_call_target="tpu_custom_call" | custom-call | tf_op jit(solution)/shard_map/composite_bricks/pallas_call | solution.py:136
  (2 shorter events, 0.0 us)
Async XLA Ops:
  0.0 1.0 %copy-start = (f32[2,64,1024]{2,1,0:T(8,128)S(1)}, f32[2,64,1024]{2,1,0:T(8,128)}, u32[]{:S(2)}) copy-start(f32[2,64,1024]{2,1,0:T(8,128)} %field_ref.1) | copy-start | bytes 1572868
  21.5 6.6 %copy-start.4 = (bf16[257]{0:T(512)(128)(2,1)S(1)}, bf16[257]{0:T(512)(128)(2,1)}, u32[]{:S(2)}) copy-start(bf16[257]{0:T(512)(128)(2,1)} %param.8) | copy-start | bytes 1546
  21.5 13.3 %copy-start.1 = (bf16[3,257]{1,0:T(4,128)(2,1)S(1)}, bf16[3,257]{1,0:T(4,128)(2,1)}, u32[]{:S(2)}) copy-start(bf16[3,257]{1,0:T(4,128)(2,1)} %color_ref.1) | copy-start | bytes 4630
  21.5 7.1 %collective-permute-start = (f32[16,2,8,128]{3,2,1,0:T(8,128)S(1)}, f32[16,2,8,128]{3,2,1,0:T(8,128)S(1)}, u32[]{:S(2)}, u32[]{:S(2)}) collective-permute-start(f32[16,2,8,128]{3,2,1,0:T(8,128)S(1)} %get-tuple-element.6), channel_id=1, source_target_pairs={{0,2},{2,4},{4,6},{6,8},{8,10},{10,12},{12,14},{14,16},{16,18},{18... | collective-permute-start | bytes 393224 | tf_op jit(solution)/shard_map/ppermute | solution.py:160
  26.1 8.7 %copy-start.2 = (s32[16]{0:T(128)S(1)}, s32[16]{0:T(128)}, u32[]{:S(2)}) copy-start(s32[16]{0:T(128)} %order_ref.1) | copy-start | bytes 196
  26.1 8.7 %copy-start.3 = (f32[3]{0:T(128)S(1)}, f32[3]{0:T(128)}, u32[]{:S(2)}) copy-start(f32[3]{0:T(128)} %light_ref.1) | copy-start | bytes 40
  26.2 8.7 %collective-permute-start.1 = (f32[16,2,8,128]{3,2,1,0:T(8,128)S(1)}, f32[16,2,8,128]{3,2,1,0:T(8,128)S(1)}, u32[]{:S(2)}, u32[]{:S(2)}) collective-permute-start(f32[16,2,8,128]{3,2,1,0:T(8,128)S(1)} %get-tuple-element.5), channel_id=1, source_target_pairs={{2,0},{4,2},{6,4},{8,6},{10,8},{12,10},{14,12},{16,14},{18,16},{20... | collective-permute-start | bytes 393224 | tf_op jit(solution)/shard_map/ppermute | solution.py:161

commit v2 on v1

v2 whole, which is shorter than its diff:
```python
import functools

import jax
import jax.numpy as jnp
from jax import lax
from jax.experimental import pallas as pl
from jax.experimental.pallas import tpu as pltpu
from jax.sharding import PartitionSpec as P

SUB, LANES = 8, 128


def pack_kernel(row_groups, field_ref, *rest):
    *out_refs, staged = rest
    depth, rows, cols = field_ref.shape
    chunks = cols // LANES
    tile_rows = sum(len(group) for group in row_groups)
    block = depth * chunks
    for k in range(depth):
        for j in range(rows // SUB):
            for c in range(chunks):
                lines = field_ref[k, j * SUB:(j + 1) * SUB, c * LANES:(c + 1) * LANES]
                staged[pl.ds(j * SUB * block + k * chunks + c, SUB, stride=block), :] = lines
    for group, out_ref in zip(row_groups, out_refs):
        for t in range(rows // tile_rows):
            for i, r in enumerate(group):
                source, target = (t * tile_rows + r) * block, (t * len(group) + i) * block
                out_ref[target:target + block, :] = staged[source:source + block, :]


def packed(field, tiles, row_groups):
    depth, rows, cols = field.shape
    chunks = cols // LANES
    shapes = [(tiles * len(group) * depth * chunks, LANES) for group in row_groups]
    vmem = pl.BlockSpec(memory_space=pltpu.VMEM)
    flat = pl.pallas_call(
        functools.partial(pack_kernel, row_groups),
        out_shape=[jax.ShapeDtypeStruct(shape, field.dtype) for shape in shapes],
        in_specs=[vmem],
        out_specs=[vmem] * len(shapes),
        scratch_shapes=[pltpu.VMEM((rows * depth * chunks, LANES), field.dtype)],
        compiler_params=pltpu.CompilerParams(vmem_limit_bytes=16 << 20),
        name="pack_rows",
    )(field)
    return [x.reshape(tiles, len(group), depth, chunks, LANES) for x, group in zip(flat, row_groups)]


def shifted(x, axis, shift):
    return pltpu.roll(x, shift % x.shape[axis], axis)


def brick_positions(order_ref, brick_at):
    def place(b, carry):
        brick_at[order_ref[b]] = b
        return carry

    lax.fori_loop(0, order_ref.shape[0], place, 0)


def table_lookup(color_ref, opacity_ref, shape):
    bins = color_ref.shape[1] - 1
    halves = bins // LANES
    table = jnp.concatenate(
        [color_ref[...].astype(jnp.float32), opacity_ref[...].astype(jnp.float32)], axis=0)
    lower = table[:, :bins]
    slope = table[:, 1:] - lower

    def spread(values, channel, half):
        row = values[channel:channel + 1, half * LANES:(half + 1) * LANES]
        return jnp.broadcast_to(row, shape)

    lows = [[spread(lower, c, h) for h in range(halves)] for c in range(4)]
    slopes = [[spread(slope, c, h) for h in range(halves)] for c in range(4)]

    def pick(tables, low_bits, upper_half):
        found = [jnp.take_along_axis(t, low_bits, axis=1, mode="promise_in_bounds") for t in tables]
        result = found[0]
        for h in range(1, halves):
            result = jnp.where(upper_half[h - 1], found[h], result)
        return result

    def look_up(x):
        scaled = x * float(bins)
        index = jnp.minimum(scaled.astype(jnp.int32), bins - 1)
        fraction = scaled - index.astype(jnp.float32)
        low_bits = index & (LANES - 1)
        upper_half = [index >= h * LANES for h in range(1, halves)]
        blend = [
            pick(lows[c], low_bits, upper_half) + fraction * pick(slopes[c], low_bits, upper_half)
            for c in range(4)
        ]
        return blend[:3], blend[3]

    return look_up


def column_differences(shape):
    lane = lax.broadcasted_iota(jnp.int32, shape, 1)
    chunk = lax.broadcasted_iota(jnp.int32, shape, 0)
    at_first, at_last = lane == 0, lane == shape[1] - 1
    at_left = at_first & (chunk == 0)
    at_right = at_last & (chunk == shape[0] - 1)

    def difference(x):
        right = shifted(x, 1, -1)
        right = jnp.where(at_last, shifted(right, 0, -1), right)
        right = jnp.where(at_right, 0.0, right)
        left = shifted(x, 1, 1)
        left = jnp.where(at_first, shifted(left, 0, 1), left)
        left = jnp.where(at_left, 0.0, left)
        return right - left

    return difference


def depth_differences(field):
    last = len(field) - 1
    made = {}
    for k in range(last + 1):
        ends = (min(k + 1, last), max(k - 1, 0))
        if ends not in made:
            made[ends] = field[ends[0]] - field[ends[1]]
    return [made[(min(k + 1, last), max(k - 1, 0))] for k in range(last + 1)]


def shading_of(facing, squared_plus_one):
    return 0.25 + 0.75 * facing * facing / squared_plus_one


def edge_kernel(order_ref, light_ref, color_ref, opacity_ref, edge_ref, part_ref, keep_ref, brick_at):
    bricks, rows, depth, chunks, lanes = edge_ref.shape
    shape = (chunks, lanes)
    brick_positions(order_ref, brick_at)
    look_up = table_lookup(color_ref, opacity_ref, shape)
    column_difference = column_differences(shape)
    light = [light_ref[i] for i in range(3)]

    def step(position, keeps):
        b = brick_at[position]
        keeps = list(keeps)
        for r in range(rows):
            field = [edge_ref[b, r, k] for k in range(depth)]
            for k, (x, dz) in enumerate(zip(field, depth_differences(field))):
                dx = column_difference(x)
                color, opacity = look_up(x)
                weight = keeps[r] * opacity
                for c in range(3):
                    part_ref[b, r, k, c] = weight * color[c]
                part_ref[b, r, k, 3] = dz * light[0] + dx * light[2]
                part_ref[b, r, k, 4] = dz * dz + dx * dx + 1.0
                keeps[r] = keeps[r] - weight
        return tuple(keeps)

    keeps = lax.fori_loop(0, bricks, step, (jnp.ones(shape, jnp.float32),) * rows)
    for r in range(rows):
        keep_ref[r] = keeps[r]


def finish_kernel(edge_rows, order_ref, light_ref, color_ref, opacity_ref, edge_ref, part_ref, keep_ref,
                  up_ref, down_ref, *rest):
    inner_ref = rest[0] if len(rest) == 4 else None
    out_ref, brick_at, staged = rest[-3:]
    bricks, _, depth, chunks, lanes = edge_ref.shape
    shape = (chunks, lanes)
    rows = out_ref.shape[2]
    inner_rows = [r for r in range(rows) if r not in edge_rows]
    brick_positions(order_ref, brick_at)
    look_up = table_lookup(color_ref, opacity_ref, shape)
    column_difference = column_differences(shape)
    light = [light_ref[i] for i in range(3)]

    def load(b, r, k):
        if r < 0:
            return up_ref[b, k]
        if r >= rows:
            return down_ref[b, k]
        if r in edge_rows:
            return edge_ref[b, edge_rows.index(r), k]
        return inner_ref[b, inner_rows.index(r), k]

    def step(position, carry):
        colors, keeps = carry
        b = brick_at[position]
        colors, keeps = list(colors), list(keeps)
        for r in inner_rows:
            field = [load(b, r, k) for k in range(depth)]
            for k, (x, dz) in enumerate(zip(field, depth_differences(field))):
                dy = load(b, r + 1, k) - load(b, r - 1, k)
                dx = column_difference(x)
                facing = dz * light[0] + dy * light[1] + dx * light[2]
                squared = dz * dz + dy * dy + dx * dx
                color, opacity = look_up(x)
                weight = keeps[inner_rows.index(r)] * opacity
                shaded = weight * shading_of(facing, squared + 1.0)
                for c in range(3):
                    colors[c * rows + r] = colors[c * rows + r] + shaded * color[c]
                keeps[inner_rows.index(r)] = keeps[inner_rows.index(r)] - weight
        for i, r in enumerate(edge_rows):
            for k in range(depth):
                dy = load(b, r + 1, k) - load(b, r - 1, k)
                shading = shading_of(part_ref[b, i, k, 3] + dy * light[1], part_ref[b, i, k, 4] + dy * dy)
                for c in range(3):
                    colors[c * rows + r] = colors[c * rows + r] + shading * part_ref[b, i, k, c]
        return tuple(colors), tuple(keeps)

    zero, one = jnp.zeros(shape, jnp.float32), jnp.ones(shape, jnp.float32)
    colors, keeps = lax.fori_loop(
        0, bricks, step, ((zero,) * (3 * rows), (one,) * len(inner_rows)))
    kept = [keep_ref[edge_rows.index(r)] if r in edge_rows else keeps[inner_rows.index(r)]
            for r in range(rows)]
    for i, value in enumerate(list(colors) + [1.0 - k for k in kept]):
        staged[i * chunks:(i + 1) * chunks, :] = value
    for c in range(4):
        for q in range(chunks):
            source = pl.ds(c * rows * chunks + q, rows, stride=chunks) if rows > 1 else pl.ds(c * chunks + q, 1)
            out_ref[c, 0, :, q * LANES:(q + 1) * LANES] = staged[source, :]


def shards(scalar, bin_index, color_table, opacity_table, light_dir, view_order):
    depth, rows, cols = scalar.shape
    bricks, bands = lax.axis_size("gz"), lax.axis_size("gy")
    tile_rows = rows // bricks
    chunks = cols // LANES
    edge_rows = sorted({0, tile_rows - 1})
    inner_rows = [r for r in range(tile_rows) if r not in edge_rows]
    groups = [edge_rows] + ([inner_rows] if inner_rows else [])
    edges, *inner = [
        lax.all_to_all(x, "gz", split_axis=0, concat_axis=0, tiled=True)
        for x in packed(scalar, bricks, groups)
    ]
    along = [t * bands + g for g in range(bands) for t in range(bricks)]
    ahead = list(zip(along[:-1], along[1:]))
    back = [(j, i) for i, j in ahead]
    up = lax.ppermute(edges[:, -1], ("gz", "gy"), ahead)
    down = lax.ppermute(edges[:, 0], ("gz", "gy"), back)

    vmem = pl.BlockSpec(memory_space=pltpu.VMEM)
    smem = pl.BlockSpec(memory_space=pltpu.SMEM)
    tables = (view_order, light_dir, color_table, opacity_table[None, :])
    table_specs = [smem, smem, vmem, vmem]
    params = pltpu.CompilerParams(vmem_limit_bytes=32 << 20)
    order_scratch = pltpu.SMEM((bricks,), jnp.int32)
    cells = bricks * depth * cols
    parts, keeps = pl.pallas_call(
        edge_kernel,
        out_shape=[
            jax.ShapeDtypeStruct((bricks, len(edge_rows), depth, 5, chunks, LANES), jnp.float32),
            jax.ShapeDtypeStruct((len(edge_rows), chunks, LANES), jnp.float32),
        ],
        in_specs=table_specs + [vmem],
        out_specs=[vmem, vmem],
        scratch_shapes=[order_scratch],
        compiler_params=params,
        cost_estimate=pl.CostEstimate(
            flops=100 * cells * len(edge_rows), bytes_accessed=24 * cells * len(edge_rows), transcendentals=0),
        name="edge_rows",
    )(*tables, edges)
    return pl.pallas_call(
        functools.partial(finish_kernel, edge_rows),
        out_shape=jax.ShapeDtypeStruct((4, 1, tile_rows, cols), jnp.float32),
        in_specs=table_specs + [vmem] * (5 + len(inner)),
        out_specs=vmem,
        scratch_shapes=[order_scratch, pltpu.VMEM((4 * tile_rows * chunks, LANES), jnp.float32)],
        compiler_params=params,
        cost_estimate=pl.CostEstimate(
            flops=100 * cells * tile_rows, bytes_accessed=24 * cells * tile_rows, transcendentals=0),
        name="inner_rows",
    )(*tables, edges, parts, keeps, up, down, *inner)


def solution(mesh):
    in_specs = (P("gz", "gy", None), P("gz", "gy", None), P(), P(), P(), P())
    out_specs = P(None, "gy", "gz", None)
    return jax.shard_map(shards, mesh=mesh, in_specs=in_specs, out_specs=out_specs, check_vma=False)
```

time: 41.4 us -> 45.7 us (1.10)
  the two profiles are of different devices: /device:TPU:6 before, /device:TPU:1 now
where the time goes in v2:
time: 45.7 us; the launch traced here: 45.4 us
  starting transfers between devices  15.4 us (34%)
  blocking collectives  15.2 us (33%)
  Pallas kernels  10 us (22%)
  waiting for transfers between devices  3.66 us (8%)
  local copies, waits for them, and re-layouts  1.08 us (2%)
    all_to_all x1, blocking collectives, shards(): lax.all_to_all(x, 'gz', split_axis=0, concat_axis=0, tiled=True)  15.2 us
    ppermute x1, starting transfers between devices, shards(): down = lax.ppermute(edges[:, 0], ('gz', 'gy'), back)  8.64 us
    pallas_call x1, Pallas kernels, shards(): pl.pallas_call(functools.partial(finish_kernel, edge_rows), out_shape=jax...  4.9 us
    all_to_all x1, starting transfers between devices, shards(): lax.all_to_all(x, 'gz', split_axis=0, concat_axis=0, tiled=True)  4.79 us
    pallas_call x1, Pallas kernels, shards(): pl.pallas_call(edge_kernel, out_shape=[jax.ShapeDtypeStruct((bricks, len(...  4.22 us
    ppermute x1, waiting for transfers between devices, shards(): up = lax.ppermute(edges[:, -1], ('gz', 'gy'), ahead)  3.66 us
    ppermute x1, starting transfers between devices, shards(): up = lax.ppermute(edges[:, -1], ('gz', 'gy'), ahead)  1.92 us
    unnamed x10, local copies, waits for them, and re-layouts  1.06 us
  transfers between devices with their start and end apart: 3, of which 1 were waited for; matrix products, arithmetic and copies ran while one was open for 0% of the time, Pallas kernels for 9%

profile of v2, /device:TPU:1, one launch (start us, length us, event | category | flops | bytes accessed | tf_op | source)
XLA Modules:
  0.0 45.4 jit_solution(7132609039701653231)
XLA Ops:
  0.0 0.0 copy-start
  0.0 1.0 %copy-done = f32[2,64,1024]{2,1,0:T(8,128)S(1)} copy-done((f32[2,64,1024]{2,1,0:T(8,128)S(1)}, f32[2,64,1024]{2,1,0:T(8,128)}, u32[]{:S(2)}) %copy-start) | copy-done | bytes 524312
  1.0 0.0 copy-start.4
  1.0 0.0 copy-start.1
  1.0 0.0 copy-start.2
  1.0 0.0 copy-start.3
  1.1 0.9 %pack_rows.1 = (f32[512,128]{1,0:T(8,128)S(1)}, f32[512,128]{1,0:T(8,128)}) custom-call(f32[2,64,1024]{2,1,0:T(8,128)S(1)} %copy-done), custom_call_target="tpu_custom_call" | custom-call | tf_op jit(solution)/shard_map/pack_rows/pallas_call | solution.py:36
  1.9 15.2 %all_to_all.10.edge_ref = f32[16,2,2,8,128]{4,3,2,1,0:T(8,128)S(1)} all-to-all(f32[16,2,2,8,128]{4,3,2,1,0:T(8,128)S(1)} %bitcast.10), channel_id=1, replica_groups=mesh['gz'=16,'gy'=2] {'gz'}, dimensions={0} | all-to-all | bytes 524288 | tf_op jit(solution)/shard_map/all_to_all | solution.py:228
  17.1 4.8 %all-to-all-start.1 = ((f32[16,2,2,8,128]{4,3,2,1,0:T(8,128)}), f32[16,2,2,8,128]{4,3,2,1,0:T(8,128)S(1)}, u32[]{:S(2)}, u32[]{:S(2)}) async-start(f32[16,2,2,8,128]{4,3,2,1,0:T(8,128)} %bitcast.3), calls=%async_computation.1 | async-start | bytes 524288 | tf_op jit(solution)/shard_map/all_to_all | solution.py:228
  21.9 8.6 %collective-permute-start.1 = (f32[16,2,8,128]{3,2,1,0:T(8,128)S(1)}, f32[16,2,8,128]{3,2,1,0:T(8,128)S(1)}, u32[]{:S(2)}, u32[]{:S(2)}) collective-permute-start(f32[16,2,8,128]{3,2,1,0:T(8,128)S(1)} %get-tuple-element.13), channel_id=1, source_target_pairs={{2,0},{4,2},{6,4},{8,6},{10,8},{12,10},{14,12},{16,14},{18,16},{20... | collective-permute-start | bytes 393224 | tf_op jit(solution)/shard_map/ppermute | solution.py:235
  30.6 1.9 %collective-permute-start = (f32[16,2,8,128]{3,2,1,0:T(8,128)S(1)}, f32[16,2,8,128]{3,2,1,0:T(8,128)S(1)}, u32[]{:S(2)}, u32[]{:S(2)}) collective-permute-start(f32[16,2,8,128]{3,2,1,0:T(8,128)S(1)} %get-tuple-element.14), channel_id=1, source_target_pairs={{0,2},{2,4},{4,6},{6,8},{8,10},{10,12},{12,14},{14,16},{16,18},{18... | collective-permute-start | bytes 393224 | tf_op jit(solution)/shard_map/ppermute | solution.py:234
  32.5 0.0 copy-done.4
  32.5 0.0 copy-done.1
  32.6 0.0 copy-done.2
  32.6 0.0 copy-done.3
  32.6 4.2 %edge_rows.1 = (f32[16,2,2,5,8,128]{5,4,3,2,1,0:T(8,128)S(1)}, f32[2,8,128]{2,1,0:T(8,128)S(1)}) custom-call(s32[16]{0:T(128)S(1)} %copy-done.2, f32[3]{0:T(128)S(1)} %copy-done.3, bf16[3,257]{1,0:T(4,128)(2,1)S(1)} %copy-done.1, bf16[1,257]{1,0:T(2,128)(2,1)S(1)} %broadcast_in_dim.3.opacity_ref, f32[16,2,2,8,128]{4,3,2,1,0:T(8,128)S(1)} %all_to_all.10.edge_ref), custom_call_target="tpu_custom_call" | custom-call | flops 6553600 | bytes 1572864 | tf_op jit(solution)/shard_map/edge_rows/pallas_call | solution.py:244
  36.8 0.0 all-to-all-done.1.rest_0_
  36.8 0.0 collective-permute-done.1.down_ref
  36.8 3.7 %collective-permute-done.up_ref = f32[16,2,8,128]{3,2,1,0:T(8,128)S(1)} collective-permute-done((f32[16,2,8,128]{3,2,1,0:T(8,128)S(1)}, f32[16,2,8,128]{3,2,1,0:T(8,128)S(1)}, u32[]{:S(2)}, u32[]{:S(2)}) %collective-permute-start) | collective-permute-done | bytes 131104 | tf_op jit(solution)/shard_map/ppermute | solution.py:234
  40.5 4.9 %inner_rows.1 = f32[4,1,4,1024]{3,2,1,0:T(4,128)} custom-call(s32[16]{0:T(128)S(1)} %copy-done.2, f32[3]{0:T(128)S(1)} %copy-done.3, bf16[3,257]{1,0:T(4,128)(2,1)S(1)} %copy-done.1, bf16[1,257]{1,0:T(2,128)(2,1)S(1)} %broadcast_in_dim.3.opacity_ref, f32[16,2,2,8,128]{4,3,2,1,0:T(8,128)S(1)} %all_to_all.10.edge_ref, ...), custom_call_target="tpu_custom_call" | custom-call | flops 13107200 | bytes 3145728 | tf_op jit(solution)/shard_map/inner_rows/pallas_call | solution.py:258
  (2 shorter events, 0.0 us)
Async XLA Ops:
  0.0 1.0 %copy-start = (f32[2,64,1024]{2,1,0:T(8,128)S(1)}, f32[2,64,1024]{2,1,0:T(8,128)}, u32[]{:S(2)}) copy-start(f32[2,64,1024]{2,1,0:T(8,128)} %field_ref.1) | copy-start | bytes 1572868
  1.0 31.5 %copy-start.4 = (bf16[257]{0:T(512)(128)(2,1)S(1)}, bf16[257]{0:T(512)(128)(2,1)}, u32[]{:S(2)}) copy-start(bf16[257]{0:T(512)(128)(2,1)} %param.8) | copy-start | bytes 1546
  1.0 31.5 %copy-start.1 = (bf16[3,257]{1,0:T(4,128)(2,1)S(1)}, bf16[3,257]{1,0:T(4,128)(2,1)}, u32[]{:S(2)}) copy-start(bf16[3,257]{1,0:T(4,128)(2,1)} %color_ref.3) | copy-start | bytes 4630
  1.0 31.5 %copy-start.2 = (s32[16]{0:T(128)S(1)}, s32[16]{0:T(128)}, u32[]{:S(2)}) copy-start(s32[16]{0:T(128)} %order_ref.3) | copy-start | bytes 196
  1.0 31.5 %copy-start.3 = (f32[3]{0:T(128)S(1)}, f32[3]{0:T(128)}, u32[]{:S(2)}) copy-start(f32[3]{0:T(128)} %light_ref.3) | copy-start | bytes 40
  17.1 19.7 %all-to-all-start.1 = ((f32[16,2,2,8,128]{4,3,2,1,0:T(8,128)}), f32[16,2,2,8,128]{4,3,2,1,0:T(8,128)S(1)}, u32[]{:S(2)}, u32[]{:S(2)}) async-start(f32[16,2,2,8,128]{4,3,2,1,0:T(8,128)} %bitcast.3), calls=%async_computation.1 | async-start | bytes 524288 | tf_op jit(solution)/shard_map/all_to_all | solution.py:228
  21.9 14.9 %collective-permute-start.1 = (f32[16,2,8,128]{3,2,1,0:T(8,128)S(1)}, f32[16,2,8,128]{3,2,1,0:T(8,128)S(1)}, u32[]{:S(2)}, u32[]{:S(2)}) collective-permute-start(f32[16,2,8,128]{3,2,1,0:T(8,128)S(1)} %get-tuple-element.13), channel_id=1, source_target_pairs={{2,0},{4,2},{6,4},{8,6},{10,8},{12,10},{14,12},{16,14},{18,16},{20... | collective-permute-start | bytes 393224 | tf_op jit(solution)/shard_map/ppermute | solution.py:235
  30.6 9.9 %collective-permute-start = (f32[16,2,8,128]{3,2,1,0:T(8,128)S(1)}, f32[16,2,8,128]{3,2,1,0:T(8,128)S(1)}, u32[]{:S(2)}, u32[]{:S(2)}) collective-permute-start(f32[16,2,8,128]{3,2,1,0:T(8,128)S(1)} %get-tuple-element.14), channel_id=1, source_target_pairs={{0,2},{2,4},{4,6},{6,8},{8,10},{10,12},{12,14},{14,16},{16,18},{18... | collective-permute-start | bytes 393224 | tf_op jit(solution)/shard_map/ppermute | solution.py:234

commit v3 on v2

v3 whole, which is shorter than its diff:
```python
import functools

import jax
import jax.numpy as jnp
from jax import lax
from jax.experimental import pallas as pl
from jax.experimental.pallas import tpu as pltpu
from jax.sharding import PartitionSpec as P

SUB, LANES = 8, 128
COLOR_UNIT, COLOR_SPAN = 2 ** 11, 2 ** 12
OPACITY_UNIT, OPACITY_BITS = 2 ** 18, 16
OPACITY_SPAN = 2 ** OPACITY_BITS


def pack_kernel(field_ref, out_ref, staged):
    depth, rows, cols = field_ref.shape
    tiles, padded_rows, _, chunks, _ = out_ref.shape
    tile_rows = padded_rows - 2
    block = depth * chunks
    for k in range(depth):
        for j in range(rows // SUB):
            for c in range(chunks):
                lines = field_ref[k, j * SUB:(j + 1) * SUB, c * LANES:(c + 1) * LANES]
                staged[pl.ds(j * SUB * block + k * chunks + c, SUB, stride=block), :] = lines
    for t in range(tiles):
        for i in range(padded_rows):
            r = (t * tile_rows + i - 1) % rows
            for k in range(depth):
                start = (r * depth + k) * chunks
                out_ref[t, i, k] = staged[start:start + chunks, :]


def packed(field, tiles):
    depth, rows, cols = field.shape
    chunks = cols // LANES
    vmem = pl.BlockSpec(memory_space=pltpu.VMEM)
    shape = (tiles, rows // tiles + 2, depth, chunks, LANES)
    return pl.pallas_call(
        pack_kernel,
        out_shape=jax.ShapeDtypeStruct(shape, field.dtype),
        in_specs=[vmem],
        out_specs=vmem,
        scratch_shapes=[pltpu.VMEM((rows * depth * chunks, LANES), field.dtype)],
        compiler_params=pltpu.CompilerParams(vmem_limit_bytes=16 << 20),
        name="pack_rows",
    )(field)


def shifted(x, axis, shift):
    return pltpu.roll(x, shift % x.shape[axis], axis)


def brick_positions(order_ref, brick_at):
    def place(b, carry):
        brick_at[order_ref[b]] = b
        return carry

    lax.fori_loop(0, order_ref.shape[0], place, 0)


def table_lookup(color_ref, opacity_ref, shape):
    bins = color_ref.shape[1] - 1
    halves = bins // LANES

    def parts(values, unit):
        scaled = values.astype(jnp.float32) * float(unit)
        return scaled[:, :bins], scaled[:, 1:] - scaled[:, :bins]

    low, slope = parts(color_ref[...], COLOR_UNIT)
    color_words = slope + low * (1.0 / COLOR_SPAN)
    low, slope = parts(opacity_ref[...], OPACITY_UNIT)
    opacity_words = slope.astype(jnp.int32) * OPACITY_SPAN + low.astype(jnp.int32)

    def spread(words):
        return [jnp.broadcast_to(words[:, h * LANES:(h + 1) * LANES], shape) for h in range(halves)]

    tables = [spread(color_words[c:c + 1]) for c in range(3)] + [spread(opacity_words)]

    def look_up(x):
        scaled = x * float(bins)
        index = jnp.minimum(scaled.astype(jnp.int32), bins - 1)
        fraction = scaled - index.astype(jnp.float32)
        low_bits = index & (LANES - 1)
        words = []
        for table in tables:
            word = jnp.take_along_axis(table[0], low_bits, axis=1, mode="promise_in_bounds")
            for h in range(1, halves):
                found = jnp.take_along_axis(table[h], low_bits, axis=1, mode="promise_in_bounds")
                word = jnp.where(index >= h * LANES, found, word)
            words.append(word)
        color = []
        small = fraction * (1.0 / COLOR_SPAN)
        for word in words[:3]:
            rise = jnp.floor(word)
            color.append((word - rise) + small * rise)
        rise = (words[3] >> OPACITY_BITS).astype(jnp.float32)
        start = (words[3] & (OPACITY_SPAN - 1)).astype(jnp.float32)
        return color, (start + fraction * rise) * (1.0 / OPACITY_UNIT)

    return look_up


def column_differences(shape):
    lane = lax.broadcasted_iota(jnp.int32, shape, 1)
    chunk = lax.broadcasted_iota(jnp.int32, shape, 0)
    at_first, at_last = lane == 0, lane == shape[1] - 1
    at_left = at_first & (chunk == 0)
    at_right = at_last & (chunk == shape[0] - 1)

    def difference(x):
        right = shifted(x, 1, -1)
        right = jnp.where(at_last, shifted(right, 0, -1), right)
        right = jnp.where(at_right, 0.0, right)
        left = shifted(x, 1, 1)
        left = jnp.where(at_first, shifted(left, 0, 1), left)
        left = jnp.where(at_left, 0.0, left)
        return right - left

    return difference


def depth_differences(field):
    last = len(field) - 1
    made = {}
    for k in range(last + 1):
        ends = (min(k + 1, last), max(k - 1, 0))
        if ends not in made:
            made[ends] = field[ends[0]] - field[ends[1]]
    return [made[(min(k + 1, last), max(k - 1, 0))] for k in range(last + 1)]


def shading_of(facing, squared_plus_one):
    return 0.25 + 0.75 * facing * facing / squared_plus_one


def main_kernel(edge_rows, order_ref, light_ref, color_ref, opacity_ref, tile_ref,
                part_ref, color_sum_ref, keep_ref, brick_at):
    bricks, padded_rows, depth, chunks, lanes = tile_ref.shape
    rows = padded_rows - 2
    inner_rows = [r for r in range(rows) if r not in edge_rows]
    shape = (chunks, lanes)
    brick_positions(order_ref, brick_at)
    look_up = table_lookup(color_ref, opacity_ref, shape)
    column_difference = column_differences(shape)
    light = [light_ref[i] for i in range(3)]

    def step(position, carry):
        b = brick_at[position]
        colors, keeps = list(carry[0]), list(carry[1])
        for r in range(rows):
            field = [tile_ref[b, r + 1, k] for k in range(depth)]
            for k, (x, dz) in enumerate(zip(field, depth_differences(field))):
                dx = column_difference(x)
                color, opacity = look_up(x)
                weight = keeps[r] * opacity
                facing = dz * light[0] + dx * light[2]
                squared = dz * dz + dx * dx + 1.0
                if r in edge_rows:
                    i = edge_rows.index(r)
                    for c in range(3):
                        part_ref[b, i, k, c] = weight * color[c]
                    part_ref[b, i, k, 3] = facing
                    part_ref[b, i, k, 4] = squared
                else:
                    i = inner_rows.index(r)
                    dy = tile_ref[b, r + 2, k] - tile_ref[b, r, k]
                    shaded = weight * shading_of(facing + dy * light[1], squared + dy * dy)
                    for c in range(3):
                        at = c * len(inner_rows) + i
                        colors[at] = colors[at] + shaded * color[c]
                keeps[r] = keeps[r] - weight
        return tuple(colors), tuple(keeps)

    zero, one = jnp.zeros(shape, jnp.float32), jnp.ones(shape, jnp.float32)
    colors, keeps = lax.fori_loop(0, bricks, step, ((zero,) * (3 * len(inner_rows)), (one,) * rows))
    for i, value in enumerate(colors):
        color_sum_ref[i] = value
    for r, value in enumerate(keeps):
        keep_ref[r] = value


def finish_kernel(edge_rows, ends_ref, light_ref, tile_ref, other_ref, part_ref, color_sum_ref, keep_ref,
                  out_ref, staged):
    bricks, padded_rows, depth, chunks, lanes = tile_ref.shape
    rows = padded_rows - 2
    inner_rows = [r for r in range(rows) if r not in edge_rows]
    shape = (chunks, lanes)
    light_rows = light_ref[1]
    is_first = jnp.full(shape, ends_ref[0], jnp.int32) == 1
    is_last = jnp.full(shape, ends_ref[1], jnp.int32) == 1

    def step(b, colors):
        colors = list(colors)
        for i, r in enumerate(edge_rows):
            for k in range(depth):
                above, below = tile_ref[b, r, k], tile_ref[b, r + 2, k]
                if r == 0:
                    above = jnp.where(is_first, other_ref[b, k], above)
                if r == rows - 1:
                    below = jnp.where(is_last, other_ref[b, k], below)
                dy = below - above
                shading = shading_of(part_ref[b, i, k, 3] + dy * light_rows, part_ref[b, i, k, 4] + dy * dy)
                for c in range(3):
                    at = c * len(edge_rows) + i
                    colors[at] = colors[at] + shading * part_ref[b, i, k, c]
        return tuple(colors)

    zero = jnp.zeros(shape, jnp.float32)
    edge_colors = lax.fori_loop(0, bricks, step, (zero,) * (3 * len(edge_rows)))
    for r in range(rows):
        for c in range(3):
            if r in edge_rows:
                value = edge_colors[c * len(edge_rows) + edge_rows.index(r)]
            else:
                value = color_sum_ref[c * len(inner_rows) + inner_rows.index(r)]
            at = (c * rows + r) * chunks
            staged[at:at + chunks, :] = value * (COLOR_SPAN / COLOR_UNIT)
        at = (3 * rows + r) * chunks
        staged[at:at + chunks, :] = 1.0 - keep_ref[r]
    for c in range(4):
        for q in range(chunks):
            source = pl.ds(c * rows * chunks + q, rows, stride=chunks) if rows > 1 else pl.ds(c * chunks + q, 1)
            out_ref[c, 0, :, q * LANES:(q + 1) * LANES] = staged[source, :]


def shards(scalar, bin_index, color_table, opacity_table, light_dir, view_order):
    depth, rows, cols = scalar.shape
    bricks, bands = lax.axis_size("gz"), lax.axis_size("gy")
    tile_rows = rows // bricks
    chunks = cols // LANES
    edge_rows = sorted({0, tile_rows - 1})
    inner_count = tile_rows - len(edge_rows)
    tiles = lax.all_to_all(packed(scalar, bricks), "gz", split_axis=0, concat_axis=0, tiled=True)

    here = lax.axis_index("gz")
    ends = jnp.stack([here == 0, here == bricks - 1]).astype(jnp.int32)
    last = bricks - 1
    pairs = [(g, g + 1) for g in range(bands - 1)]
    pairs += [(last * bands + g + 1, last * bands + g) for g in range(bands - 1)]
    wrapped = jnp.where(here == 0, tiles[:, 0], tiles[:, -1])
    other = lax.ppermute(wrapped, ("gz", "gy"), pairs)

    vmem = pl.BlockSpec(memory_space=pltpu.VMEM)
    smem = pl.BlockSpec(memory_space=pltpu.SMEM)
    params = pltpu.CompilerParams(vmem_limit_bytes=32 << 20)
    cells = bricks * depth * cols
    parts, color_sums, keeps = pl.pallas_call(
        functools.partial(main_kernel, edge_rows),
        out_shape=[
            jax.ShapeDtypeStruct((bricks, len(edge_rows), depth, 5, chunks, LANES), jnp.float32),
            jax.ShapeDtypeStruct((max(3 * inner_count, 1), chunks, LANES), jnp.float32),
            jax.ShapeDtypeStruct((tile_rows, chunks, LANES), jnp.float32),
        ],
        in_specs=[smem, smem, vmem, vmem, vmem],
        out_specs=[vmem, vmem, vmem],
        scratch_shapes=[pltpu.SMEM((bricks,), jnp.int32)],
        compiler_params=params,
        cost_estimate=pl.CostEstimate(
            flops=100 * cells * tile_rows, bytes_accessed=24 * cells * tile_rows, transcendentals=0),
        name="main_rows",
    )(view_order, light_dir, color_table, opacity_table[None, :], tiles)
    return pl.pallas_call(
        functools.partial(finish_kernel, edge_rows),
        out_shape=jax.ShapeDtypeStruct((4, 1, tile_rows, cols), jnp.float32),
        in_specs=[smem, smem, vmem, vmem, vmem, vmem, vmem],
        out_specs=vmem,
        scratch_shapes=[pltpu.VMEM((4 * tile_rows * chunks, LANES), jnp.float32)],
        compiler_params=params,
        cost_estimate=pl.CostEstimate(
            flops=10 * cells * tile_rows, bytes_accessed=24 * cells * tile_rows, transcendentals=0),
        name="edge_rows",
    )(ends, light_dir, tiles, other, parts, color_sums, keeps)


def solution(mesh):
    in_specs = (P("gz", "gy", None), P("gz", "gy", None), P(), P(), P(), P())
    out_specs = P(None, "gy", "gz", None)
    return jax.shard_map(shards, mesh=mesh, in_specs=in_specs, out_specs=out_specs, check_vma=False)
```

time: 45.7 us -> 38.5 us (0.84)
  the two profiles are of different devices: /device:TPU:1 before, /device:TPU:0 now
where the time goes in v3:
time: 38.5 us; the launch traced here: 38.2 us
  waiting for transfers between devices  19.7 us (51%)
  starting transfers between devices  9.75 us (25%)
  Pallas kernels  7.45 us (19%)
  local copies, waits for them, and re-layouts  1.06 us (3%)
    all_to_all x1, waiting for transfers between devices, shards(): lax.all_to_all(packed(scalar, bricks), 'gz', split_axis=0, concat_axis=0,...  19.7 us
    all_to_all x1, starting transfers between devices, shards(): lax.all_to_all(packed(scalar, bricks), 'gz', split_axis=0, concat_axis=0,...  8.46 us
    pallas_call x1, Pallas kernels, shards(): pl.pallas_call(functools.partial(main_kernel, edge_rows), out_shape=[jax....  4.86 us
    pallas_call x1, Pallas kernels, shards(): pl.pallas_call(functools.partial(finish_kernel, edge_rows), out_shape=jax...  1.5 us
    ppermute x1, starting transfers between devices, shards(): other = lax.ppermute(wrapped, ('gz', 'gy'), pairs)  1.3 us
    pallas_call x1, Pallas kernels, packed(): pl.pallas_call(pack_kernel, out_shape=jax.ShapeDtypeStruct(shape, field.d...  1.09 us
    unnamed x10, local copies, waits for them, and re-layouts  1.06 us
  transfers between devices with their start and end apart: 2, of which 1 were waited for; matrix products, arithmetic and copies ran while one was open for 0% of the time, Pallas kernels for 13%

profile of v3, /device:TPU:0, one launch (start us, length us, event | category | flops | bytes accessed | tf_op | source)
XLA Modules:
  0.0 38.2 jit_solution(2661875743799972078)
XLA Ops:
  0.0 0.0 copy-start
  0.0 1.0 %copy-done = f32[2,64,1024]{2,1,0:T(8,128)S(1)} copy-done((f32[2,64,1024]{2,1,0:T(8,128)S(1)}, f32[2,64,1024]{2,1,0:T(8,128)}, u32[]{:S(2)}) %copy-start) | copy-done | bytes 524312
  1.0 1.1 %pack_rows.1 = f32[16,6,2,8,128]{4,3,2,1,0:T(8,128)} custom-call(f32[2,64,1024]{2,1,0:T(8,128)S(1)} %copy-done), custom_call_target="tpu_custom_call" | custom-call | tf_op jit(solution)/shard_map/pack_rows/pallas_call | solution.py:39
  2.1 0.0 copy-start.4
  2.1 0.0 copy-start.1
  2.1 0.0 copy-start.2
  2.1 0.0 copy-start.3
  2.1 8.5 %all-to-all-start = ((f32[16,6,2,8,128]{4,3,2,1,0:T(8,128)}), f32[16,6,2,8,128]{4,3,2,1,0:T(8,128)S(1)}, u32[]{:S(2)}, u32[]{:S(2)}) async-start(f32[16,6,2,8,128]{4,3,2,1,0:T(8,128)} %pack_rows.1), calls=%async_computation | async-start | bytes 1572864 | tf_op jit(solution)/shard_map/all_to_all | solution.py:234
  10.6 19.7 %all-to-all-done.tile_ref = f32[16,6,2,8,128]{4,3,2,1,0:T(8,128)S(1)} async-done(((f32[16,6,2,8,128]{4,3,2,1,0:T(8,128)}), f32[16,6,2,8,128]{4,3,2,1,0:T(8,128)S(1)}, u32[]{:S(2)}, u32[]{:S(2)}) %all-to-all-start) | async-done | bytes 786464 | tf_op jit(solution)/shard_map/all_to_all | solution.py:234
  30.4 1.3 %collective-permute-start = (f32[16,2,8,128]{3,2,1,0:T(8,128)S(1)}, f32[16,2,8,128]{3,2,1,0:T(8,128)S(1)}, u32[]{:S(2)}, u32[]{:S(2)}) collective-permute-start(f32[16,2,8,128]{3,2,1,0:T(8,128)S(1)} %fusion.1), channel_id=1, source_target_pairs={{0,1},{31,30}} | collective-permute-start | bytes 393224 | tf_op jit(solution)/shard_map/ppermute | solution.py:242
  31.7 0.0 copy-done.4
  31.7 0.1 add_convert_fusion.ends_ref
  31.8 0.0 copy-done.1
  31.8 0.0 copy-done.2
  31.8 0.0 copy-done.3
  31.8 4.9 %main_rows.1 = (f32[16,2,2,5,8,128]{5,4,3,2,1,0:T(8,128)S(1)}, f32[6,8,128]{2,1,0:T(8,128)S(1)}, f32[4,8,128]{2,1,0:T(8,128)S(1)}) custom-call(s32[16]{0:T(128)S(1)} %copy-done.3, f32[3]{0:T(128)S(1)} %copy-done.2, bf16[3,257]{1,0:T(4,128)(2,1)S(1)} %copy-done.1, bf16[1,257]{1,0:T(2,128)(2,1)S(1)} %broadcast_in_dim.3.opacity_ref, ...), custom_call_target="tpu_custom_call" | custom-call | flops 13107200 | bytes 3145728 | tf_op jit(solution)/shard_map/main_rows/pallas_call | solution.py:248
  36.7 0.0 collective-permute-done.other_ref
  36.7 1.5 %edge_rows.1 = f32[4,1,4,1024]{3,2,1,0:T(4,128)} custom-call(s32[2]{0:T(128)S(1)} %add_convert_fusion.ends_ref, f32[3]{0:T(128)S(1)} %copy-done.2, f32[16,6,2,8,128]{4,3,2,1,0:T(8,128)S(1)} %all-to-all-done.tile_ref, f32[16,2,8,128]{3,2,1,0:T(8,128)S(1)} %collective-permute-done.other_ref, f32[16,2,2,5,8,128]{5,4,3,2,1,0:T(8,128)S(1)} %get-tuple-element.8.part_ref, ...), custom_call_target="tpu_custom_call" | custom-call | flops 1310720 | bytes 3145728 | tf_op jit(solution)/shard_map/edge_rows/pallas_call | solution.py:263
  (2 shorter events, 0.0 us)
Async XLA Ops:
  0.0 1.0 %copy-start = (f32[2,64,1024]{2,1,0:T(8,128)S(1)}, f32[2,64,1024]{2,1,0:T(8,128)}, u32[]{:S(2)}) copy-start(f32[2,64,1024]{2,1,0:T(8,128)} %field_ref.1) | copy-start | bytes 1572868
  2.1 29.6 %copy-start.4 = (bf16[257]{0:T(512)(128)(2,1)S(1)}, bf16[257]{0:T(512)(128)(2,1)}, u32[]{:S(2)}) copy-start(bf16[257]{0:T(512)(128)(2,1)} %param.8) | copy-start | bytes 1546
  2.1 29.7 %copy-start.1 = (bf16[3,257]{1,0:T(4,128)(2,1)S(1)}, bf16[3,257]{1,0:T(4,128)(2,1)}, u32[]{:S(2)}) copy-start(bf16[3,257]{1,0:T(4,128)(2,1)} %color_ref.1) | copy-start | bytes 4630
  2.1 29.7 %copy-start.2 = (f32[3]{0:T(128)S(1)}, f32[3]{0:T(128)}, u32[]{:S(2)}) copy-start(f32[3]{0:T(128)} %light_ref.3) | copy-start | bytes 40
  2.1 29.7 %copy-start.3 = (s32[16]{0:T(128)S(1)}, s32[16]{0:T(128)}, u32[]{:S(2)}) copy-start(s32[16]{0:T(128)} %order_ref.1) | copy-start | bytes 196
  2.1 28.2 %all-to-all-start = ((f32[16,6,2,8,128]{4,3,2,1,0:T(8,128)}), f32[16,6,2,8,128]{4,3,2,1,0:T(8,128)S(1)}, u32[]{:S(2)}, u32[]{:S(2)}) async-start(f32[16,6,2,8,128]{4,3,2,1,0:T(8,128)} %pack_rows.1), calls=%async_computation | async-start | bytes 1572864 | tf_op jit(solution)/shard_map/all_to_all | solution.py:234
  30.4 6.3 %collective-permute-start = (f32[16,2,8,128]{3,2,1,0:T(8,128)S(1)}, f32[16,2,8,128]{3,2,1,0:T(8,128)S(1)}, u32[]{:S(2)}, u32[]{:S(2)}) collective-permute-start(f32[16,2,8,128]{3,2,1,0:T(8,128)S(1)} %fusion.1), channel_id=1, source_target_pairs={{0,1},{31,30}} | collective-permute-start | bytes 393224 | tf_op jit(solution)/shard_map/ppermute | solution.py:242

commit v4 on v3

--- a/solution.py
+++ b/solution.py
@@ -20,15 +20,15 @@
     block = depth * chunks
     for k in range(depth):
         for j in range(rows // SUB):
-            for c in range(chunks):
-                lines = field_ref[k, j * SUB:(j + 1) * SUB, c * LANES:(c + 1) * LANES]
-                staged[pl.ds(j * SUB * block + k * chunks + c, SUB, stride=block), :] = lines
+            lines = [field_ref[k, j * SUB:(j + 1) * SUB, c * LANES:(c + 1) * LANES] for c in range(chunks)]
+            for c, value in enumerate(lines):
+                staged[pl.ds(j * SUB * block + k * chunks + c, SUB, stride=block), :] = value
     for t in range(tiles):
-        for i in range(padded_rows):
-            r = (t * tile_rows + i - 1) % rows
+        starts = [((t * tile_rows + i - 1) % rows) * block for i in range(padded_rows)]
+        blocks = [staged[start:start + block, :] for start in starts]
+        for i, value in enumerate(blocks):
             for k in range(depth):
-                start = (r * depth + k) * chunks
-                out_ref[t, i, k] = staged[start:start + chunks, :]
+                out_ref[t, i, k] = value[k * chunks:(k + 1) * chunks]
 
 
 def packed(field, tiles):
@@ -131,7 +131,9 @@
 
 
 def shading_of(facing, squared_plus_one):
-    return 0.25 + 0.75 * facing * facing / squared_plus_one
+    near = pltpu.reciprocal(squared_plus_one, approx=True)
+    inverse = near * (2.0 - squared_plus_one * near)
+    return 0.25 + (0.75 * facing) * (facing * inverse)
 
 
 def main_kernel(edge_rows, order_ref, light_ref, color_ref, opacity_ref, tile_ref,
@@ -144,36 +146,41 @@
     look_up = table_lookup(color_ref, opacity_ref, shape)
     column_difference = column_differences(shape)
     light = [light_ref[i] for i in range(3)]
-
-    def step(position, carry):
-        b = brick_at[position]
+    together = 2 if bricks % 2 == 0 else 1
+
+    def step(trip, carry):
         colors, keeps = list(carry[0]), list(carry[1])
-        for r in range(rows):
-            field = [tile_ref[b, r + 1, k] for k in range(depth)]
-            for k, (x, dz) in enumerate(zip(field, depth_differences(field))):
-                dx = column_difference(x)
-                color, opacity = look_up(x)
-                weight = keeps[r] * opacity
-                facing = dz * light[0] + dx * light[2]
-                squared = dz * dz + dx * dx + 1.0
-                if r in edge_rows:
-                    i = edge_rows.index(r)
-                    for c in range(3):
-                        part_ref[b, i, k, c] = weight * color[c]
-                    part_ref[b, i, k, 3] = facing
-                    part_ref[b, i, k, 4] = squared
-                else:
-                    i = inner_rows.index(r)
-                    dy = tile_ref[b, r + 2, k] - tile_ref[b, r, k]
-                    shaded = weight * shading_of(facing + dy * light[1], squared + dy * dy)
-                    for c in range(3):
-                        at = c * len(inner_rows) + i
-                        colors[at] = colors[at] + shaded * color[c]
-                keeps[r] = keeps[r] - weight
+        at = [brick_at[trip * together + u] for u in range(together)]
+        fields = [[[tile_ref[b, r, k] for k in range(depth)] for r in range(padded_rows)] for b in at]
+        kept = []
+        for b, field in zip(at, fields):
+            for r in range(rows):
+                for k, dz in enumerate(depth_differences(field[r + 1])):
+                    x = field[r + 1][k]
+                    dx = column_difference(x)
+                    color, opacity = look_up(x)
+                    weight = keeps[r] * opacity
+                    facing = dz * light[0] + dx * light[2]
+                    squared = dz * dz + dx * dx + 1.0
+                    if r in edge_rows:
+                        values = [weight * color[c] for c in range(3)] + [facing, squared]
+                        kept.append((b, edge_rows.index(r), k, values))
+                    else:
+                        i = inner_rows.index(r)
+                        dy = field[r + 2][k] - field[r][k]
+                        shaded = weight * shading_of(facing + dy * light[1], squared + dy * dy)
+                        for c in range(3):
+                            slot = c * len(inner_rows) + i
+                            colors[slot] = colors[slot] + shaded * color[c]
+                    keeps[r] = keeps[r] - weight
+        for b, i, k, values in kept:
+            for v, value in enumerate(values):
+                part_ref[b, i, k, v] = value
         return tuple(colors), tuple(keeps)
 
     zero, one = jnp.zeros(shape, jnp.float32), jnp.ones(shape, jnp.float32)
-    colors, keeps = lax.fori_loop(0, bricks, step, ((zero,) * (3 * len(inner_rows)), (one,) * rows))
+    colors, keeps = lax.fori_loop(
+        0, bricks // together, step, ((zero,) * (3 * len(inner_rows)), (one,) * rows))
     for i, value in enumerate(colors):
         color_sum_ref[i] = value
     for r, value in enumerate(keeps):
@@ -190,24 +197,29 @@
     is_first = jnp.full(shape, ends_ref[0], jnp.int32) == 1
     is_last = jnp.full(shape, ends_ref[1], jnp.int32) == 1
 
-    def step(b, colors):
+    together = 4 if bricks % 4 == 0 else 1
+
+    def step(trip, colors):
         colors = list(colors)
-        for i, r in enumerate(edge_rows):
-            for k in range(depth):
-                above, below = tile_ref[b, r, k], tile_ref[b, r + 2, k]
-                if r == 0:
-                    above = jnp.where(is_first, other_ref[b, k], above)
-                if r == rows - 1:
-                    below = jnp.where(is_last, other_ref[b, k], below)
-                dy = below - above
-                shading = shading_of(part_ref[b, i, k, 3] + dy * light_rows, part_ref[b, i, k, 4] + dy * dy)
-                for c in range(3):
-                    at = c * len(edge_rows) + i
-                    colors[at] = colors[at] + shading * part_ref[b, i, k, c]
+        for u in range(together):
+            b = trip * together + u
+            for i, r in enumerate(edge_rows):
+                for k in range(depth):
+                    above, below = tile_ref[b, r, k], tile_ref[b, r + 2, k]
+                    if r == 0:
+                        above = jnp.where(is_first, other_ref[b, k], above)
+                    if r == rows - 1:
+                        below = jnp.where(is_last, other_ref[b, k], below)
+                    dy = below - above
+                    facing = part_ref[b, i, k, 3] + dy * light_rows
+                    shading = shading_of(facing, part_ref[b, i, k, 4] + dy * dy)
+                    for c in range(3):
+                        slot = c * len(edge_rows) + i
+                        colors[slot] = colors[slot] + shading * part_ref[b, i, k, c]
         return tuple(colors)
 
     zero = jnp.zeros(shape, jnp.float32)
-    edge_colors = lax.fori_loop(0, bricks, step, (zero,) * (3 * len(edge_rows)))
+    edge_colors = lax.fori_loop(0, bricks // together, step, (zero,) * (3 * len(edge_rows)))
     for r in range(rows):
         for c in range(3):
             if r in edge_rows:

time: 38.5 us -> 37.3 us (0.969)
  Pallas kernels: 7.45 us -> 6.29 us
    pallas_call x1, Pallas kernels: 4.86 us -> 3.81 us  [shards(): pl.pallas_call(functools.partial(main_kernel, edge_rows), out_shape=[jax....]
  transfers between devices with their start and end apart: 2 -> 2, of which waited for: 1 -> 1; matrix products, arithmetic and copies ran while one was open for 0% -> 0% of each run, Pallas kernels for 13% -> 10%
where the time goes in v4:
time: 37.3 us; the launch traced here: 37 us
  waiting for transfers between devices  19.7 us (53%)
  starting transfers between devices  9.75 us (26%)
  Pallas kernels  6.29 us (17%)
  local copies, waits for them, and re-layouts  1.06 us (3%)
    all_to_all x1, waiting for transfers between devices, shards(): lax.all_to_all(packed(scalar, bricks), 'gz', split_axis=0, concat_axis=0,...  19.7 us
    all_to_all x1, starting transfers between devices, shards(): lax.all_to_all(packed(scalar, bricks), 'gz', split_axis=0, concat_axis=0,...  8.46 us
    pallas_call x1, Pallas kernels, shards(): pl.pallas_call(functools.partial(main_kernel, edge_rows), out_shape=[jax....  3.81 us
    pallas_call x1, Pallas kernels, shards(): pl.pallas_call(functools.partial(finish_kernel, edge_rows), out_shape=jax...  1.4 us
    ppermute x1, starting transfers between devices, shards(): other = lax.ppermute(wrapped, ('gz', 'gy'), pairs)  1.3 us
    pallas_call x1, Pallas kernels, packed(): pl.pallas_call(pack_kernel, out_shape=jax.ShapeDtypeStruct(shape, field.d...  1.09 us
    unnamed x10, local copies, waits for them, and re-layouts  1.06 us
  transfers between devices with their start and end apart: 2, of which 1 were waited for; matrix products, arithmetic and copies ran while one was open for 0% of the time, Pallas kernels for 10%

profile of v4, /device:TPU:0, one launch (start us, length us, event | category | flops | bytes accessed | tf_op | source)
XLA Modules:
  0.0 37.0 jit_solution(10759084654200161696)
XLA Ops:
  0.0 0.0 copy-start
  0.0 1.0 %copy-done = f32[2,64,1024]{2,1,0:T(8,128)S(1)} copy-done((f32[2,64,1024]{2,1,0:T(8,128)S(1)}, f32[2,64,1024]{2,1,0:T(8,128)}, u32[]{:S(2)}) %copy-start) | copy-done | bytes 524312
  1.0 1.1 %pack_rows.1 = f32[16,6,2,8,128]{4,3,2,1,0:T(8,128)} custom-call(f32[2,64,1024]{2,1,0:T(8,128)S(1)} %copy-done), custom_call_target="tpu_custom_call" | custom-call | tf_op jit(solution)/shard_map/pack_rows/pallas_call | solution.py:39
  2.1 0.0 copy-start.4
  2.1 0.0 copy-start.1
  2.1 0.0 copy-start.2
  2.1 0.0 copy-start.3
  2.1 8.5 %all-to-all-start = ((f32[16,6,2,8,128]{4,3,2,1,0:T(8,128)}), f32[16,6,2,8,128]{4,3,2,1,0:T(8,128)S(1)}, u32[]{:S(2)}, u32[]{:S(2)}) async-start(f32[16,6,2,8,128]{4,3,2,1,0:T(8,128)} %pack_rows.1), calls=%async_computation | async-start | bytes 1572864 | tf_op jit(solution)/shard_map/all_to_all | solution.py:246
  10.6 19.7 %all-to-all-done.tile_ref = f32[16,6,2,8,128]{4,3,2,1,0:T(8,128)S(1)} async-done(((f32[16,6,2,8,128]{4,3,2,1,0:T(8,128)}), f32[16,6,2,8,128]{4,3,2,1,0:T(8,128)S(1)}, u32[]{:S(2)}, u32[]{:S(2)}) %all-to-all-start) | async-done | bytes 786464 | tf_op jit(solution)/shard_map/all_to_all | solution.py:246
  30.4 1.3 %collective-permute-start = (f32[16,2,8,128]{3,2,1,0:T(8,128)S(1)}, f32[16,2,8,128]{3,2,1,0:T(8,128)S(1)}, u32[]{:S(2)}, u32[]{:S(2)}) collective-permute-start(f32[16,2,8,128]{3,2,1,0:T(8,128)S(1)} %fusion.1), channel_id=1, source_target_pairs={{0,1},{31,30}} | collective-permute-start | bytes 393224 | tf_op jit(solution)/shard_map/ppermute | solution.py:254
  31.7 0.0 copy-done.4
  31.7 0.1 add_convert_fusion.ends_ref
  31.8 0.0 copy-done.1
  31.8 0.0 copy-done.2
  31.8 0.0 copy-done.3
  31.8 3.8 %main_rows.1 = (f32[16,2,2,5,8,128]{5,4,3,2,1,0:T(8,128)S(1)}, f32[6,8,128]{2,1,0:T(8,128)S(1)}, f32[4,8,128]{2,1,0:T(8,128)S(1)}) custom-call(s32[16]{0:T(128)S(1)} %copy-done.3, f32[3]{0:T(128)S(1)} %copy-done.2, bf16[3,257]{1,0:T(4,128)(2,1)S(1)} %copy-done.1, bf16[1,257]{1,0:T(2,128)(2,1)S(1)} %broadcast_in_dim.3.opacity_ref, ...), custom_call_target="tpu_custom_call" | custom-call | flops 13107200 | bytes 3145728 | tf_op jit(solution)/shard_map/main_rows/pallas_call | solution.py:260
  35.6 0.0 collective-permute-done.other_ref
  35.6 1.4 %edge_rows.1 = f32[4,1,4,1024]{3,2,1,0:T(4,128)} custom-call(s32[2]{0:T(128)S(1)} %add_convert_fusion.ends_ref, f32[3]{0:T(128)S(1)} %copy-done.2, f32[16,6,2,8,128]{4,3,2,1,0:T(8,128)S(1)} %all-to-all-done.tile_ref, f32[16,2,8,128]{3,2,1,0:T(8,128)S(1)} %collective-permute-done.other_ref, f32[16,2,2,5,8,128]{5,4,3,2,1,0:T(8,128)S(1)} %get-tuple-element.8.part_ref, ...), custom_call_target="tpu_custom_call" | custom-call | flops 1310720 | bytes 3145728 | tf_op jit(solution)/shard_map/edge_rows/pallas_call | solution.py:275
  (2 shorter events, 0.0 us)
Async XLA Ops:
  0.0 1.0 %copy-start = (f32[2,64,1024]{2,1,0:T(8,128)S(1)}, f32[2,64,1024]{2,1,0:T(8,128)}, u32[]{:S(2)}) copy-start(f32[2,64,1024]{2,1,0:T(8,128)} %field_ref.1) | copy-start | bytes 1572868
  2.1 29.6 %copy-start.4 = (bf16[257]{0:T(512)(128)(2,1)S(1)}, bf16[257]{0:T(512)(128)(2,1)}, u32[]{:S(2)}) copy-start(bf16[257]{0:T(512)(128)(2,1)} %param.8) | copy-start | bytes 1546
  2.1 29.7 %copy-start.1 = (bf16[3,257]{1,0:T(4,128)(2,1)S(1)}, bf16[3,257]{1,0:T(4,128)(2,1)}, u32[]{:S(2)}) copy-start(bf16[3,257]{1,0:T(4,128)(2,1)} %color_ref.1) | copy-start | bytes 4630
  2.1 29.7 %copy-start.2 = (f32[3]{0:T(128)S(1)}, f32[3]{0:T(128)}, u32[]{:S(2)}) copy-start(f32[3]{0:T(128)} %light_ref.3) | copy-start | bytes 40
  2.1 29.7 %copy-start.3 = (s32[16]{0:T(128)S(1)}, s32[16]{0:T(128)}, u32[]{:S(2)}) copy-start(s32[16]{0:T(128)} %order_ref.1) | copy-start | bytes 196
  2.1 28.2 %all-to-all-start = ((f32[16,6,2,8,128]{4,3,2,1,0:T(8,128)}), f32[16,6,2,8,128]{4,3,2,1,0:T(8,128)S(1)}, u32[]{:S(2)}, u32[]{:S(2)}) async-start(f32[16,6,2,8,128]{4,3,2,1,0:T(8,128)} %pack_rows.1), calls=%async_computation | async-start | bytes 1572864 | tf_op jit(solution)/shard_map/all_to_all | solution.py:246
  30.4 5.2 %collective-permute-start = (f32[16,2,8,128]{3,2,1,0:T(8,128)S(1)}, f32[16,2,8,128]{3,2,1,0:T(8,128)S(1)}, u32[]{:S(2)}, u32[]{:S(2)}) collective-permute-start(f32[16,2,8,128]{3,2,1,0:T(8,128)S(1)} %fusion.1), channel_id=1, source_target_pairs={{0,1},{31,30}} | collective-permute-start | bytes 393224 | tf_op jit(solution)/shard_map/ppermute | solution.py:254

commit v5 on v4

--- a/solution.py
+++ b/solution.py
@@ -13,55 +13,56 @@
 OPACITY_SPAN = 2 ** OPACITY_BITS
 
 
-def pack_kernel(field_ref, out_ref, staged):
+def pack_kernel(field_ref, out_ref):
     depth, rows, cols = field_ref.shape
-    tiles, padded_rows, _, chunks, _ = out_ref.shape
-    tile_rows = padded_rows - 2
+    chunks = cols // LANES
     block = depth * chunks
+    tiles = out_ref.shape[0] // block - rows
+    tiles //= 2
+    tile_rows = rows // tiles
+    padded_rows = tile_rows + 2
+    piece = min(SUB, tile_rows)
     for k in range(depth):
-        for j in range(rows // SUB):
-            lines = [field_ref[k, j * SUB:(j + 1) * SUB, c * LANES:(c + 1) * LANES] for c in range(chunks)]
-            for c, value in enumerate(lines):
-                staged[pl.ds(j * SUB * block + k * chunks + c, SUB, stride=block), :] = value
+        for c in range(chunks):
+            lines = [field_ref[k, r:r + piece, c * LANES:(c + 1) * LANES] for r in range(0, rows, piece)]
+            for i, value in enumerate(lines):
+                t, r = divmod(i * piece, tile_rows)
+                at = (t * padded_rows + r + 1) * block + k * chunks + c
+                out_ref[pl.ds(at, piece, stride=block), :] = value
     for t in range(tiles):
-        starts = [((t * tile_rows + i - 1) % rows) * block for i in range(padded_rows)]
-        blocks = [staged[start:start + block, :] for start in starts]
-        for i, value in enumerate(blocks):
-            for k in range(depth):
-                out_ref[t, i, k] = value[k * chunks:(k + 1) * chunks]
+        before, after = (t - 1) % tiles, (t + 1) % tiles
+        copies = [((before * padded_rows + tile_rows) * block, t * padded_rows * block),
+                  ((after * padded_rows + 1) * block, (t * padded_rows + tile_rows + 1) * block)]
+        values = [out_ref[source:source + block, :] for source, _ in copies]
+        for value, (_, target) in zip(values, copies):
+            out_ref[target:target + block, :] = value
 
 
 def packed(field, tiles):
     depth, rows, cols = field.shape
     chunks = cols // LANES
+    padded_rows = rows // tiles + 2
     vmem = pl.BlockSpec(memory_space=pltpu.VMEM)
-    shape = (tiles, rows // tiles + 2, depth, chunks, LANES)
-    return pl.pallas_call(
+    flat = pl.pallas_call(
         pack_kernel,
-        out_shape=jax.ShapeDtypeStruct(shape, field.dtype),
+        out_shape=jax.ShapeDtypeStruct((tiles * padded_rows * depth * chunks, LANES), field.dtype),
         in_specs=[vmem],
         out_specs=vmem,
-        scratch_shapes=[pltpu.VMEM((rows * depth * chunks, LANES), field.dtype)],
         compiler_params=pltpu.CompilerParams(vmem_limit_bytes=16 << 20),
         name="pack_rows",
     )(field)
+    return flat.reshape(tiles, padded_rows, depth, chunks, LANES)
 
 
 def shifted(x, axis, shift):
     return pltpu.roll(x, shift % x.shape[axis], axis)
 
 
-def brick_positions(order_ref, brick_at):
-    def place(b, carry):
-        brick_at[order_ref[b]] = b
-        return carry
-
-    lax.fori_loop(0, order_ref.shape[0], place, 0)
-
-
-def table_lookup(color_ref, opacity_ref, shape):
+def prepare_kernel(bands_end_ref, light_ref, color_ref, opacity_ref,
+                   color_word_ref, opacity_word_ref, light_rows_ref, end_ref):
     bins = color_ref.shape[1] - 1
-    halves = bins // LANES
+    _, halves, chunks, lanes = color_word_ref.shape
+    shape = (chunks, lanes)
 
     def parts(values, unit):
         scaled = values.astype(jnp.float32) * float(unit)
@@ -71,31 +72,43 @@
     color_words = slope + low * (1.0 / COLOR_SPAN)
     low, slope = parts(opacity_ref[...], OPACITY_UNIT)
     opacity_words = slope.astype(jnp.int32) * OPACITY_SPAN + low.astype(jnp.int32)
-
-    def spread(words):
-        return [jnp.broadcast_to(words[:, h * LANES:(h + 1) * LANES], shape) for h in range(halves)]
-
-    tables = [spread(color_words[c:c + 1]) for c in range(3)] + [spread(opacity_words)]
+    for h in range(halves):
+        span = slice(h * lanes, (h + 1) * lanes)
+        for c in range(3):
+            color_word_ref[c, h] = jnp.broadcast_to(color_words[c:c + 1, span], shape)
+        opacity_word_ref[h] = jnp.broadcast_to(opacity_words[:, span], shape)
+    for i in range(3):
+        light_rows_ref[i] = jnp.full(shape, light_ref[i], jnp.float32)
+    for i in range(2):
+        end_ref[i] = jnp.full(shape, bands_end_ref[i], jnp.int32)
+
+
+def table_lookup(color_word_ref, opacity_word_ref):
+    _, halves, _, lanes = color_word_ref.shape
+    bins = halves * lanes
 
     def look_up(x):
         scaled = x * float(bins)
         index = jnp.minimum(scaled.astype(jnp.int32), bins - 1)
         fraction = scaled - index.astype(jnp.float32)
-        low_bits = index & (LANES - 1)
-        words = []
-        for table in tables:
-            word = jnp.take_along_axis(table[0], low_bits, axis=1, mode="promise_in_bounds")
+        low_bits = index & (lanes - 1)
+
+        def gathered(table):
+            found = [jnp.take_along_axis(t, low_bits, axis=1, mode="promise_in_bounds") for t in table]
+            word = found[0]
             for h in range(1, halves):
-                found = jnp.take_along_axis(table[h], low_bits, axis=1, mode="promise_in_bounds")
-                word = jnp.where(index >= h * LANES, found, word)
-            words.append(word)
+                word = jnp.where(index >= h * lanes, found[h], word)
+            return word
+
         color = []
         small = fraction * (1.0 / COLOR_SPAN)
-        for word in words[:3]:
+        for c in range(3):
+            word = gathered([color_word_ref[c, h] for h in range(halves)])
             rise = jnp.floor(word)
             color.append((word - rise) + small * rise)
-        rise = (words[3] >> OPACITY_BITS).astype(jnp.float32)
-        start = (words[3] & (OPACITY_SPAN - 1)).astype(jnp.float32)
+        word = gathered([opacity_word_ref[h] for h in range(halves)])
+        rise = (word >> OPACITY_BITS).astype(jnp.float32)
+        start = (word & (OPACITY_SPAN - 1)).astype(jnp.float32)
         return color, (start + fraction * rise) * (1.0 / OPACITY_UNIT)
 
     return look_up
@@ -136,14 +149,13 @@
     return 0.25 + (0.75 * facing) * (facing * inverse)
 
 
-def main_kernel(edge_rows, order_ref, light_ref, color_ref, opacity_ref, tile_ref,
-                part_ref, color_sum_ref, keep_ref, brick_at):
+def main_kernel(edge_rows, brick_at, light_ref, color_word_ref, opacity_word_ref, tile_ref,
+                part_ref, color_sum_ref, keep_ref):
     bricks, padded_rows, depth, chunks, lanes = tile_ref.shape
     rows = padded_rows - 2
     inner_rows = [r for r in range(rows) if r not in edge_rows]
     shape = (chunks, lanes)
-    brick_positions(order_ref, brick_at)
-    look_up = table_lookup(color_ref, opacity_ref, shape)
+    look_up = table_lookup(color_word_ref, opacity_word_ref)
     column_difference = column_differences(shape)
     light = [light_ref[i] for i in range(3)]
     together = 2 if bricks % 2 == 0 else 1
@@ -187,15 +199,14 @@
         keep_ref[r] = value
 
 
-def finish_kernel(edge_rows, ends_ref, light_ref, tile_ref, other_ref, part_ref, color_sum_ref, keep_ref,
+def finish_kernel(edge_rows, end_ref, light_ref, tile_ref, other_ref, part_ref, color_sum_ref, keep_ref,
                   out_ref, staged):
     bricks, padded_rows, depth, chunks, lanes = tile_ref.shape
     rows = padded_rows - 2
     inner_rows = [r for r in range(rows) if r not in edge_rows]
     shape = (chunks, lanes)
     light_rows = light_ref[1]
-    is_first = jnp.full(shape, ends_ref[0], jnp.int32) == 1
-    is_last = jnp.full(shape, ends_ref[1], jnp.int32) == 1
+    is_first, is_last = end_ref[0] == 1, end_ref[1] == 1
 
     together = 4 if bricks % 4 == 0 else 1
 
@@ -257,6 +268,24 @@
     smem = pl.BlockSpec(memory_space=pltpu.SMEM)
     params = pltpu.CompilerParams(vmem_limit_bytes=32 << 20)
     cells = bricks * depth * cols
+    lines = (chunks, LANES)
+    halves = (color_table.shape[1] - 1) // LANES
+    color_words, opacity_words, light_rows, end_rows = pl.pallas_call(
+        prepare_kernel,
+        out_shape=[
+            jax.ShapeDtypeStruct((3, halves) + lines, jnp.float32),
+            jax.ShapeDtypeStruct((halves,) + lines, jnp.int32),
+            jax.ShapeDtypeStruct((3,) + lines, jnp.float32),
+            jax.ShapeDtypeStruct((2,) + lines, jnp.int32),
+        ],
+        in_specs=[smem, smem, vmem, vmem],
+        out_specs=[vmem] * 4,
+        compiler_params=params,
+        name="prepare_tables",
+    )(ends, light_dir, color_table, opacity_table[None, :])
+    positions = jnp.arange(bricks, dtype=jnp.int32)
+    at_position = view_order[None, :] == positions[:, None]
+    brick_at = jnp.sum(jnp.where(at_position, positions[None, :], 0), axis=1)
     parts, color_sums, keeps = pl.pallas_call(
         functools.partial(main_kernel, edge_rows),
         out_shape=[
@@ -264,25 +293,24 @@
             jax.ShapeDtypeStruct((max(3 * inner_count, 1), chunks, LANES), jnp.float32),
             jax.ShapeDtypeStruct((tile_rows, chunks, LANES), jnp.float32),
         ],
-        in_specs=[smem, smem, vmem, vmem, vmem],
+        in_specs=[smem] + [vmem] * 4,
         out_specs=[vmem, vmem, vmem],
-        scratch_shapes=[pltpu.SMEM((bricks,), jnp.int32)],
         compiler_params=params,
         cost_estimate=pl.CostEstimate(
             flops=100 * cells * tile_rows, bytes_accessed=24 * cells * tile_rows, transcendentals=0),
         name="main_rows",
-    )(view_order, light_dir, color_table, opacity_table[None, :], tiles)
+    )(brick_at, light_rows, color_words, opacity_words, tiles)
     return pl.pallas_call(
         functools.partial(finish_kernel, edge_rows),
         out_shape=jax.ShapeDtypeStruct((4, 1, tile_rows, cols), jnp.float32),
-        in_specs=[smem, smem, vmem, vmem, vmem, vmem, vmem],
+        in_specs=[vmem] * 7,
         out_specs=vmem,
         scratch_shapes=[pltpu.VMEM((4 * tile_rows * chunks, LANES), jnp.float32)],
         compiler_params=params,
         cost_estimate=pl.CostEstimate(
             flops=10 * cells * tile_rows, bytes_accessed=24 * cells * tile_rows, transcendentals=0),
         name="edge_rows",
-    )(ends, light_dir, tiles, other, parts, color_sums, keeps)
+    )(end_rows, light_rows, tiles, other, parts, color_sums, keeps)
 
 
 def solution(mesh):

time: 37.3 us -> 37 us (level)
  Pallas kernels: 6.29 us -> 5.88 us
    pallas_call x1 -> x2, Pallas kernels: 1.09 us -> 1.87 us  [the longest x1 1.17 us: packed(): pl.pallas_call(pack_kernel, out_shape=jax.ShapeDtypeStruct((tiles * padde...]
    pallas_call x1, Pallas kernels: 3.81 us -> 3.15 us  [shards(): pl.pallas_call(functools.partial(main_kernel, edge_rows), out_shape=[jax....]
    pallas_call x1, Pallas kernels: 1.4 us -> 0.86 us  [shards(): pl.pallas_call(functools.partial(finish_kernel, edge_rows), out_shape=jax...]
  transfers between devices with their start and end apart: 2 -> 2, of which waited for: 1 -> 1; matrix products, arithmetic and copies ran while one was open for 0% -> 1% of each run, Pallas kernels for 10% -> 10%
where the time goes in v5:
time: 37 us; the launch traced here: 36.7 us
  waiting for transfers between devices  19.7 us (53%)
  starting transfers between devices  9.75 us (26%)
  Pallas kernels  5.88 us (16%)
  local copies, waits for them, and re-layouts  1.06 us (3%)
    all_to_all x1, waiting for transfers between devices, shards(): lax.all_to_all(packed(scalar, bricks), 'gz', split_axis=0, concat_axis=0,...  19.7 us
    all_to_all x1, starting transfers between devices, shards(): lax.all_to_all(packed(scalar, bricks), 'gz', split_axis=0, concat_axis=0,...  8.46 us
    pallas_call x1, Pallas kernels, shards(): pl.pallas_call(functools.partial(main_kernel, edge_rows), out_shape=[jax....  3.15 us
    ppermute x1, starting transfers between devices, shards(): other = lax.ppermute(wrapped, ('gz', 'gy'), pairs)  1.3 us
    pallas_call x1, Pallas kernels, packed(): pl.pallas_call(pack_kernel, out_shape=jax.ShapeDtypeStruct((tiles * padde...  1.17 us
    unnamed x10, local copies, waits for them, and re-layouts  1.06 us
    pallas_call x1, Pallas kernels, shards(): pl.pallas_call(functools.partial(finish_kernel, edge_rows), out_shape=jax...  0.86 us
  transfers between devices with their start and end apart: 2, of which 1 were waited for; matrix products, arithmetic and copies ran while one was open for 1% of the time, Pallas kernels for 10%

profile of v5, /device:TPU:0, one launch (start us, length us, event | category | flops | bytes accessed | tf_op | source)
XLA Modules:
  0.0 36.7 jit_solution(12695378912125635644)
XLA Ops:
  0.0 0.0 copy-start
  0.0 1.0 %copy-done = f32[2,64,1024]{2,1,0:T(8,128)S(1)} copy-done((f32[2,64,1024]{2,1,0:T(8,128)S(1)}, f32[2,64,1024]{2,1,0:T(8,128)}, u32[]{:S(2)}) %copy-start) | copy-done | bytes 524312
  1.0 1.2 %pack_rows.1 = f32[1536,128]{1,0:T(8,128)} custom-call(f32[2,64,1024]{2,1,0:T(8,128)S(1)} %copy-done), custom_call_target="tpu_custom_call" | custom-call | tf_op jit(solution)/shard_map/pack_rows/pallas_call | solution.py:46
  2.2 0.0 copy-start.3
  2.2 0.0 copy-start.1
  2.2 0.0 copy-start.2
  2.2 0.0 copy-start.4
  2.2 8.5 %all-to-all-start = ((f32[16,6,2,8,128]{4,3,2,1,0:T(8,128)}), f32[16,6,2,8,128]{4,3,2,1,0:T(8,128)S(1)}, u32[]{:S(2)}, u32[]{:S(2)}) async-start(f32[16,6,2,8,128]{4,3,2,1,0:T(8,128)} %bitcast.2), calls=%async_computation | async-start | bytes 1572864 | tf_op jit(solution)/shard_map/all_to_all | solution.py:257
  10.7 19.7 %all-to-all-done.tile_ref = f32[16,6,2,8,128]{4,3,2,1,0:T(8,128)S(1)} async-done(((f32[16,6,2,8,128]{4,3,2,1,0:T(8,128)}), f32[16,6,2,8,128]{4,3,2,1,0:T(8,128)S(1)}, u32[]{:S(2)}, u32[]{:S(2)}) %all-to-all-start) | async-done | bytes 786464 | tf_op jit(solution)/shard_map/all_to_all | solution.py:257
  30.5 1.3 %collective-permute-start = (f32[16,2,8,128]{3,2,1,0:T(8,128)S(1)}, f32[16,2,8,128]{3,2,1,0:T(8,128)S(1)}, u32[]{:S(2)}, u32[]{:S(2)}) collective-permute-start(f32[16,2,8,128]{3,2,1,0:T(8,128)S(1)} %fusion.1), channel_id=1, source_target_pairs={{0,1},{31,30}} | collective-permute-start | bytes 393224 | tf_op jit(solution)/shard_map/ppermute | solution.py:265
  31.8 0.1 add_convert_fusion.bands_end_ref
  31.8 0.0 copy-done.3
  31.9 0.0 copy-done.1
  31.9 0.0 copy-done.2
  31.9 0.7 %prepare_tables.1 = (f32[3,2,8,128]{3,2,1,0:T(8,128)S(1)}, s32[2,8,128]{2,1,0:T(8,128)S(1)}, f32[3,8,128]{2,1,0:T(8,128)S(1)}, s32[2,8,128]{2,1,0:T(8,128)S(1)}) custom-call(s32[2]{0:T(128)S(1)} %add_convert_fusion.bands_end_ref, f32[3]{0:T(128)S(1)} %copy-done.2, bf16[3,257]{1,0:T(4,128)(2,1)S(1)} %copy-done.1, bf16[1,257]{1,0:T(2,128)(2,1)S(1)} %broadcast_in_dim.18.opacity_ref), custom_call_target="tpu_custom_call" | custom-call | tf_op jit(solution)/shard_map/prepare_tables/pallas_call | solution.py:273
  32.6 0.0 copy-done.4
  32.6 0.1 select_reduce_fusion.brick_at
  32.7 3.2 %main_rows.1 = (f32[16,2,2,5,8,128]{5,4,3,2,1,0:T(8,128)S(1)}, f32[6,8,128]{2,1,0:T(8,128)S(1)}, f32[4,8,128]{2,1,0:T(8,128)S(1)}) custom-call(s32[16]{0:T(128)S(1)} %select_reduce_fusion.brick_at, f32[3,8,128]{2,1,0:T(8,128)S(1)} %get-tuple-element.13.light_ref, f32[3,2,8,128]{3,2,1,0:T(8,128)S(1)} %get-tuple-element.14.color_word_ref, ...), custom_call_target="tpu_custom_call" | custom-call | flops 13107200 | bytes 3145728 | tf_op jit(solution)/shard_map/main_rows/pallas_call | solution.py:289
  35.8 0.0 collective-permute-done.other_ref
  35.9 0.9 %edge_rows.1 = f32[4,1,4,1024]{3,2,1,0:T(4,128)} custom-call(s32[2,8,128]{2,1,0:T(8,128)S(1)} %get-tuple-element.12.end_ref, f32[3,8,128]{2,1,0:T(8,128)S(1)} %get-tuple-element.13.light_ref, f32[16,6,2,8,128]{4,3,2,1,0:T(8,128)S(1)} %all-to-all-done.tile_ref, f32[16,2,8,128]{3,2,1,0:T(8,128)S(1)} %collective-permute-done.other_ref, ...), custom_call_target="tpu_custom_call" | custom-call | flops 1310720 | bytes 3145728 | tf_op jit(solution)/shard_map/edge_rows/pallas_call | solution.py:303
  (2 shorter events, 0.0 us)
Async XLA Ops:
  0.0 1.0 %copy-start = (f32[2,64,1024]{2,1,0:T(8,128)S(1)}, f32[2,64,1024]{2,1,0:T(8,128)}, u32[]{:S(2)}) copy-start(f32[2,64,1024]{2,1,0:T(8,128)} %field_ref.1) | copy-start | bytes 1572868
  2.2 29.6 %copy-start.3 = (bf16[257]{0:T(512)(128)(2,1)S(1)}, bf16[257]{0:T(512)(128)(2,1)}, u32[]{:S(2)}) copy-start(bf16[257]{0:T(512)(128)(2,1)} %param.8) | copy-start | bytes 1546
  2.2 29.6 %copy-start.1 = (bf16[3,257]{1,0:T(4,128)(2,1)S(1)}, bf16[3,257]{1,0:T(4,128)(2,1)}, u32[]{:S(2)}) copy-start(bf16[3,257]{1,0:T(4,128)(2,1)} %color_ref.1) | copy-start | bytes 4630
  2.2 29.6 %copy-start.2 = (f32[3]{0:T(128)S(1)}, f32[3]{0:T(128)}, u32[]{:S(2)}) copy-start(f32[3]{0:T(128)} %light_ref.1) | copy-start | bytes 40
  2.2 30.3 %copy-start.4 = (s32[16]{0:T(128)S(1)}, s32[16]{0:T(128)}, u32[]{:S(2)}) copy-start(s32[16]{0:T(128)} %param.10) | copy-start | bytes 196
  2.2 28.2 %all-to-all-start = ((f32[16,6,2,8,128]{4,3,2,1,0:T(8,128)}), f32[16,6,2,8,128]{4,3,2,1,0:T(8,128)S(1)}, u32[]{:S(2)}, u32[]{:S(2)}) async-start(f32[16,6,2,8,128]{4,3,2,1,0:T(8,128)} %bitcast.2), calls=%async_computation | async-start | bytes 1572864 | tf_op jit(solution)/shard_map/all_to_all | solution.py:257
  30.5 5.4 %collective-permute-start = (f32[16,2,8,128]{3,2,1,0:T(8,128)S(1)}, f32[16,2,8,128]{3,2,1,0:T(8,128)S(1)}, u32[]{:S(2)}, u32[]{:S(2)}) collective-permute-start(f32[16,2,8,128]{3,2,1,0:T(8,128)S(1)} %fusion.1), channel_id=1, source_target_pairs={{0,1},{31,30}} | collective-permute-start | bytes 393224 | tf_op jit(solution)/shard_map/ppermute | solution.py:265

commit v6 on v5

--- a/solution.py
+++ b/solution.py
@@ -13,53 +13,56 @@
 OPACITY_SPAN = 2 ** OPACITY_BITS
 
 
-def pack_kernel(field_ref, out_ref):
+def pack_kernel(field_ref, out_ref, staged):
     depth, rows, cols = field_ref.shape
-    chunks = cols // LANES
+    tiles, padded_rows, _, chunks, _ = out_ref.shape
+    tile_rows = padded_rows - 2
     block = depth * chunks
-    tiles = out_ref.shape[0] // block - rows
-    tiles //= 2
-    tile_rows = rows // tiles
-    padded_rows = tile_rows + 2
-    piece = min(SUB, tile_rows)
-    for k in range(depth):
-        for c in range(chunks):
-            lines = [field_ref[k, r:r + piece, c * LANES:(c + 1) * LANES] for r in range(0, rows, piece)]
-            for i, value in enumerate(lines):
-                t, r = divmod(i * piece, tile_rows)
-                at = (t * padded_rows + r + 1) * block + k * chunks + c
-                out_ref[pl.ds(at, piece, stride=block), :] = value
-    for t in range(tiles):
-        before, after = (t - 1) % tiles, (t + 1) % tiles
-        copies = [((before * padded_rows + tile_rows) * block, t * padded_rows * block),
-                  ((after * padded_rows + 1) * block, (t * padded_rows + tile_rows + 1) * block)]
-        values = [out_ref[source:source + block, :] for source, _ in copies]
-        for value, (_, target) in zip(values, copies):
-            out_ref[target:target + block, :] = value
+
+    def spread(j, carry):
+        start = pl.multiple_of(j * SUB, SUB)
+        for k in range(depth):
+            lines = [field_ref[k, pl.ds(start, SUB), c * LANES:(c + 1) * LANES] for c in range(chunks)]
+            for c, value in enumerate(lines):
+                staged[pl.ds(start * block + k * chunks + c, SUB, stride=block), :] = value
+        return carry
+
+    def place(t, carry):
+        values = []
+        for i in range(padded_rows):
+            start = lax.rem(t * tile_rows + i - 1 + rows, rows) * block
+            values.append(staged[pl.ds(pl.multiple_of(start, block), block), :])
+        for i, value in enumerate(values):
+            for k in range(depth):
+                out_ref[t, i, k] = value[k * chunks:(k + 1) * chunks]
+        return carry
+
+    lax.fori_loop(0, rows // SUB, spread, 0)
+    lax.fori_loop(0, tiles, place, 0)
 
 
 def packed(field, tiles):
     depth, rows, cols = field.shape
     chunks = cols // LANES
-    padded_rows = rows // tiles + 2
     vmem = pl.BlockSpec(memory_space=pltpu.VMEM)
-    flat = pl.pallas_call(
+    shape = (tiles, rows // tiles + 2, depth, chunks, LANES)
+    return pl.pallas_call(
         pack_kernel,
-        out_shape=jax.ShapeDtypeStruct((tiles * padded_rows * depth * chunks, LANES), field.dtype),
+        out_shape=jax.ShapeDtypeStruct(shape, field.dtype),
         in_specs=[vmem],
         out_specs=vmem,
+        scratch_shapes=[pltpu.VMEM((rows * depth * chunks, LANES), field.dtype)],
         compiler_params=pltpu.CompilerParams(vmem_limit_bytes=16 << 20),
         name="pack_rows",
     )(field)
-    return flat.reshape(tiles, padded_rows, depth, chunks, LANES)
 
 
 def shifted(x, axis, shift):
     return pltpu.roll(x, shift % x.shape[axis], axis)
 
 
-def prepare_kernel(bands_end_ref, light_ref, color_ref, opacity_ref,
-                   color_word_ref, opacity_word_ref, light_rows_ref, end_ref):
+def prepare_kernel(bands_end_ref, order_ref, light_ref, color_ref, opacity_ref,
+                   brick_at_ref, color_word_ref, opacity_word_ref, light_rows_ref, end_ref):
     bins = color_ref.shape[1] - 1
     _, halves, chunks, lanes = color_word_ref.shape
     shape = (chunks, lanes)
@@ -81,6 +84,8 @@
         light_rows_ref[i] = jnp.full(shape, light_ref[i], jnp.float32)
     for i in range(2):
         end_ref[i] = jnp.full(shape, bands_end_ref[i], jnp.int32)
+    for b in range(order_ref.shape[0]):
+        brick_at_ref[order_ref[b]] = b
 
 
 def table_lookup(color_word_ref, opacity_word_ref):
@@ -158,7 +163,7 @@
     look_up = table_lookup(color_word_ref, opacity_word_ref)
     column_difference = column_differences(shape)
     light = [light_ref[i] for i in range(3)]
-    together = 2 if bricks % 2 == 0 else 1
+    together = 1
 
     def step(trip, carry):
         colors, keeps = list(carry[0]), list(carry[1])
@@ -261,8 +266,6 @@
     last = bricks - 1
     pairs = [(g, g + 1) for g in range(bands - 1)]
     pairs += [(last * bands + g + 1, last * bands + g) for g in range(bands - 1)]
-    wrapped = jnp.where(here == 0, tiles[:, 0], tiles[:, -1])
-    other = lax.ppermute(wrapped, ("gz", "gy"), pairs)
 
     vmem = pl.BlockSpec(memory_space=pltpu.VMEM)
     smem = pl.BlockSpec(memory_space=pltpu.SMEM)
@@ -270,22 +273,22 @@
     cells = bricks * depth * cols
     lines = (chunks, LANES)
     halves = (color_table.shape[1] - 1) // LANES
-    color_words, opacity_words, light_rows, end_rows = pl.pallas_call(
+    brick_at, color_words, opacity_words, light_rows, end_rows = pl.pallas_call(
         prepare_kernel,
         out_shape=[
+            jax.ShapeDtypeStruct((bricks,), jnp.int32),
             jax.ShapeDtypeStruct((3, halves) + lines, jnp.float32),
             jax.ShapeDtypeStruct((halves,) + lines, jnp.int32),
             jax.ShapeDtypeStruct((3,) + lines, jnp.float32),
             jax.ShapeDtypeStruct((2,) + lines, jnp.int32),
         ],
-        in_specs=[smem, smem, vmem, vmem],
-        out_specs=[vmem] * 4,
+        in_specs=[smem, smem, smem, vmem, vmem],
+        out_specs=[smem] + [vmem] * 4,
         compiler_params=params,
         name="prepare_tables",
-    )(ends, light_dir, color_table, opacity_table[None, :])
-    positions = jnp.arange(bricks, dtype=jnp.int32)
-    at_position = view_order[None, :] == positions[:, None]
-    brick_at = jnp.sum(jnp.where(at_position, positions[None, :], 0), axis=1)
+    )(ends, view_order, light_dir, color_table, opacity_table[None, :])
+    wrapped = jnp.where(end_rows[0] == 1, tiles[:, 0], tiles[:, -1])
+    other = lax.ppermute(wrapped, ("gz", "gy"), pairs)
     parts, color_sums, keeps = pl.pallas_call(
         functools.partial(main_kernel, edge_rows),
         out_shape=[

time: 37 us -> 36.7 us (level)
  waiting for transfers between devices: 19.7 us -> 18.4 us
  Pallas kernels: 5.88 us -> 7.17 us
    all_to_all x1, waiting for transfers between devices: 19.7 us -> 18.4 us  [shards(): lax.all_to_all(packed(scalar, bricks), 'gz', split_axis=0, concat_axis=0,...]
    pallas_call x2, Pallas kernels: 1.87 us -> 2.55 us  [the longest x1 1.38 us: packed(): pl.pallas_call(pack_kernel, out_shape=jax.ShapeDtypeStruct(shape, field.d...]
    pallas_call x1, Pallas kernels: 3.15 us -> 3.76 us  [shards(): pl.pallas_call(functools.partial(main_kernel, edge_rows), out_shape=[jax....]
  transfers between devices with their start and end apart: 2 -> 2, of which waited for: 1 -> 1; matrix products, arithmetic and copies ran while one was open for 1% -> 0% of each run, Pallas kernels for 10% -> 13%
where the time goes in v6:
time: 36.7 us; the launch traced here: 36.5 us
  waiting for transfers between devices  18.4 us (50%)
  starting transfers between devices  9.61 us (26%)
  Pallas kernels  7.17 us (20%)
  local copies, waits for them, and re-layouts  1.06 us (3%)
    all_to_all x1, waiting for transfers between devices, shards(): lax.all_to_all(packed(scalar, bricks), 'gz', split_axis=0, concat_axis=0,...  18.4 us
    all_to_all x1, starting transfers between devices, shards(): lax.all_to_all(packed(scalar, bricks), 'gz', split_axis=0, concat_axis=0,...  8.31 us
    pallas_call x1, Pallas kernels, shards(): pl.pallas_call(functools.partial(main_kernel, edge_rows), out_shape=[jax....  3.76 us
    pallas_call x1, Pallas kernels, packed(): pl.pallas_call(pack_kernel, out_shape=jax.ShapeDtypeStruct(shape, field.d...  1.38 us
    ppermute x1, starting transfers between devices, shards(): other = lax.ppermute(wrapped, ('gz', 'gy'), pairs)  1.3 us
    pallas_call x1, Pallas kernels, shards(): pl.pallas_call(prepare_kernel, out_shape=[jax.ShapeDtypeStruct((bricks,),...  1.16 us
    unnamed x10, local copies, waits for them, and re-layouts  1.06 us
    pallas_call x1, Pallas kernels, shards(): pl.pallas_call(functools.partial(finish_kernel, edge_rows), out_shape=jax...  0.86 us
  transfers between devices with their start and end apart: 2, of which 1 were waited for; matrix products, arithmetic and copies ran while one was open for 0% of the time, Pallas kernels for 13%

profile of v6, /device:TPU:0, one launch (start us, length us, event | category | flops | bytes accessed | tf_op | source)
XLA Modules:
  0.0 36.5 jit_solution(9470627454151741947)
XLA Ops:
  0.0 0.0 copy-start
  0.0 1.0 %copy-done = f32[2,64,1024]{2,1,0:T(8,128)S(1)} copy-done((f32[2,64,1024]{2,1,0:T(8,128)S(1)}, f32[2,64,1024]{2,1,0:T(8,128)}, u32[]{:S(2)}) %copy-start) | copy-done | bytes 524312
  1.0 0.0 copy-start.4
  1.0 0.0 copy-start.1
  1.0 0.0 copy-start.2
  1.0 0.0 copy-start.3
  1.1 1.4 %pack_rows.1 = f32[16,6,2,8,128]{4,3,2,1,0:T(8,128)} custom-call(f32[2,64,1024]{2,1,0:T(8,128)S(1)} %copy-done), custom_call_target="tpu_custom_call" | custom-call | tf_op jit(solution)/shard_map/pack_rows/pallas_call | solution.py:49
  2.4 8.3 %all-to-all-start = ((f32[16,6,2,8,128]{4,3,2,1,0:T(8,128)}), f32[16,6,2,8,128]{4,3,2,1,0:T(8,128)S(1)}, u32[]{:S(2)}, u32[]{:S(2)}) async-start(f32[16,6,2,8,128]{4,3,2,1,0:T(8,128)} %pack_rows.1), calls=%async_computation | async-start | bytes 1572864 | tf_op jit(solution)/shard_map/all_to_all | solution.py:262
  10.8 0.0 copy-done.4
  10.8 0.1 add_convert_fusion.bands_end_ref
  10.9 0.0 copy-done.1
  10.9 0.0 copy-done.2
  10.9 0.0 copy-done.3
  10.9 1.2 %prepare_tables.1 = (s32[16]{0:T(128)S(1)}, f32[3,2,8,128]{3,2,1,0:T(8,128)S(1)}, s32[2,8,128]{2,1,0:T(8,128)S(1)}, f32[3,8,128]{2,1,0:T(8,128)S(1)}, s32[2,8,128]{2,1,0:T(8,128)S(1)}) custom-call(s32[2]{0:T(128)S(1)} %add_convert_fusion.bands_end_ref, s32[16]{0:T(128)S(1)} %copy-done.2, f32[3]{0:T(128)S(1)} %copy-done.3, bf16[3,257]{1,0:T(4,128)(2,1)S(1)} %copy-done.1, ...), custom_call_target="tpu_custom_call" | custom-call | tf_op jit(solution)/shard_map/prepare_tables/pallas_call | solution.py:276
  12.1 18.4 %all-to-all-done.tile_ref = f32[16,6,2,8,128]{4,3,2,1,0:T(8,128)S(1)} async-done(((f32[16,6,2,8,128]{4,3,2,1,0:T(8,128)}), f32[16,6,2,8,128]{4,3,2,1,0:T(8,128)S(1)}, u32[]{:S(2)}, u32[]{:S(2)}) %all-to-all-start) | async-done | bytes 786464 | tf_op jit(solution)/shard_map/all_to_all | solution.py:262
  30.5 1.3 %collective-permute-start = (f32[16,2,8,128]{3,2,1,0:T(8,128)S(1)}, f32[16,2,8,128]{3,2,1,0:T(8,128)S(1)}, u32[]{:S(2)}, u32[]{:S(2)}) collective-permute-start(f32[16,2,8,128]{3,2,1,0:T(8,128)S(1)} %fusion), channel_id=1, source_target_pairs={{0,1},{31,30}} | collective-permute-start | bytes 393224 | tf_op jit(solution)/shard_map/ppermute | solution.py:291
  31.8 3.8 %main_rows.1 = (f32[16,2,2,5,8,128]{5,4,3,2,1,0:T(8,128)S(1)}, f32[6,8,128]{2,1,0:T(8,128)S(1)}, f32[4,8,128]{2,1,0:T(8,128)S(1)}) custom-call(s32[16]{0:T(128)S(1)} %get-tuple-element.15.brick_at, f32[3,8,128]{2,1,0:T(8,128)S(1)} %get-tuple-element.14.light_ref, f32[3,2,8,128]{3,2,1,0:T(8,128)S(1)} %get-tuple-element.16.color_word_ref, ...), custom_call_target="tpu_custom_call" | custom-call | flops 13107200 | bytes 3145728 | tf_op jit(solution)/shard_map/main_rows/pallas_call | solution.py:292
  35.6 0.0 collective-permute-done.other_ref
  35.6 0.9 %edge_rows.1 = f32[4,1,4,1024]{3,2,1,0:T(4,128)} custom-call(s32[2,8,128]{2,1,0:T(8,128)S(1)} %get-tuple-element.13.end_ref, f32[3,8,128]{2,1,0:T(8,128)S(1)} %get-tuple-element.14.light_ref, f32[16,6,2,8,128]{4,3,2,1,0:T(8,128)S(1)} %all-to-all-done.tile_ref, f32[16,2,8,128]{3,2,1,0:T(8,128)S(1)} %collective-permute-done.other_ref, ...), custom_call_target="tpu_custom_call" | custom-call | flops 1310720 | bytes 3145728 | tf_op jit(solution)/shard_map/edge_rows/pallas_call | solution.py:306
  (3 shorter events, 0.0 us)
Async XLA Ops:
  0.0 1.0 %copy-start = (f32[2,64,1024]{2,1,0:T(8,128)S(1)}, f32[2,64,1024]{2,1,0:T(8,128)}, u32[]{:S(2)}) copy-start(f32[2,64,1024]{2,1,0:T(8,128)} %field_ref.1) | copy-start | bytes 1572868
  1.0 9.7 %copy-start.4 = (bf16[257]{0:T(512)(128)(2,1)S(1)}, bf16[257]{0:T(512)(128)(2,1)}, u32[]{:S(2)}) copy-start(bf16[257]{0:T(512)(128)(2,1)} %param.8) | copy-start | bytes 1546
  1.0 9.8 %copy-start.1 = (bf16[3,257]{1,0:T(4,128)(2,1)S(1)}, bf16[3,257]{1,0:T(4,128)(2,1)}, u32[]{:S(2)}) copy-start(bf16[3,257]{1,0:T(4,128)(2,1)} %color_ref.1) | copy-start | bytes 4630
  1.0 9.8 %copy-start.2 = (s32[16]{0:T(128)S(1)}, s32[16]{0:T(128)}, u32[]{:S(2)}) copy-start(s32[16]{0:T(128)} %order_ref.1) | copy-start | bytes 196
  1.0 9.8 %copy-start.3 = (f32[3]{0:T(128)S(1)}, f32[3]{0:T(128)}, u32[]{:S(2)}) copy-start(f32[3]{0:T(128)} %light_ref.1) | copy-start | bytes 40
  2.4 28.1 %all-to-all-start = ((f32[16,6,2,8,128]{4,3,2,1,0:T(8,128)}), f32[16,6,2,8,128]{4,3,2,1,0:T(8,128)S(1)}, u32[]{:S(2)}, u32[]{:S(2)}) async-start(f32[16,6,2,8,128]{4,3,2,1,0:T(8,128)} %pack_rows.1), calls=%async_computation | async-start | bytes 1572864 | tf_op jit(solution)/shard_map/all_to_all | solution.py:262
  30.5 5.1 %collective-permute-start = (f32[16,2,8,128]{3,2,1,0:T(8,128)S(1)}, f32[16,2,8,128]{3,2,1,0:T(8,128)S(1)}, u32[]{:S(2)}, u32[]{:S(2)}) collective-permute-start(f32[16,2,8,128]{3,2,1,0:T(8,128)S(1)} %fusion), channel_id=1, source_target_pairs={{0,1},{31,30}} | collective-permute-start | bytes 393224 | tf_op jit(solution)/shard_map/ppermute | solution.py:291

commit v7 on v6

--- a/solution.py
+++ b/solution.py
@@ -13,56 +13,65 @@
 OPACITY_SPAN = 2 ** OPACITY_BITS
 
 
-def pack_kernel(field_ref, out_ref, staged):
+def pack_kernel(field_ref, *rest):
+    *out_refs, staged = rest
     depth, rows, cols = field_ref.shape
-    tiles, padded_rows, _, chunks, _ = out_ref.shape
+    padded_rows, _, chunks, _ = out_refs[0].shape
     tile_rows = padded_rows - 2
     block = depth * chunks
-
-    def spread(j, carry):
-        start = pl.multiple_of(j * SUB, SUB)
-        for k in range(depth):
-            lines = [field_ref[k, pl.ds(start, SUB), c * LANES:(c + 1) * LANES] for c in range(chunks)]
+    here = lax.axis_index("gz")
+    for k in range(depth):
+        for j in range(rows // SUB):
+            lines = [field_ref[k, j * SUB:(j + 1) * SUB, c * LANES:(c + 1) * LANES] for c in range(chunks)]
             for c, value in enumerate(lines):
-                staged[pl.ds(start * block + k * chunks + c, SUB, stride=block), :] = value
-        return carry
-
-    def place(t, carry):
+                staged[pl.ds(j * SUB * block + k * chunks + c, SUB, stride=block), :] = value
+    for step, out_ref in enumerate(out_refs):
+        tile = here ^ step
         values = []
         for i in range(padded_rows):
-            start = lax.rem(t * tile_rows + i - 1 + rows, rows) * block
+            start = lax.rem(tile * tile_rows + i - 1 + rows, rows) * block
             values.append(staged[pl.ds(pl.multiple_of(start, block), block), :])
         for i, value in enumerate(values):
             for k in range(depth):
-                out_ref[t, i, k] = value[k * chunks:(k + 1) * chunks]
-        return carry
-
-    lax.fori_loop(0, rows // SUB, spread, 0)
-    lax.fori_loop(0, tiles, place, 0)
+                out_ref[i, k] = value[k * chunks:(k + 1) * chunks]
 
 
 def packed(field, tiles):
     depth, rows, cols = field.shape
     chunks = cols // LANES
     vmem = pl.BlockSpec(memory_space=pltpu.VMEM)
-    shape = (tiles, rows // tiles + 2, depth, chunks, LANES)
+    shape = (rows // tiles + 2, depth, chunks, LANES)
     return pl.pallas_call(
         pack_kernel,
-        out_shape=jax.ShapeDtypeStruct(shape, field.dtype),
+        out_shape=[jax.ShapeDtypeStruct(shape, field.dtype)] * tiles,
         in_specs=[vmem],
-        out_specs=vmem,
+        out_specs=[vmem] * tiles,
         scratch_shapes=[pltpu.VMEM((rows * depth * chunks, LANES), field.dtype)],
         compiler_params=pltpu.CompilerParams(vmem_limit_bytes=16 << 20),
         name="pack_rows",
     )(field)
 
 
+def collect_kernel(slot_ref, end_ref, *rest):
+    *tile_refs, tiles_ref, wrapped_ref = rest
+    padded_rows, depth, chunks, lanes = tile_refs[0].shape
+    is_first = end_ref[0] == 1
+    for step, tile_ref in enumerate(tile_refs):
+        slot = slot_ref[step]
+        values = [[tile_ref[i, k] for k in range(depth)] for i in range(padded_rows)]
+        for i in range(padded_rows):
+            for k in range(depth):
+                tiles_ref[slot, i, k] = values[i][k]
+        for k in range(depth):
+            wrapped_ref[slot, k] = jnp.where(is_first, values[0][k], values[-1][k])
+
+
 def shifted(x, axis, shift):
     return pltpu.roll(x, shift % x.shape[axis], axis)
 
 
 def prepare_kernel(bands_end_ref, order_ref, light_ref, color_ref, opacity_ref,
-                   brick_at_ref, color_word_ref, opacity_word_ref, light_rows_ref, end_ref):
+                   slot_ref, color_word_ref, opacity_word_ref, light_rows_ref, end_ref):
     bins = color_ref.shape[1] - 1
     _, halves, chunks, lanes = color_word_ref.shape
     shape = (chunks, lanes)
@@ -84,8 +93,10 @@
         light_rows_ref[i] = jnp.full(shape, light_ref[i], jnp.float32)
     for i in range(2):
         end_ref[i] = jnp.full(shape, bands_end_ref[i], jnp.int32)
-    for b in range(order_ref.shape[0]):
-        brick_at_ref[order_ref[b]] = b
+    here = lax.axis_index("gz")
+    bricks = order_ref.shape[0]
+    for step in range(bricks):
+        slot_ref[step] = order_ref[here ^ step]
 
 
 def table_lookup(color_word_ref, opacity_word_ref):
@@ -154,7 +165,7 @@
     return 0.25 + (0.75 * facing) * (facing * inverse)
 
 
-def main_kernel(edge_rows, brick_at, light_ref, color_word_ref, opacity_word_ref, tile_ref,
+def main_kernel(edge_rows, light_ref, color_word_ref, opacity_word_ref, tile_ref,
                 part_ref, color_sum_ref, keep_ref):
     bricks, padded_rows, depth, chunks, lanes = tile_ref.shape
     rows = padded_rows - 2
@@ -163,11 +174,11 @@
     look_up = table_lookup(color_word_ref, opacity_word_ref)
     column_difference = column_differences(shape)
     light = [light_ref[i] for i in range(3)]
-    together = 1
+    together = 2 if bricks % 2 == 0 else 1
 
     def step(trip, carry):
         colors, keeps = list(carry[0]), list(carry[1])
-        at = [brick_at[trip * together + u] for u in range(together)]
+        at = [trip * together + u for u in range(together)]
         fields = [[[tile_ref[b, r, k] for k in range(depth)] for r in range(padded_rows)] for b in at]
         kept = []
         for b, field in zip(at, fields):
@@ -259,7 +270,12 @@
     chunks = cols // LANES
     edge_rows = sorted({0, tile_rows - 1})
     inner_count = tile_rows - len(edge_rows)
-    tiles = lax.all_to_all(packed(scalar, bricks), "gz", split_axis=0, concat_axis=0, tiled=True)
+    arrived = list(packed(scalar, bricks))
+    half = bricks // 2
+    for step in [s for s in range(1, bricks) if s & half] + [s for s in range(1, bricks) if not s & half]:
+        to = [t ^ step for t in range(bricks)]
+        steps = [(t * bands + g, to[t] * bands + g) for t in range(bricks) for g in range(bands)]
+        arrived[step] = lax.ppermute(arrived[step], ("gz", "gy"), steps)
 
     here = lax.axis_index("gz")
     ends = jnp.stack([here == 0, here == bricks - 1]).astype(jnp.int32)
@@ -273,7 +289,7 @@
     cells = bricks * depth * cols
     lines = (chunks, LANES)
     halves = (color_table.shape[1] - 1) // LANES
-    brick_at, color_words, opacity_words, light_rows, end_rows = pl.pallas_call(
+    slots, color_words, opacity_words, light_rows, end_rows = pl.pallas_call(
         prepare_kernel,
         out_shape=[
             jax.ShapeDtypeStruct((bricks,), jnp.int32),
@@ -287,7 +303,17 @@
         compiler_params=params,
         name="prepare_tables",
     )(ends, view_order, light_dir, color_table, opacity_table[None, :])
-    wrapped = jnp.where(end_rows[0] == 1, tiles[:, 0], tiles[:, -1])
+    tiles, wrapped = pl.pallas_call(
+        collect_kernel,
+        out_shape=[
+            jax.ShapeDtypeStruct((bricks, tile_rows + 2, depth) + lines, jnp.float32),
+            jax.ShapeDtypeStruct((bricks, depth) + lines, jnp.float32),
+        ],
+        in_specs=[smem] + [vmem] * (bricks + 1),
+        out_specs=[vmem, vmem],
+        compiler_params=params,
+        name="collect_tiles",
+    )(slots, end_rows, *arrived)
     other = lax.ppermute(wrapped, ("gz", "gy"), pairs)
     parts, color_sums, keeps = pl.pallas_call(
         functools.partial(main_kernel, edge_rows),
@@ -296,13 +322,13 @@
             jax.ShapeDtypeStruct((max(3 * inner_count, 1), chunks, LANES), jnp.float32),
             jax.ShapeDtypeStruct((tile_rows, chunks, LANES), jnp.float32),
         ],
-        in_specs=[smem] + [vmem] * 4,
+        in_specs=[vmem] * 4,
         out_specs=[vmem, vmem, vmem],
         compiler_params=params,
         cost_estimate=pl.CostEstimate(
             flops=100 * cells * tile_rows, bytes_accessed=24 * cells * tile_rows, transcendentals=0),
         name="main_rows",
-    )(brick_at, light_rows, color_words, opacity_words, tiles)
+    )(light_rows, color_words, opacity_words, tiles)
     return pl.pallas_call(
         functools.partial(finish_kernel, edge_rows),
         out_shape=jax.ShapeDtypeStruct((4, 1, tile_rows, cols), jnp.float32),

time: 36.7 us -> 42.6 us (1.16)
  starting transfers between devices: 9.61 us -> 29.3 us
  waiting for transfers between devices: 18.4 us -> 3.54 us
  local copies, waits for them, and re-layouts: 1.06 us -> 3.72 us
  Pallas kernels: 7.17 us -> 5.68 us
    ppermute x0 -> x15, starting transfers between devices: none -> 28 us  [shards(): arrived[step] = lax.ppermute(arrived[step], ('gz', 'gy'), steps)]
    all_to_all x1 -> x0, waiting for transfers between devices: 18.4 us -> none  [shards(): lax.all_to_all(packed(scalar, bricks), 'gz', split_axis=0, concat_axis=0,...]
    all_to_all x1 -> x0, starting transfers between devices: 8.31 us -> none  [shards(): lax.all_to_all(packed(scalar, bricks), 'gz', split_axis=0, concat_axis=0,...]
    ppermute x0 -> x15, waiting for transfers between devices: none -> 3.54 us  [shards(): arrived[step] = lax.ppermute(arrived[step], ('gz', 'gy'), steps)]
    unnamed x10 -> x8, local copies, waits for them, and re-layouts: 1.06 us -> 3.03 us
    pallas_call x1, Pallas kernels: 3.76 us -> 2.61 us  [shards(): pl.pallas_call(functools.partial(main_kernel, edge_rows), out_shape=[jax....]
    broadcast_in_dim x1, local copies, waits for them, and re-layouts: 0.01 us -> 0.68 us  [shards(): opacity_table[None, :]]
    pallas_call x1 -> x2, Pallas kernels: 1.38 us -> 0.98 us  [the longest x1 0.61 us: shards(): pl.pallas_call(collect_kernel, out_shape=[jax.ShapeDtypeStruct((bricks, t...]
  transfers between devices with their start and end apart: 2 -> 16, of which waited for: 1 -> 1; matrix products, arithmetic and copies ran while one was open for 0% -> 2% of each run, Pallas kernels for 13% -> 9%
where the time goes in v7:
time: 42.6 us; the launch traced here: 42.4 us
  starting transfers between devices  29.3 us (69%)
  Pallas kernels  5.68 us (13%)
  local copies, waits for them, and re-layouts  3.72 us (9%)
  waiting for transfers between devices  3.54 us (8%)
    ppermute x15, starting transfers between devices, shards(): arrived[step] = lax.ppermute(arrived[step], ('gz', 'gy'), steps)  28 us
    ppermute x15, waiting for transfers between devices, shards(): arrived[step] = lax.ppermute(arrived[step], ('gz', 'gy'), steps)  3.54 us
    unnamed x8, local copies, waits for them, and re-layouts  3.03 us
    pallas_call x1, Pallas kernels, shards(): pl.pallas_call(functools.partial(main_kernel, edge_rows), out_shape=[jax....  2.61 us
    ppermute x1, starting transfers between devices, shards(): other = lax.ppermute(wrapped, ('gz', 'gy'), pairs)  1.3 us
    pallas_call x1, Pallas kernels, shards(): pl.pallas_call(prepare_kernel, out_shape=[jax.ShapeDtypeStruct((bricks,),...  1.23 us
    pallas_call x1, Pallas kernels, shards(): pl.pallas_call(functools.partial(finish_kernel, edge_rows), out_shape=jax...  0.86 us
  transfers between devices with their start and end apart: 16, of which 1 were waited for; matrix products, arithmetic and copies ran while one was open for 2% of the time, Pallas kernels for 9%

profile of v7, /device:TPU:0, one launch (start us, length us, event | category | flops | bytes accessed | tf_op | source)
XLA Modules:
  0.0 42.4 jit_solution(8847859526813884886)
XLA Ops:
  0.0 0.0 copy-start
  0.0 1.0 %copy-done = f32[2,64,1024]{2,1,0:T(8,128)S(1)} copy-done((f32[2,64,1024]{2,1,0:T(8,128)S(1)}, f32[2,64,1024]{2,1,0:T(8,128)}, u32[]{:S(2)}) %copy-start) | copy-done | bytes 524312
  1.0 0.4 pack_rows.1
  1.4 3.0 %collective-permute-start = (f32[6,2,8,128]{3,2,1,0:T(8,128)S(1)}, f32[6,2,8,128]{3,2,1,0:T(8,128)S(1)}, u32[]{:S(2)}, u32[]{:S(2)}) collective-permute-start(f32[6,2,8,128]{3,2,1,0:T(8,128)S(1)} %get-tuple-element.35), channel_id=1, source_target_pairs={{0,2},{1,3},{2,0},{3,1},{4,6},{5,7},{6,4},{7,5},{8,10},{9,11},{10,... | collective-permute-start | bytes 147464 | tf_op jit(solution)/shard_map/ppermute | solution.py:278
  4.4 1.5 %collective-permute-start.1 = (f32[6,2,8,128]{3,2,1,0:T(8,128)S(1)}, f32[6,2,8,128]{3,2,1,0:T(8,128)S(1)}, u32[]{:S(2)}, u32[]{:S(2)}) collective-permute-start(f32[6,2,8,128]{3,2,1,0:T(8,128)S(1)} %get-tuple-element.36), channel_id=1, source_target_pairs={{0,4},{1,5},{2,6},{3,7},{4,0},{5,1},{6,2},{7,3},{8,12},{9,13},{10,... | collective-permute-start | bytes 147464 | tf_op jit(solution)/shard_map/ppermute | solution.py:278
  6.0 0.0 collective-permute-start.2
  6.0 2.0 %collective-permute-start.3 = (f32[6,2,8,128]{3,2,1,0:T(8,128)S(1)}, f32[6,2,8,128]{3,2,1,0:T(8,128)S(1)}, u32[]{:S(2)}, u32[]{:S(2)}) collective-permute-start(f32[6,2,8,128]{3,2,1,0:T(8,128)S(1)} %get-tuple-element.38), channel_id=1, source_target_pairs={{0,8},{1,9},{2,10},{3,11},{4,12},{5,13},{6,14},{7,15},{8,0},{9,1},... | collective-permute-start | bytes 147464 | tf_op jit(solution)/shard_map/ppermute | solution.py:278
  8.0 1.4 %collective-permute-start.4 = (f32[6,2,8,128]{3,2,1,0:T(8,128)S(1)}, f32[6,2,8,128]{3,2,1,0:T(8,128)S(1)}, u32[]{:S(2)}, u32[]{:S(2)}) collective-permute-start(f32[6,2,8,128]{3,2,1,0:T(8,128)S(1)} %get-tuple-element.39), channel_id=1, source_target_pairs={{0,10},{1,11},{2,8},{3,9},{4,14},{5,15},{6,12},{7,13},{8,2},{9,3},... | collective-permute-start | bytes 147464 | tf_op jit(solution)/shard_map/ppermute | solution.py:278
  9.4 0.0 collective-permute-done.rest_1_
  9.4 2.5 %collective-permute-start.5 = (f32[6,2,8,128]{3,2,1,0:T(8,128)S(1)}, f32[6,2,8,128]{3,2,1,0:T(8,128)S(1)}, u32[]{:S(2)}, u32[]{:S(2)}) collective-permute-start(f32[6,2,8,128]{3,2,1,0:T(8,128)S(1)} %get-tuple-element.40), channel_id=1, source_target_pairs={{0,12},{1,13},{2,14},{3,15},{4,8},{5,9},{6,10},{7,11},{8,4},{9,5},... | collective-permute-start | bytes 147464 | tf_op jit(solution)/shard_map/ppermute | solution.py:278
  11.9 0.0 collective-permute-done.1.rest_2_
  11.9 0.0 collective-permute-start.6
  12.0 0.0 collective-permute-done.2.rest_3_
  12.0 2.9 %collective-permute-start.7 = (f32[6,2,8,128]{3,2,1,0:T(8,128)S(1)}, f32[6,2,8,128]{3,2,1,0:T(8,128)S(1)}, u32[]{:S(2)}, u32[]{:S(2)}) collective-permute-start(f32[6,2,8,128]{3,2,1,0:T(8,128)S(1)} %get-tuple-element.42), channel_id=1, source_target_pairs={{0,16},{1,17},{2,18},{3,19},{4,20},{5,21},{6,22},{7,23},{8,24},{9,... | collective-permute-start | bytes 147464 | tf_op jit(solution)/shard_map/ppermute | solution.py:278
  14.9 0.0 collective-permute-done.3.rest_4_
  14.9 1.3 %collective-permute-start.8 = (f32[6,2,8,128]{3,2,1,0:T(8,128)S(1)}, f32[6,2,8,128]{3,2,1,0:T(8,128)S(1)}, u32[]{:S(2)}, u32[]{:S(2)}) collective-permute-start(f32[6,2,8,128]{3,2,1,0:T(8,128)S(1)} %get-tuple-element.43), channel_id=1, source_target_pairs={{0,18},{1,19},{2,16},{3,17},{4,22},{5,23},{6,20},{7,21},{8,26},{9,... | collective-permute-start | bytes 147464 | tf_op jit(solution)/shard_map/ppermute | solution.py:278
  16.1 0.0 collective-permute-done.4.rest_5_
  16.2 3.5 %collective-permute-start.9 = (f32[6,2,8,128]{3,2,1,0:T(8,128)S(1)}, f32[6,2,8,128]{3,2,1,0:T(8,128)S(1)}, u32[]{:S(2)}, u32[]{:S(2)}) collective-permute-start(f32[6,2,8,128]{3,2,1,0:T(8,128)S(1)} %get-tuple-element.44), channel_id=1, source_target_pairs={{0,20},{1,21},{2,22},{3,23},{4,16},{5,17},{6,18},{7,19},{8,28},{9,... | collective-permute-start | bytes 147464 | tf_op jit(solution)/shard_map/ppermute | solution.py:278
  19.7 0.0 collective-permute-done.5.rest_6_
  19.7 0.0 collective-permute-start.10
  19.7 0.0 collective-permute-done.6.rest_7_
  19.7 3.8 %collective-permute-start.11 = (f32[6,2,8,128]{3,2,1,0:T(8,128)S(1)}, f32[6,2,8,128]{3,2,1,0:T(8,128)S(1)}, u32[]{:S(2)}, u32[]{:S(2)}) collective-permute-start(f32[6,2,8,128]{3,2,1,0:T(8,128)S(1)} %get-tuple-element.46), channel_id=1, source_target_pairs={{0,24},{1,25},{2,26},{3,27},{4,28},{5,29},{6,30},{7,31},{8,16},{9,... | collective-permute-start | bytes 147464 | tf_op jit(solution)/shard_map/ppermute | solution.py:278
  23.6 0.0 collective-permute-done.7.rest_8_
  23.6 1.2 %collective-permute-start.12 = (f32[6,2,8,128]{3,2,1,0:T(8,128)S(1)}, f32[6,2,8,128]{3,2,1,0:T(8,128)S(1)}, u32[]{:S(2)}, u32[]{:S(2)}) collective-permute-start(f32[6,2,8,128]{3,2,1,0:T(8,128)S(1)} %get-tuple-element.47), channel_id=1, source_target_pairs={{0,26},{1,27},{2,24},{3,25},{4,30},{5,31},{6,28},{7,29},{8,18},{9,... | collective-permute-start | bytes 147464 | tf_op jit(solution)/shard_map/ppermute | solution.py:278
  24.7 0.0 collective-permute-done.8.rest_9_
  24.7 4.6 %collective-permute-start.13 = (f32[6,2,8,128]{3,2,1,0:T(8,128)S(1)}, f32[6,2,8,128]{3,2,1,0:T(8,128)S(1)}, u32[]{:S(2)}, u32[]{:S(2)}) collective-permute-start(f32[6,2,8,128]{3,2,1,0:T(8,128)S(1)} %get-tuple-element.48), channel_id=1, source_target_pairs={{0,28},{1,29},{2,30},{3,31},{4,24},{5,25},{6,26},{7,27},{8,20},{9,... | collective-permute-start | bytes 147464 | tf_op jit(solution)/shard_map/ppermute | solution.py:278
  29.3 0.0 collective-permute-done.9.rest_10_
  29.3 0.1 collective-permute-start.14
  29.4 0.1 add_convert_fusion.bands_end_ref
  29.5 0.7 %broadcast_in_dim.3.opacity_ref = bf16[1,257]{1,0:T(2,128)(2,1)S(1)} reshape(bf16[257]{0:T(512)(128)(2,1)} %param.8) | data formatting | bytes 1028 | tf_op jit(solution)/shard_map/broadcast_in_dim | solution.py:305
  30.2 0.0 copy-start.1
  30.2 0.7 %copy-done.1 = bf16[3,257]{1,0:T(4,128)(2,1)S(1)} copy-done((bf16[3,257]{1,0:T(4,128)(2,1)S(1)}, bf16[3,257]{1,0:T(4,128)(2,1)}, u32[]{:S(2)}) %copy-start.1) | copy-done | bytes 1566
  30.9 0.0 copy-start.2
  30.9 0.7 %copy-done.2 = s32[16]{0:T(128)S(1)} copy-done((s32[16]{0:T(128)S(1)}, s32[16]{0:T(128)}, u32[]{:S(2)}) %copy-start.2) | copy-done | bytes 88
  31.5 0.0 copy-start.3
  31.5 0.7 %copy-done.3 = f32[3]{0:T(128)S(1)} copy-done((f32[3]{0:T(128)S(1)}, f32[3]{0:T(128)}, u32[]{:S(2)}) %copy-start.3) | copy-done | bytes 36
  32.2 1.2 %prepare_tables.1 = (s32[16]{0:T(128)S(1)}, f32[3,2,8,128]{3,2,1,0:T(8,128)S(1)}, s32[2,8,128]{2,1,0:T(8,128)S(1)}, f32[3,8,128]{2,1,0:T(8,128)S(1)}, s32[2,8,128]{2,1,0:T(8,128)S(1)}) custom-call(s32[2]{0:T(128)S(1)} %add_convert_fusion.bands_end_ref, s32[16]{0:T(128)S(1)} %copy-done.2, f32[3]{0:T(128)S(1)} %copy-done.3, bf16[3,257]{1,0:T(4,128)(2,1)S(1)} %copy-done.1, ...), custom_call_target="tpu_custom_call" | custom-call | tf_op jit(solution)/shard_map/prepare_tables/pallas_call | solution.py:292
  33.4 0.0 collective-permute-done.10.rest_11_
  33.4 0.0 collective-permute-done.11.rest_12_
  33.4 0.0 collective-permute-done.12.rest_13_
  33.4 0.0 collective-permute-done.13.rest_14_
  33.5 3.5 %collective-permute-done.14.rest_15_ = f32[6,2,8,128]{3,2,1,0:T(8,128)S(1)} collective-permute-done((f32[6,2,8,128]{3,2,1,0:T(8,128)S(1)}, f32[6,2,8,128]{3,2,1,0:T(8,128)S(1)}, u32[]{:S(2)}, u32[]{:S(2)}) %collective-permute-start.14) | collective-permute-done | bytes 49184 | tf_op jit(solution)/shard_map/ppermute | solution.py:278
  37.0 0.6 %collect_tiles.1 = (f32[16,6,2,8,128]{4,3,2,1,0:T(8,128)S(1)}, f32[16,2,8,128]{3,2,1,0:T(8,128)S(1)}) custom-call(s32[16]{0:T(128)S(1)} %get-tuple-element.33.slot_ref, s32[2,8,128]{2,1,0:T(8,128)S(1)} %get-tuple-element.31.end_ref, f32[6,2,8,128]{3,2,1,0:T(8,128)S(1)} %get-tuple-element.34.rest_0_, f32[6,2,8,128]{3,2,1,0:T(8,128)S(1)} %collective-permute-done.rest_1_, ...), custom_call_target="tpu_custom_call" | custom-call | tf_op jit(solution)/shard_map/collect_tiles/pallas_call | solution.py:306
  37.6 1.3 %collective-permute-start.15 = (f32[16,2,8,128]{3,2,1,0:T(8,128)S(1)}, f32[16,2,8,128]{3,2,1,0:T(8,128)S(1)}, u32[]{:S(2)}, u32[]{:S(2)}) collective-permute-start(f32[16,2,8,128]{3,2,1,0:T(8,128)S(1)} %get-tuple-element.51), channel_id=1, source_target_pairs={{0,1},{31,30}} | collective-permute-start | bytes 393224 | tf_op jit(solution)/shard_map/ppermute | solution.py:317
  38.9 2.6 %main_rows.1 = (f32[16,2,2,5,8,128]{5,4,3,2,1,0:T(8,128)S(1)}, f32[6,8,128]{2,1,0:T(8,128)S(1)}, f32[4,8,128]{2,1,0:T(8,128)S(1)}) custom-call(f32[3,8,128]{2,1,0:T(8,128)S(1)} %get-tuple-element.32.light_ref, f32[3,2,8,128]{3,2,1,0:T(8,128)S(1)} %get-tuple-element.52.color_word_ref, s32[2,8,128]{2,1,0:T(8,128)S(1)} %get-tuple-element.53.opacity_word_ref, ...), custom_call_target="tpu_custom_call" | custom-call | flops 13107200 | bytes 3145728 | tf_op jit(solution)/shard_map/main_rows/pallas_call | solution.py:318
  41.5 0.0 collective-permute-done.15.other_ref
  41.5 0.9 %edge_rows.1 = f32[4,1,4,1024]{3,2,1,0:T(4,128)} custom-call(s32[2,8,128]{2,1,0:T(8,128)S(1)} %get-tuple-element.31.end_ref, f32[3,8,128]{2,1,0:T(8,128)S(1)} %get-tuple-element.32.light_ref, f32[16,6,2,8,128]{4,3,2,1,0:T(8,128)S(1)} %get-tuple-element.50.tile_ref, f32[16,2,8,128]{3,2,1,0:T(8,128)S(1)} %collective-permute-done.15.other_ref, ...), custom_call_target="tpu_custom_call" | custom-call | flops 1310720 | bytes 3145728 | tf_op jit(solution)/shard_map/edge_rows/pallas_call | solution.py:332
Async XLA Ops:
  0.0 1.0 %copy-start = (f32[2,64,1024]{2,1,0:T(8,128)S(1)}, f32[2,64,1024]{2,1,0:T(8,128)}, u32[]{:S(2)}) copy-start(f32[2,64,1024]{2,1,0:T(8,128)} %field_ref.1) | copy-start | bytes 1572868
  1.4 8.0 %collective-permute-start = (f32[6,2,8,128]{3,2,1,0:T(8,128)S(1)}, f32[6,2,8,128]{3,2,1,0:T(8,128)S(1)}, u32[]{:S(2)}, u32[]{:S(2)}) collective-permute-start(f32[6,2,8,128]{3,2,1,0:T(8,128)S(1)} %get-tuple-element.35), channel_id=1, source_target_pairs={{0,2},{1,3},{2,0},{3,1},{4,6},{5,7},{6,4},{7,5},{8,10},{9,11},{10,... | collective-permute-start | bytes 147464 | tf_op jit(solution)/shard_map/ppermute | solution.py:278
  4.4 7.5 %collective-permute-start.1 = (f32[6,2,8,128]{3,2,1,0:T(8,128)S(1)}, f32[6,2,8,128]{3,2,1,0:T(8,128)S(1)}, u32[]{:S(2)}, u32[]{:S(2)}) collective-permute-start(f32[6,2,8,128]{3,2,1,0:T(8,128)S(1)} %get-tuple-element.36), channel_id=1, source_target_pairs={{0,4},{1,5},{2,6},{3,7},{4,0},{5,1},{6,2},{7,3},{8,12},{9,13},{10,... | collective-permute-start | bytes 147464 | tf_op jit(solution)/shard_map/ppermute | solution.py:278
  6.0 6.0 %collective-permute-start.2 = (f32[6,2,8,128]{3,2,1,0:T(8,128)S(1)}, f32[6,2,8,128]{3,2,1,0:T(8,128)S(1)}, u32[]{:S(2)}, u32[]{:S(2)}) collective-permute-start(f32[6,2,8,128]{3,2,1,0:T(8,128)S(1)} %get-tuple-element.37), channel_id=1, source_target_pairs={{0,6},{1,7},{2,4},{3,5},{4,2},{5,3},{6,0},{7,1},{8,14},{9,15},{10,... | collective-permute-start | bytes 147464 | tf_op jit(solution)/shard_map/ppermute | solution.py:278
  6.0 8.9 %collective-permute-start.3 = (f32[6,2,8,128]{3,2,1,0:T(8,128)S(1)}, f32[6,2,8,128]{3,2,1,0:T(8,128)S(1)}, u32[]{:S(2)}, u32[]{:S(2)}) collective-permute-start(f32[6,2,8,128]{3,2,1,0:T(8,128)S(1)} %get-tuple-element.38), channel_id=1, source_target_pairs={{0,8},{1,9},{2,10},{3,11},{4,12},{5,13},{6,14},{7,15},{8,0},{9,1},... | collective-permute-start | bytes 147464 | tf_op jit(solution)/shard_map/ppermute | solution.py:278
  8.0 8.1 %collective-permute-start.4 = (f32[6,2,8,128]{3,2,1,0:T(8,128)S(1)}, f32[6,2,8,128]{3,2,1,0:T(8,128)S(1)}, u32[]{:S(2)}, u32[]{:S(2)}) collective-permute-start(f32[6,2,8,128]{3,2,1,0:T(8,128)S(1)} %get-tuple-element.39), channel_id=1, source_target_pairs={{0,10},{1,11},{2,8},{3,9},{4,14},{5,15},{6,12},{7,13},{8,2},{9,3},... | collective-permute-start | bytes 147464 | tf_op jit(solution)/shard_map/ppermute | solution.py:278
  9.4 10.3 %collective-permute-start.5 = (f32[6,2,8,128]{3,2,1,0:T(8,128)S(1)}, f32[6,2,8,128]{3,2,1,0:T(8,128)S(1)}, u32[]{:S(2)}, u32[]{:S(2)}) collective-permute-start(f32[6,2,8,128]{3,2,1,0:T(8,128)S(1)} %get-tuple-element.40), channel_id=1, source_target_pairs={{0,12},{1,13},{2,14},{3,15},{4,8},{5,9},{6,10},{7,11},{8,4},{9,5},... | collective-permute-start | bytes 147464 | tf_op jit(solution)/shard_map/ppermute | solution.py:278
  11.9 7.8 %collective-permute-start.6 = (f32[6,2,8,128]{3,2,1,0:T(8,128)S(1)}, f32[6,2,8,128]{3,2,1,0:T(8,128)S(1)}, u32[]{:S(2)}, u32[]{:S(2)}) collective-permute-start(f32[6,2,8,128]{3,2,1,0:T(8,128)S(1)} %get-tuple-element.41), channel_id=1, source_target_pairs={{0,14},{1,15},{2,12},{3,13},{4,10},{5,11},{6,8},{7,9},{8,6},{9,7},... | collective-permute-start | bytes 147464 | tf_op jit(solution)/shard_map/ppermute | solution.py:278
  12.0 11.6 %collective-permute-start.7 = (f32[6,2,8,128]{3,2,1,0:T(8,128)S(1)}, f32[6,2,8,128]{3,2,1,0:T(8,128)S(1)}, u32[]{:S(2)}, u32[]{:S(2)}) collective-permute-start(f32[6,2,8,128]{3,2,1,0:T(8,128)S(1)} %get-tuple-element.42), channel_id=1, source_target_pairs={{0,16},{1,17},{2,18},{3,19},{4,20},{5,21},{6,22},{7,23},{8,24},{9,... | collective-permute-start | bytes 147464 | tf_op jit(solution)/shard_map/ppermute | solution.py:278
  14.9 9.8 %collective-permute-start.8 = (f32[6,2,8,128]{3,2,1,0:T(8,128)S(1)}, f32[6,2,8,128]{3,2,1,0:T(8,128)S(1)}, u32[]{:S(2)}, u32[]{:S(2)}) collective-permute-start(f32[6,2,8,128]{3,2,1,0:T(8,128)S(1)} %get-tuple-element.43), channel_id=1, source_target_pairs={{0,18},{1,19},{2,16},{3,17},{4,22},{5,23},{6,20},{7,21},{8,26},{9,... | collective-permute-start | bytes 147464 | tf_op jit(solution)/shard_map/ppermute | solution.py:278
  16.2 13.1 %collective-permute-start.9 = (f32[6,2,8,128]{3,2,1,0:T(8,128)S(1)}, f32[6,2,8,128]{3,2,1,0:T(8,128)S(1)}, u32[]{:S(2)}, u32[]{:S(2)}) collective-permute-start(f32[6,2,8,128]{3,2,1,0:T(8,128)S(1)} %get-tuple-element.44), channel_id=1, source_target_pairs={{0,20},{1,21},{2,22},{3,23},{4,16},{5,17},{6,18},{7,19},{8,28},{9,... | collective-permute-start | bytes 147464 | tf_op jit(solution)/shard_map/ppermute | solution.py:278
  19.7 13.7 %collective-permute-start.10 = (f32[6,2,8,128]{3,2,1,0:T(8,128)S(1)}, f32[6,2,8,128]{3,2,1,0:T(8,128)S(1)}, u32[]{:S(2)}, u32[]{:S(2)}) collective-permute-start(f32[6,2,8,128]{3,2,1,0:T(8,128)S(1)} %get-tuple-element.45), channel_id=1, source_target_pairs={{0,22},{1,23},{2,20},{3,21},{4,18},{5,19},{6,16},{7,17},{8,30},{9,... | collective-permute-start | bytes 147464 | tf_op jit(solution)/shard_map/ppermute | solution.py:278
  19.7 13.7 %collective-permute-start.11 = (f32[6,2,8,128]{3,2,1,0:T(8,128)S(1)}, f32[6,2,8,128]{3,2,1,0:T(8,128)S(1)}, u32[]{:S(2)}, u32[]{:S(2)}) collective-permute-start(f32[6,2,8,128]{3,2,1,0:T(8,128)S(1)} %get-tuple-element.46), channel_id=1, source_target_pairs={{0,24},{1,25},{2,26},{3,27},{4,28},{5,29},{6,30},{7,31},{8,16},{9,... | collective-permute-start | bytes 147464 | tf_op jit(solution)/shard_map/ppermute | solution.py:278
  23.6 9.9 %collective-permute-start.12 = (f32[6,2,8,128]{3,2,1,0:T(8,128)S(1)}, f32[6,2,8,128]{3,2,1,0:T(8,128)S(1)}, u32[]{:S(2)}, u32[]{:S(2)}) collective-permute-start(f32[6,2,8,128]{3,2,1,0:T(8,128)S(1)} %get-tuple-element.47), channel_id=1, source_target_pairs={{0,26},{1,27},{2,24},{3,25},{4,30},{5,31},{6,28},{7,29},{8,18},{9,... | collective-permute-start | bytes 147464 | tf_op jit(solution)/shard_map/ppermute | solution.py:278
  24.7 8.7 %collective-permute-start.13 = (f32[6,2,8,128]{3,2,1,0:T(8,128)S(1)}, f32[6,2,8,128]{3,2,1,0:T(8,128)S(1)}, u32[]{:S(2)}, u32[]{:S(2)}) collective-permute-start(f32[6,2,8,128]{3,2,1,0:T(8,128)S(1)} %get-tuple-element.48), channel_id=1, source_target_pairs={{0,28},{1,29},{2,30},{3,31},{4,24},{5,25},{6,26},{7,27},{8,20},{9,... | collective-permute-start | bytes 147464 | tf_op jit(solution)/shard_map/ppermute | solution.py:278
  29.3 7.7 %collective-permute-start.14 = (f32[6,2,8,128]{3,2,1,0:T(8,128)S(1)}, f32[6,2,8,128]{3,2,1,0:T(8,128)S(1)}, u32[]{:S(2)}, u32[]{:S(2)}) collective-permute-start(f32[6,2,8,128]{3,2,1,0:T(8,128)S(1)} %get-tuple-element.49), channel_id=1, source_target_pairs={{0,30},{1,31},{2,28},{3,29},{4,26},{5,27},{6,24},{7,25},{8,22},{9,... | collective-permute-start | bytes 147464 | tf_op jit(solution)/shard_map/ppermute | solution.py:278
  30.2 0.7 %copy-start.1 = (bf16[3,257]{1,0:T(4,128)(2,1)S(1)}, bf16[3,257]{1,0:T(4,128)(2,1)}, u32[]{:S(2)}) copy-start(bf16[3,257]{1,0:T(4,128)(2,1)} %color_ref.1) | copy-start | bytes 4630
  30.9 0.7 %copy-start.2 = (s32[16]{0:T(128)S(1)}, s32[16]{0:T(128)}, u32[]{:S(2)}) copy-start(s32[16]{0:T(128)} %order_ref.1) | copy-start | bytes 196
  31.5 0.7 %copy-start.3 = (f32[3]{0:T(128)S(1)}, f32[3]{0:T(128)}, u32[]{:S(2)}) copy-start(f32[3]{0:T(128)} %light_ref.1) | copy-start | bytes 40
  37.6 3.9 %collective-permute-start.15 = (f32[16,2,8,128]{3,2,1,0:T(8,128)S(1)}, f32[16,2,8,128]{3,2,1,0:T(8,128)S(1)}, u32[]{:S(2)}, u32[]{:S(2)}) collective-permute-start(f32[16,2,8,128]{3,2,1,0:T(8,128)S(1)} %get-tuple-element.51), channel_id=1, source_target_pairs={{0,1},{31,30}} | collective-permute-start | bytes 393224 | tf_op jit(solution)/shard_map/ppermute | solution.py:317

commit v8 on v6

--- a/solution.py
+++ b/solution.py
@@ -19,26 +19,17 @@
     tile_rows = padded_rows - 2
     block = depth * chunks
 
-    def spread(j, carry):
-        start = pl.multiple_of(j * SUB, SUB)
-        for k in range(depth):
-            lines = [field_ref[k, pl.ds(start, SUB), c * LANES:(c + 1) * LANES] for c in range(chunks)]
+    for k in range(depth):
+        for j in range(rows // SUB):
+            lines = [field_ref[k, j * SUB:(j + 1) * SUB, c * LANES:(c + 1) * LANES] for c in range(chunks)]
             for c, value in enumerate(lines):
-                staged[pl.ds(start * block + k * chunks + c, SUB, stride=block), :] = value
-        return carry
-
-    def place(t, carry):
-        values = []
-        for i in range(padded_rows):
-            start = lax.rem(t * tile_rows + i - 1 + rows, rows) * block
-            values.append(staged[pl.ds(pl.multiple_of(start, block), block), :])
-        for i, value in enumerate(values):
+                staged[pl.ds(j * SUB * block + k * chunks + c, SUB, stride=block), :] = value
+    for t in range(tiles):
+        starts = [((t * tile_rows + i - 1) % rows) * block for i in range(padded_rows)]
+        blocks = [staged[start:start + block, :] for start in starts]
+        for i, value in enumerate(blocks):
             for k in range(depth):
                 out_ref[t, i, k] = value[k * chunks:(k + 1) * chunks]
-        return carry
-
-    lax.fori_loop(0, rows // SUB, spread, 0)
-    lax.fori_loop(0, tiles, place, 0)
 
 
 def packed(field, tiles):
@@ -48,7 +39,7 @@
     shape = (tiles, rows // tiles + 2, depth, chunks, LANES)
     return pl.pallas_call(
         pack_kernel,
-        out_shape=jax.ShapeDtypeStruct(shape, field.dtype),
+        out_shape=pltpu.VMEM(shape, field.dtype),
         in_specs=[vmem],
         out_specs=vmem,
         scratch_shapes=[pltpu.VMEM((rows * depth * chunks, LANES), field.dtype)],
@@ -163,7 +154,7 @@
     look_up = table_lookup(color_word_ref, opacity_word_ref)
     column_difference = column_differences(shape)
     light = [light_ref[i] for i in range(3)]
-    together = 1
+    together = 2 if bricks % 2 == 0 else 1
 
     def step(trip, carry):
         colors, keeps = list(carry[0]), list(carry[1])
@@ -276,7 +267,7 @@
     brick_at, color_words, opacity_words, light_rows, end_rows = pl.pallas_call(
         prepare_kernel,
         out_shape=[
-            jax.ShapeDtypeStruct((bricks,), jnp.int32),
+            pltpu.SMEM((bricks,), jnp.int32),
             jax.ShapeDtypeStruct((3, halves) + lines, jnp.float32),
             jax.ShapeDtypeStruct((halves,) + lines, jnp.int32),
             jax.ShapeDtypeStruct((3,) + lines, jnp.float32),

time: 36.7 us -> 35.3 us (0.962)
  Pallas kernels: 7.17 us -> 5.26 us
  waiting for transfers between devices: 18.4 us -> 18.9 us
    pallas_call x1, Pallas kernels: 3.76 us -> 2.61 us  [shards(): pl.pallas_call(functools.partial(main_kernel, edge_rows), out_shape=[jax....]
    pallas_call x2, Pallas kernels: 2.55 us -> 1.78 us  [the longest x1 1.08 us: packed(): pl.pallas_call(pack_kernel, out_shape=pltpu.VMEM(shape, field.dtype), in_...]
    all_to_all x1, waiting for transfers between devices: 18.4 us -> 18.9 us  [shards(): lax.all_to_all(packed(scalar, bricks), 'gz', split_axis=0, concat_axis=0,...]
  transfers between devices with their start and end apart: 2 -> 2, of which waited for: 1 -> 1; matrix products, arithmetic and copies ran while one was open for 0% -> 0% of each run, Pallas kernels for 13% -> 9%
where the time goes in v8:
time: 35.3 us; the launch traced here: 35 us
  waiting for transfers between devices  18.9 us (54%)
  starting transfers between devices  9.61 us (27%)
  Pallas kernels  5.26 us (15%)
  local copies, waits for them, and re-layouts  1.06 us (3%)
    all_to_all x1, waiting for transfers between devices, shards(): lax.all_to_all(packed(scalar, bricks), 'gz', split_axis=0, concat_axis=0,...  18.9 us
    all_to_all x1, starting transfers between devices, shards(): lax.all_to_all(packed(scalar, bricks), 'gz', split_axis=0, concat_axis=0,...  8.31 us
    pallas_call x1, Pallas kernels, shards(): pl.pallas_call(functools.partial(main_kernel, edge_rows), out_shape=[jax....  2.61 us
    ppermute x1, starting transfers between devices, shards(): other = lax.ppermute(wrapped, ('gz', 'gy'), pairs)  1.3 us
    pallas_call x1, Pallas kernels, packed(): pl.pallas_call(pack_kernel, out_shape=pltpu.VMEM(shape, field.dtype), in_...  1.08 us
    unnamed x10, local copies, waits for them, and re-layouts  1.06 us
    pallas_call x1, Pallas kernels, shards(): pl.pallas_call(functools.partial(finish_kernel, edge_rows), out_shape=jax...  0.87 us
  transfers between devices with their start and end apart: 2, of which 1 were waited for; matrix products, arithmetic and copies ran while one was open for 0% of the time, Pallas kernels for 9%

profile of v8, /device:TPU:0, one launch (start us, length us, event | category | flops | bytes accessed | tf_op | source)
XLA Modules:
  0.0 35.0 jit_solution(16993545666581488377)
XLA Ops:
  0.0 0.0 copy-start
  0.0 1.0 %copy-done = f32[2,64,1024]{2,1,0:T(8,128)S(1)} copy-done((f32[2,64,1024]{2,1,0:T(8,128)S(1)}, f32[2,64,1024]{2,1,0:T(8,128)}, u32[]{:S(2)}) %copy-start) | copy-done | bytes 524312
  1.0 0.0 copy-start.4
  1.0 0.0 copy-start.1
  1.0 0.0 copy-start.2
  1.0 0.0 copy-start.3
  1.1 1.1 %pack_rows.1 = f32[16,6,2,8,128]{4,3,2,1,0:T(8,128)} custom-call(f32[2,64,1024]{2,1,0:T(8,128)S(1)} %copy-done), custom_call_target="tpu_custom_call" | custom-call | tf_op jit(solution)/shard_map/pack_rows/pallas_call | solution.py:40
  2.1 8.3 %all-to-all-start = ((f32[16,6,2,8,128]{4,3,2,1,0:T(8,128)}), f32[16,6,2,8,128]{4,3,2,1,0:T(8,128)S(1)}, u32[]{:S(2)}, u32[]{:S(2)}) async-start(f32[16,6,2,8,128]{4,3,2,1,0:T(8,128)} %pack_rows.1), calls=%async_computation | async-start | bytes 1572864 | tf_op jit(solution)/shard_map/all_to_all | solution.py:253
  10.5 0.0 copy-done.4
  10.5 0.1 add_convert_fusion.bands_end_ref
  10.6 0.0 copy-done.1
  10.6 0.0 copy-done.2
  10.6 0.0 copy-done.3
  10.6 0.7 %prepare_tables.1 = (s32[16]{0:T(128)S(4)}, f32[3,2,8,128]{3,2,1,0:T(8,128)S(1)}, s32[2,8,128]{2,1,0:T(8,128)S(1)}, f32[3,8,128]{2,1,0:T(8,128)S(1)}, s32[2,8,128]{2,1,0:T(8,128)S(1)}) custom-call(s32[2]{0:T(128)S(1)} %add_convert_fusion.bands_end_ref, s32[16]{0:T(128)S(1)} %copy-done.2, f32[3]{0:T(128)S(1)} %copy-done.3, bf16[3,257]{1,0:T(4,128)(2,1)S(1)} %copy-done.1, ...), custom_call_target="tpu_custom_call" | custom-call | tf_op jit(solution)/shard_map/prepare_tables/pallas_call | solution.py:267
  11.3 18.9 %all-to-all-done.tile_ref = f32[16,6,2,8,128]{4,3,2,1,0:T(8,128)S(1)} async-done(((f32[16,6,2,8,128]{4,3,2,1,0:T(8,128)}), f32[16,6,2,8,128]{4,3,2,1,0:T(8,128)S(1)}, u32[]{:S(2)}, u32[]{:S(2)}) %all-to-all-start) | async-done | bytes 786464 | tf_op jit(solution)/shard_map/all_to_all | solution.py:253
  30.2 1.3 %collective-permute-start = (f32[16,2,8,128]{3,2,1,0:T(8,128)S(1)}, f32[16,2,8,128]{3,2,1,0:T(8,128)S(1)}, u32[]{:S(2)}, u32[]{:S(2)}) collective-permute-start(f32[16,2,8,128]{3,2,1,0:T(8,128)S(1)} %fusion), channel_id=1, source_target_pairs={{0,1},{31,30}} | collective-permute-start | bytes 393224 | tf_op jit(solution)/shard_map/ppermute | solution.py:282
  31.5 2.6 %main_rows.1 = (f32[16,2,2,5,8,128]{5,4,3,2,1,0:T(8,128)S(1)}, f32[6,8,128]{2,1,0:T(8,128)S(1)}, f32[4,8,128]{2,1,0:T(8,128)S(1)}) custom-call(s32[16]{0:T(128)S(4)} %get-tuple-element.15.brick_at, f32[3,8,128]{2,1,0:T(8,128)S(1)} %get-tuple-element.14.light_ref, f32[3,2,8,128]{3,2,1,0:T(8,128)S(1)} %get-tuple-element.16.color_word_ref, ...), custom_call_target="tpu_custom_call" | custom-call | flops 13107200 | bytes 3145728 | tf_op jit(solution)/shard_map/main_rows/pallas_call | solution.py:283
  34.1 0.0 collective-permute-done.other_ref
  34.2 0.9 %edge_rows.1 = f32[4,1,4,1024]{3,2,1,0:T(4,128)} custom-call(s32[2,8,128]{2,1,0:T(8,128)S(1)} %get-tuple-element.13.end_ref, f32[3,8,128]{2,1,0:T(8,128)S(1)} %get-tuple-element.14.light_ref, f32[16,6,2,8,128]{4,3,2,1,0:T(8,128)S(1)} %all-to-all-done.tile_ref, f32[16,2,8,128]{3,2,1,0:T(8,128)S(1)} %collective-permute-done.other_ref, ...), custom_call_target="tpu_custom_call" | custom-call | flops 1310720 | bytes 3145728 | tf_op jit(solution)/shard_map/edge_rows/pallas_call | solution.py:297
  (3 shorter events, 0.0 us)
Async XLA Ops:
  0.0 1.0 %copy-start = (f32[2,64,1024]{2,1,0:T(8,128)S(1)}, f32[2,64,1024]{2,1,0:T(8,128)}, u32[]{:S(2)}) copy-start(f32[2,64,1024]{2,1,0:T(8,128)} %field_ref.1) | copy-start | bytes 1572868
  1.0 9.4 %copy-start.4 = (bf16[257]{0:T(512)(128)(2,1)S(1)}, bf16[257]{0:T(512)(128)(2,1)}, u32[]{:S(2)}) copy-start(bf16[257]{0:T(512)(128)(2,1)} %param.8) | copy-start | bytes 1546
  1.0 9.5 %copy-start.1 = (bf16[3,257]{1,0:T(4,128)(2,1)S(1)}, bf16[3,257]{1,0:T(4,128)(2,1)}, u32[]{:S(2)}) copy-start(bf16[3,257]{1,0:T(4,128)(2,1)} %color_ref.1) | copy-start | bytes 4630
  1.0 9.5 %copy-start.2 = (s32[16]{0:T(128)S(1)}, s32[16]{0:T(128)}, u32[]{:S(2)}) copy-start(s32[16]{0:T(128)} %order_ref.1) | copy-start | bytes 196
  1.0 9.5 %copy-start.3 = (f32[3]{0:T(128)S(1)}, f32[3]{0:T(128)}, u32[]{:S(2)}) copy-start(f32[3]{0:T(128)} %light_ref.1) | copy-start | bytes 40
  2.1 28.1 %all-to-all-start = ((f32[16,6,2,8,128]{4,3,2,1,0:T(8,128)}), f32[16,6,2,8,128]{4,3,2,1,0:T(8,128)S(1)}, u32[]{:S(2)}, u32[]{:S(2)}) async-start(f32[16,6,2,8,128]{4,3,2,1,0:T(8,128)} %pack_rows.1), calls=%async_computation | async-start | bytes 1572864 | tf_op jit(solution)/shard_map/all_to_all | solution.py:253
  30.2 3.9 %collective-permute-start = (f32[16,2,8,128]{3,2,1,0:T(8,128)S(1)}, f32[16,2,8,128]{3,2,1,0:T(8,128)S(1)}, u32[]{:S(2)}, u32[]{:S(2)}) collective-permute-start(f32[16,2,8,128]{3,2,1,0:T(8,128)S(1)} %fusion), channel_id=1, source_target_pairs={{0,1},{31,30}} | collective-permute-start | bytes 393224 | tf_op jit(solution)/shard_map/ppermute | solution.py:282

commit v9 on v8

--- a/solution.py
+++ b/solution.py
@@ -13,6 +13,11 @@
 OPACITY_SPAN = 2 ** OPACITY_BITS
 
 
+def exchange_order(tiles):
+    parts = 4 if tiles % 4 == 0 else 1
+    return [(i % parts) * (tiles // parts) + i // parts for i in range(tiles)]
+
+
 def pack_kernel(field_ref, out_ref, staged):
     depth, rows, cols = field_ref.shape
     tiles, padded_rows, _, chunks, _ = out_ref.shape
@@ -24,12 +29,12 @@
             lines = [field_ref[k, j * SUB:(j + 1) * SUB, c * LANES:(c + 1) * LANES] for c in range(chunks)]
             for c, value in enumerate(lines):
                 staged[pl.ds(j * SUB * block + k * chunks + c, SUB, stride=block), :] = value
-    for t in range(tiles):
+    for place, t in enumerate(exchange_order(tiles)):
         starts = [((t * tile_rows + i - 1) % rows) * block for i in range(padded_rows)]
         blocks = [staged[start:start + block, :] for start in starts]
         for i, value in enumerate(blocks):
             for k in range(depth):
-                out_ref[t, i, k] = value[k * chunks:(k + 1) * chunks]
+                out_ref[place, i, k] = value[k * chunks:(k + 1) * chunks]
 
 
 def packed(field, tiles):
@@ -75,8 +80,8 @@
         light_rows_ref[i] = jnp.full(shape, light_ref[i], jnp.float32)
     for i in range(2):
         end_ref[i] = jnp.full(shape, bands_end_ref[i], jnp.int32)
-    for b in range(order_ref.shape[0]):
-        brick_at_ref[order_ref[b]] = b
+    for place, b in enumerate(exchange_order(order_ref.shape[0])):
+        brick_at_ref[order_ref[b]] = place
 
 
 def table_lookup(color_word_ref, opacity_word_ref):
@@ -250,7 +255,9 @@
     chunks = cols // LANES
     edge_rows = sorted({0, tile_rows - 1})
     inner_count = tile_rows - len(edge_rows)
-    tiles = lax.all_to_all(packed(scalar, bricks), "gz", split_axis=0, concat_axis=0, tiled=True)
+    tiles = lax.all_to_all(
+        packed(scalar, bricks), "gz", split_axis=0, concat_axis=0, tiled=True,
+        axis_index_groups=[exchange_order(bricks)])
 
     here = lax.axis_index("gz")
     ends = jnp.stack([here == 0, here == bricks - 1]).astype(jnp.int32)

time: 35.3 us -> 37.4 us (1.059)
  waiting for transfers between devices: 18.9 us -> 21 us
    all_to_all x1, waiting for transfers between devices: 18.9 us -> 21 us  [shards(): lax.all_to_all(packed(scalar, bricks), 'gz', split_axis=0, concat_axis=0,...]
where the time goes in v9:
time: 37.4 us; the launch traced here: 37.1 us
  waiting for transfers between devices  21 us (56%)
  starting transfers between devices  9.61 us (26%)
  Pallas kernels  5.26 us (14%)
  local copies, waits for them, and re-layouts  1.06 us (3%)
    all_to_all x1, waiting for transfers between devices, shards(): lax.all_to_all(packed(scalar, bricks), 'gz', split_axis=0, concat_axis=0,...  21 us
    all_to_all x1, starting transfers between devices, shards(): lax.all_to_all(packed(scalar, bricks), 'gz', split_axis=0, concat_axis=0,...  8.31 us
    pallas_call x1, Pallas kernels, shards(): pl.pallas_call(functools.partial(main_kernel, edge_rows), out_shape=[jax....  2.61 us
    ppermute x1, starting transfers between devices, shards(): other = lax.ppermute(wrapped, ('gz', 'gy'), pairs)  1.3 us
    pallas_call x1, Pallas kernels, packed(): pl.pallas_call(pack_kernel, out_shape=pltpu.VMEM(shape, field.dtype), in_...  1.08 us
    unnamed x10, local copies, waits for them, and re-layouts  1.06 us
    pallas_call x1, Pallas kernels, shards(): pl.pallas_call(functools.partial(finish_kernel, edge_rows), out_shape=jax...  0.87 us
  transfers between devices with their start and end apart: 2, of which 1 were waited for; matrix products, arithmetic and copies ran while one was open for 0% of the time, Pallas kernels for 9%

profile of v9, /device:TPU:0, one launch (start us, length us, event | category | flops | bytes accessed | tf_op | source)
XLA Modules:
  0.0 37.1 jit_solution(8707099057587093967)
XLA Ops:
  0.0 0.0 copy-start
  0.0 1.0 %copy-done = f32[2,64,1024]{2,1,0:T(8,128)S(1)} copy-done((f32[2,64,1024]{2,1,0:T(8,128)S(1)}, f32[2,64,1024]{2,1,0:T(8,128)}, u32[]{:S(2)}) %copy-start) | copy-done | bytes 524312
  1.0 0.0 copy-start.4
  1.0 0.0 copy-start.1
  1.0 0.0 copy-start.2
  1.0 0.0 copy-start.3
  1.1 1.1 %pack_rows.1 = f32[16,6,2,8,128]{4,3,2,1,0:T(8,128)} custom-call(f32[2,64,1024]{2,1,0:T(8,128)S(1)} %copy-done), custom_call_target="tpu_custom_call" | custom-call | tf_op jit(solution)/shard_map/pack_rows/pallas_call | solution.py:45
  2.1 8.3 %all-to-all-start = ((f32[16,6,2,8,128]{4,3,2,1,0:T(8,128)}), f32[16,6,2,8,128]{4,3,2,1,0:T(8,128)S(1)}, u32[]{:S(2)}, u32[]{:S(2)}) async-start(f32[16,6,2,8,128]{4,3,2,1,0:T(8,128)} %pack_rows.1), calls=%async_computation | async-start | bytes 1572864 | tf_op jit(solution)/shard_map/all_to_all | solution.py:258
  10.5 0.0 copy-done.4
  10.5 0.1 add_convert_fusion.bands_end_ref
  10.6 0.0 copy-done.1
  10.6 0.0 copy-done.2
  10.6 0.0 copy-done.3
  10.6 0.7 %prepare_tables.1 = (s32[16]{0:T(128)S(4)}, f32[3,2,8,128]{3,2,1,0:T(8,128)S(1)}, s32[2,8,128]{2,1,0:T(8,128)S(1)}, f32[3,8,128]{2,1,0:T(8,128)S(1)}, s32[2,8,128]{2,1,0:T(8,128)S(1)}) custom-call(s32[2]{0:T(128)S(1)} %add_convert_fusion.bands_end_ref, s32[16]{0:T(128)S(1)} %copy-done.2, f32[3]{0:T(128)S(1)} %copy-done.3, bf16[3,257]{1,0:T(4,128)(2,1)S(1)} %copy-done.1, ...), custom_call_target="tpu_custom_call" | custom-call | tf_op jit(solution)/shard_map/prepare_tables/pallas_call | solution.py:274
  11.3 21.0 %all-to-all-done.tile_ref = f32[16,6,2,8,128]{4,3,2,1,0:T(8,128)S(1)} async-done(((f32[16,6,2,8,128]{4,3,2,1,0:T(8,128)}), f32[16,6,2,8,128]{4,3,2,1,0:T(8,128)S(1)}, u32[]{:S(2)}, u32[]{:S(2)}) %all-to-all-start) | async-done | bytes 786464 | tf_op jit(solution)/shard_map/all_to_all | solution.py:258
  32.3 1.3 %collective-permute-start = (f32[16,2,8,128]{3,2,1,0:T(8,128)S(1)}, f32[16,2,8,128]{3,2,1,0:T(8,128)S(1)}, u32[]{:S(2)}, u32[]{:S(2)}) collective-permute-start(f32[16,2,8,128]{3,2,1,0:T(8,128)S(1)} %fusion), channel_id=1, source_target_pairs={{0,1},{31,30}} | collective-permute-start | bytes 393224 | tf_op jit(solution)/shard_map/ppermute | solution.py:289
  33.6 2.6 %main_rows.1 = (f32[16,2,2,5,8,128]{5,4,3,2,1,0:T(8,128)S(1)}, f32[6,8,128]{2,1,0:T(8,128)S(1)}, f32[4,8,128]{2,1,0:T(8,128)S(1)}) custom-call(s32[16]{0:T(128)S(4)} %get-tuple-element.15.brick_at, f32[3,8,128]{2,1,0:T(8,128)S(1)} %get-tuple-element.14.light_ref, f32[3,2,8,128]{3,2,1,0:T(8,128)S(1)} %get-tuple-element.16.color_word_ref, ...), custom_call_target="tpu_custom_call" | custom-call | flops 13107200 | bytes 3145728 | tf_op jit(solution)/shard_map/main_rows/pallas_call | solution.py:290
  36.2 0.0 collective-permute-done.other_ref
  36.3 0.9 %edge_rows.1 = f32[4,1,4,1024]{3,2,1,0:T(4,128)} custom-call(s32[2,8,128]{2,1,0:T(8,128)S(1)} %get-tuple-element.13.end_ref, f32[3,8,128]{2,1,0:T(8,128)S(1)} %get-tuple-element.14.light_ref, f32[16,6,2,8,128]{4,3,2,1,0:T(8,128)S(1)} %all-to-all-done.tile_ref, f32[16,2,8,128]{3,2,1,0:T(8,128)S(1)} %collective-permute-done.other_ref, ...), custom_call_target="tpu_custom_call" | custom-call | flops 1310720 | bytes 3145728 | tf_op jit(solution)/shard_map/edge_rows/pallas_call | solution.py:304
  (3 shorter events, 0.0 us)
Async XLA Ops:
  0.0 1.0 %copy-start = (f32[2,64,1024]{2,1,0:T(8,128)S(1)}, f32[2,64,1024]{2,1,0:T(8,128)}, u32[]{:S(2)}) copy-start(f32[2,64,1024]{2,1,0:T(8,128)} %field_ref.1) | copy-start | bytes 1572868
  1.0 9.4 %copy-start.4 = (bf16[257]{0:T(512)(128)(2,1)S(1)}, bf16[257]{0:T(512)(128)(2,1)}, u32[]{:S(2)}) copy-start(bf16[257]{0:T(512)(128)(2,1)} %param.8) | copy-start | bytes 1546
  1.0 9.5 %copy-start.1 = (bf16[3,257]{1,0:T(4,128)(2,1)S(1)}, bf16[3,257]{1,0:T(4,128)(2,1)}, u32[]{:S(2)}) copy-start(bf16[3,257]{1,0:T(4,128)(2,1)} %color_ref.1) | copy-start | bytes 4630
  1.0 9.5 %copy-start.2 = (s32[16]{0:T(128)S(1)}, s32[16]{0:T(128)}, u32[]{:S(2)}) copy-start(s32[16]{0:T(128)} %order_ref.1) | copy-start | bytes 196
  1.0 9.5 %copy-start.3 = (f32[3]{0:T(128)S(1)}, f32[3]{0:T(128)}, u32[]{:S(2)}) copy-start(f32[3]{0:T(128)} %light_ref.1) | copy-start | bytes 40
  2.1 30.2 %all-to-all-start = ((f32[16,6,2,8,128]{4,3,2,1,0:T(8,128)}), f32[16,6,2,8,128]{4,3,2,1,0:T(8,128)S(1)}, u32[]{:S(2)}, u32[]{:S(2)}) async-start(f32[16,6,2,8,128]{4,3,2,1,0:T(8,128)} %pack_rows.1), calls=%async_computation | async-start | bytes 1572864 | tf_op jit(solution)/shard_map/all_to_all | solution.py:258
  32.3 3.9 %collective-permute-start = (f32[16,2,8,128]{3,2,1,0:T(8,128)S(1)}, f32[16,2,8,128]{3,2,1,0:T(8,128)S(1)}, u32[]{:S(2)}, u32[]{:S(2)}) collective-permute-start(f32[16,2,8,128]{3,2,1,0:T(8,128)S(1)} %fusion), channel_id=1, source_target_pairs={{0,1},{31,30}} | collective-permute-start | bytes 393224 | tf_op jit(solution)/shard_map/ppermute | solution.py:289

commit v10 on v9

--- a/solution.py
+++ b/solution.py
@@ -14,8 +14,7 @@
 
 
 def exchange_order(tiles):
-    parts = 4 if tiles % 4 == 0 else 1
-    return [(i % parts) * (tiles // parts) + i // parts for i in range(tiles)]
+    return list(range(tiles))[::-1]
 
 
 def pack_kernel(field_ref, out_ref, staged):

time: 37.4 us -> 35.6 us (0.952)
  waiting for transfers between devices: 21 us -> 17.1 us
  starting transfers between devices: 9.61 us -> 11.7 us
    all_to_all x1, waiting for transfers between devices: 21 us -> 17.1 us  [shards(): lax.all_to_all(packed(scalar, bricks), 'gz', split_axis=0, concat_axis=0,...]
    all_to_all x1, starting transfers between devices: 8.31 us -> 10.4 us  [shards(): lax.all_to_all(packed(scalar, bricks), 'gz', split_axis=0, concat_axis=0,...]
where the time goes in v10:
time: 35.6 us; the launch traced here: 35.3 us
  waiting for transfers between devices  17.1 us (48%)
  starting transfers between devices  11.7 us (33%)
  Pallas kernels  5.26 us (15%)
  local copies, waits for them, and re-layouts  1.06 us (3%)
    all_to_all x1, waiting for transfers between devices, shards(): lax.all_to_all(packed(scalar, bricks), 'gz', split_axis=0, concat_axis=0,...  17.1 us
    all_to_all x1, starting transfers between devices, shards(): lax.all_to_all(packed(scalar, bricks), 'gz', split_axis=0, concat_axis=0,...  10.4 us
    pallas_call x1, Pallas kernels, shards(): pl.pallas_call(functools.partial(main_kernel, edge_rows), out_shape=[jax....  2.61 us
    ppermute x1, starting transfers between devices, shards(): other = lax.ppermute(wrapped, ('gz', 'gy'), pairs)  1.3 us
    pallas_call x1, Pallas kernels, packed(): pl.pallas_call(pack_kernel, out_shape=pltpu.VMEM(shape, field.dtype), in_...  1.08 us
    unnamed x10, local copies, waits for them, and re-layouts  1.06 us
    pallas_call x1, Pallas kernels, shards(): pl.pallas_call(functools.partial(finish_kernel, edge_rows), out_shape=jax...  0.87 us
  transfers between devices with their start and end apart: 2, of which 1 were waited for; matrix products, arithmetic and copies ran while one was open for 0% of the time, Pallas kernels for 9%

profile of v10, /device:TPU:0, one launch (start us, length us, event | category | flops | bytes accessed | tf_op | source)
XLA Modules:
  0.0 35.3 jit_solution(11608496574787637236)
XLA Ops:
  0.0 0.0 copy-start
  0.0 1.0 %copy-done = f32[2,64,1024]{2,1,0:T(8,128)S(1)} copy-done((f32[2,64,1024]{2,1,0:T(8,128)S(1)}, f32[2,64,1024]{2,1,0:T(8,128)}, u32[]{:S(2)}) %copy-start) | copy-done | bytes 524312
  1.0 0.0 copy-start.4
  1.0 0.0 copy-start.1
  1.0 0.0 copy-start.2
  1.0 0.0 copy-start.3
  1.1 1.1 %pack_rows.1 = f32[16,6,2,8,128]{4,3,2,1,0:T(8,128)} custom-call(f32[2,64,1024]{2,1,0:T(8,128)S(1)} %copy-done), custom_call_target="tpu_custom_call" | custom-call | tf_op jit(solution)/shard_map/pack_rows/pallas_call | solution.py:44
  2.1 10.4 %all-to-all-start = ((f32[16,6,2,8,128]{4,3,2,1,0:T(8,128)}), f32[16,6,2,8,128]{4,3,2,1,0:T(8,128)S(1)}, u32[]{:S(2)}, u32[]{:S(2)}) async-start(f32[16,6,2,8,128]{4,3,2,1,0:T(8,128)} %pack_rows.1), calls=%async_computation | async-start | bytes 1572864 | tf_op jit(solution)/shard_map/all_to_all | solution.py:257
  12.6 0.0 copy-done.4
  12.6 0.1 add_convert_fusion.bands_end_ref
  12.7 0.0 copy-done.1
  12.7 0.0 copy-done.2
  12.7 0.0 copy-done.3
  12.7 0.7 %prepare_tables.1 = (s32[16]{0:T(128)S(4)}, f32[3,2,8,128]{3,2,1,0:T(8,128)S(1)}, s32[2,8,128]{2,1,0:T(8,128)S(1)}, f32[3,8,128]{2,1,0:T(8,128)S(1)}, s32[2,8,128]{2,1,0:T(8,128)S(1)}) custom-call(s32[2]{0:T(128)S(1)} %add_convert_fusion.bands_end_ref, s32[16]{0:T(128)S(1)} %copy-done.2, f32[3]{0:T(128)S(1)} %copy-done.3, bf16[3,257]{1,0:T(4,128)(2,1)S(1)} %copy-done.1, ...), custom_call_target="tpu_custom_call" | custom-call | tf_op jit(solution)/shard_map/prepare_tables/pallas_call | solution.py:273
  13.4 17.1 %all-to-all-done.tile_ref = f32[16,6,2,8,128]{4,3,2,1,0:T(8,128)S(1)} async-done(((f32[16,6,2,8,128]{4,3,2,1,0:T(8,128)}), f32[16,6,2,8,128]{4,3,2,1,0:T(8,128)S(1)}, u32[]{:S(2)}, u32[]{:S(2)}) %all-to-all-start) | async-done | bytes 786464 | tf_op jit(solution)/shard_map/all_to_all | solution.py:257
  30.5 1.3 %collective-permute-start = (f32[16,2,8,128]{3,2,1,0:T(8,128)S(1)}, f32[16,2,8,128]{3,2,1,0:T(8,128)S(1)}, u32[]{:S(2)}, u32[]{:S(2)}) collective-permute-start(f32[16,2,8,128]{3,2,1,0:T(8,128)S(1)} %fusion), channel_id=1, source_target_pairs={{0,1},{31,30}} | collective-permute-start | bytes 393224 | tf_op jit(solution)/shard_map/ppermute | solution.py:288
  31.8 2.6 %main_rows.1 = (f32[16,2,2,5,8,128]{5,4,3,2,1,0:T(8,128)S(1)}, f32[6,8,128]{2,1,0:T(8,128)S(1)}, f32[4,8,128]{2,1,0:T(8,128)S(1)}) custom-call(s32[16]{0:T(128)S(4)} %get-tuple-element.15.brick_at, f32[3,8,128]{2,1,0:T(8,128)S(1)} %get-tuple-element.14.light_ref, f32[3,2,8,128]{3,2,1,0:T(8,128)S(1)} %get-tuple-element.16.color_word_ref, ...), custom_call_target="tpu_custom_call" | custom-call | flops 13107200 | bytes 3145728 | tf_op jit(solution)/shard_map/main_rows/pallas_call | solution.py:289
  34.4 0.0 collective-permute-done.other_ref
  34.5 0.9 %edge_rows.1 = f32[4,1,4,1024]{3,2,1,0:T(4,128)} custom-call(s32[2,8,128]{2,1,0:T(8,128)S(1)} %get-tuple-element.13.end_ref, f32[3,8,128]{2,1,0:T(8,128)S(1)} %get-tuple-element.14.light_ref, f32[16,6,2,8,128]{4,3,2,1,0:T(8,128)S(1)} %all-to-all-done.tile_ref, f32[16,2,8,128]{3,2,1,0:T(8,128)S(1)} %collective-permute-done.other_ref, ...), custom_call_target="tpu_custom_call" | custom-call | flops 1310720 | bytes 3145728 | tf_op jit(solution)/shard_map/edge_rows/pallas_call | solution.py:303
  (3 shorter events, 0.0 us)
Async XLA Ops:
  0.0 1.0 %copy-start = (f32[2,64,1024]{2,1,0:T(8,128)S(1)}, f32[2,64,1024]{2,1,0:T(8,128)}, u32[]{:S(2)}) copy-start(f32[2,64,1024]{2,1,0:T(8,128)} %field_ref.1) | copy-start | bytes 1572868
  1.0 11.5 %copy-start.4 = (bf16[257]{0:T(512)(128)(2,1)S(1)}, bf16[257]{0:T(512)(128)(2,1)}, u32[]{:S(2)}) copy-start(bf16[257]{0:T(512)(128)(2,1)} %param.8) | copy-start | bytes 1546
  1.0 11.6 %copy-start.1 = (bf16[3,257]{1,0:T(4,128)(2,1)S(1)}, bf16[3,257]{1,0:T(4,128)(2,1)}, u32[]{:S(2)}) copy-start(bf16[3,257]{1,0:T(4,128)(2,1)} %color_ref.1) | copy-start | bytes 4630
  1.0 11.6 %copy-start.2 = (s32[16]{0:T(128)S(1)}, s32[16]{0:T(128)}, u32[]{:S(2)}) copy-start(s32[16]{0:T(128)} %order_ref.1) | copy-start | bytes 196
  1.0 11.6 %copy-start.3 = (f32[3]{0:T(128)S(1)}, f32[3]{0:T(128)}, u32[]{:S(2)}) copy-start(f32[3]{0:T(128)} %light_ref.1) | copy-start | bytes 40
  2.1 28.4 %all-to-all-start = ((f32[16,6,2,8,128]{4,3,2,1,0:T(8,128)}), f32[16,6,2,8,128]{4,3,2,1,0:T(8,128)S(1)}, u32[]{:S(2)}, u32[]{:S(2)}) async-start(f32[16,6,2,8,128]{4,3,2,1,0:T(8,128)} %pack_rows.1), calls=%async_computation | async-start | bytes 1572864 | tf_op jit(solution)/shard_map/all_to_all | solution.py:257
  30.5 3.9 %collective-permute-start = (f32[16,2,8,128]{3,2,1,0:T(8,128)S(1)}, f32[16,2,8,128]{3,2,1,0:T(8,128)S(1)}, u32[]{:S(2)}, u32[]{:S(2)}) collective-permute-start(f32[16,2,8,128]{3,2,1,0:T(8,128)S(1)} %fusion), channel_id=1, source_target_pairs={{0,1},{31,30}} | collective-permute-start | bytes 393224 | tf_op jit(solution)/shard_map/ppermute | solution.py:288

commit v11 on v10

--- a/solution.py
+++ b/solution.py
@@ -14,7 +14,8 @@
 
 
 def exchange_order(tiles):
-    return list(range(tiles))[::-1]
+    flip = tiles - tiles // 4 if tiles & (tiles - 1) == 0 else 0
+    return [t ^ flip for t in range(tiles)]
 
 
 def pack_kernel(field_ref, out_ref, staged):

time: 35.6 us -> 34.1 us (0.958)
  starting transfers between devices: 11.7 us -> 10.1 us
    all_to_all x1, starting transfers between devices: 10.4 us -> 8.79 us  [shards(): lax.all_to_all(packed(scalar, bricks), 'gz', split_axis=0, concat_axis=0,...]
  transfers between devices with their start and end apart: 2 -> 2, of which waited for: 1 -> 1; matrix products, arithmetic and copies ran while one was open for 0% -> 0% of each run, Pallas kernels for 9% -> 10%
where the time goes in v11:
time: 34.1 us; the launch traced here: 33.9 us
  waiting for transfers between devices  17.3 us (51%)
  starting transfers between devices  10.1 us (30%)
  Pallas kernels  5.26 us (15%)
  local copies, waits for them, and re-layouts  1.06 us (3%)
    all_to_all x1, waiting for transfers between devices, shards(): lax.all_to_all(packed(scalar, bricks), 'gz', split_axis=0, concat_axis=0,...  17.3 us
    all_to_all x1, starting transfers between devices, shards(): lax.all_to_all(packed(scalar, bricks), 'gz', split_axis=0, concat_axis=0,...  8.79 us
    pallas_call x1, Pallas kernels, shards(): pl.pallas_call(functools.partial(main_kernel, edge_rows), out_shape=[jax....  2.61 us
    ppermute x1, starting transfers between devices, shards(): other = lax.ppermute(wrapped, ('gz', 'gy'), pairs)  1.3 us
    pallas_call x1, Pallas kernels, packed(): pl.pallas_call(pack_kernel, out_shape=pltpu.VMEM(shape, field.dtype), in_...  1.08 us
    unnamed x10, local copies, waits for them, and re-layouts  1.06 us
    pallas_call x1, Pallas kernels, shards(): pl.pallas_call(functools.partial(finish_kernel, edge_rows), out_shape=jax...  0.87 us
    pallas_call x1, Pallas kernels, shards(): pl.pallas_call(prepare_kernel, out_shape=[pltpu.SMEM((bricks,), jnp.int32...  0.7 us
  transfers between devices with their start and end apart: 2, of which 1 were waited for; matrix products, arithmetic and copies ran while one was open for 0% of the time, Pallas kernels for 10%

profile of v11, /device:TPU:0, one launch (start us, length us, event | category | flops | bytes accessed | tf_op | source)
XLA Modules:
  0.0 33.9 jit_solution(15265627826223886059)
XLA Ops:
  0.0 0.0 copy-start
  0.0 1.0 %copy-done = f32[2,64,1024]{2,1,0:T(8,128)S(1)} copy-done((f32[2,64,1024]{2,1,0:T(8,128)S(1)}, f32[2,64,1024]{2,1,0:T(8,128)}, u32[]{:S(2)}) %copy-start) | copy-done | bytes 524312
  1.0 0.0 copy-start.4
  1.0 0.0 copy-start.1
  1.0 0.0 copy-start.2
  1.0 0.0 copy-start.3
  1.1 1.1 %pack_rows.1 = f32[16,6,2,8,128]{4,3,2,1,0:T(8,128)} custom-call(f32[2,64,1024]{2,1,0:T(8,128)S(1)} %copy-done), custom_call_target="tpu_custom_call" | custom-call | tf_op jit(solution)/shard_map/pack_rows/pallas_call | solution.py:45
  2.1 8.8 %all-to-all-start = ((f32[16,6,2,8,128]{4,3,2,1,0:T(8,128)}), f32[16,6,2,8,128]{4,3,2,1,0:T(8,128)S(1)}, u32[]{:S(2)}, u32[]{:S(2)}) async-start(f32[16,6,2,8,128]{4,3,2,1,0:T(8,128)} %pack_rows.1), calls=%async_computation | async-start | bytes 1572864 | tf_op jit(solution)/shard_map/all_to_all | solution.py:258
  10.9 0.0 copy-done.4
  10.9 0.1 add_convert_fusion.bands_end_ref
  11.0 0.0 copy-done.1
  11.0 0.0 copy-done.2
  11.0 0.0 copy-done.3
  11.0 0.7 %prepare_tables.1 = (s32[16]{0:T(128)S(4)}, f32[3,2,8,128]{3,2,1,0:T(8,128)S(1)}, s32[2,8,128]{2,1,0:T(8,128)S(1)}, f32[3,8,128]{2,1,0:T(8,128)S(1)}, s32[2,8,128]{2,1,0:T(8,128)S(1)}) custom-call(s32[2]{0:T(128)S(1)} %add_convert_fusion.bands_end_ref, s32[16]{0:T(128)S(1)} %copy-done.2, f32[3]{0:T(128)S(1)} %copy-done.3, bf16[3,257]{1,0:T(4,128)(2,1)S(1)} %copy-done.1, ...), custom_call_target="tpu_custom_call" | custom-call | tf_op jit(solution)/shard_map/prepare_tables/pallas_call | solution.py:274
  11.8 17.3 %all-to-all-done.tile_ref = f32[16,6,2,8,128]{4,3,2,1,0:T(8,128)S(1)} async-done(((f32[16,6,2,8,128]{4,3,2,1,0:T(8,128)}), f32[16,6,2,8,128]{4,3,2,1,0:T(8,128)S(1)}, u32[]{:S(2)}, u32[]{:S(2)}) %all-to-all-start) | async-done | bytes 786464 | tf_op jit(solution)/shard_map/all_to_all | solution.py:258
  29.1 1.3 %collective-permute-start = (f32[16,2,8,128]{3,2,1,0:T(8,128)S(1)}, f32[16,2,8,128]{3,2,1,0:T(8,128)S(1)}, u32[]{:S(2)}, u32[]{:S(2)}) collective-permute-start(f32[16,2,8,128]{3,2,1,0:T(8,128)S(1)} %fusion), channel_id=1, source_target_pairs={{0,1},{31,30}} | collective-permute-start | bytes 393224 | tf_op jit(solution)/shard_map/ppermute | solution.py:289
  30.4 2.6 %main_rows.1 = (f32[16,2,2,5,8,128]{5,4,3,2,1,0:T(8,128)S(1)}, f32[6,8,128]{2,1,0:T(8,128)S(1)}, f32[4,8,128]{2,1,0:T(8,128)S(1)}) custom-call(s32[16]{0:T(128)S(4)} %get-tuple-element.15.brick_at, f32[3,8,128]{2,1,0:T(8,128)S(1)} %get-tuple-element.14.light_ref, f32[3,2,8,128]{3,2,1,0:T(8,128)S(1)} %get-tuple-element.16.color_word_ref, ...), custom_call_target="tpu_custom_call" | custom-call | flops 13107200 | bytes 3145728 | tf_op jit(solution)/shard_map/main_rows/pallas_call | solution.py:290
  33.0 0.0 collective-permute-done.other_ref
  33.0 0.9 %edge_rows.1 = f32[4,1,4,1024]{3,2,1,0:T(4,128)} custom-call(s32[2,8,128]{2,1,0:T(8,128)S(1)} %get-tuple-element.13.end_ref, f32[3,8,128]{2,1,0:T(8,128)S(1)} %get-tuple-element.14.light_ref, f32[16,6,2,8,128]{4,3,2,1,0:T(8,128)S(1)} %all-to-all-done.tile_ref, f32[16,2,8,128]{3,2,1,0:T(8,128)S(1)} %collective-permute-done.other_ref, ...), custom_call_target="tpu_custom_call" | custom-call | flops 1310720 | bytes 3145728 | tf_op jit(solution)/shard_map/edge_rows/pallas_call | solution.py:304
  (3 shorter events, 0.0 us)
Async XLA Ops:
  0.0 1.0 %copy-start = (f32[2,64,1024]{2,1,0:T(8,128)S(1)}, f32[2,64,1024]{2,1,0:T(8,128)}, u32[]{:S(2)}) copy-start(f32[2,64,1024]{2,1,0:T(8,128)} %field_ref.1) | copy-start | bytes 1572868
  1.0 9.9 %copy-start.4 = (bf16[257]{0:T(512)(128)(2,1)S(1)}, bf16[257]{0:T(512)(128)(2,1)}, u32[]{:S(2)}) copy-start(bf16[257]{0:T(512)(128)(2,1)} %param.8) | copy-start | bytes 1546
  1.0 10.0 %copy-start.1 = (bf16[3,257]{1,0:T(4,128)(2,1)S(1)}, bf16[3,257]{1,0:T(4,128)(2,1)}, u32[]{:S(2)}) copy-start(bf16[3,257]{1,0:T(4,128)(2,1)} %color_ref.1) | copy-start | bytes 4630
  1.0 10.0 %copy-start.2 = (s32[16]{0:T(128)S(1)}, s32[16]{0:T(128)}, u32[]{:S(2)}) copy-start(s32[16]{0:T(128)} %order_ref.1) | copy-start | bytes 196
  1.0 10.0 %copy-start.3 = (f32[3]{0:T(128)S(1)}, f32[3]{0:T(128)}, u32[]{:S(2)}) copy-start(f32[3]{0:T(128)} %light_ref.1) | copy-start | bytes 40
  2.1 26.9 %all-to-all-start = ((f32[16,6,2,8,128]{4,3,2,1,0:T(8,128)}), f32[16,6,2,8,128]{4,3,2,1,0:T(8,128)S(1)}, u32[]{:S(2)}, u32[]{:S(2)}) async-start(f32[16,6,2,8,128]{4,3,2,1,0:T(8,128)} %pack_rows.1), calls=%async_computation | async-start | bytes 1572864 | tf_op jit(solution)/shard_map/all_to_all | solution.py:258
  29.1 3.9 %collective-permute-start = (f32[16,2,8,128]{3,2,1,0:T(8,128)S(1)}, f32[16,2,8,128]{3,2,1,0:T(8,128)S(1)}, u32[]{:S(2)}, u32[]{:S(2)}) collective-permute-start(f32[16,2,8,128]{3,2,1,0:T(8,128)S(1)} %fusion), channel_id=1, source_target_pairs={{0,1},{31,30}} | collective-permute-start | bytes 393224 | tf_op jit(solution)/shard_map/ppermute | solution.py:289

commit v12 on v11

--- a/solution.py
+++ b/solution.py
@@ -1,4 +1,5 @@
 import functools
+import math
 
 import jax
 import jax.numpy as jnp
@@ -18,39 +19,68 @@
     return [t ^ flip for t in range(tiles)]
 
 
-def pack_kernel(field_ref, out_ref, staged):
+def pack_kernel(tiles, field_ref, out_ref, field, spread, in_sems, out_sems):
     depth, rows, cols = field_ref.shape
-    tiles, padded_rows, _, chunks, _ = out_ref.shape
-    tile_rows = padded_rows - 2
+    chunks = cols // LANES
     block = depth * chunks
-
-    for k in range(depth):
-        for j in range(rows // SUB):
-            lines = [field_ref[k, j * SUB:(j + 1) * SUB, c * LANES:(c + 1) * LANES] for c in range(chunks)]
-            for c, value in enumerate(lines):
-                staged[pl.ds(j * SUB * block + k * chunks + c, SUB, stride=block), :] = value
-    for place, t in enumerate(exchange_order(tiles)):
-        starts = [((t * tile_rows + i - 1) % rows) * block for i in range(padded_rows)]
-        blocks = [staged[start:start + block, :] for start in starts]
-        for i, value in enumerate(blocks):
-            for k in range(depth):
-                out_ref[place, i, k] = value[k * chunks:(k + 1) * chunks]
+    tile_rows = rows // tiles
+    pieces = in_sems.shape[0]
+    piece_rows = rows // pieces
+    order = exchange_order(tiles)
+
+    def copy_in(p):
+        part = pl.ds(p * piece_rows, piece_rows)
+        return pltpu.make_async_copy(field_ref.at[:, part], field.at[:, part], in_sems.at[p])
+
+    def copy_out(t):
+        part = spread.at[pl.ds(t * tile_rows * block, (tile_rows + 2) * block)]
+        return pltpu.make_async_copy(part, out_ref.at[order.index(t)], out_sems.at[t])
+
+    for p in range(pieces):
+        copy_in(p).start()
+    started = 0
+    for p in range(pieces):
+        copy_in(p).wait()
+        for k in range(depth):
+            for row in range(p * piece_rows, (p + 1) * piece_rows, SUB):
+                lines = [field[k, row:row + SUB, c * LANES:(c + 1) * LANES] for c in range(chunks)]
+                for c, value in enumerate(lines):
+                    spread[pl.ds((row + 1) * block + k * chunks + c, SUB, stride=block), :] = value
+        if p == 0:
+            spread[(rows + 1) * block:, :] = spread[block:2 * block, :]
+        if p == pieces - 1:
+            spread[:block, :] = spread[rows * block:(rows + 1) * block, :]
+        ready = [t for t in range(1, tiles) if (t + 1) * tile_rows < (p + 1) * piece_rows]
+        if p == pieces - 1:
+            ready = list(range(1, tiles)) + [0]
+        for t in ready[started:]:
+            copy_out(t).start()
+        started = len(ready)
+    for t in range(tiles):
+        copy_out(t).wait()
 
 
 def packed(field, tiles):
     depth, rows, cols = field.shape
     chunks = cols // LANES
-    vmem = pl.BlockSpec(memory_space=pltpu.VMEM)
-    shape = (tiles, rows // tiles + 2, depth, chunks, LANES)
-    return pl.pallas_call(
-        pack_kernel,
-        out_shape=pltpu.VMEM(shape, field.dtype),
-        in_specs=[vmem],
-        out_specs=vmem,
-        scratch_shapes=[pltpu.VMEM((rows * depth * chunks, LANES), field.dtype)],
+    padded_rows = rows // tiles + 2
+    pieces = 4 if rows % (4 * SUB) == 0 else 1
+    hbm = pl.BlockSpec(memory_space=pltpu.HBM)
+    flat = pl.pallas_call(
+        functools.partial(pack_kernel, tiles),
+        out_shape=jax.ShapeDtypeStruct((tiles, padded_rows * depth * chunks, LANES), field.dtype),
+        in_specs=[hbm],
+        out_specs=hbm,
+        scratch_shapes=[
+            pltpu.VMEM((depth, rows, cols), field.dtype),
+            pltpu.VMEM(((rows + 2) * depth * chunks, LANES), field.dtype),
+            pltpu.SemaphoreType.DMA((pieces,)),
+            pltpu.SemaphoreType.DMA((tiles,)),
+        ],
         compiler_params=pltpu.CompilerParams(vmem_limit_bytes=16 << 20),
         name="pack_rows",
     )(field)
+    return flat.reshape(tiles, padded_rows, depth, chunks, LANES)
 
 
 def shifted(x, axis, shift):
@@ -77,7 +107,7 @@
             color_word_ref[c, h] = jnp.broadcast_to(color_words[c:c + 1, span], shape)
         opacity_word_ref[h] = jnp.broadcast_to(opacity_words[:, span], shape)
     for i in range(3):
-        light_rows_ref[i] = jnp.full(shape, light_ref[i], jnp.float32)
+        light_rows_ref[i] = jnp.full(shape, light_ref[i], jnp.float32) * math.sqrt(0.75)
     for i in range(2):
         end_ref[i] = jnp.full(shape, bands_end_ref[i], jnp.int32)
     for place, b in enumerate(exchange_order(order_ref.shape[0])):
@@ -147,7 +177,7 @@
 def shading_of(facing, squared_plus_one):
     near = pltpu.reciprocal(squared_plus_one, approx=True)
     inverse = near * (2.0 - squared_plus_one * near)
-    return 0.25 + (0.75 * facing) * (facing * inverse)
+    return 0.25 + (facing * facing) * inverse
 
 
 def main_kernel(edge_rows, brick_at, light_ref, color_word_ref, opacity_word_ref, tile_ref,
@@ -159,7 +189,7 @@
     look_up = table_lookup(color_word_ref, opacity_word_ref)
     column_difference = column_differences(shape)
     light = [light_ref[i] for i in range(3)]
-    together = 2 if bricks % 2 == 0 else 1
+    together = 4 if bricks % 4 == 0 else 1
 
     def step(trip, carry):
         colors, keeps = list(carry[0]), list(carry[1])
@@ -209,7 +239,7 @@
     light_rows = light_ref[1]
     is_first, is_last = end_ref[0] == 1, end_ref[1] == 1
 
-    together = 4 if bricks % 4 == 0 else 1
+    together = 8 if bricks % 8 == 0 else 1
 
     def step(trip, colors):
         colors = list(colors)

time: 34.1 us -> 34.2 us (level)
    pallas_call x1, Pallas kernels: 1.08 us -> 1.46 us  [packed(): pl.pallas_call(functools.partial(pack_kernel, tiles), out_shape=jax.Shape...]
  transfers between devices with their start and end apart: 2 -> 2, of which waited for: 1 -> 1; matrix products, arithmetic and copies ran while one was open for 0% -> 0% of each run, Pallas kernels for 10% -> 9%
where the time goes in v12:
time: 34.2 us; the launch traced here: 33.9 us
  waiting for transfers between devices  17.3 us (51%)
  starting transfers between devices  10.1 us (30%)
  Pallas kernels  5.29 us (15%)
  local copies, waits for them, and re-layouts  1.06 us (3%)
    all_to_all x1, waiting for transfers between devices, shards(): lax.all_to_all(packed(scalar, bricks), 'gz', split_axis=0, concat_axis=0,...  17.3 us
    all_to_all x1, starting transfers between devices, shards(): lax.all_to_all(packed(scalar, bricks), 'gz', split_axis=0, concat_axis=0,...  8.8 us
    pallas_call x1, Pallas kernels, shards(): pl.pallas_call(functools.partial(main_kernel, edge_rows), out_shape=[jax....  2.29 us
    pallas_call x1, Pallas kernels, packed(): pl.pallas_call(functools.partial(pack_kernel, tiles), out_shape=jax.Shape...  1.46 us
    ppermute x1, starting transfers between devices, shards(): other = lax.ppermute(wrapped, ('gz', 'gy'), pairs)  1.3 us
    unnamed x10, local copies, waits for them, and re-layouts  1.06 us
    pallas_call x1, Pallas kernels, shards(): pl.pallas_call(functools.partial(finish_kernel, edge_rows), out_shape=jax...  0.84 us
    pallas_call x1, Pallas kernels, shards(): pl.pallas_call(prepare_kernel, out_shape=[pltpu.SMEM((bricks,), jnp.int32...  0.7 us
  transfers between devices with their start and end apart: 2, of which 1 were waited for; matrix products, arithmetic and copies ran while one was open for 0% of the time, Pallas kernels for 9%

profile of v12, /device:TPU:0, one launch (start us, length us, event | category | flops | bytes accessed | tf_op | source)
XLA Modules:
  0.0 33.9 jit_solution(16343145243490026221)
XLA Ops:
  0.0 0.0 copy-start
  0.0 1.0 %copy-done = f32[2,64,1024]{2,1,0:T(8,128)S(1)} copy-done((f32[2,64,1024]{2,1,0:T(8,128)S(1)}, f32[2,64,1024]{2,1,0:T(8,128)}, u32[]{:S(2)}) %copy-start) | copy-done | bytes 524312
  1.0 0.0 copy-start.4
  1.0 0.0 copy-start.1
  1.0 0.0 copy-start.2
  1.0 0.0 copy-start.3
  1.1 1.5 %pack_rows.1 = f32[16,96,128]{2,1,0:T(8,128)} custom-call(f32[2,64,1024]{2,1,0:T(8,128)S(1)} %copy-done), custom_call_target="tpu_custom_call" | custom-call | tf_op jit(solution)/shard_map/pack_rows/pallas_call | solution.py:69
  2.5 8.8 %all-to-all-start = ((f32[16,6,2,8,128]{4,3,2,1,0:T(8,128)}), f32[16,6,2,8,128]{4,3,2,1,0:T(8,128)S(1)}, u32[]{:S(2)}, u32[]{:S(2)}) async-start(f32[16,6,2,8,128]{4,3,2,1,0:T(8,128)} %bitcast.2), calls=%async_computation | async-start | bytes 1572864 | tf_op jit(solution)/shard_map/all_to_all | solution.py:288
  11.3 0.0 copy-done.4
  11.3 0.1 add_convert_fusion.bands_end_ref
  11.4 0.0 copy-done.1
  11.4 0.0 copy-done.2
  11.4 0.0 copy-done.3
  11.4 0.7 %prepare_tables.1 = (s32[16]{0:T(128)S(4)}, f32[3,2,8,128]{3,2,1,0:T(8,128)S(1)}, s32[2,8,128]{2,1,0:T(8,128)S(1)}, f32[3,8,128]{2,1,0:T(8,128)S(1)}, s32[2,8,128]{2,1,0:T(8,128)S(1)}) custom-call(s32[2]{0:T(128)S(1)} %add_convert_fusion.bands_end_ref, s32[16]{0:T(128)S(1)} %copy-done.2, f32[3]{0:T(128)S(1)} %copy-done.3, bf16[3,257]{1,0:T(4,128)(2,1)S(1)} %copy-done.1, ...), custom_call_target="tpu_custom_call" | custom-call | tf_op jit(solution)/shard_map/prepare_tables/pallas_call | solution.py:304
  12.1 17.3 %all-to-all-done.tile_ref = f32[16,6,2,8,128]{4,3,2,1,0:T(8,128)S(1)} async-done(((f32[16,6,2,8,128]{4,3,2,1,0:T(8,128)}), f32[16,6,2,8,128]{4,3,2,1,0:T(8,128)S(1)}, u32[]{:S(2)}, u32[]{:S(2)}) %all-to-all-start) | async-done | bytes 786464 | tf_op jit(solution)/shard_map/all_to_all | solution.py:288
  29.5 1.3 %collective-permute-start = (f32[16,2,8,128]{3,2,1,0:T(8,128)S(1)}, f32[16,2,8,128]{3,2,1,0:T(8,128)S(1)}, u32[]{:S(2)}, u32[]{:S(2)}) collective-permute-start(f32[16,2,8,128]{3,2,1,0:T(8,128)S(1)} %fusion), channel_id=1, source_target_pairs={{0,1},{31,30}} | collective-permute-start | bytes 393224 | tf_op jit(solution)/shard_map/ppermute | solution.py:319
  30.8 2.3 %main_rows.1 = (f32[16,2,2,5,8,128]{5,4,3,2,1,0:T(8,128)S(1)}, f32[6,8,128]{2,1,0:T(8,128)S(1)}, f32[4,8,128]{2,1,0:T(8,128)S(1)}) custom-call(s32[16]{0:T(128)S(4)} %get-tuple-element.15.brick_at, f32[3,8,128]{2,1,0:T(8,128)S(1)} %get-tuple-element.14.light_ref, f32[3,2,8,128]{3,2,1,0:T(8,128)S(1)} %get-tuple-element.16.color_word_ref, ...), custom_call_target="tpu_custom_call" | custom-call | flops 13107200 | bytes 3145728 | tf_op jit(solution)/shard_map/main_rows/pallas_call | solution.py:320
  33.1 0.0 collective-permute-done.other_ref
  33.1 0.8 %edge_rows.1 = f32[4,1,4,1024]{3,2,1,0:T(4,128)} custom-call(s32[2,8,128]{2,1,0:T(8,128)S(1)} %get-tuple-element.13.end_ref, f32[3,8,128]{2,1,0:T(8,128)S(1)} %get-tuple-element.14.light_ref, f32[16,6,2,8,128]{4,3,2,1,0:T(8,128)S(1)} %all-to-all-done.tile_ref, f32[16,2,8,128]{3,2,1,0:T(8,128)S(1)} %collective-permute-done.other_ref, ...), custom_call_target="tpu_custom_call" | custom-call | flops 1310720 | bytes 3145728 | tf_op jit(solution)/shard_map/edge_rows/pallas_call | solution.py:334
  (3 shorter events, 0.0 us)
Async XLA Ops:
  0.0 1.0 %copy-start = (f32[2,64,1024]{2,1,0:T(8,128)S(1)}, f32[2,64,1024]{2,1,0:T(8,128)}, u32[]{:S(2)}) copy-start(f32[2,64,1024]{2,1,0:T(8,128)} %field_ref.1) | copy-start | bytes 1572868
  1.0 10.3 %copy-start.4 = (bf16[257]{0:T(512)(128)(2,1)S(1)}, bf16[257]{0:T(512)(128)(2,1)}, u32[]{:S(2)}) copy-start(bf16[257]{0:T(512)(128)(2,1)} %param.8) | copy-start | bytes 1546
  1.0 10.4 %copy-start.1 = (bf16[3,257]{1,0:T(4,128)(2,1)S(1)}, bf16[3,257]{1,0:T(4,128)(2,1)}, u32[]{:S(2)}) copy-start(bf16[3,257]{1,0:T(4,128)(2,1)} %color_ref.1) | copy-start | bytes 4630
  1.0 10.4 %copy-start.2 = (s32[16]{0:T(128)S(1)}, s32[16]{0:T(128)}, u32[]{:S(2)}) copy-start(s32[16]{0:T(128)} %order_ref.1) | copy-start | bytes 196
  1.0 10.4 %copy-start.3 = (f32[3]{0:T(128)S(1)}, f32[3]{0:T(128)}, u32[]{:S(2)}) copy-start(f32[3]{0:T(128)} %light_ref.1) | copy-start | bytes 40
  2.5 26.9 %all-to-all-start = ((f32[16,6,2,8,128]{4,3,2,1,0:T(8,128)}), f32[16,6,2,8,128]{4,3,2,1,0:T(8,128)S(1)}, u32[]{:S(2)}, u32[]{:S(2)}) async-start(f32[16,6,2,8,128]{4,3,2,1,0:T(8,128)} %bitcast.2), calls=%async_computation | async-start | bytes 1572864 | tf_op jit(solution)/shard_map/all_to_all | solution.py:288
  29.5 3.6 %collective-permute-start = (f32[16,2,8,128]{3,2,1,0:T(8,128)S(1)}, f32[16,2,8,128]{3,2,1,0:T(8,128)S(1)}, u32[]{:S(2)}, u32[]{:S(2)}) collective-permute-start(f32[16,2,8,128]{3,2,1,0:T(8,128)S(1)} %fusion), channel_id=1, source_target_pairs={{0,1},{31,30}} | collective-permute-start | bytes 393224 | tf_op jit(solution)/shard_map/ppermute | solution.py:319

commit v13 on v12

--- a/solution.py
+++ b/solution.py
@@ -79,7 +79,7 @@
         ],
         compiler_params=pltpu.CompilerParams(vmem_limit_bytes=16 << 20),
         name="pack_rows",
-    )(field)
+    )(pltpu.with_memory_space_constraint(field, pltpu.HBM))
     return flat.reshape(tiles, padded_rows, depth, chunks, LANES)
 
 

time: 34.2 us -> 33.8 us (0.988)
  local copies, waits for them, and re-layouts: 1.06 us -> 0.02 us
  Pallas kernels: 5.29 us -> 5.95 us
    unnamed x10 -> x8, local copies, waits for them, and re-layouts: 1.06 us -> 0.01 us
    pallas_call x1, Pallas kernels: 1.46 us -> 2.12 us  [packed(): pl.pallas_call(functools.partial(pack_kernel, tiles), out_shape=jax.Shape...]
where the time goes in v13:
time: 33.8 us; the launch traced here: 33.5 us
  waiting for transfers between devices  17.3 us (51%)
  starting transfers between devices  10.1 us (30%)
  Pallas kernels  5.95 us (18%)
    all_to_all x1, waiting for transfers between devices, shards(): lax.all_to_all(packed(scalar, bricks), 'gz', split_axis=0, concat_axis=0,...  17.3 us
    all_to_all x1, starting transfers between devices, shards(): lax.all_to_all(packed(scalar, bricks), 'gz', split_axis=0, concat_axis=0,...  8.8 us
    pallas_call x1, Pallas kernels, shards(): pl.pallas_call(functools.partial(main_kernel, edge_rows), out_shape=[jax....  2.29 us
    pallas_call x1, Pallas kernels, packed(): pl.pallas_call(functools.partial(pack_kernel, tiles), out_shape=jax.Shape...  2.12 us
    ppermute x1, starting transfers between devices, shards(): other = lax.ppermute(wrapped, ('gz', 'gy'), pairs)  1.3 us
    pallas_call x1, Pallas kernels, shards(): pl.pallas_call(functools.partial(finish_kernel, edge_rows), out_shape=jax...  0.84 us
    pallas_call x1, Pallas kernels, shards(): pl.pallas_call(prepare_kernel, out_shape=[pltpu.SMEM((bricks,), jnp.int32...  0.7 us
  transfers between devices with their start and end apart: 2, of which 1 were waited for; matrix products, arithmetic and copies ran while one was open for 0% of the time, Pallas kernels for 9%

profile of v13, /device:TPU:0, one launch (start us, length us, event | category | flops | bytes accessed | tf_op | source)
XLA Modules:
  0.0 33.5 jit_solution(17376594649983173292)
XLA Ops:
  0.0 0.0 copy-start.3
  0.0 0.0 copy-start.1
  0.0 0.0 copy-start.2
  0.0 0.0 copy-start
  0.0 2.1 %pack_rows.1 = f32[16,96,128]{2,1,0:T(8,128)} custom-call(f32[2,64,1024]{2,1,0:T(8,128)} %field_ref.1), custom_call_target="tpu_custom_call" | custom-call | tf_op jit(solution)/shard_map/pack_rows/pallas_call | solution.py:69
  2.1 8.8 %all-to-all-start = ((f32[16,6,2,8,128]{4,3,2,1,0:T(8,128)}), f32[16,6,2,8,128]{4,3,2,1,0:T(8,128)S(1)}, u32[]{:S(2)}, u32[]{:S(2)}) async-start(f32[16,6,2,8,128]{4,3,2,1,0:T(8,128)} %bitcast.2), calls=%async_computation | async-start | bytes 1572864 | tf_op jit(solution)/shard_map/all_to_all | solution.py:288
  10.9 0.0 copy-done.3
  11.0 0.1 add_convert_fusion.bands_end_ref
  11.0 0.0 copy-done.1
  11.0 0.0 copy-done.2
  11.0 0.0 copy-done
  11.0 0.7 %prepare_tables.1 = (s32[16]{0:T(128)S(4)}, f32[3,2,8,128]{3,2,1,0:T(8,128)S(1)}, s32[2,8,128]{2,1,0:T(8,128)S(1)}, f32[3,8,128]{2,1,0:T(8,128)S(1)}, s32[2,8,128]{2,1,0:T(8,128)S(1)}) custom-call(s32[2]{0:T(128)S(1)} %add_convert_fusion.bands_end_ref, s32[16]{0:T(128)S(1)} %copy-done.1, f32[3]{0:T(128)S(1)} %copy-done.2, bf16[3,257]{1,0:T(4,128)(2,1)S(1)} %copy-done, ...), custom_call_target="tpu_custom_call" | custom-call | tf_op jit(solution)/shard_map/prepare_tables/pallas_call | solution.py:304
  11.8 17.3 %all-to-all-done.tile_ref = f32[16,6,2,8,128]{4,3,2,1,0:T(8,128)S(1)} async-done(((f32[16,6,2,8,128]{4,3,2,1,0:T(8,128)}), f32[16,6,2,8,128]{4,3,2,1,0:T(8,128)S(1)}, u32[]{:S(2)}, u32[]{:S(2)}) %all-to-all-start) | async-done | bytes 786464 | tf_op jit(solution)/shard_map/all_to_all | solution.py:288
  29.1 1.3 %collective-permute-start = (f32[16,2,8,128]{3,2,1,0:T(8,128)S(1)}, f32[16,2,8,128]{3,2,1,0:T(8,128)S(1)}, u32[]{:S(2)}, u32[]{:S(2)}) collective-permute-start(f32[16,2,8,128]{3,2,1,0:T(8,128)S(1)} %fusion), channel_id=1, source_target_pairs={{0,1},{31,30}} | collective-permute-start | bytes 393224 | tf_op jit(solution)/shard_map/ppermute | solution.py:319
  30.4 2.3 %main_rows.1 = (f32[16,2,2,5,8,128]{5,4,3,2,1,0:T(8,128)S(1)}, f32[6,8,128]{2,1,0:T(8,128)S(1)}, f32[4,8,128]{2,1,0:T(8,128)S(1)}) custom-call(s32[16]{0:T(128)S(4)} %get-tuple-element.15.brick_at, f32[3,8,128]{2,1,0:T(8,128)S(1)} %get-tuple-element.14.light_ref, f32[3,2,8,128]{3,2,1,0:T(8,128)S(1)} %get-tuple-element.16.color_word_ref, ...), custom_call_target="tpu_custom_call" | custom-call | flops 13107200 | bytes 3145728 | tf_op jit(solution)/shard_map/main_rows/pallas_call | solution.py:320
  32.7 0.0 collective-permute-done.other_ref
  32.7 0.8 %edge_rows.1 = f32[4,1,4,1024]{3,2,1,0:T(4,128)} custom-call(s32[2,8,128]{2,1,0:T(8,128)S(1)} %get-tuple-element.13.end_ref, f32[3,8,128]{2,1,0:T(8,128)S(1)} %get-tuple-element.14.light_ref, f32[16,6,2,8,128]{4,3,2,1,0:T(8,128)S(1)} %all-to-all-done.tile_ref, f32[16,2,8,128]{3,2,1,0:T(8,128)S(1)} %collective-permute-done.other_ref, ...), custom_call_target="tpu_custom_call" | custom-call | flops 1310720 | bytes 3145728 | tf_op jit(solution)/shard_map/edge_rows/pallas_call | solution.py:334
  (3 shorter events, 0.0 us)
Async XLA Ops:
  0.0 10.9 %copy-start.3 = (bf16[257]{0:T(512)(128)(2,1)S(1)}, bf16[257]{0:T(512)(128)(2,1)}, u32[]{:S(2)}) copy-start(bf16[257]{0:T(512)(128)(2,1)} %param.8) | copy-start | bytes 1546
  0.0 11.0 %copy-start.1 = (s32[16]{0:T(128)S(1)}, s32[16]{0:T(128)}, u32[]{:S(2)}) copy-start(s32[16]{0:T(128)} %order_ref.1) | copy-start | bytes 196
  0.0 11.0 %copy-start.2 = (f32[3]{0:T(128)S(1)}, f32[3]{0:T(128)}, u32[]{:S(2)}) copy-start(f32[3]{0:T(128)} %light_ref.1) | copy-start | bytes 40
  0.0 11.0 %copy-start = (bf16[3,257]{1,0:T(4,128)(2,1)S(1)}, bf16[3,257]{1,0:T(4,128)(2,1)}, u32[]{:S(2)}) copy-start(bf16[3,257]{1,0:T(4,128)(2,1)} %color_ref.1) | copy-start | bytes 4630
  2.1 26.9 %all-to-all-start = ((f32[16,6,2,8,128]{4,3,2,1,0:T(8,128)}), f32[16,6,2,8,128]{4,3,2,1,0:T(8,128)S(1)}, u32[]{:S(2)}, u32[]{:S(2)}) async-start(f32[16,6,2,8,128]{4,3,2,1,0:T(8,128)} %bitcast.2), calls=%async_computation | async-start | bytes 1572864 | tf_op jit(solution)/shard_map/all_to_all | solution.py:288
  29.1 3.6 %collective-permute-start = (f32[16,2,8,128]{3,2,1,0:T(8,128)S(1)}, f32[16,2,8,128]{3,2,1,0:T(8,128)S(1)}, u32[]{:S(2)}, u32[]{:S(2)}) collective-permute-start(f32[16,2,8,128]{3,2,1,0:T(8,128)S(1)} %fusion), channel_id=1, source_target_pairs={{0,1},{31,30}} | collective-permute-start | bytes 393224 | tf_op jit(solution)/shard_map/ppermute | solution.py:319

commit v14 on v13

--- a/solution.py
+++ b/solution.py
@@ -15,7 +15,7 @@
 
 
 def exchange_order(tiles):
-    flip = tiles - tiles // 4 if tiles & (tiles - 1) == 0 else 0
+    flip = tiles - tiles // 8 if tiles & (tiles - 1) == 0 else 0
     return [t ^ flip for t in range(tiles)]
 
 

time: 33.8 us -> 35.2 us (1.041)
  starting transfers between devices: 10.1 us -> 10.8 us
  waiting for transfers between devices: 17.3 us -> 18 us
    all_to_all x1, waiting for transfers between devices: 17.3 us -> 18 us  [shards(): lax.all_to_all(packed(scalar, bricks), 'gz', split_axis=0, concat_axis=0,...]
    all_to_all x1, starting transfers between devices: 8.8 us -> 9.51 us  [shards(): lax.all_to_all(packed(scalar, bricks), 'gz', split_axis=0, concat_axis=0,...]
where the time goes in v14:
time: 35.2 us; the launch traced here: 35 us
  waiting for transfers between devices  18 us (51%)
  starting transfers between devices  10.8 us (31%)
  Pallas kernels  5.96 us (17%)
    all_to_all x1, waiting for transfers between devices, shards(): lax.all_to_all(packed(scalar, bricks), 'gz', split_axis=0, concat_axis=0,...  18 us
    all_to_all x1, starting transfers between devices, shards(): lax.all_to_all(packed(scalar, bricks), 'gz', split_axis=0, concat_axis=0,...  9.51 us
    pallas_call x1, Pallas kernels, shards(): pl.pallas_call(functools.partial(main_kernel, edge_rows), out_shape=[jax....  2.29 us
    pallas_call x1, Pallas kernels, packed(): pl.pallas_call(functools.partial(pack_kernel, tiles), out_shape=jax.Shape...  2.12 us
    ppermute x1, starting transfers between devices, shards(): other = lax.ppermute(wrapped, ('gz', 'gy'), pairs)  1.3 us
    pallas_call x1, Pallas kernels, shards(): pl.pallas_call(functools.partial(finish_kernel, edge_rows), out_shape=jax...  0.84 us
  transfers between devices with their start and end apart: 2, of which 1 were waited for; matrix products, arithmetic and copies ran while one was open for 0% of the time, Pallas kernels for 9%

profile of v14, /device:TPU:0, one launch (start us, length us, event | category | flops | bytes accessed | tf_op | source)
XLA Modules:
  0.0 35.0 jit_solution(15043993637009388840)
XLA Ops:
  0.0 0.0 copy-start.3
  0.0 0.0 copy-start.1
  0.0 0.0 copy-start.2
  0.0 0.0 copy-start
  0.0 2.1 %pack_rows.1 = f32[16,96,128]{2,1,0:T(8,128)} custom-call(f32[2,64,1024]{2,1,0:T(8,128)} %field_ref.1), custom_call_target="tpu_custom_call" | custom-call | tf_op jit(solution)/shard_map/pack_rows/pallas_call | solution.py:69
  2.1 9.5 %all-to-all-start = ((f32[16,6,2,8,128]{4,3,2,1,0:T(8,128)}), f32[16,6,2,8,128]{4,3,2,1,0:T(8,128)S(1)}, u32[]{:S(2)}, u32[]{:S(2)}) async-start(f32[16,6,2,8,128]{4,3,2,1,0:T(8,128)} %bitcast.2), calls=%async_computation | async-start | bytes 1572864 | tf_op jit(solution)/shard_map/all_to_all | solution.py:288
  11.6 0.0 copy-done.3
  11.7 0.1 add_convert_fusion.bands_end_ref
  11.7 0.0 copy-done.1
  11.7 0.0 copy-done.2
  11.7 0.0 copy-done
  11.7 0.7 %prepare_tables.1 = (s32[16]{0:T(128)S(4)}, f32[3,2,8,128]{3,2,1,0:T(8,128)S(1)}, s32[2,8,128]{2,1,0:T(8,128)S(1)}, f32[3,8,128]{2,1,0:T(8,128)S(1)}, s32[2,8,128]{2,1,0:T(8,128)S(1)}) custom-call(s32[2]{0:T(128)S(1)} %add_convert_fusion.bands_end_ref, s32[16]{0:T(128)S(1)} %copy-done.1, f32[3]{0:T(128)S(1)} %copy-done.2, bf16[3,257]{1,0:T(4,128)(2,1)S(1)} %copy-done, ...), custom_call_target="tpu_custom_call" | custom-call | tf_op jit(solution)/shard_map/prepare_tables/pallas_call | solution.py:304
  12.5 18.0 %all-to-all-done.tile_ref = f32[16,6,2,8,128]{4,3,2,1,0:T(8,128)S(1)} async-done(((f32[16,6,2,8,128]{4,3,2,1,0:T(8,128)}), f32[16,6,2,8,128]{4,3,2,1,0:T(8,128)S(1)}, u32[]{:S(2)}, u32[]{:S(2)}) %all-to-all-start) | async-done | bytes 786464 | tf_op jit(solution)/shard_map/all_to_all | solution.py:288
  30.5 1.3 %collective-permute-start = (f32[16,2,8,128]{3,2,1,0:T(8,128)S(1)}, f32[16,2,8,128]{3,2,1,0:T(8,128)S(1)}, u32[]{:S(2)}, u32[]{:S(2)}) collective-permute-start(f32[16,2,8,128]{3,2,1,0:T(8,128)S(1)} %fusion), channel_id=1, source_target_pairs={{0,1},{31,30}} | collective-permute-start | bytes 393224 | tf_op jit(solution)/shard_map/ppermute | solution.py:319
  31.8 2.3 %main_rows.1 = (f32[16,2,2,5,8,128]{5,4,3,2,1,0:T(8,128)S(1)}, f32[6,8,128]{2,1,0:T(8,128)S(1)}, f32[4,8,128]{2,1,0:T(8,128)S(1)}) custom-call(s32[16]{0:T(128)S(4)} %get-tuple-element.15.brick_at, f32[3,8,128]{2,1,0:T(8,128)S(1)} %get-tuple-element.14.light_ref, f32[3,2,8,128]{3,2,1,0:T(8,128)S(1)} %get-tuple-element.16.color_word_ref, ...), custom_call_target="tpu_custom_call" | custom-call | flops 13107200 | bytes 3145728 | tf_op jit(solution)/shard_map/main_rows/pallas_call | solution.py:320
  34.1 0.0 collective-permute-done.other_ref
  34.1 0.8 %edge_rows.1 = f32[4,1,4,1024]{3,2,1,0:T(4,128)} custom-call(s32[2,8,128]{2,1,0:T(8,128)S(1)} %get-tuple-element.13.end_ref, f32[3,8,128]{2,1,0:T(8,128)S(1)} %get-tuple-element.14.light_ref, f32[16,6,2,8,128]{4,3,2,1,0:T(8,128)S(1)} %all-to-all-done.tile_ref, f32[16,2,8,128]{3,2,1,0:T(8,128)S(1)} %collective-permute-done.other_ref, ...), custom_call_target="tpu_custom_call" | custom-call | flops 1310720 | bytes 3145728 | tf_op jit(solution)/shard_map/edge_rows/pallas_call | solution.py:334
  (3 shorter events, 0.0 us)
Async XLA Ops:
  0.0 11.6 %copy-start.3 = (bf16[257]{0:T(512)(128)(2,1)S(1)}, bf16[257]{0:T(512)(128)(2,1)}, u32[]{:S(2)}) copy-start(bf16[257]{0:T(512)(128)(2,1)} %param.8) | copy-start | bytes 1546
  0.0 11.7 %copy-start.1 = (s32[16]{0:T(128)S(1)}, s32[16]{0:T(128)}, u32[]{:S(2)}) copy-start(s32[16]{0:T(128)} %order_ref.1) | copy-start | bytes 196
  0.0 11.7 %copy-start.2 = (f32[3]{0:T(128)S(1)}, f32[3]{0:T(128)}, u32[]{:S(2)}) copy-start(f32[3]{0:T(128)} %light_ref.1) | copy-start | bytes 40
  0.0 11.7 %copy-start = (bf16[3,257]{1,0:T(4,128)(2,1)S(1)}, bf16[3,257]{1,0:T(4,128)(2,1)}, u32[]{:S(2)}) copy-start(bf16[3,257]{1,0:T(4,128)(2,1)} %color_ref.1) | copy-start | bytes 4630
  2.1 28.4 %all-to-all-start = ((f32[16,6,2,8,128]{4,3,2,1,0:T(8,128)}), f32[16,6,2,8,128]{4,3,2,1,0:T(8,128)S(1)}, u32[]{:S(2)}, u32[]{:S(2)}) async-start(f32[16,6,2,8,128]{4,3,2,1,0:T(8,128)} %bitcast.2), calls=%async_computation | async-start | bytes 1572864 | tf_op jit(solution)/shard_map/all_to_all | solution.py:288
  30.5 3.6 %collective-permute-start = (f32[16,2,8,128]{3,2,1,0:T(8,128)S(1)}, f32[16,2,8,128]{3,2,1,0:T(8,128)S(1)}, u32[]{:S(2)}, u32[]{:S(2)}) collective-permute-start(f32[16,2,8,128]{3,2,1,0:T(8,128)S(1)} %fusion), channel_id=1, source_target_pairs={{0,1},{31,30}} | collective-permute-start | bytes 393224 | tf_op jit(solution)/shard_map/ppermute | solution.py:319

commit v15 on v14

--- a/solution.py
+++ b/solution.py
@@ -15,8 +15,10 @@
 
 
 def exchange_order(tiles):
-    flip = tiles - tiles // 8 if tiles & (tiles - 1) == 0 else 0
-    return [t ^ flip for t in range(tiles)]
+    ranks = sorted(range(tiles), key=lambda rank: (rank.bit_count(), rank))
+    chips = [0] + sorted(range(1, tiles), key=lambda chip: (-chip.bit_count(), -chip))
+    placed = dict(zip(ranks, chips))
+    return [placed[rank] for rank in range(tiles)]
 
 
 def pack_kernel(tiles, field_ref, out_ref, field, spread, in_sems, out_sems):

time: 35.2 us -> 36.1 us (1.026)
  waiting for transfers between devices: 18 us -> 20.1 us
  starting transfers between devices: 10.8 us -> 9.62 us
    all_to_all x1, waiting for transfers between devices: 18 us -> 20.1 us  [shards(): lax.all_to_all(packed(scalar, bricks), 'gz', split_axis=0, concat_axis=0,...]
    all_to_all x1, starting transfers between devices: 9.51 us -> 8.32 us  [shards(): lax.all_to_all(packed(scalar, bricks), 'gz', split_axis=0, concat_axis=0,...]
  transfers between devices with their start and end apart: 2 -> 2, of which waited for: 1 -> 1; matrix products, arithmetic and copies ran while one was open for 0% -> 0% of each run, Pallas kernels for 9% -> 8%
where the time goes in v15:
time: 36.1 us; the launch traced here: 35.9 us
  waiting for transfers between devices  20.1 us (56%)
  starting transfers between devices  9.62 us (27%)
  Pallas kernels  5.97 us (17%)
    all_to_all x1, waiting for transfers between devices, shards(): lax.all_to_all(packed(scalar, bricks), 'gz', split_axis=0, concat_axis=0,...  20.1 us
    all_to_all x1, starting transfers between devices, shards(): lax.all_to_all(packed(scalar, bricks), 'gz', split_axis=0, concat_axis=0,...  8.32 us
    pallas_call x1, Pallas kernels, shards(): pl.pallas_call(functools.partial(main_kernel, edge_rows), out_shape=[jax....  2.29 us
    pallas_call x1, Pallas kernels, packed(): pl.pallas_call(functools.partial(pack_kernel, tiles), out_shape=jax.Shape...  2.13 us
    ppermute x1, starting transfers between devices, shards(): other = lax.ppermute(wrapped, ('gz', 'gy'), pairs)  1.3 us
    pallas_call x1, Pallas kernels, shards(): pl.pallas_call(functools.partial(finish_kernel, edge_rows), out_shape=jax...  0.84 us
  transfers between devices with their start and end apart: 2, of which 1 were waited for; matrix products, arithmetic and copies ran while one was open for 0% of the time, Pallas kernels for 8%

profile of v15, /device:TPU:0, one launch (start us, length us, event | category | flops | bytes accessed | tf_op | source)
XLA Modules:
  0.0 35.9 jit_solution(7922420961972302464)
XLA Ops:
  0.0 0.0 copy-start.3
  0.0 0.0 copy-start.1
  0.0 0.0 copy-start.2
  0.0 0.0 copy-start
  0.0 2.1 %pack_rows.1 = f32[16,96,128]{2,1,0:T(8,128)} custom-call(f32[2,64,1024]{2,1,0:T(8,128)} %field_ref.1), custom_call_target="tpu_custom_call" | custom-call | tf_op jit(solution)/shard_map/pack_rows/pallas_call | solution.py:71
  2.1 8.3 %all-to-all-start = ((f32[16,6,2,8,128]{4,3,2,1,0:T(8,128)}), f32[16,6,2,8,128]{4,3,2,1,0:T(8,128)S(1)}, u32[]{:S(2)}, u32[]{:S(2)}) async-start(f32[16,6,2,8,128]{4,3,2,1,0:T(8,128)} %bitcast.2), calls=%async_computation | async-start | bytes 1572864 | tf_op jit(solution)/shard_map/all_to_all | solution.py:290
  10.5 0.0 copy-done.3
  10.5 0.1 add_convert_fusion.bands_end_ref
  10.6 0.0 copy-done.1
  10.6 0.0 copy-done.2
  10.6 0.0 copy-done
  10.6 0.7 %prepare_tables.1 = (s32[16]{0:T(128)S(4)}, f32[3,2,8,128]{3,2,1,0:T(8,128)S(1)}, s32[2,8,128]{2,1,0:T(8,128)S(1)}, f32[3,8,128]{2,1,0:T(8,128)S(1)}, s32[2,8,128]{2,1,0:T(8,128)S(1)}) custom-call(s32[2]{0:T(128)S(1)} %add_convert_fusion.bands_end_ref, s32[16]{0:T(128)S(1)} %copy-done.1, f32[3]{0:T(128)S(1)} %copy-done.2, bf16[3,257]{1,0:T(4,128)(2,1)S(1)} %copy-done, ...), custom_call_target="tpu_custom_call" | custom-call | tf_op jit(solution)/shard_map/prepare_tables/pallas_call | solution.py:306
  11.3 20.1 %all-to-all-done.tile_ref = f32[16,6,2,8,128]{4,3,2,1,0:T(8,128)S(1)} async-done(((f32[16,6,2,8,128]{4,3,2,1,0:T(8,128)}), f32[16,6,2,8,128]{4,3,2,1,0:T(8,128)S(1)}, u32[]{:S(2)}, u32[]{:S(2)}) %all-to-all-start) | async-done | bytes 786464 | tf_op jit(solution)/shard_map/all_to_all | solution.py:290
  31.4 1.3 %collective-permute-start = (f32[16,2,8,128]{3,2,1,0:T(8,128)S(1)}, f32[16,2,8,128]{3,2,1,0:T(8,128)S(1)}, u32[]{:S(2)}, u32[]{:S(2)}) collective-permute-start(f32[16,2,8,128]{3,2,1,0:T(8,128)S(1)} %fusion), channel_id=1, source_target_pairs={{0,1},{31,30}} | collective-permute-start | bytes 393224 | tf_op jit(solution)/shard_map/ppermute | solution.py:321
  32.7 2.3 %main_rows.1 = (f32[16,2,2,5,8,128]{5,4,3,2,1,0:T(8,128)S(1)}, f32[6,8,128]{2,1,0:T(8,128)S(1)}, f32[4,8,128]{2,1,0:T(8,128)S(1)}) custom-call(s32[16]{0:T(128)S(4)} %get-tuple-element.15.brick_at, f32[3,8,128]{2,1,0:T(8,128)S(1)} %get-tuple-element.14.light_ref, f32[3,2,8,128]{3,2,1,0:T(8,128)S(1)} %get-tuple-element.16.color_word_ref, ...), custom_call_target="tpu_custom_call" | custom-call | flops 13107200 | bytes 3145728 | tf_op jit(solution)/shard_map/main_rows/pallas_call | solution.py:322
  35.0 0.0 collective-permute-done.other_ref
  35.0 0.8 %edge_rows.1 = f32[4,1,4,1024]{3,2,1,0:T(4,128)} custom-call(s32[2,8,128]{2,1,0:T(8,128)S(1)} %get-tuple-element.13.end_ref, f32[3,8,128]{2,1,0:T(8,128)S(1)} %get-tuple-element.14.light_ref, f32[16,6,2,8,128]{4,3,2,1,0:T(8,128)S(1)} %all-to-all-done.tile_ref, f32[16,2,8,128]{3,2,1,0:T(8,128)S(1)} %collective-permute-done.other_ref, ...), custom_call_target="tpu_custom_call" | custom-call | flops 1310720 | bytes 3145728 | tf_op jit(solution)/shard_map/edge_rows/pallas_call | solution.py:336
  (3 shorter events, 0.0 us)
Async XLA Ops:
  0.0 10.5 %copy-start.3 = (bf16[257]{0:T(512)(128)(2,1)S(1)}, bf16[257]{0:T(512)(128)(2,1)}, u32[]{:S(2)}) copy-start(bf16[257]{0:T(512)(128)(2,1)} %param.8) | copy-start | bytes 1546
  0.0 10.6 %copy-start.1 = (s32[16]{0:T(128)S(1)}, s32[16]{0:T(128)}, u32[]{:S(2)}) copy-start(s32[16]{0:T(128)} %order_ref.1) | copy-start | bytes 196
  0.0 10.6 %copy-start.2 = (f32[3]{0:T(128)S(1)}, f32[3]{0:T(128)}, u32[]{:S(2)}) copy-start(f32[3]{0:T(128)} %light_ref.1) | copy-start | bytes 40
  0.0 10.6 %copy-start = (bf16[3,257]{1,0:T(4,128)(2,1)S(1)}, bf16[3,257]{1,0:T(4,128)(2,1)}, u32[]{:S(2)}) copy-start(bf16[3,257]{1,0:T(4,128)(2,1)} %color_ref.1) | copy-start | bytes 4630
  2.1 29.2 %all-to-all-start = ((f32[16,6,2,8,128]{4,3,2,1,0:T(8,128)}), f32[16,6,2,8,128]{4,3,2,1,0:T(8,128)S(1)}, u32[]{:S(2)}, u32[]{:S(2)}) async-start(f32[16,6,2,8,128]{4,3,2,1,0:T(8,128)} %bitcast.2), calls=%async_computation | async-start | bytes 1572864 | tf_op jit(solution)/shard_map/all_to_all | solution.py:290
  31.4 3.6 %collective-permute-start = (f32[16,2,8,128]{3,2,1,0:T(8,128)S(1)}, f32[16,2,8,128]{3,2,1,0:T(8,128)S(1)}, u32[]{:S(2)}, u32[]{:S(2)}) collective-permute-start(f32[16,2,8,128]{3,2,1,0:T(8,128)S(1)} %fusion), channel_id=1, source_target_pairs={{0,1},{31,30}} | collective-permute-start | bytes 393224 | tf_op jit(solution)/shard_map/ppermute | solution.py:321

commit v16 on v13

--- a/solution.py
+++ b/solution.py
@@ -19,26 +19,32 @@
     return [t ^ flip for t in range(tiles)]
 
 
-def pack_kernel(tiles, field_ref, out_ref, field, spread, in_sems, out_sems):
+def pack_kernel(tiles, field_ref, order_ref, light_ref, color_ref, opacity_ref,
+                out_ref, brick_at_ref, color_word_ref, opacity_word_ref, light_rows_ref, end_ref,
+                field, spread, order, light, color, opacity, sems, table_sems):
     depth, rows, cols = field_ref.shape
     chunks = cols // LANES
     block = depth * chunks
     tile_rows = rows // tiles
-    pieces = in_sems.shape[0]
+    pieces = sems.shape[0]
     piece_rows = rows // pieces
-    order = exchange_order(tiles)
 
     def copy_in(p):
         part = pl.ds(p * piece_rows, piece_rows)
-        return pltpu.make_async_copy(field_ref.at[:, part], field.at[:, part], in_sems.at[p])
-
-    def copy_out(t):
-        part = spread.at[pl.ds(t * tile_rows * block, (tile_rows + 2) * block)]
-        return pltpu.make_async_copy(part, out_ref.at[order.index(t)], out_sems.at[t])
-
+        return pltpu.make_async_copy(field_ref.at[:, part], field.at[:, part], sems.at[p])
+
+    table_copies = [
+        pltpu.make_async_copy(source, target, table_sems.at[i])
+        for i, (source, target) in enumerate(
+            [(color_ref, color), (opacity_ref, opacity), (order_ref, order), (light_ref, light)])
+    ]
+    for copy in table_copies:
+        copy.start()
     for p in range(pieces):
         copy_in(p).start()
-    started = 0
+    for copy in table_copies:
+        copy.wait()
+    prepare(order, light, color, opacity, brick_at_ref, color_word_ref, opacity_word_ref, light_rows_ref, end_ref)
     for p in range(pieces):
         copy_in(p).wait()
         for k in range(depth):
@@ -46,49 +52,16 @@
                 lines = [field[k, row:row + SUB, c * LANES:(c + 1) * LANES] for c in range(chunks)]
                 for c, value in enumerate(lines):
                     spread[pl.ds((row + 1) * block + k * chunks + c, SUB, stride=block), :] = value
-        if p == 0:
-            spread[(rows + 1) * block:, :] = spread[block:2 * block, :]
-        if p == pieces - 1:
-            spread[:block, :] = spread[rows * block:(rows + 1) * block, :]
-        ready = [t for t in range(1, tiles) if (t + 1) * tile_rows < (p + 1) * piece_rows]
-        if p == pieces - 1:
-            ready = list(range(1, tiles)) + [0]
-        for t in ready[started:]:
-            copy_out(t).start()
-        started = len(ready)
-    for t in range(tiles):
-        copy_out(t).wait()
-
-
-def packed(field, tiles):
-    depth, rows, cols = field.shape
-    chunks = cols // LANES
-    padded_rows = rows // tiles + 2
-    pieces = 4 if rows % (4 * SUB) == 0 else 1
-    hbm = pl.BlockSpec(memory_space=pltpu.HBM)
-    flat = pl.pallas_call(
-        functools.partial(pack_kernel, tiles),
-        out_shape=jax.ShapeDtypeStruct((tiles, padded_rows * depth * chunks, LANES), field.dtype),
-        in_specs=[hbm],
-        out_specs=hbm,
-        scratch_shapes=[
-            pltpu.VMEM((depth, rows, cols), field.dtype),
-            pltpu.VMEM(((rows + 2) * depth * chunks, LANES), field.dtype),
-            pltpu.SemaphoreType.DMA((pieces,)),
-            pltpu.SemaphoreType.DMA((tiles,)),
-        ],
-        compiler_params=pltpu.CompilerParams(vmem_limit_bytes=16 << 20),
-        name="pack_rows",
-    )(pltpu.with_memory_space_constraint(field, pltpu.HBM))
-    return flat.reshape(tiles, padded_rows, depth, chunks, LANES)
-
-
-def shifted(x, axis, shift):
-    return pltpu.roll(x, shift % x.shape[axis], axis)
-
-
-def prepare_kernel(bands_end_ref, order_ref, light_ref, color_ref, opacity_ref,
-                   brick_at_ref, color_word_ref, opacity_word_ref, light_rows_ref, end_ref):
+    spread[(rows + 1) * block:, :] = spread[block:2 * block, :]
+    spread[:block, :] = spread[rows * block:(rows + 1) * block, :]
+    size = (tile_rows + 2) * block
+    for place, t in enumerate(exchange_order(tiles)):
+        start = t * tile_rows * block
+        out_ref[place] = spread[start:start + size, :]
+
+
+def prepare(order_ref, light_ref, color_ref, opacity_ref,
+            brick_at_ref, color_word_ref, opacity_word_ref, light_rows_ref, end_ref):
     bins = color_ref.shape[1] - 1
     _, halves, chunks, lanes = color_word_ref.shape
     shape = (chunks, lanes)
@@ -99,7 +72,7 @@
 
     low, slope = parts(color_ref[...], COLOR_UNIT)
     color_words = slope + low * (1.0 / COLOR_SPAN)
-    low, slope = parts(opacity_ref[...], OPACITY_UNIT)
+    low, slope = parts(opacity_ref[...].reshape(1, bins + 1), OPACITY_UNIT)
     opacity_words = slope.astype(jnp.int32) * OPACITY_SPAN + low.astype(jnp.int32)
     for h in range(halves):
         span = slice(h * lanes, (h + 1) * lanes)
@@ -108,10 +81,15 @@
         opacity_word_ref[h] = jnp.broadcast_to(opacity_words[:, span], shape)
     for i in range(3):
         light_rows_ref[i] = jnp.full(shape, light_ref[i], jnp.float32) * math.sqrt(0.75)
-    for i in range(2):
-        end_ref[i] = jnp.full(shape, bands_end_ref[i], jnp.int32)
+    here, last = lax.axis_index("gz"), order_ref.shape[0] - 1
+    for i, place in enumerate([here == 0, here == last, here != 0]):
+        end_ref[i] = jnp.full(shape, place.astype(jnp.float32), jnp.float32)
     for place, b in enumerate(exchange_order(order_ref.shape[0])):
         brick_at_ref[order_ref[b]] = place
+
+
+def shifted(x, axis, shift):
+    return pltpu.roll(x, shift % x.shape[axis], axis)
 
 
 def table_lookup(color_word_ref, opacity_word_ref):
@@ -237,7 +215,7 @@
     inner_rows = [r for r in range(rows) if r not in edge_rows]
     shape = (chunks, lanes)
     light_rows = light_ref[1]
-    is_first, is_last = end_ref[0] == 1, end_ref[1] == 1
+    is_first, is_last = end_ref[0] == 1.0, end_ref[1] == 1.0
 
     together = 8 if bricks % 8 == 0 else 1
 
@@ -285,37 +263,48 @@
     chunks = cols // LANES
     edge_rows = sorted({0, tile_rows - 1})
     inner_count = tile_rows - len(edge_rows)
-    tiles = lax.all_to_all(
-        packed(scalar, bricks), "gz", split_axis=0, concat_axis=0, tiled=True,
-        axis_index_groups=[exchange_order(bricks)])
-
-    here = lax.axis_index("gz")
-    ends = jnp.stack([here == 0, here == bricks - 1]).astype(jnp.int32)
-    last = bricks - 1
-    pairs = [(g, g + 1) for g in range(bands - 1)]
-    pairs += [(last * bands + g + 1, last * bands + g) for g in range(bands - 1)]
-
     vmem = pl.BlockSpec(memory_space=pltpu.VMEM)
     smem = pl.BlockSpec(memory_space=pltpu.SMEM)
     params = pltpu.CompilerParams(vmem_limit_bytes=32 << 20)
     cells = bricks * depth * cols
     lines = (chunks, LANES)
     halves = (color_table.shape[1] - 1) // LANES
-    brick_at, color_words, opacity_words, light_rows, end_rows = pl.pallas_call(
-        prepare_kernel,
+    pieces = 4 if rows % (4 * SUB) == 0 else 1
+    hbm = pl.BlockSpec(memory_space=pltpu.HBM)
+    given = [scalar, view_order, light_dir, color_table, opacity_table]
+    sent, brick_at, color_words, opacity_words, light_rows, end_rows = pl.pallas_call(
+        functools.partial(pack_kernel, bricks),
         out_shape=[
+            pltpu.VMEM((bricks, (tile_rows + 2) * depth * chunks, LANES), jnp.float32),
             pltpu.SMEM((bricks,), jnp.int32),
             jax.ShapeDtypeStruct((3, halves) + lines, jnp.float32),
             jax.ShapeDtypeStruct((halves,) + lines, jnp.int32),
             jax.ShapeDtypeStruct((3,) + lines, jnp.float32),
-            jax.ShapeDtypeStruct((2,) + lines, jnp.int32),
+            jax.ShapeDtypeStruct((3,) + lines, jnp.float32),
         ],
-        in_specs=[smem, smem, smem, vmem, vmem],
-        out_specs=[smem] + [vmem] * 4,
+        in_specs=[hbm] * 5,
+        out_specs=[vmem, smem] + [vmem] * 4,
+        scratch_shapes=[
+            pltpu.VMEM(scalar.shape, scalar.dtype),
+            pltpu.VMEM(((rows + 2) * depth * chunks, LANES), scalar.dtype),
+            pltpu.SMEM(view_order.shape, view_order.dtype),
+            pltpu.SMEM(light_dir.shape, light_dir.dtype),
+            pltpu.VMEM(color_table.shape, color_table.dtype),
+            pltpu.VMEM(opacity_table.shape, opacity_table.dtype),
+            pltpu.SemaphoreType.DMA((pieces,)),
+            pltpu.SemaphoreType.DMA((4,)),
+        ],
         compiler_params=params,
-        name="prepare_tables",
-    )(ends, view_order, light_dir, color_table, opacity_table[None, :])
-    wrapped = jnp.where(end_rows[0] == 1, tiles[:, 0], tiles[:, -1])
+        name="pack_rows",
+    )(*[pltpu.with_memory_space_constraint(x, pltpu.HBM) for x in given])
+    arrived = lax.all_to_all(
+        sent, "gz", split_axis=0, concat_axis=0, tiled=True, axis_index_groups=[exchange_order(bricks)])
+    tiles = arrived.reshape(bricks, tile_rows + 2, depth, chunks, LANES)
+
+    last = bricks - 1
+    pairs = [(g, g + 1) for g in range(bands - 1)]
+    pairs += [(last * bands + g + 1, last * bands + g) for g in range(bands - 1)]
+    wrapped = tiles[:, 0] * end_rows[0] + tiles[:, -1] * end_rows[2]
     other = lax.ppermute(wrapped, ("gz", "gy"), pairs)
     parts, color_sums, keeps = pl.pallas_call(
         functools.partial(main_kernel, edge_rows),

time: 33.8 us -> 33.8 us (level)
  waiting for transfers between devices: 17.3 us -> 18.1 us
  Pallas kernels: 5.95 us -> 5.31 us
    all_to_all x1, waiting for transfers between devices: 17.3 us -> 18.1 us  [shards(): lax.all_to_all(sent, 'gz', split_axis=0, concat_axis=0, tiled=True, axis_...]
    pallas_call x2 -> x1, Pallas kernels: 2.82 us -> 2.18 us  [shards(): pl.pallas_call(functools.partial(pack_kernel, bricks), out_shape=[pltpu.V...]
  transfers between devices with their start and end apart: 2 -> 2, of which waited for: 1 -> 1; matrix products, arithmetic and copies ran while one was open for 0% -> 0% of each run, Pallas kernels for 9% -> 7%
where the time goes in v16:
time: 33.8 us; the launch traced here: 33.6 us
  waiting for transfers between devices  18.1 us (54%)
  starting transfers between devices  10.1 us (30%)
  Pallas kernels  5.31 us (16%)
    all_to_all x1, waiting for transfers between devices, shards(): lax.all_to_all(sent, 'gz', split_axis=0, concat_axis=0, tiled=True, axis_...  18.1 us
    all_to_all x1, starting transfers between devices, shards(): lax.all_to_all(sent, 'gz', split_axis=0, concat_axis=0, tiled=True, axis_...  8.8 us
    pallas_call x1, Pallas kernels, shards(): pl.pallas_call(functools.partial(main_kernel, edge_rows), out_shape=[jax....  2.29 us
    pallas_call x1, Pallas kernels, shards(): pl.pallas_call(functools.partial(pack_kernel, bricks), out_shape=[pltpu.V...  2.18 us
    ppermute x1, starting transfers between devices, shards(): other = lax.ppermute(wrapped, ('gz', 'gy'), pairs)  1.3 us
    pallas_call x1, Pallas kernels, shards(): pl.pallas_call(functools.partial(finish_kernel, edge_rows), out_shape=jax...  0.84 us
  transfers between devices with their start and end apart: 2, of which 1 were waited for; matrix products, arithmetic and copies ran while one was open for 0% of the time, Pallas kernels for 7%

profile of v16, /device:TPU:0, one launch (start us, length us, event | category | flops | bytes accessed | tf_op | source)
XLA Modules:
  0.0 33.6 jit_solution(18170477731118847570)
XLA Ops:
  0.0 2.2 %pack_rows.1 = (f32[16,96,128]{2,1,0:T(8,128)}, s32[16]{0:T(128)S(4)}, f32[3,2,8,128]{3,2,1,0:T(8,128)S(1)}, s32[2,8,128]{2,1,0:T(8,128)S(1)}, f32[3,8,128]{2,1,0:T(8,128)S(1)}, /*index=5*/f32[3,8,128]{2,1,0:T(8,128)S(1)}) custom-call(f32[2,64,1024]{2,1,0:T(8,128)} %field_ref.1, s32[16]{0:T(128)} %order_ref.1, f32[3]{0:T(128)} %light_ref.1, ...), custom_call_target="tpu_custom_call" | custom-call | tf_op jit(solution)/shard_map/pack_rows/pallas_call | solution.py:275
  2.2 8.8 %all-to-all-start = ((f32[16,96,128]{2,1,0:T(8,128)}), f32[16,96,128]{2,1,0:T(8,128)S(1)}, u32[]{:S(2)}, u32[]{:S(2)}) async-start(f32[16,96,128]{2,1,0:T(8,128)} %get-tuple-element.16), calls=%async_computation | async-start | bytes 1572864 | tf_op jit(solution)/shard_map/all_to_all | solution.py:300
  11.0 18.1 %all-to-all-done = f32[16,96,128]{2,1,0:T(8,128)S(1)} async-done(((f32[16,96,128]{2,1,0:T(8,128)}), f32[16,96,128]{2,1,0:T(8,128)S(1)}, u32[]{:S(2)}, u32[]{:S(2)}) %all-to-all-start) | async-done | bytes 786464 | tf_op jit(solution)/shard_map/all_to_all | solution.py:300
  29.1 1.3 %collective-permute-start = (f32[16,2,8,128]{3,2,1,0:T(8,128)S(1)}, f32[16,2,8,128]{3,2,1,0:T(8,128)S(1)}, u32[]{:S(2)}, u32[]{:S(2)}) collective-permute-start(f32[16,2,8,128]{3,2,1,0:T(8,128)S(1)} %fusion.1), channel_id=1, source_target_pairs={{0,1},{31,30}} | collective-permute-start | bytes 393224 | tf_op jit(solution)/shard_map/ppermute | solution.py:308
  30.4 2.3 %main_rows.1 = (f32[16,2,2,5,8,128]{5,4,3,2,1,0:T(8,128)S(1)}, f32[6,8,128]{2,1,0:T(8,128)S(1)}, f32[4,8,128]{2,1,0:T(8,128)S(1)}) custom-call(s32[16]{0:T(128)S(4)} %get-tuple-element.17.brick_at, f32[3,8,128]{2,1,0:T(8,128)S(1)} %get-tuple-element.15.light_ref, f32[3,2,8,128]{3,2,1,0:T(8,128)S(1)} %get-tuple-element.18.color_word_ref, ...), custom_call_target="tpu_custom_call" | custom-call | flops 13107200 | bytes 3145728 | tf_op jit(solution)/shard_map/main_rows/pallas_call | solution.py:309
  32.7 0.0 collective-permute-done.other_ref
  32.7 0.8 %edge_rows.1 = f32[4,1,4,1024]{3,2,1,0:T(4,128)} custom-call(f32[3,8,128]{2,1,0:T(8,128)S(1)} %get-tuple-element.14.end_ref, f32[3,8,128]{2,1,0:T(8,128)S(1)} %get-tuple-element.15.light_ref, f32[16,6,2,8,128]{4,3,2,1,0:T(8,128)S(1)} %bitcast.23, f32[16,2,8,128]{3,2,1,0:T(8,128)S(1)} %collective-permute-done.other_ref, ...), custom_call_target="tpu_custom_call" | custom-call | flops 1310720 | bytes 3145728 | tf_op jit(solution)/shard_map/edge_rows/pallas_call | solution.py:323
  (2 shorter events, 0.0 us)
Async XLA Ops:
  2.2 26.9 %all-to-all-start = ((f32[16,96,128]{2,1,0:T(8,128)}), f32[16,96,128]{2,1,0:T(8,128)S(1)}, u32[]{:S(2)}, u32[]{:S(2)}) async-start(f32[16,96,128]{2,1,0:T(8,128)} %get-tuple-element.16), calls=%async_computation | async-start | bytes 1572864 | tf_op jit(solution)/shard_map/all_to_all | solution.py:300
  29.1 3.6 %collective-permute-start = (f32[16,2,8,128]{3,2,1,0:T(8,128)S(1)}, f32[16,2,8,128]{3,2,1,0:T(8,128)S(1)}, u32[]{:S(2)}, u32[]{:S(2)}) collective-permute-start(f32[16,2,8,128]{3,2,1,0:T(8,128)S(1)} %fusion.1), channel_id=1, source_target_pairs={{0,1},{31,30}} | collective-permute-start | bytes 393224 | tf_op jit(solution)/shard_map/ppermute | solution.py:308

commit v17 on v16

--- a/solution.py
+++ b/solution.py
@@ -20,7 +20,7 @@
 
 
 def pack_kernel(tiles, field_ref, order_ref, light_ref, color_ref, opacity_ref,
-                out_ref, brick_at_ref, color_word_ref, opacity_word_ref, light_rows_ref, end_ref,
+                out_ref, brick_at_ref, color_word_ref, opacity_word_ref, light_rows_ref, first_ref, last_ref, later_ref,
                 field, spread, order, light, color, opacity, sems, table_sems):
     depth, rows, cols = field_ref.shape
     chunks = cols // LANES
@@ -44,7 +44,7 @@
         copy_in(p).start()
     for copy in table_copies:
         copy.wait()
-    prepare(order, light, color, opacity, brick_at_ref, color_word_ref, opacity_word_ref, light_rows_ref, end_ref)
+    prepare(order, light, color, opacity, brick_at_ref, color_word_ref, opacity_word_ref, light_rows_ref, first_ref, last_ref, later_ref)
     for p in range(pieces):
         copy_in(p).wait()
         for k in range(depth):
@@ -61,7 +61,7 @@
 
 
 def prepare(order_ref, light_ref, color_ref, opacity_ref,
-            brick_at_ref, color_word_ref, opacity_word_ref, light_rows_ref, end_ref):
+            brick_at_ref, color_word_ref, opacity_word_ref, light_rows_ref, first_ref, last_ref, later_ref):
     bins = color_ref.shape[1] - 1
     _, halves, chunks, lanes = color_word_ref.shape
     shape = (chunks, lanes)
@@ -82,8 +82,8 @@
     for i in range(3):
         light_rows_ref[i] = jnp.full(shape, light_ref[i], jnp.float32) * math.sqrt(0.75)
     here, last = lax.axis_index("gz"), order_ref.shape[0] - 1
-    for i, place in enumerate([here == 0, here == last, here != 0]):
-        end_ref[i] = jnp.full(shape, place.astype(jnp.float32), jnp.float32)
+    for ref, place in [(first_ref, here == 0), (last_ref, here == last), (later_ref, here != 0)]:
+        ref[...] = jnp.full(shape, place.astype(jnp.float32), jnp.float32)
     for place, b in enumerate(exchange_order(order_ref.shape[0])):
         brick_at_ref[order_ref[b]] = place
 
@@ -208,14 +208,14 @@
         keep_ref[r] = value
 
 
-def finish_kernel(edge_rows, end_ref, light_ref, tile_ref, other_ref, part_ref, color_sum_ref, keep_ref,
+def finish_kernel(edge_rows, first_ref, last_ref, light_ref, tile_ref, other_ref, part_ref, color_sum_ref, keep_ref,
                   out_ref, staged):
     bricks, padded_rows, depth, chunks, lanes = tile_ref.shape
     rows = padded_rows - 2
     inner_rows = [r for r in range(rows) if r not in edge_rows]
     shape = (chunks, lanes)
     light_rows = light_ref[1]
-    is_first, is_last = end_ref[0] == 1.0, end_ref[1] == 1.0
+    is_first, is_last = first_ref[...] == 1.0, last_ref[...] == 1.0
 
     together = 8 if bricks % 8 == 0 else 1
 
@@ -272,7 +272,7 @@
     pieces = 4 if rows % (4 * SUB) == 0 else 1
     hbm = pl.BlockSpec(memory_space=pltpu.HBM)
     given = [scalar, view_order, light_dir, color_table, opacity_table]
-    sent, brick_at, color_words, opacity_words, light_rows, end_rows = pl.pallas_call(
+    sent, brick_at, color_words, opacity_words, light_rows, first, final, later = pl.pallas_call(
         functools.partial(pack_kernel, bricks),
         out_shape=[
             pltpu.VMEM((bricks, (tile_rows + 2) * depth * chunks, LANES), jnp.float32),
@@ -280,10 +280,9 @@
             jax.ShapeDtypeStruct((3, halves) + lines, jnp.float32),
             jax.ShapeDtypeStruct((halves,) + lines, jnp.int32),
             jax.ShapeDtypeStruct((3,) + lines, jnp.float32),
-            jax.ShapeDtypeStruct((3,) + lines, jnp.float32),
-        ],
+        ] + [jax.ShapeDtypeStruct(lines, jnp.float32)] * 3,
         in_specs=[hbm] * 5,
-        out_specs=[vmem, smem] + [vmem] * 4,
+        out_specs=[vmem, smem] + [vmem] * 6,
         scratch_shapes=[
             pltpu.VMEM(scalar.shape, scalar.dtype),
             pltpu.VMEM(((rows + 2) * depth * chunks, LANES), scalar.dtype),
@@ -304,7 +303,7 @@
     last = bricks - 1
     pairs = [(g, g + 1) for g in range(bands - 1)]
     pairs += [(last * bands + g + 1, last * bands + g) for g in range(bands - 1)]
-    wrapped = tiles[:, 0] * end_rows[0] + tiles[:, -1] * end_rows[2]
+    wrapped = tiles[:, 0] * first + tiles[:, -1] * later
     other = lax.ppermute(wrapped, ("gz", "gy"), pairs)
     parts, color_sums, keeps = pl.pallas_call(
         functools.partial(main_kernel, edge_rows),
@@ -323,14 +322,14 @@
     return pl.pallas_call(
         functools.partial(finish_kernel, edge_rows),
         out_shape=jax.ShapeDtypeStruct((4, 1, tile_rows, cols), jnp.float32),
-        in_specs=[vmem] * 7,
+        in_specs=[vmem] * 8,
         out_specs=vmem,
         scratch_shapes=[pltpu.VMEM((4 * tile_rows * chunks, LANES), jnp.float32)],
         compiler_params=params,
         cost_estimate=pl.CostEstimate(
             flops=10 * cells * tile_rows, bytes_accessed=24 * cells * tile_rows, transcendentals=0),
         name="edge_rows",
-    )(end_rows, light_rows, tiles, other, parts, color_sums, keeps)
+    )(first, final, light_rows, tiles, other, parts, color_sums, keeps)
 
 
 def solution(mesh):

time: 33.8 us -> 33.8 us (level)
  blocking collectives: 0 us -> 27.8 us
  waiting for transfers between devices: 18.1 us -> 0.01 us
  starting transfers between devices: 10.1 us -> 1.3 us
  Pallas kernels: 5.31 us -> 4.42 us
    all_to_all x0 -> x1, blocking collectives: none -> 27.8 us  [shards(): lax.all_to_all(sent, 'gz', split_axis=0, concat_axis=0, tiled=True, axis_...]
    all_to_all x1 -> x0, waiting for transfers between devices: 18.1 us -> none  [shards(): lax.all_to_all(sent, 'gz', split_axis=0, concat_axis=0, tiled=True, axis_...]
    all_to_all x1 -> x0, starting transfers between devices: 8.8 us -> none  [shards(): lax.all_to_all(sent, 'gz', split_axis=0, concat_axis=0, tiled=True, axis_...]
    pallas_call x1, Pallas kernels: 2.18 us -> 1.28 us  [shards(): pl.pallas_call(functools.partial(pack_kernel, bricks), out_shape=[pltpu.V...]
  transfers between devices with their start and end apart: 2 -> 1, of which waited for: 1 -> 0; matrix products, arithmetic and copies ran while one was open for 0% -> 0% of each run, Pallas kernels for 7% -> 7%
where the time goes in v17:
time: 33.8 us; the launch traced here: 33.5 us
  blocking collectives  27.8 us (82%)
  Pallas kernels  4.42 us (13%)
  starting transfers between devices  1.3 us (4%)
    all_to_all x1, blocking collectives, shards(): lax.all_to_all(sent, 'gz', split_axis=0, concat_axis=0, tiled=True, axis_...  27.8 us
    pallas_call x1, Pallas kernels, shards(): pl.pallas_call(functools.partial(main_kernel, edge_rows), out_shape=[jax....  2.3 us
    ppermute x1, starting transfers between devices, shards(): other = lax.ppermute(wrapped, ('gz', 'gy'), pairs)  1.3 us
    pallas_call x1, Pallas kernels, shards(): pl.pallas_call(functools.partial(pack_kernel, bricks), out_shape=[pltpu.V...  1.28 us
    pallas_call x1, Pallas kernels, shards(): pl.pallas_call(functools.partial(finish_kernel, edge_rows), out_shape=jax...  0.84 us
  transfers between devices with their start and end apart: 1, of which 0 were waited for; matrix products, arithmetic and copies ran while one was open for 0% of the time, Pallas kernels for 7%

profile of v17, /device:TPU:0, one launch (start us, length us, event | category | flops | bytes accessed | tf_op | source)
XLA Modules:
  0.0 33.5 jit_solution(8488672291356298486)
XLA Ops:
  0.0 1.3 %pack_rows.1 = (f32[16,96,128]{2,1,0:T(8,128)S(1)}, s32[16]{0:T(128)S(4)}, f32[3,2,8,128]{3,2,1,0:T(8,128)S(1)}, s32[2,8,128]{2,1,0:T(8,128)S(1)}, f32[3,8,128]{...) custom-call(f32[2,64,1024]{2,1,0:T(8,128)} %field_ref.1, s32[16]{0:T(128)} %order_ref.1, ...), custom_call_target="tpu_custom_call" | custom-call | tf_op jit(solution)/shard_map/pack_rows/pallas_call | solution.py:275
  1.3 27.8 %all_to_all.5 = f32[16,96,128]{2,1,0:T(8,128)S(1)} all-to-all(f32[16,96,128]{2,1,0:T(8,128)S(1)} %get-tuple-element.19), channel_id=1, replica_groups={{24,26,28,30,16,18,20,22,8,10,12,14,0,2,4,6},{25,27,29,31,17,19,21,23,9..., dimensions={0} | all-to-all | bytes 1572864 | tf_op jit(solution)/shard_map/all_to_all | solution.py:299
  29.1 1.3 %collective-permute-start = (f32[16,2,8,128]{3,2,1,0:T(8,128)S(1)}, f32[16,2,8,128]{3,2,1,0:T(8,128)S(1)}, u32[]{:S(2)}, u32[]{:S(2)}) collective-permute-start(f32[16,2,8,128]{3,2,1,0:T(8,128)S(1)} %fusion.1), channel_id=1, source_target_pairs={{0,1},{31,30}} | collective-permute-start | bytes 393224 | tf_op jit(solution)/shard_map/ppermute | solution.py:307
  30.4 2.3 %main_rows.1 = (f32[16,2,2,5,8,128]{5,4,3,2,1,0:T(8,128)S(1)}, f32[6,8,128]{2,1,0:T(8,128)S(1)}, f32[4,8,128]{2,1,0:T(8,128)S(1)}) custom-call(s32[16]{0:T(128)S(4)} %get-tuple-element.21.brick_at, f32[3,8,128]{2,1,0:T(8,128)S(1)} %get-tuple-element.18.light_ref, f32[3,2,8,128]{3,2,1,0:T(8,128)S(1)} %get-tuple-element.22.color_word_ref, ...), custom_call_target="tpu_custom_call" | custom-call | flops 13107200 | bytes 3145728 | tf_op jit(solution)/shard_map/main_rows/pallas_call | solution.py:308
  32.7 0.0 collective-permute-done.other_ref
  32.7 0.8 %edge_rows.1 = f32[4,1,4,1024]{3,2,1,0:T(4,128)} custom-call(f32[8,128]{1,0:T(8,128)S(1)} %get-tuple-element.16.first_ref, f32[8,128]{1,0:T(8,128)S(1)} %get-tuple-element.17.last_ref, f32[3,8,128]{2,1,0:T(8,128)S(1)} %get-tuple-element.18.light_ref, f32[16,6,2,8,128]{4,3,2,1,0:T(8,128)S(1)} %bitcast.19, ...), custom_call_target="tpu_custom_call" | custom-call | flops 1310720 | bytes 3145728 | tf_op jit(solution)/shard_map/edge_rows/pallas_call | solution.py:322
  (1 shorter events, 0.0 us)
Async XLA Ops:
  29.1 3.6 %collective-permute-start = (f32[16,2,8,128]{3,2,1,0:T(8,128)S(1)}, f32[16,2,8,128]{3,2,1,0:T(8,128)S(1)}, u32[]{:S(2)}, u32[]{:S(2)}) collective-permute-start(f32[16,2,8,128]{3,2,1,0:T(8,128)S(1)} %fusion.1), channel_id=1, source_target_pairs={{0,1},{31,30}} | collective-permute-start | bytes 393224 | tf_op jit(solution)/shard_map/ppermute | solution.py:307

commit v18 on v17

--- a/solution.py
+++ b/solution.py
@@ -15,8 +15,8 @@
 
 
 def exchange_order(tiles):
-    flip = tiles - tiles // 4 if tiles & (tiles - 1) == 0 else 0
-    return [t ^ flip for t in range(tiles)]
+    parts = 4 if tiles % 4 == 0 else 1
+    return [(parts - 1 - i % parts) * (tiles // parts) + i // parts for i in range(tiles)]
 
 
 def pack_kernel(tiles, field_ref, order_ref, light_ref, color_ref, opacity_ref,

time: 33.8 us -> 32.4 us (0.959)
  blocking collectives: 27.8 us -> 26.1 us
    all_to_all x1, blocking collectives: 27.8 us -> 26.1 us  [shards(): lax.all_to_all(sent, 'gz', split_axis=0, concat_axis=0, tiled=True, axis_...]
where the time goes in v18:
time: 32.4 us; the launch traced here: 32.1 us
  blocking collectives  26.1 us (81%)
  Pallas kernels  4.42 us (14%)
  starting transfers between devices  1.6 us (5%)
    all_to_all x1, blocking collectives, shards(): lax.all_to_all(sent, 'gz', split_axis=0, concat_axis=0, tiled=True, axis_...  26.1 us
    pallas_call x1, Pallas kernels, shards(): pl.pallas_call(functools.partial(main_kernel, edge_rows), out_shape=[jax....  2.3 us
    ppermute x1, starting transfers between devices, shards(): other = lax.ppermute(wrapped, ('gz', 'gy'), pairs)  1.6 us
    pallas_call x1, Pallas kernels, shards(): pl.pallas_call(functools.partial(pack_kernel, bricks), out_shape=[pltpu.V...  1.28 us
    pallas_call x1, Pallas kernels, shards(): pl.pallas_call(functools.partial(finish_kernel, edge_rows), out_shape=jax...  0.84 us
  transfers between devices with their start and end apart: 1, of which 0 were waited for; matrix products, arithmetic and copies ran while one was open for 0% of the time, Pallas kernels for 7%

profile of v18, /device:TPU:0, one launch (start us, length us, event | category | flops | bytes accessed | tf_op | source)
XLA Modules:
  0.0 32.1 jit_solution(9802069469671740966)
XLA Ops:
  0.0 1.3 %pack_rows.1 = (f32[16,96,128]{2,1,0:T(8,128)S(1)}, s32[16]{0:T(128)S(4)}, f32[3,2,8,128]{3,2,1,0:T(8,128)S(1)}, s32[2,8,128]{2,1,0:T(8,128)S(1)}, f32[3,8,128]{...) custom-call(f32[2,64,1024]{2,1,0:T(8,128)} %field_ref.1, s32[16]{0:T(128)} %order_ref.1, ...), custom_call_target="tpu_custom_call" | custom-call | tf_op jit(solution)/shard_map/pack_rows/pallas_call | solution.py:275
  1.3 26.1 %all_to_all.5 = f32[16,96,128]{2,1,0:T(8,128)S(1)} all-to-all(f32[16,96,128]{2,1,0:T(8,128)S(1)} %get-tuple-element.19), channel_id=1, replica_groups={{24,16,8,0,26,18,10,2,28,20,12,4,30,22,14,6},{25,17,9,1,27,19,11,3,29,2..., dimensions={0} | all-to-all | bytes 1572864 | tf_op jit(solution)/shard_map/all_to_all | solution.py:299
  27.4 1.6 %collective-permute-start = (f32[16,2,8,128]{3,2,1,0:T(8,128)S(1)}, f32[16,2,8,128]{3,2,1,0:T(8,128)S(1)}, u32[]{:S(2)}, u32[]{:S(2)}) collective-permute-start(f32[16,2,8,128]{3,2,1,0:T(8,128)S(1)} %fusion.1), channel_id=1, source_target_pairs={{0,1},{31,30}} | collective-permute-start | bytes 393224 | tf_op jit(solution)/shard_map/ppermute | solution.py:307
  29.0 2.3 %main_rows.1 = (f32[16,2,2,5,8,128]{5,4,3,2,1,0:T(8,128)S(1)}, f32[6,8,128]{2,1,0:T(8,128)S(1)}, f32[4,8,128]{2,1,0:T(8,128)S(1)}) custom-call(s32[16]{0:T(128)S(4)} %get-tuple-element.21.brick_at, f32[3,8,128]{2,1,0:T(8,128)S(1)} %get-tuple-element.18.light_ref, f32[3,2,8,128]{3,2,1,0:T(8,128)S(1)} %get-tuple-element.22.color_word_ref, ...), custom_call_target="tpu_custom_call" | custom-call | flops 13107200 | bytes 3145728 | tf_op jit(solution)/shard_map/main_rows/pallas_call | solution.py:308
  31.3 0.0 collective-permute-done.other_ref
  31.3 0.8 %edge_rows.1 = f32[4,1,4,1024]{3,2,1,0:T(4,128)} custom-call(f32[8,128]{1,0:T(8,128)S(1)} %get-tuple-element.16.first_ref, f32[8,128]{1,0:T(8,128)S(1)} %get-tuple-element.17.last_ref, f32[3,8,128]{2,1,0:T(8,128)S(1)} %get-tuple-element.18.light_ref, f32[16,6,2,8,128]{4,3,2,1,0:T(8,128)S(1)} %bitcast.19, ...), custom_call_target="tpu_custom_call" | custom-call | flops 1310720 | bytes 3145728 | tf_op jit(solution)/shard_map/edge_rows/pallas_call | solution.py:322
  (1 shorter events, 0.0 us)
Async XLA Ops:
  27.4 3.9 %collective-permute-start = (f32[16,2,8,128]{3,2,1,0:T(8,128)S(1)}, f32[16,2,8,128]{3,2,1,0:T(8,128)S(1)}, u32[]{:S(2)}, u32[]{:S(2)}) collective-permute-start(f32[16,2,8,128]{3,2,1,0:T(8,128)S(1)} %fusion.1), channel_id=1, source_target_pairs={{0,1},{31,30}} | collective-permute-start | bytes 393224 | tf_op jit(solution)/shard_map/ppermute | solution.py:307

commit v19 on v18

--- a/solution.py
+++ b/solution.py
@@ -16,7 +16,9 @@
 
 def exchange_order(tiles):
     parts = 4 if tiles % 4 == 0 else 1
-    return [(parts - 1 - i % parts) * (tiles // parts) + i // parts for i in range(tiles)]
+    size = tiles // parts
+    walk = [i ^ (i >> 1) for i in range(size)] if size & (size - 1) == 0 else range(size)
+    return [(parts - 1 - p) * size + i for i in walk for p in range(parts)]
 
 
 def pack_kernel(tiles, field_ref, order_ref, light_ref, color_ref, opacity_ref,

time: 32.4 us -> 32.4 us (level)
    all_to_all x1, blocking collectives: 26.1 us -> 26.4 us  [shards(): lax.all_to_all(sent, 'gz', split_axis=0, concat_axis=0, tiled=True, axis_...]
where the time goes in v19:
time: 32.4 us; the launch traced here: 32.2 us
  blocking collectives  26.4 us (81%)
  Pallas kernels  4.42 us (14%)
  starting transfers between devices  1.3 us (4%)
    all_to_all x1, blocking collectives, shards(): lax.all_to_all(sent, 'gz', split_axis=0, concat_axis=0, tiled=True, axis_...  26.4 us
    pallas_call x1, Pallas kernels, shards(): pl.pallas_call(functools.partial(main_kernel, edge_rows), out_shape=[jax....  2.3 us
    ppermute x1, starting transfers between devices, shards(): other = lax.ppermute(wrapped, ('gz', 'gy'), pairs)  1.3 us
    pallas_call x1, Pallas kernels, shards(): pl.pallas_call(functools.partial(pack_kernel, bricks), out_shape=[pltpu.V...  1.28 us
    pallas_call x1, Pallas kernels, shards(): pl.pallas_call(functools.partial(finish_kernel, edge_rows), out_shape=jax...  0.84 us
  transfers between devices with their start and end apart: 1, of which 0 were waited for; matrix products, arithmetic and copies ran while one was open for 0% of the time, Pallas kernels for 7%

profile of v19, /device:TPU:0, one launch (start us, length us, event | category | flops | bytes accessed | tf_op | source)
XLA Modules:
  0.0 32.2 jit_solution(18116422825517476200)
XLA Ops:
  0.0 1.3 %pack_rows.1 = (f32[16,96,128]{2,1,0:T(8,128)S(1)}, s32[16]{0:T(128)S(4)}, f32[3,2,8,128]{3,2,1,0:T(8,128)S(1)}, s32[2,8,128]{2,1,0:T(8,128)S(1)}, f32[3,8,128]{...) custom-call(f32[2,64,1024]{2,1,0:T(8,128)} %field_ref.1, s32[16]{0:T(128)} %order_ref.1, ...), custom_call_target="tpu_custom_call" | custom-call | tf_op jit(solution)/shard_map/pack_rows/pallas_call | solution.py:277
  1.3 26.4 %all_to_all.5 = f32[16,96,128]{2,1,0:T(8,128)S(1)} all-to-all(f32[16,96,128]{2,1,0:T(8,128)S(1)} %get-tuple-element.19), channel_id=1, replica_groups={{24,16,8,0,26,18,10,2,30,22,14,6,28,20,12,4},{25,17,9,1,27,19,11,3,31,2..., dimensions={0} | all-to-all | bytes 1572864 | tf_op jit(solution)/shard_map/all_to_all | solution.py:301
  27.7 1.3 %collective-permute-start = (f32[16,2,8,128]{3,2,1,0:T(8,128)S(1)}, f32[16,2,8,128]{3,2,1,0:T(8,128)S(1)}, u32[]{:S(2)}, u32[]{:S(2)}) collective-permute-start(f32[16,2,8,128]{3,2,1,0:T(8,128)S(1)} %fusion.1), channel_id=1, source_target_pairs={{0,1},{31,30}} | collective-permute-start | bytes 393224 | tf_op jit(solution)/shard_map/ppermute | solution.py:309
  29.0 2.3 %main_rows.1 = (f32[16,2,2,5,8,128]{5,4,3,2,1,0:T(8,128)S(1)}, f32[6,8,128]{2,1,0:T(8,128)S(1)}, f32[4,8,128]{2,1,0:T(8,128)S(1)}) custom-call(s32[16]{0:T(128)S(4)} %get-tuple-element.21.brick_at, f32[3,8,128]{2,1,0:T(8,128)S(1)} %get-tuple-element.18.light_ref, f32[3,2,8,128]{3,2,1,0:T(8,128)S(1)} %get-tuple-element.22.color_word_ref, ...), custom_call_target="tpu_custom_call" | custom-call | flops 13107200 | bytes 3145728 | tf_op jit(solution)/shard_map/main_rows/pallas_call | solution.py:310
  31.3 0.0 collective-permute-done.other_ref
  31.3 0.8 %edge_rows.1 = f32[4,1,4,1024]{3,2,1,0:T(4,128)} custom-call(f32[8,128]{1,0:T(8,128)S(1)} %get-tuple-element.16.first_ref, f32[8,128]{1,0:T(8,128)S(1)} %get-tuple-element.17.last_ref, f32[3,8,128]{2,1,0:T(8,128)S(1)} %get-tuple-element.18.light_ref, f32[16,6,2,8,128]{4,3,2,1,0:T(8,128)S(1)} %bitcast.19, ...), custom_call_target="tpu_custom_call" | custom-call | flops 1310720 | bytes 3145728 | tf_op jit(solution)/shard_map/edge_rows/pallas_call | solution.py:324
  (1 shorter events, 0.0 us)
Async XLA Ops:
  27.7 3.6 %collective-permute-start = (f32[16,2,8,128]{3,2,1,0:T(8,128)S(1)}, f32[16,2,8,128]{3,2,1,0:T(8,128)S(1)}, u32[]{:S(2)}, u32[]{:S(2)}) collective-permute-start(f32[16,2,8,128]{3,2,1,0:T(8,128)S(1)} %fusion.1), channel_id=1, source_target_pairs={{0,1},{31,30}} | collective-permute-start | bytes 393224 | tf_op jit(solution)/shard_map/ppermute | solution.py:309

commit v20 on v19

--- a/solution.py
+++ b/solution.py
@@ -18,7 +18,8 @@
     parts = 4 if tiles % 4 == 0 else 1
     size = tiles // parts
     walk = [i ^ (i >> 1) for i in range(size)] if size & (size - 1) == 0 else range(size)
-    return [(parts - 1 - p) * size + i for i in walk for p in range(parts)]
+    down, up = range(parts)[::-1], range(parts)
+    return [p * size + i for turn, i in enumerate(walk) for p in (up if turn % 2 else down)]
 
 
 def pack_kernel(tiles, field_ref, order_ref, light_ref, color_ref, opacity_ref,

time: 32.4 us -> 33.2 us (1.025)
  blocking collectives: 26.4 us -> 27 us
    all_to_all x1, blocking collectives: 26.4 us -> 27 us  [shards(): lax.all_to_all(sent, 'gz', split_axis=0, concat_axis=0, tiled=True, axis_...]
where the time goes in v20:
time: 33.2 us; the launch traced here: 33 us
  blocking collectives  27 us (81%)
  Pallas kernels  4.42 us (13%)
  starting transfers between devices  1.45 us (4%)
    all_to_all x1, blocking collectives, shards(): lax.all_to_all(sent, 'gz', split_axis=0, concat_axis=0, tiled=True, axis_...  27 us
    pallas_call x1, Pallas kernels, shards(): pl.pallas_call(functools.partial(main_kernel, edge_rows), out_shape=[jax....  2.3 us
    ppermute x1, starting transfers between devices, shards(): other = lax.ppermute(wrapped, ('gz', 'gy'), pairs)  1.45 us
    pallas_call x1, Pallas kernels, shards(): pl.pallas_call(functools.partial(pack_kernel, bricks), out_shape=[pltpu.V...  1.28 us
    pallas_call x1, Pallas kernels, shards(): pl.pallas_call(functools.partial(finish_kernel, edge_rows), out_shape=jax...  0.84 us
  transfers between devices with their start and end apart: 1, of which 0 were waited for; matrix products, arithmetic and copies ran while one was open for 0% of the time, Pallas kernels for 7%

profile of v20, /device:TPU:0, one launch (start us, length us, event | category | flops | bytes accessed | tf_op | source)
XLA Modules:
  0.0 33.0 jit_solution(11078280619963009698)
XLA Ops:
  0.0 1.3 %pack_rows.1 = (f32[16,96,128]{2,1,0:T(8,128)S(1)}, s32[16]{0:T(128)S(4)}, f32[3,2,8,128]{3,2,1,0:T(8,128)S(1)}, s32[2,8,128]{2,1,0:T(8,128)S(1)}, f32[3,8,128]{...) custom-call(f32[2,64,1024]{2,1,0:T(8,128)} %field_ref.1, s32[16]{0:T(128)} %order_ref.1, ...), custom_call_target="tpu_custom_call" | custom-call | tf_op jit(solution)/shard_map/pack_rows/pallas_call | solution.py:278
  1.3 27.0 %all_to_all.5 = f32[16,96,128]{2,1,0:T(8,128)S(1)} all-to-all(f32[16,96,128]{2,1,0:T(8,128)S(1)} %get-tuple-element.19), channel_id=1, replica_groups={{24,16,8,0,2,10,18,26,30,22,14,6,4,12,20,28},{25,17,9,1,3,11,19,27,31,2..., dimensions={0} | all-to-all | bytes 1572864 | tf_op jit(solution)/shard_map/all_to_all | solution.py:302
  28.4 1.4 %collective-permute-start = (f32[16,2,8,128]{3,2,1,0:T(8,128)S(1)}, f32[16,2,8,128]{3,2,1,0:T(8,128)S(1)}, u32[]{:S(2)}, u32[]{:S(2)}) collective-permute-start(f32[16,2,8,128]{3,2,1,0:T(8,128)S(1)} %fusion.1), channel_id=1, source_target_pairs={{0,1},{31,30}} | collective-permute-start | bytes 393224 | tf_op jit(solution)/shard_map/ppermute | solution.py:310
  29.8 2.3 %main_rows.1 = (f32[16,2,2,5,8,128]{5,4,3,2,1,0:T(8,128)S(1)}, f32[6,8,128]{2,1,0:T(8,128)S(1)}, f32[4,8,128]{2,1,0:T(8,128)S(1)}) custom-call(s32[16]{0:T(128)S(4)} %get-tuple-element.21.brick_at, f32[3,8,128]{2,1,0:T(8,128)S(1)} %get-tuple-element.18.light_ref, f32[3,2,8,128]{3,2,1,0:T(8,128)S(1)} %get-tuple-element.22.color_word_ref, ...), custom_call_target="tpu_custom_call" | custom-call | flops 13107200 | bytes 3145728 | tf_op jit(solution)/shard_map/main_rows/pallas_call | solution.py:311
  32.1 0.0 collective-permute-done.other_ref
  32.1 0.8 %edge_rows.1 = f32[4,1,4,1024]{3,2,1,0:T(4,128)} custom-call(f32[8,128]{1,0:T(8,128)S(1)} %get-tuple-element.16.first_ref, f32[8,128]{1,0:T(8,128)S(1)} %get-tuple-element.17.last_ref, f32[3,8,128]{2,1,0:T(8,128)S(1)} %get-tuple-element.18.light_ref, f32[16,6,2,8,128]{4,3,2,1,0:T(8,128)S(1)} %bitcast.19, ...), custom_call_target="tpu_custom_call" | custom-call | flops 1310720 | bytes 3145728 | tf_op jit(solution)/shard_map/edge_rows/pallas_call | solution.py:325
  (1 shorter events, 0.0 us)
Async XLA Ops:
  28.4 3.8 %collective-permute-start = (f32[16,2,8,128]{3,2,1,0:T(8,128)S(1)}, f32[16,2,8,128]{3,2,1,0:T(8,128)S(1)}, u32[]{:S(2)}, u32[]{:S(2)}) collective-permute-start(f32[16,2,8,128]{3,2,1,0:T(8,128)S(1)} %fusion.1), channel_id=1, source_target_pairs={{0,1},{31,30}} | collective-permute-start | bytes 393224 | tf_op jit(solution)/shard_map/ppermute | solution.py:310

commit v21 on v18

--- a/solution.py
+++ b/solution.py
@@ -167,7 +167,7 @@
     look_up = table_lookup(color_word_ref, opacity_word_ref)
     column_difference = column_differences(shape)
     light = [light_ref[i] for i in range(3)]
-    together = 4 if bricks % 4 == 0 else 1
+    together = 8 if bricks % 8 == 0 else 1
 
     def step(trip, carry):
         colors, keeps = list(carry[0]), list(carry[1])
@@ -217,7 +217,7 @@
     light_rows = light_ref[1]
     is_first, is_last = first_ref[...] == 1.0, last_ref[...] == 1.0
 
-    together = 8 if bricks % 8 == 0 else 1
+    together = 16 if bricks % 16 == 0 else 1
 
     def step(trip, colors):
         colors = list(colors)

time: 32.4 us -> 32.1 us (level)
  no operation moved by 1% of the time
where the time goes in v21:
time: 32.1 us; the launch traced here: 31.9 us
  blocking collectives  26.1 us (81%)
  Pallas kernels  4.2 us (13%)
  starting transfers between devices  1.6 us (5%)
    all_to_all x1, blocking collectives, shards(): lax.all_to_all(sent, 'gz', split_axis=0, concat_axis=0, tiled=True, axis_...  26.1 us
    pallas_call x1, Pallas kernels, shards(): pl.pallas_call(functools.partial(main_kernel, edge_rows), out_shape=[jax....  2.1 us
    ppermute x1, starting transfers between devices, shards(): other = lax.ppermute(wrapped, ('gz', 'gy'), pairs)  1.6 us
    pallas_call x1, Pallas kernels, shards(): pl.pallas_call(functools.partial(pack_kernel, bricks), out_shape=[pltpu.V...  1.28 us
    pallas_call x1, Pallas kernels, shards(): pl.pallas_call(functools.partial(finish_kernel, edge_rows), out_shape=jax...  0.82 us
  transfers between devices with their start and end apart: 1, of which 0 were waited for; matrix products, arithmetic and copies ran while one was open for 0% of the time, Pallas kernels for 7%

profile of v21, /device:TPU:0, one launch (start us, length us, event | category | flops | bytes accessed | tf_op | source)
XLA Modules:
  0.0 31.9 jit_solution(12176502655293473576)
XLA Ops:
  0.0 1.3 %pack_rows.1 = (f32[16,96,128]{2,1,0:T(8,128)S(1)}, s32[16]{0:T(128)S(4)}, f32[3,2,8,128]{3,2,1,0:T(8,128)S(1)}, s32[2,8,128]{2,1,0:T(8,128)S(1)}, f32[3,8,128]{...) custom-call(f32[2,64,1024]{2,1,0:T(8,128)} %field_ref.1, s32[16]{0:T(128)} %order_ref.1, ...), custom_call_target="tpu_custom_call" | custom-call | tf_op jit(solution)/shard_map/pack_rows/pallas_call | solution.py:275
  1.3 26.1 %all_to_all.5 = f32[16,96,128]{2,1,0:T(8,128)S(1)} all-to-all(f32[16,96,128]{2,1,0:T(8,128)S(1)} %get-tuple-element.19), channel_id=1, replica_groups={{24,16,8,0,26,18,10,2,28,20,12,4,30,22,14,6},{25,17,9,1,27,19,11,3,29,2..., dimensions={0} | all-to-all | bytes 1572864 | tf_op jit(solution)/shard_map/all_to_all | solution.py:299
  27.4 1.6 %collective-permute-start = (f32[16,2,8,128]{3,2,1,0:T(8,128)S(1)}, f32[16,2,8,128]{3,2,1,0:T(8,128)S(1)}, u32[]{:S(2)}, u32[]{:S(2)}) collective-permute-start(f32[16,2,8,128]{3,2,1,0:T(8,128)S(1)} %fusion.1), channel_id=1, source_target_pairs={{0,1},{31,30}} | collective-permute-start | bytes 393224 | tf_op jit(solution)/shard_map/ppermute | solution.py:307
  29.0 2.1 %main_rows.1 = (f32[16,2,2,5,8,128]{5,4,3,2,1,0:T(8,128)S(1)}, f32[6,8,128]{2,1,0:T(8,128)S(1)}, f32[4,8,128]{2,1,0:T(8,128)S(1)}) custom-call(s32[16]{0:T(128)S(4)} %get-tuple-element.21.brick_at, f32[3,8,128]{2,1,0:T(8,128)S(1)} %get-tuple-element.18.light_ref, f32[3,2,8,128]{3,2,1,0:T(8,128)S(1)} %get-tuple-element.22.color_word_ref, ...), custom_call_target="tpu_custom_call" | custom-call | flops 13107200 | bytes 3145728 | tf_op jit(solution)/shard_map/main_rows/pallas_call | solution.py:308
  31.1 0.0 collective-permute-done.other_ref
  31.1 0.8 %edge_rows.1 = f32[4,1,4,1024]{3,2,1,0:T(4,128)} custom-call(f32[8,128]{1,0:T(8,128)S(1)} %get-tuple-element.16.first_ref, f32[8,128]{1,0:T(8,128)S(1)} %get-tuple-element.17.last_ref, f32[3,8,128]{2,1,0:T(8,128)S(1)} %get-tuple-element.18.light_ref, f32[16,6,2,8,128]{4,3,2,1,0:T(8,128)S(1)} %bitcast.19, ...), custom_call_target="tpu_custom_call" | custom-call | flops 1310720 | bytes 3145728 | tf_op jit(solution)/shard_map/edge_rows/pallas_call | solution.py:322
  (1 shorter events, 0.0 us)
Async XLA Ops:
  27.4 3.7 %collective-permute-start = (f32[16,2,8,128]{3,2,1,0:T(8,128)S(1)}, f32[16,2,8,128]{3,2,1,0:T(8,128)S(1)}, u32[]{:S(2)}, u32[]{:S(2)}) collective-permute-start(f32[16,2,8,128]{3,2,1,0:T(8,128)S(1)} %fusion.1), channel_id=1, source_target_pairs={{0,1},{31,30}} | collective-permute-start | bytes 393224 | tf_op jit(solution)/shard_map/ppermute | solution.py:307

commit v22 on v21

--- a/solution.py
+++ b/solution.py
@@ -153,9 +153,7 @@
 
 
 def shading_of(facing, squared_plus_one):
-    near = pltpu.reciprocal(squared_plus_one, approx=True)
-    inverse = near * (2.0 - squared_plus_one * near)
-    return 0.25 + (facing * facing) * inverse
+    return 0.25 + (facing * facing) * pltpu.reciprocal(squared_plus_one, approx=True)
 
 
 def main_kernel(edge_rows, brick_at, light_ref, color_word_ref, opacity_word_ref, tile_ref,
@@ -182,7 +180,7 @@
                     color, opacity = look_up(x)
                     weight = keeps[r] * opacity
                     facing = dz * light[0] + dx * light[2]
-                    squared = dz * dz + dx * dx + 1.0
+                    squared = (dz * dz + 1.0) + dx * dx
                     if r in edge_rows:
                         values = [weight * color[c] for c in range(3)] + [facing, squared]
                         kept.append((b, edge_rows.index(r), k, values))

time: 32.1 us -> 32.1 us (level)
  no operation moved by 1% of the time
where the time goes in v22:
time: 32.1 us; the launch traced here: 31.9 us
  blocking collectives  26.1 us (81%)
  Pallas kernels  4.17 us (13%)
  starting transfers between devices  1.6 us (5%)
    all_to_all x1, blocking collectives, shards(): lax.all_to_all(sent, 'gz', split_axis=0, concat_axis=0, tiled=True, axis_...  26.1 us
    pallas_call x1, Pallas kernels, shards(): pl.pallas_call(functools.partial(main_kernel, edge_rows), out_shape=[jax....  2.09 us
    ppermute x1, starting transfers between devices, shards(): other = lax.ppermute(wrapped, ('gz', 'gy'), pairs)  1.6 us
    pallas_call x1, Pallas kernels, shards(): pl.pallas_call(functools.partial(pack_kernel, bricks), out_shape=[pltpu.V...  1.28 us
    pallas_call x1, Pallas kernels, shards(): pl.pallas_call(functools.partial(finish_kernel, edge_rows), out_shape=jax...  0.8 us
  transfers between devices with their start and end apart: 1, of which 0 were waited for; matrix products, arithmetic and copies ran while one was open for 0% of the time, Pallas kernels for 7%

profile of v22, /device:TPU:0, one launch (start us, length us, event | category | flops | bytes accessed | tf_op | source)
XLA Modules:
  0.0 31.9 jit_solution(11876148803092200293)
XLA Ops:
  0.0 1.3 %pack_rows.1 = (f32[16,96,128]{2,1,0:T(8,128)S(1)}, s32[16]{0:T(128)S(4)}, f32[3,2,8,128]{3,2,1,0:T(8,128)S(1)}, s32[2,8,128]{2,1,0:T(8,128)S(1)}, f32[3,8,128]{...) custom-call(f32[2,64,1024]{2,1,0:T(8,128)} %field_ref.1, s32[16]{0:T(128)} %order_ref.1, ...), custom_call_target="tpu_custom_call" | custom-call | tf_op jit(solution)/shard_map/pack_rows/pallas_call | solution.py:273
  1.3 26.1 %all_to_all.5 = f32[16,96,128]{2,1,0:T(8,128)S(1)} all-to-all(f32[16,96,128]{2,1,0:T(8,128)S(1)} %get-tuple-element.19), channel_id=1, replica_groups={{24,16,8,0,26,18,10,2,28,20,12,4,30,22,14,6},{25,17,9,1,27,19,11,3,29,2..., dimensions={0} | all-to-all | bytes 1572864 | tf_op jit(solution)/shard_map/all_to_all | solution.py:297
  27.4 1.6 %collective-permute-start = (f32[16,2,8,128]{3,2,1,0:T(8,128)S(1)}, f32[16,2,8,128]{3,2,1,0:T(8,128)S(1)}, u32[]{:S(2)}, u32[]{:S(2)}) collective-permute-start(f32[16,2,8,128]{3,2,1,0:T(8,128)S(1)} %fusion.1), channel_id=1, source_target_pairs={{0,1},{31,30}} | collective-permute-start | bytes 393224 | tf_op jit(solution)/shard_map/ppermute | solution.py:305
  29.0 2.1 %main_rows.1 = (f32[16,2,2,5,8,128]{5,4,3,2,1,0:T(8,128)S(1)}, f32[6,8,128]{2,1,0:T(8,128)S(1)}, f32[4,8,128]{2,1,0:T(8,128)S(1)}) custom-call(s32[16]{0:T(128)S(4)} %get-tuple-element.21.brick_at, f32[3,8,128]{2,1,0:T(8,128)S(1)} %get-tuple-element.18.light_ref, f32[3,2,8,128]{3,2,1,0:T(8,128)S(1)} %get-tuple-element.22.color_word_ref, ...), custom_call_target="tpu_custom_call" | custom-call | flops 13107200 | bytes 3145728 | tf_op jit(solution)/shard_map/main_rows/pallas_call | solution.py:306
  31.1 0.0 collective-permute-done.other_ref
  31.1 0.8 %edge_rows.1 = f32[4,1,4,1024]{3,2,1,0:T(4,128)} custom-call(f32[8,128]{1,0:T(8,128)S(1)} %get-tuple-element.16.first_ref, f32[8,128]{1,0:T(8,128)S(1)} %get-tuple-element.17.last_ref, f32[3,8,128]{2,1,0:T(8,128)S(1)} %get-tuple-element.18.light_ref, f32[16,6,2,8,128]{4,3,2,1,0:T(8,128)S(1)} %bitcast.19, ...), custom_call_target="tpu_custom_call" | custom-call | flops 1310720 | bytes 3145728 | tf_op jit(solution)/shard_map/edge_rows/pallas_call | solution.py:320
  (1 shorter events, 0.0 us)
Async XLA Ops:
  27.4 3.7 %collective-permute-start = (f32[16,2,8,128]{3,2,1,0:T(8,128)S(1)}, f32[16,2,8,128]{3,2,1,0:T(8,128)S(1)}, u32[]{:S(2)}, u32[]{:S(2)}) collective-permute-start(f32[16,2,8,128]{3,2,1,0:T(8,128)S(1)} %fusion.1), channel_id=1, source_target_pairs={{0,1},{31,30}} | collective-permute-start | bytes 393224 | tf_op jit(solution)/shard_map/ppermute | solution.py:305

commit v23 on v22

--- a/solution.py
+++ b/solution.py
@@ -9,9 +9,7 @@
 from jax.sharding import PartitionSpec as P
 
 SUB, LANES = 8, 128
-COLOR_UNIT, COLOR_SPAN = 2 ** 11, 2 ** 12
-OPACITY_UNIT, OPACITY_BITS = 2 ** 18, 16
-OPACITY_SPAN = 2 ** OPACITY_BITS
+COLOR_UNIT, COLOR_LEAST, OPACITY_UNIT = 2 ** 11, 204, 2 ** 18
 
 
 def exchange_order(tiles):
@@ -20,7 +18,7 @@
 
 
 def pack_kernel(tiles, field_ref, order_ref, light_ref, color_ref, opacity_ref,
-                out_ref, brick_at_ref, color_word_ref, opacity_word_ref, light_rows_ref, first_ref, last_ref, later_ref,
+                out_ref, brick_at_ref, word_ref, light_rows_ref, first_ref, last_ref, later_ref,
                 field, spread, order, light, color, opacity, sems, table_sems):
     depth, rows, cols = field_ref.shape
     chunks = cols // LANES
@@ -44,7 +42,7 @@
         copy_in(p).start()
     for copy in table_copies:
         copy.wait()
-    prepare(order, light, color, opacity, brick_at_ref, color_word_ref, opacity_word_ref, light_rows_ref, first_ref, last_ref, later_ref)
+    prepare(order, light, color, opacity, brick_at_ref, word_ref, light_rows_ref, first_ref, last_ref, later_ref)
     for p in range(pieces):
         copy_in(p).wait()
         for k in range(depth):
@@ -61,24 +59,23 @@
 
 
 def prepare(order_ref, light_ref, color_ref, opacity_ref,
-            brick_at_ref, color_word_ref, opacity_word_ref, light_rows_ref, first_ref, last_ref, later_ref):
+            brick_at_ref, word_ref, light_rows_ref, first_ref, last_ref, later_ref):
     bins = color_ref.shape[1] - 1
-    _, halves, chunks, lanes = color_word_ref.shape
+    _, halves, chunks, lanes = word_ref.shape
     shape = (chunks, lanes)
 
     def parts(values, unit):
-        scaled = values.astype(jnp.float32) * float(unit)
+        scaled = (values.astype(jnp.float32) * float(unit)).astype(jnp.int32)
         return scaled[:, :bins], scaled[:, 1:] - scaled[:, :bins]
 
-    low, slope = parts(color_ref[...], COLOR_UNIT)
-    color_words = slope + low * (1.0 / COLOR_SPAN)
-    low, slope = parts(opacity_ref[...].reshape(1, bins + 1), OPACITY_UNIT)
-    opacity_words = slope.astype(jnp.int32) * OPACITY_SPAN + low.astype(jnp.int32)
-    for h in range(halves):
-        span = slice(h * lanes, (h + 1) * lanes)
-        for c in range(3):
-            color_word_ref[c, h] = jnp.broadcast_to(color_words[c:c + 1, span], shape)
-        opacity_word_ref[h] = jnp.broadcast_to(opacity_words[:, span], shape)
+    start, slope = parts(opacity_ref[...].reshape(1, bins + 1), OPACITY_UNIT)
+    pieces = [start & 511, (start >> 9) + ((slope & 31) << 4), (slope >> 5) & 511]
+    start, slope = parts(color_ref[...], COLOR_UNIT)
+    upper = (slope << 20) + ((start - COLOR_LEAST) << 9)
+    for c in range(3):
+        word = upper[c:c + 1] + pieces[c]
+        for h in range(halves):
+            word_ref[c, h] = jnp.broadcast_to(word[:, h * lanes:(h + 1) * lanes], shape)
     for i in range(3):
         light_rows_ref[i] = jnp.full(shape, light_ref[i], jnp.float32) * math.sqrt(0.75)
     here, last = lax.axis_index("gz"), order_ref.shape[0] - 1
@@ -92,8 +89,8 @@
     return pltpu.roll(x, shift % x.shape[axis], axis)
 
 
-def table_lookup(color_word_ref, opacity_word_ref):
-    _, halves, _, lanes = color_word_ref.shape
+def table_lookup(word_ref):
+    _, halves, _, lanes = word_ref.shape
     bins = halves * lanes
 
     def look_up(x):
@@ -101,24 +98,25 @@
         index = jnp.minimum(scaled.astype(jnp.int32), bins - 1)
         fraction = scaled - index.astype(jnp.float32)
         low_bits = index & (lanes - 1)
-
-        def gathered(table):
-            found = [jnp.take_along_axis(t, low_bits, axis=1, mode="promise_in_bounds") for t in table]
+        words = []
+        for c in range(3):
+            found = [
+                jnp.take_along_axis(word_ref[c, h], low_bits, axis=1, mode="promise_in_bounds")
+                for h in range(halves)
+            ]
             word = found[0]
             for h in range(1, halves):
                 word = jnp.where(index >= h * lanes, found[h], word)
-            return word
-
-        color = []
-        small = fraction * (1.0 / COLOR_SPAN)
-        for c in range(3):
-            word = gathered([color_word_ref[c, h] for h in range(halves)])
-            rise = jnp.floor(word)
-            color.append((word - rise) + small * rise)
-        word = gathered([opacity_word_ref[h] for h in range(halves)])
-        rise = (word >> OPACITY_BITS).astype(jnp.float32)
-        start = (word & (OPACITY_SPAN - 1)).astype(jnp.float32)
-        return color, (start + fraction * rise) * (1.0 / OPACITY_UNIT)
+            words.append(word)
+
+        def blended(start, slope):
+            return start.astype(jnp.float32) + fraction * slope.astype(jnp.float32)
+
+        color = [blended(((w >> 9) & 2047) + COLOR_LEAST, w >> 20) for w in words]
+        low, middle, high = words
+        start = (low & 511) + ((middle & 15) << 9)
+        slope = ((high << 23) >> 18) + ((middle >> 4) & 31)
+        return color, blended(start, slope) * (1.0 / OPACITY_UNIT)
 
     return look_up
 
@@ -156,13 +154,13 @@
     return 0.25 + (facing * facing) * pltpu.reciprocal(squared_plus_one, approx=True)
 
 
-def main_kernel(edge_rows, brick_at, light_ref, color_word_ref, opacity_word_ref, tile_ref,
+def main_kernel(edge_rows, brick_at, light_ref, word_ref, tile_ref,
                 part_ref, color_sum_ref, keep_ref):
     bricks, padded_rows, depth, chunks, lanes = tile_ref.shape
     rows = padded_rows - 2
     inner_rows = [r for r in range(rows) if r not in edge_rows]
     shape = (chunks, lanes)
-    look_up = table_lookup(color_word_ref, opacity_word_ref)
+    look_up = table_lookup(word_ref)
     column_difference = column_differences(shape)
     light = [light_ref[i] for i in range(3)]
     together = 8 if bricks % 8 == 0 else 1
@@ -245,7 +243,7 @@
             else:
                 value = color_sum_ref[c * len(inner_rows) + inner_rows.index(r)]
             at = (c * rows + r) * chunks
-            staged[at:at + chunks, :] = value * (COLOR_SPAN / COLOR_UNIT)
+            staged[at:at + chunks, :] = value * (1.0 / COLOR_UNIT)
         at = (3 * rows + r) * chunks
         staged[at:at + chunks, :] = 1.0 - keep_ref[r]
     for c in range(4):
@@ -270,17 +268,16 @@
     pieces = 4 if rows % (4 * SUB) == 0 else 1
     hbm = pl.BlockSpec(memory_space=pltpu.HBM)
     given = [scalar, view_order, light_dir, color_table, opacity_table]
-    sent, brick_at, color_words, opacity_words, light_rows, first, final, later = pl.pallas_call(
+    sent, brick_at, words, light_rows, first, final, later = pl.pallas_call(
         functools.partial(pack_kernel, bricks),
         out_shape=[
             pltpu.VMEM((bricks, (tile_rows + 2) * depth * chunks, LANES), jnp.float32),
             pltpu.SMEM((bricks,), jnp.int32),
-            jax.ShapeDtypeStruct((3, halves) + lines, jnp.float32),
-            jax.ShapeDtypeStruct((halves,) + lines, jnp.int32),
+            jax.ShapeDtypeStruct((3, halves) + lines, jnp.int32),
             jax.ShapeDtypeStruct((3,) + lines, jnp.float32),
         ] + [jax.ShapeDtypeStruct(lines, jnp.float32)] * 3,
         in_specs=[hbm] * 5,
-        out_specs=[vmem, smem] + [vmem] * 6,
+        out_specs=[vmem, smem] + [vmem] * 5,
         scratch_shapes=[
             pltpu.VMEM(scalar.shape, scalar.dtype),
             pltpu.VMEM(((rows + 2) * depth * chunks, LANES), scalar.dtype),
@@ -310,13 +307,13 @@
             jax.ShapeDtypeStruct((max(3 * inner_count, 1), chunks, LANES), jnp.float32),
             jax.ShapeDtypeStruct((tile_rows, chunks, LANES), jnp.float32),
         ],
-        in_specs=[smem] + [vmem] * 4,
+        in_specs=[smem] + [vmem] * 3,
         out_specs=[vmem, vmem, vmem],
         compiler_params=params,
         cost_estimate=pl.CostEstimate(
             flops=100 * cells * tile_rows, bytes_accessed=24 * cells * tile_rows, transcendentals=0),
         name="main_rows",
-    )(brick_at, light_rows, color_words, opacity_words, tiles)
+    )(brick_at, light_rows, words, tiles)
     return pl.pallas_call(
         functools.partial(finish_kernel, edge_rows),
         out_shape=jax.ShapeDtypeStruct((4, 1, tile_rows, cols), jnp.float32),

time: 32.1 us -> 31.9 us (level)
  transfers between devices with their start and end apart: 1 -> 1, of which waited for: 0 -> 0; matrix products, arithmetic and copies ran while one was open for 0% -> 0% of each run, Pallas kernels for 7% -> 6%
where the time goes in v23:
time: 31.9 us; the launch traced here: 31.7 us
  blocking collectives  26.1 us (82%)
  Pallas kernels  4.02 us (13%)
  starting transfers between devices  1.6 us (5%)
    all_to_all x1, blocking collectives, shards(): lax.all_to_all(sent, 'gz', split_axis=0, concat_axis=0, tiled=True, axis_...  26.1 us
    pallas_call x1, Pallas kernels, shards(): pl.pallas_call(functools.partial(main_kernel, edge_rows), out_shape=[jax....  1.82 us
    ppermute x1, starting transfers between devices, shards(): other = lax.ppermute(wrapped, ('gz', 'gy'), pairs)  1.6 us
    pallas_call x1, Pallas kernels, shards(): pl.pallas_call(functools.partial(pack_kernel, bricks), out_shape=[pltpu.V...  1.37 us
    pallas_call x1, Pallas kernels, shards(): pl.pallas_call(functools.partial(finish_kernel, edge_rows), out_shape=jax...  0.82 us
  transfers between devices with their start and end apart: 1, of which 0 were waited for; matrix products, arithmetic and copies ran while one was open for 0% of the time, Pallas kernels for 6%

profile of v23, /device:TPU:0, one launch (start us, length us, event | category | flops | bytes accessed | tf_op | source)
XLA Modules:
  0.0 31.7 jit_solution(15904357009575680103)
XLA Ops:
  0.0 1.4 %pack_rows.1 = (f32[16,96,128]{2,1,0:T(8,128)S(1)}, s32[16]{0:T(128)S(4)}, s32[3,2,8,128]{3,2,1,0:T(8,128)S(1)}, f32[3,8,128]{2,1,0:T(8,128)S(1)}, f32[8,128]{1,...) custom-call(f32[2,64,1024]{2,1,0:T(8,128)} %field_ref.1, s32[16]{0:T(128)} %order_ref.1, f32[3]{0:T(128)} %light_ref.1, ...), custom_call_target="tpu_custom_call" | custom-call | tf_op jit(solution)/shard_map/pack_rows/pallas_call | solution.py:271
  1.4 26.1 %all_to_all.5 = f32[16,96,128]{2,1,0:T(8,128)S(1)} all-to-all(f32[16,96,128]{2,1,0:T(8,128)S(1)} %get-tuple-element.18), channel_id=1, replica_groups={{24,16,8,0,26,18,10,2,28,20,12,4,30,22,14,6},{25,17,9,1,27,19,11,3,29,2..., dimensions={0} | all-to-all | bytes 1572864 | tf_op jit(solution)/shard_map/all_to_all | solution.py:294
  27.5 1.6 %collective-permute-start = (f32[16,2,8,128]{3,2,1,0:T(8,128)S(1)}, f32[16,2,8,128]{3,2,1,0:T(8,128)S(1)}, u32[]{:S(2)}, u32[]{:S(2)}) collective-permute-start(f32[16,2,8,128]{3,2,1,0:T(8,128)S(1)} %fusion.1), channel_id=1, source_target_pairs={{0,1},{31,30}} | collective-permute-start | bytes 393224 | tf_op jit(solution)/shard_map/ppermute | solution.py:302
  29.1 1.8 %main_rows.1 = (f32[16,2,2,5,8,128]{5,4,3,2,1,0:T(8,128)S(1)}, f32[6,8,128]{2,1,0:T(8,128)S(1)}, f32[4,8,128]{2,1,0:T(8,128)S(1)}) custom-call(s32[16]{0:T(128)S(4)} %get-tuple-element.20.brick_at, f32[3,8,128]{2,1,0:T(8,128)S(1)} %get-tuple-element.17.light_ref, s32[3,2,8,128]{3,2,1,0:T(8,128)S(1)} %get-tuple-element.21.word_ref, ...), custom_call_target="tpu_custom_call" | custom-call | flops 13107200 | bytes 3145728 | tf_op jit(solution)/shard_map/main_rows/pallas_call | solution.py:303
  30.9 0.0 collective-permute-done.other_ref
  30.9 0.8 %edge_rows.1 = f32[4,1,4,1024]{3,2,1,0:T(4,128)} custom-call(f32[8,128]{1,0:T(8,128)S(1)} %get-tuple-element.15.first_ref, f32[8,128]{1,0:T(8,128)S(1)} %get-tuple-element.16.last_ref, f32[3,8,128]{2,1,0:T(8,128)S(1)} %get-tuple-element.17.light_ref, f32[16,6,2,8,128]{4,3,2,1,0:T(8,128)S(1)} %bitcast.19, ...), custom_call_target="tpu_custom_call" | custom-call | flops 1310720 | bytes 3145728 | tf_op jit(solution)/shard_map/edge_rows/pallas_call | solution.py:317
  (1 shorter events, 0.0 us)
Async XLA Ops:
  27.5 3.4 %collective-permute-start = (f32[16,2,8,128]{3,2,1,0:T(8,128)S(1)}, f32[16,2,8,128]{3,2,1,0:T(8,128)S(1)}, u32[]{:S(2)}, u32[]{:S(2)}) collective-permute-start(f32[16,2,8,128]{3,2,1,0:T(8,128)S(1)} %fusion.1), channel_id=1, source_target_pairs={{0,1},{31,30}} | collective-permute-start | bytes 393224 | tf_op jit(solution)/shard_map/ppermute | solution.py:302

commit v24 on v23

--- a/solution.py
+++ b/solution.py
@@ -14,7 +14,8 @@
 
 def exchange_order(tiles):
     parts = 4 if tiles % 4 == 0 else 1
-    return [(parts - 1 - i % parts) * (tiles // parts) + i // parts for i in range(tiles)]
+    size = tiles // parts
+    return [p * size + i for i in range(size)[::-1] for p in range(parts)[::-1]]
 
 
 def pack_kernel(tiles, field_ref, order_ref, light_ref, color_ref, opacity_ref,
@@ -42,14 +43,14 @@
         copy_in(p).start()
     for copy in table_copies:
         copy.wait()
-    prepare(order, light, color, opacity, brick_at_ref, word_ref, light_rows_ref, first_ref, last_ref, later_ref)
     for p in range(pieces):
         copy_in(p).wait()
-        for k in range(depth):
-            for row in range(p * piece_rows, (p + 1) * piece_rows, SUB):
-                lines = [field[k, row:row + SUB, c * LANES:(c + 1) * LANES] for c in range(chunks)]
-                for c, value in enumerate(lines):
-                    spread[pl.ds((row + 1) * block + k * chunks + c, SUB, stride=block), :] = value
+    prepare(order, light, color, opacity, brick_at_ref, word_ref, light_rows_ref, first_ref, last_ref, later_ref)
+    for k in range(depth):
+        for row in range(0, rows, SUB):
+            lines = [field[k, row:row + SUB, c * LANES:(c + 1) * LANES] for c in range(chunks)]
+            for c, value in enumerate(lines):
+                spread[pl.ds((row + 1) * block + k * chunks + c, SUB, stride=block), :] = value
     spread[(rows + 1) * block:, :] = spread[block:2 * block, :]
     spread[:block, :] = spread[rows * block:(rows + 1) * block, :]
     size = (tile_rows + 2) * block

time: 31.9 us -> 34 us (1.066)
  blocking collectives: 26.1 us -> 27.5 us
    all_to_all x1, blocking collectives: 26.1 us -> 27.5 us  [shards(): lax.all_to_all(sent, 'gz', split_axis=0, concat_axis=0, tiled=True, axis_...]
  transfers between devices with their start and end apart: 1 -> 1, of which waited for: 0 -> 0; matrix products, arithmetic and copies ran while one was open for 0% -> 0% of each run, Pallas kernels for 6% -> 5%
where the time goes in v24:
time: 34 us; the launch traced here: 33.8 us
  blocking collectives  27.5 us (81%)
  Pallas kernels  4.32 us (13%)
  starting transfers between devices  1.93 us (6%)
    all_to_all x1, blocking collectives, shards(): lax.all_to_all(sent, 'gz', split_axis=0, concat_axis=0, tiled=True, axis_...  27.5 us
    ppermute x1, starting transfers between devices, shards(): other = lax.ppermute(wrapped, ('gz', 'gy'), pairs)  1.93 us
    pallas_call x1, Pallas kernels, shards(): pl.pallas_call(functools.partial(main_kernel, edge_rows), out_shape=[jax....  1.82 us
    pallas_call x1, Pallas kernels, shards(): pl.pallas_call(functools.partial(pack_kernel, bricks), out_shape=[pltpu.V...  1.67 us
    pallas_call x1, Pallas kernels, shards(): pl.pallas_call(functools.partial(finish_kernel, edge_rows), out_shape=jax...  0.82 us
  transfers between devices with their start and end apart: 1, of which 0 were waited for; matrix products, arithmetic and copies ran while one was open for 0% of the time, Pallas kernels for 5%

profile of v24, /device:TPU:0, one launch (start us, length us, event | category | flops | bytes accessed | tf_op | source)
XLA Modules:
  0.0 33.8 jit_solution(4614485317589537766)
XLA Ops:
  0.0 1.7 %pack_rows.1 = (f32[16,96,128]{2,1,0:T(8,128)S(1)}, s32[16]{0:T(128)S(4)}, s32[3,2,8,128]{3,2,1,0:T(8,128)S(1)}, f32[3,8,128]{2,1,0:T(8,128)S(1)}, f32[8,128]{1,...) custom-call(f32[2,64,1024]{2,1,0:T(8,128)} %field_ref.1, s32[16]{0:T(128)} %order_ref.1, f32[3]{0:T(128)} %light_ref.1, ...), custom_call_target="tpu_custom_call" | custom-call | tf_op jit(solution)/shard_map/pack_rows/pallas_call | solution.py:272
  1.7 27.5 %all_to_all.5 = f32[16,96,128]{2,1,0:T(8,128)S(1)} all-to-all(f32[16,96,128]{2,1,0:T(8,128)S(1)} %get-tuple-element.18), channel_id=1, replica_groups={{30,22,14,6,28,20,12,4,26,18,10,2,24,16,8,0},{31,23,15,7,29,21,13,5,27,..., dimensions={0} | all-to-all | bytes 1572864 | tf_op jit(solution)/shard_map/all_to_all | solution.py:295
  29.2 1.9 %collective-permute-start = (f32[16,2,8,128]{3,2,1,0:T(8,128)S(1)}, f32[16,2,8,128]{3,2,1,0:T(8,128)S(1)}, u32[]{:S(2)}, u32[]{:S(2)}) collective-permute-start(f32[16,2,8,128]{3,2,1,0:T(8,128)S(1)} %fusion.1), channel_id=1, source_target_pairs={{0,1},{31,30}} | collective-permute-start | bytes 393224 | tf_op jit(solution)/shard_map/ppermute | solution.py:303
  31.1 1.8 %main_rows.1 = (f32[16,2,2,5,8,128]{5,4,3,2,1,0:T(8,128)S(1)}, f32[6,8,128]{2,1,0:T(8,128)S(1)}, f32[4,8,128]{2,1,0:T(8,128)S(1)}) custom-call(s32[16]{0:T(128)S(4)} %get-tuple-element.20.brick_at, f32[3,8,128]{2,1,0:T(8,128)S(1)} %get-tuple-element.17.light_ref, s32[3,2,8,128]{3,2,1,0:T(8,128)S(1)} %get-tuple-element.21.word_ref, ...), custom_call_target="tpu_custom_call" | custom-call | flops 13107200 | bytes 3145728 | tf_op jit(solution)/shard_map/main_rows/pallas_call | solution.py:304
  33.0 0.0 collective-permute-done.other_ref
  33.0 0.8 %edge_rows.1 = f32[4,1,4,1024]{3,2,1,0:T(4,128)} custom-call(f32[8,128]{1,0:T(8,128)S(1)} %get-tuple-element.15.first_ref, f32[8,128]{1,0:T(8,128)S(1)} %get-tuple-element.16.last_ref, f32[3,8,128]{2,1,0:T(8,128)S(1)} %get-tuple-element.17.light_ref, f32[16,6,2,8,128]{4,3,2,1,0:T(8,128)S(1)} %bitcast.19, ...), custom_call_target="tpu_custom_call" | custom-call | flops 1310720 | bytes 3145728 | tf_op jit(solution)/shard_map/edge_rows/pallas_call | solution.py:318
  (1 shorter events, 0.0 us)
Async XLA Ops:
  29.2 3.8 %collective-permute-start = (f32[16,2,8,128]{3,2,1,0:T(8,128)S(1)}, f32[16,2,8,128]{3,2,1,0:T(8,128)S(1)}, u32[]{:S(2)}, u32[]{:S(2)}) collective-permute-start(f32[16,2,8,128]{3,2,1,0:T(8,128)S(1)} %fusion.1), channel_id=1, source_target_pairs={{0,1},{31,30}} | collective-permute-start | bytes 393224 | tf_op jit(solution)/shard_map/ppermute | solution.py:303

commit v25 on v23

--- a/solution.py
+++ b/solution.py
@@ -13,8 +13,9 @@
 
 
 def exchange_order(tiles):
-    parts = 4 if tiles % 4 == 0 else 1
-    return [(parts - 1 - i % parts) * (tiles // parts) + i // parts for i in range(tiles)]
+    quarters = [3, 1, 2, 0] if tiles % 4 == 0 else [0]
+    size = tiles // len(quarters)
+    return [quarter * size + i for i in range(size) for quarter in quarters]
 
 
 def pack_kernel(tiles, field_ref, order_ref, light_ref, color_ref, opacity_ref,

time: 31.9 us -> 32.8 us (1.028)
  blocking collectives: 26.1 us -> 27.2 us
    all_to_all x1, blocking collectives: 26.1 us -> 27.2 us  [shards(): lax.all_to_all(sent, 'gz', split_axis=0, concat_axis=0, tiled=True, axis_...]
where the time goes in v25:
time: 32.8 us; the launch traced here: 32.6 us
  blocking collectives  27.2 us (83%)
  Pallas kernels  4.02 us (12%)
  starting transfers between devices  1.3 us (4%)
    all_to_all x1, blocking collectives, shards(): lax.all_to_all(sent, 'gz', split_axis=0, concat_axis=0, tiled=True, axis_...  27.2 us
    pallas_call x1, Pallas kernels, shards(): pl.pallas_call(functools.partial(main_kernel, edge_rows), out_shape=[jax....  1.82 us
    pallas_call x1, Pallas kernels, shards(): pl.pallas_call(functools.partial(pack_kernel, bricks), out_shape=[pltpu.V...  1.37 us
    ppermute x1, starting transfers between devices, shards(): other = lax.ppermute(wrapped, ('gz', 'gy'), pairs)  1.3 us
    pallas_call x1, Pallas kernels, shards(): pl.pallas_call(functools.partial(finish_kernel, edge_rows), out_shape=jax...  0.82 us
  transfers between devices with their start and end apart: 1, of which 0 were waited for; matrix products, arithmetic and copies ran while one was open for 0% of the time, Pallas kernels for 6%

profile of v25, /device:TPU:0, one launch (start us, length us, event | category | flops | bytes accessed | tf_op | source)
XLA Modules:
  0.0 32.6 jit_solution(10616144022609901077)
XLA Ops:
  0.0 1.4 %pack_rows.1 = (f32[16,96,128]{2,1,0:T(8,128)S(1)}, s32[16]{0:T(128)S(4)}, s32[3,2,8,128]{3,2,1,0:T(8,128)S(1)}, f32[3,8,128]{2,1,0:T(8,128)S(1)}, f32[8,128]{1,...) custom-call(f32[2,64,1024]{2,1,0:T(8,128)} %field_ref.1, s32[16]{0:T(128)} %order_ref.1, f32[3]{0:T(128)} %light_ref.1, ...), custom_call_target="tpu_custom_call" | custom-call | tf_op jit(solution)/shard_map/pack_rows/pallas_call | solution.py:272
  1.4 27.2 %all_to_all.5 = f32[16,96,128]{2,1,0:T(8,128)S(1)} all-to-all(f32[16,96,128]{2,1,0:T(8,128)S(1)} %get-tuple-element.18), channel_id=1, replica_groups={{24,8,16,0,26,10,18,2,28,12,20,4,30,14,22,6},{25,9,17,1,27,11,19,3,29,1..., dimensions={0} | all-to-all | bytes 1572864 | tf_op jit(solution)/shard_map/all_to_all | solution.py:295
  28.7 1.3 %collective-permute-start = (f32[16,2,8,128]{3,2,1,0:T(8,128)S(1)}, f32[16,2,8,128]{3,2,1,0:T(8,128)S(1)}, u32[]{:S(2)}, u32[]{:S(2)}) collective-permute-start(f32[16,2,8,128]{3,2,1,0:T(8,128)S(1)} %fusion.1), channel_id=1, source_target_pairs={{0,1},{31,30}} | collective-permute-start | bytes 393224 | tf_op jit(solution)/shard_map/ppermute | solution.py:303
  30.0 1.8 %main_rows.1 = (f32[16,2,2,5,8,128]{5,4,3,2,1,0:T(8,128)S(1)}, f32[6,8,128]{2,1,0:T(8,128)S(1)}, f32[4,8,128]{2,1,0:T(8,128)S(1)}) custom-call(s32[16]{0:T(128)S(4)} %get-tuple-element.20.brick_at, f32[3,8,128]{2,1,0:T(8,128)S(1)} %get-tuple-element.17.light_ref, s32[3,2,8,128]{3,2,1,0:T(8,128)S(1)} %get-tuple-element.21.word_ref, ...), custom_call_target="tpu_custom_call" | custom-call | flops 13107200 | bytes 3145728 | tf_op jit(solution)/shard_map/main_rows/pallas_call | solution.py:304
  31.8 0.0 collective-permute-done.other_ref
  31.8 0.8 %edge_rows.1 = f32[4,1,4,1024]{3,2,1,0:T(4,128)} custom-call(f32[8,128]{1,0:T(8,128)S(1)} %get-tuple-element.15.first_ref, f32[8,128]{1,0:T(8,128)S(1)} %get-tuple-element.16.last_ref, f32[3,8,128]{2,1,0:T(8,128)S(1)} %get-tuple-element.17.light_ref, f32[16,6,2,8,128]{4,3,2,1,0:T(8,128)S(1)} %bitcast.19, ...), custom_call_target="tpu_custom_call" | custom-call | flops 1310720 | bytes 3145728 | tf_op jit(solution)/shard_map/edge_rows/pallas_call | solution.py:318
  (1 shorter events, 0.0 us)
Async XLA Ops:
  28.7 3.1 %collective-permute-start = (f32[16,2,8,128]{3,2,1,0:T(8,128)S(1)}, f32[16,2,8,128]{3,2,1,0:T(8,128)S(1)}, u32[]{:S(2)}, u32[]{:S(2)}) collective-permute-start(f32[16,2,8,128]{3,2,1,0:T(8,128)S(1)} %fusion.1), channel_id=1, source_target_pairs={{0,1},{31,30}} | collective-permute-start | bytes 393224 | tf_op jit(solution)/shard_map/ppermute | solution.py:303

commit v26 on v23

--- a/solution.py
+++ b/solution.py
@@ -85,10 +85,6 @@
         brick_at_ref[order_ref[b]] = place
 
 
-def shifted(x, axis, shift):
-    return pltpu.roll(x, shift % x.shape[axis], axis)
-
-
 def table_lookup(word_ref):
     _, halves, _, lanes = word_ref.shape
     bins = halves * lanes
@@ -121,23 +117,21 @@
     return look_up
 
 
-def column_differences(shape):
-    lane = lax.broadcasted_iota(jnp.int32, shape, 1)
-    chunk = lax.broadcasted_iota(jnp.int32, shape, 0)
-    at_first, at_last = lane == 0, lane == shape[1] - 1
-    at_left = at_first & (chunk == 0)
-    at_right = at_last & (chunk == shape[0] - 1)
-
-    def difference(x):
-        right = shifted(x, 1, -1)
-        right = jnp.where(at_last, shifted(right, 0, -1), right)
-        right = jnp.where(at_right, 0.0, right)
-        left = shifted(x, 1, 1)
-        left = jnp.where(at_first, shifted(left, 0, 1), left)
-        left = jnp.where(at_left, 0.0, left)
-        return right - left
-
-    return difference
+def column_differences(fields, carried_ref, first):
+    chunks, lanes = fields[0].shape
+    count = carried_ref.shape[0] // (chunks + 2)
+    lane = lax.broadcasted_iota(jnp.int32, (chunks, lanes), 1)
+    at_first, at_last = lane == 0, lane == lanes - 1
+    after = [pltpu.roll(x, lanes - 1, 1) for x in fields]
+    before = [pltpu.roll(x, 1, 1) for x in fields]
+    for i, (right, left) in enumerate(zip(after, before), first):
+        carried_ref[pl.ds(count + i, chunks, stride=count), :] = jnp.where(at_last, right, left)
+    differences = []
+    for i, (right, left) in enumerate(zip(after, before), first):
+        further = carried_ref[pl.ds(2 * count + i, chunks, stride=count), :]
+        back = carried_ref[pl.ds(i, chunks, stride=count), :]
+        differences.append(jnp.where(at_last, further, right) - jnp.where(at_first, back, left))
+    return differences
 
 
 def depth_differences(field):
@@ -155,26 +149,30 @@
 
 
 def main_kernel(edge_rows, brick_at, light_ref, word_ref, tile_ref,
-                part_ref, color_sum_ref, keep_ref):
+                part_ref, color_sum_ref, keep_ref, carried):
     bricks, padded_rows, depth, chunks, lanes = tile_ref.shape
     rows = padded_rows - 2
     inner_rows = [r for r in range(rows) if r not in edge_rows]
     shape = (chunks, lanes)
     look_up = table_lookup(word_ref)
-    column_difference = column_differences(shape)
+    border = carried.shape[0] // (chunks + 2)
+    carried[:border, :] = jnp.zeros((border, lanes), jnp.float32)
+    carried[-border:, :] = jnp.zeros((border, lanes), jnp.float32)
     light = [light_ref[i] for i in range(3)]
-    together = 8 if bricks % 8 == 0 else 1
+    together = border // (rows * depth)
 
     def step(trip, carry):
         colors, keeps = list(carry[0]), list(carry[1])
         at = [brick_at[trip * together + u] for u in range(together)]
         fields = [[[tile_ref[b, r, k] for k in range(depth)] for r in range(padded_rows)] for b in at]
         kept = []
-        for b, field in zip(at, fields):
+        for u, (b, field) in enumerate(zip(at, fields)):
+            cells = [x for line in field[1:-1] for x in line]
+            column = column_differences(cells, carried, u * len(cells))
             for r in range(rows):
                 for k, dz in enumerate(depth_differences(field[r + 1])):
                     x = field[r + 1][k]
-                    dx = column_difference(x)
+                    dx = column[r * depth + k]
                     color, opacity = look_up(x)
                     weight = keeps[r] * opacity
                     facing = dz * light[0] + dx * light[2]
@@ -265,6 +263,7 @@
     cells = bricks * depth * cols
     lines = (chunks, LANES)
     halves = (color_table.shape[1] - 1) // LANES
+    together = 8 if bricks % 8 == 0 else 1
     pieces = 4 if rows % (4 * SUB) == 0 else 1
     hbm = pl.BlockSpec(memory_space=pltpu.HBM)
     given = [scalar, view_order, light_dir, color_table, opacity_table]
@@ -309,6 +308,7 @@
         ],
         in_specs=[smem] + [vmem] * 3,
         out_specs=[vmem, vmem, vmem],
+        scratch_shapes=[pltpu.VMEM(((chunks + 2) * together * tile_rows * depth, LANES), jnp.float32)],
         compiler_params=params,
         cost_estimate=pl.CostEstimate(
             flops=100 * cells * tile_rows, bytes_accessed=24 * cells * tile_rows, transcendentals=0),

time: 31.9 us -> 32.4 us (1.016)
  Pallas kernels: 4.02 us -> 4.46 us
    pallas_call x1, Pallas kernels: 1.82 us -> 2.26 us  [shards(): pl.pallas_call(functools.partial(main_kernel, edge_rows), out_shape=[jax....]
  transfers between devices with their start and end apart: 1 -> 1, of which waited for: 0 -> 0; matrix products, arithmetic and copies ran while one was open for 0% -> 0% of each run, Pallas kernels for 6% -> 7%
where the time goes in v26:
time: 32.4 us; the launch traced here: 32.2 us
  blocking collectives  26.1 us (81%)
  Pallas kernels  4.46 us (14%)
  starting transfers between devices  1.6 us (5%)
    all_to_all x1, blocking collectives, shards(): lax.all_to_all(sent, 'gz', split_axis=0, concat_axis=0, tiled=True, axis_...  26.1 us
    pallas_call x1, Pallas kernels, shards(): pl.pallas_call(functools.partial(main_kernel, edge_rows), out_shape=[jax....  2.26 us
    ppermute x1, starting transfers between devices, shards(): other = lax.ppermute(wrapped, ('gz', 'gy'), pairs)  1.6 us
    pallas_call x1, Pallas kernels, shards(): pl.pallas_call(functools.partial(pack_kernel, bricks), out_shape=[pltpu.V...  1.37 us
    pallas_call x1, Pallas kernels, shards(): pl.pallas_call(functools.partial(finish_kernel, edge_rows), out_shape=jax...  0.82 us
  transfers between devices with their start and end apart: 1, of which 0 were waited for; matrix products, arithmetic and copies ran while one was open for 0% of the time, Pallas kernels for 7%

profile of v26, /device:TPU:0, one launch (start us, length us, event | category | flops | bytes accessed | tf_op | source)
XLA Modules:
  0.0 32.2 jit_solution(1340227487882732612)
XLA Ops:
  0.0 1.4 %pack_rows.1 = (f32[16,96,128]{2,1,0:T(8,128)S(1)}, s32[16]{0:T(128)S(4)}, s32[3,2,8,128]{3,2,1,0:T(8,128)S(1)}, f32[3,8,128]{2,1,0:T(8,128)S(1)}, f32[8,128]{1,...) custom-call(f32[2,64,1024]{2,1,0:T(8,128)} %field_ref.1, s32[16]{0:T(128)} %order_ref.1, f32[3]{0:T(128)} %light_ref.1, ...), custom_call_target="tpu_custom_call" | custom-call | tf_op jit(solution)/shard_map/pack_rows/pallas_call | solution.py:270
  1.4 26.1 %all_to_all.5 = f32[16,96,128]{2,1,0:T(8,128)S(1)} all-to-all(f32[16,96,128]{2,1,0:T(8,128)S(1)} %get-tuple-element.18), channel_id=1, replica_groups={{24,16,8,0,26,18,10,2,28,20,12,4,30,22,14,6},{25,17,9,1,27,19,11,3,29,2..., dimensions={0} | all-to-all | bytes 1572864 | tf_op jit(solution)/shard_map/all_to_all | solution.py:293
  27.5 1.6 %collective-permute-start = (f32[16,2,8,128]{3,2,1,0:T(8,128)S(1)}, f32[16,2,8,128]{3,2,1,0:T(8,128)S(1)}, u32[]{:S(2)}, u32[]{:S(2)}) collective-permute-start(f32[16,2,8,128]{3,2,1,0:T(8,128)S(1)} %fusion.1), channel_id=1, source_target_pairs={{0,1},{31,30}} | collective-permute-start | bytes 393224 | tf_op jit(solution)/shard_map/ppermute | solution.py:301
  29.1 2.3 %main_rows.1 = (f32[16,2,2,5,8,128]{5,4,3,2,1,0:T(8,128)S(1)}, f32[6,8,128]{2,1,0:T(8,128)S(1)}, f32[4,8,128]{2,1,0:T(8,128)S(1)}) custom-call(s32[16]{0:T(128)S(4)} %get-tuple-element.20.brick_at, f32[3,8,128]{2,1,0:T(8,128)S(1)} %get-tuple-element.17.light_ref, s32[3,2,8,128]{3,2,1,0:T(8,128)S(1)} %get-tuple-element.21.word_ref, ...), custom_call_target="tpu_custom_call" | custom-call | flops 13107200 | bytes 3145728 | tf_op jit(solution)/shard_map/main_rows/pallas_call | solution.py:302
  31.4 0.0 collective-permute-done.other_ref
  31.4 0.8 %edge_rows.1 = f32[4,1,4,1024]{3,2,1,0:T(4,128)} custom-call(f32[8,128]{1,0:T(8,128)S(1)} %get-tuple-element.15.first_ref, f32[8,128]{1,0:T(8,128)S(1)} %get-tuple-element.16.last_ref, f32[3,8,128]{2,1,0:T(8,128)S(1)} %get-tuple-element.17.light_ref, f32[16,6,2,8,128]{4,3,2,1,0:T(8,128)S(1)} %bitcast.19, ...), custom_call_target="tpu_custom_call" | custom-call | flops 1310720 | bytes 3145728 | tf_op jit(solution)/shard_map/edge_rows/pallas_call | solution.py:317
  (1 shorter events, 0.0 us)
Async XLA Ops:
  27.5 3.9 %collective-permute-start = (f32[16,2,8,128]{3,2,1,0:T(8,128)S(1)}, f32[16,2,8,128]{3,2,1,0:T(8,128)S(1)}, u32[]{:S(2)}, u32[]{:S(2)}) collective-permute-start(f32[16,2,8,128]{3,2,1,0:T(8,128)S(1)} %fusion.1), channel_id=1, source_target_pairs={{0,1},{31,30}} | collective-permute-start | bytes 393224 | tf_op jit(solution)/shard_map/ppermute | solution.py:301

commit v27 on v26

--- a/solution.py
+++ b/solution.py
@@ -308,7 +308,7 @@
         ],
         in_specs=[smem] + [vmem] * 3,
         out_specs=[vmem, vmem, vmem],
-        scratch_shapes=[pltpu.VMEM(((chunks + 2) * together * tile_rows * depth, LANES), jnp.float32)],
+        scratch_shapes=[pltpu.VMEM(((chunks + 2) * (together * tile_rows * depth + 1), LANES), jnp.float32)],
         compiler_params=params,
         cost_estimate=pl.CostEstimate(
             flops=100 * cells * tile_rows, bytes_accessed=24 * cells * tile_rows, transcendentals=0),

time: 32.4 us -> 31.9 us (0.985)
  Pallas kernels: 4.46 us -> 3.97 us
    pallas_call x1, Pallas kernels: 2.26 us -> 1.78 us  [shards(): pl.pallas_call(functools.partial(main_kernel, edge_rows), out_shape=[jax....]
  transfers between devices with their start and end apart: 1 -> 1, of which waited for: 0 -> 0; matrix products, arithmetic and copies ran while one was open for 0% -> 0% of each run, Pallas kernels for 7% -> 6%
where the time goes in v27:
time: 31.9 us; the launch traced here: 31.7 us
  blocking collectives  26.1 us (82%)
  Pallas kernels  3.97 us (12%)
  starting transfers between devices  1.6 us (5%)
    all_to_all x1, blocking collectives, shards(): lax.all_to_all(sent, 'gz', split_axis=0, concat_axis=0, tiled=True, axis_...  26.1 us
    pallas_call x1, Pallas kernels, shards(): pl.pallas_call(functools.partial(main_kernel, edge_rows), out_shape=[jax....  1.78 us
    ppermute x1, starting transfers between devices, shards(): other = lax.ppermute(wrapped, ('gz', 'gy'), pairs)  1.6 us
    pallas_call x1, Pallas kernels, shards(): pl.pallas_call(functools.partial(pack_kernel, bricks), out_shape=[pltpu.V...  1.37 us
    pallas_call x1, Pallas kernels, shards(): pl.pallas_call(functools.partial(finish_kernel, edge_rows), out_shape=jax...  0.82 us
  transfers between devices with their start and end apart: 1, of which 0 were waited for; matrix products, arithmetic and copies ran while one was open for 0% of the time, Pallas kernels for 6%

profile of v27, /device:TPU:0, one launch (start us, length us, event | category | flops | bytes accessed | tf_op | source)
XLA Modules:
  0.0 31.7 jit_solution(6348526185687600341)
XLA Ops:
  0.0 1.4 %pack_rows.1 = (f32[16,96,128]{2,1,0:T(8,128)S(1)}, s32[16]{0:T(128)S(4)}, s32[3,2,8,128]{3,2,1,0:T(8,128)S(1)}, f32[3,8,128]{2,1,0:T(8,128)S(1)}, f32[8,128]{1,...) custom-call(f32[2,64,1024]{2,1,0:T(8,128)} %field_ref.1, s32[16]{0:T(128)} %order_ref.1, f32[3]{0:T(128)} %light_ref.1, ...), custom_call_target="tpu_custom_call" | custom-call | tf_op jit(solution)/shard_map/pack_rows/pallas_call | solution.py:270
  1.4 26.1 %all_to_all.5 = f32[16,96,128]{2,1,0:T(8,128)S(1)} all-to-all(f32[16,96,128]{2,1,0:T(8,128)S(1)} %get-tuple-element.18), channel_id=1, replica_groups={{24,16,8,0,26,18,10,2,28,20,12,4,30,22,14,6},{25,17,9,1,27,19,11,3,29,2..., dimensions={0} | all-to-all | bytes 1572864 | tf_op jit(solution)/shard_map/all_to_all | solution.py:293
  27.5 1.6 %collective-permute-start = (f32[16,2,8,128]{3,2,1,0:T(8,128)S(1)}, f32[16,2,8,128]{3,2,1,0:T(8,128)S(1)}, u32[]{:S(2)}, u32[]{:S(2)}) collective-permute-start(f32[16,2,8,128]{3,2,1,0:T(8,128)S(1)} %fusion.1), channel_id=1, source_target_pairs={{0,1},{31,30}} | collective-permute-start | bytes 393224 | tf_op jit(solution)/shard_map/ppermute | solution.py:301
  29.1 1.8 %main_rows.1 = (f32[16,2,2,5,8,128]{5,4,3,2,1,0:T(8,128)S(1)}, f32[6,8,128]{2,1,0:T(8,128)S(1)}, f32[4,8,128]{2,1,0:T(8,128)S(1)}) custom-call(s32[16]{0:T(128)S(4)} %get-tuple-element.20.brick_at, f32[3,8,128]{2,1,0:T(8,128)S(1)} %get-tuple-element.17.light_ref, s32[3,2,8,128]{3,2,1,0:T(8,128)S(1)} %get-tuple-element.21.word_ref, ...), custom_call_target="tpu_custom_call" | custom-call | flops 13107200 | bytes 3145728 | tf_op jit(solution)/shard_map/main_rows/pallas_call | solution.py:302
  30.9 0.0 collective-permute-done.other_ref
  30.9 0.8 %edge_rows.1 = f32[4,1,4,1024]{3,2,1,0:T(4,128)} custom-call(f32[8,128]{1,0:T(8,128)S(1)} %get-tuple-element.15.first_ref, f32[8,128]{1,0:T(8,128)S(1)} %get-tuple-element.16.last_ref, f32[3,8,128]{2,1,0:T(8,128)S(1)} %get-tuple-element.17.light_ref, f32[16,6,2,8,128]{4,3,2,1,0:T(8,128)S(1)} %bitcast.19, ...), custom_call_target="tpu_custom_call" | custom-call | flops 1310720 | bytes 3145728 | tf_op jit(solution)/shard_map/edge_rows/pallas_call | solution.py:317
  (1 shorter events, 0.0 us)
Async XLA Ops:
  27.5 3.4 %collective-permute-start = (f32[16,2,8,128]{3,2,1,0:T(8,128)S(1)}, f32[16,2,8,128]{3,2,1,0:T(8,128)S(1)}, u32[]{:S(2)}, u32[]{:S(2)}) collective-permute-start(f32[16,2,8,128]{3,2,1,0:T(8,128)S(1)} %fusion.1), channel_id=1, source_target_pairs={{0,1},{31,30}} | collective-permute-start | bytes 393224 | tf_op jit(solution)/shard_map/ppermute | solution.py:301

commit v28 on v27

--- a/solution.py
+++ b/solution.py
@@ -25,6 +25,7 @@
     block = depth * chunks
     tile_rows = rows // tiles
     pieces = sems.shape[0]
+    order_of_tiles = exchange_order(tiles)
     piece_rows = rows // pieces
 
     def copy_in(p):
@@ -40,22 +41,30 @@
         copy.start()
     for p in range(pieces):
         copy_in(p).start()
-    for copy in table_copies:
-        copy.wait()
-    prepare(order, light, color, opacity, brick_at_ref, word_ref, light_rows_ref, first_ref, last_ref, later_ref)
+    size = (tile_rows + 2) * block
+    placed = 0
     for p in range(pieces):
         copy_in(p).wait()
+        rows_here = range(p * piece_rows, (p + 1) * piece_rows)
         for k in range(depth):
-            for row in range(p * piece_rows, (p + 1) * piece_rows, SUB):
+            for row in rows_here[::SUB]:
                 lines = [field[k, row:row + SUB, c * LANES:(c + 1) * LANES] for c in range(chunks)]
                 for c, value in enumerate(lines):
                     spread[pl.ds((row + 1) * block + k * chunks + c, SUB, stride=block), :] = value
-    spread[(rows + 1) * block:, :] = spread[block:2 * block, :]
-    spread[:block, :] = spread[rows * block:(rows + 1) * block, :]
-    size = (tile_rows + 2) * block
-    for place, t in enumerate(exchange_order(tiles)):
-        start = t * tile_rows * block
-        out_ref[place] = spread[start:start + size, :]
+        ready = [t for t in range(1, tiles) if (t + 1) * tile_rows in range(rows_here.stop)]
+        if p == 0:
+            spread[(rows + 1) * block:, :] = spread[block:2 * block, :]
+        if p == pieces - 1:
+            spread[:block, :] = spread[rows * block:(rows + 1) * block, :]
+            ready = list(range(1, tiles)) + [0]
+        for t in ready[placed:]:
+            start = t * tile_rows * block
+            out_ref[order_of_tiles.index(t)] = spread[start:start + size, :]
+        placed = len(ready)
+        if p == 0:
+            for copy in table_copies:
+                copy.wait()
+            prepare(order, light, color, opacity, brick_at_ref, word_ref, light_rows_ref, first_ref, last_ref, later_ref)
 
 
 def prepare(order_ref, light_ref, color_ref, opacity_ref,
@@ -264,7 +273,7 @@
     lines = (chunks, LANES)
     halves = (color_table.shape[1] - 1) // LANES
     together = 8 if bricks % 8 == 0 else 1
-    pieces = 4 if rows % (4 * SUB) == 0 else 1
+    pieces = rows // SUB
     hbm = pl.BlockSpec(memory_space=pltpu.HBM)
     given = [scalar, view_order, light_dir, color_table, opacity_table]
     sent, brick_at, words, light_rows, first, final, later = pl.pallas_call(

time: 31.9 us -> 32 us (level)
  no operation moved by 1% of the time
where the time goes in v28:
time: 32 us; the launch traced here: 31.8 us
  blocking collectives  26.1 us (82%)
  Pallas kernels  4.08 us (13%)
  starting transfers between devices  1.6 us (5%)
    all_to_all x1, blocking collectives, shards(): lax.all_to_all(sent, 'gz', split_axis=0, concat_axis=0, tiled=True, axis_...  26.1 us
    pallas_call x1, Pallas kernels, shards(): pl.pallas_call(functools.partial(main_kernel, edge_rows), out_shape=[jax....  1.78 us
    ppermute x1, starting transfers between devices, shards(): other = lax.ppermute(wrapped, ('gz', 'gy'), pairs)  1.6 us
    pallas_call x1, Pallas kernels, shards(): pl.pallas_call(functools.partial(pack_kernel, bricks), out_shape=[pltpu.V...  1.49 us
    pallas_call x1, Pallas kernels, shards(): pl.pallas_call(functools.partial(finish_kernel, edge_rows), out_shape=jax...  0.82 us
  transfers between devices with their start and end apart: 1, of which 0 were waited for; matrix products, arithmetic and copies ran while one was open for 0% of the time, Pallas kernels for 6%

profile of v28, /device:TPU:0, one launch (start us, length us, event | category | flops | bytes accessed | tf_op | source)
XLA Modules:
  0.0 31.8 jit_solution(14728961798154633310)
XLA Ops:
  0.0 1.5 %pack_rows.1 = (f32[16,96,128]{2,1,0:T(8,128)S(1)}, s32[16]{0:T(128)S(4)}, s32[3,2,8,128]{3,2,1,0:T(8,128)S(1)}, f32[3,8,128]{2,1,0:T(8,128)S(1)}, f32[8,128]{1,...) custom-call(f32[2,64,1024]{2,1,0:T(8,128)} %field_ref.1, s32[16]{0:T(128)} %order_ref.1, f32[3]{0:T(128)} %light_ref.1, ...), custom_call_target="tpu_custom_call" | custom-call | tf_op jit(solution)/shard_map/pack_rows/pallas_call | solution.py:279
  1.5 26.1 %all_to_all.5 = f32[16,96,128]{2,1,0:T(8,128)S(1)} all-to-all(f32[16,96,128]{2,1,0:T(8,128)S(1)} %get-tuple-element.18), channel_id=1, replica_groups={{24,16,8,0,26,18,10,2,28,20,12,4,30,22,14,6},{25,17,9,1,27,19,11,3,29,2..., dimensions={0} | all-to-all | bytes 1572864 | tf_op jit(solution)/shard_map/all_to_all | solution.py:302
  27.6 1.6 %collective-permute-start = (f32[16,2,8,128]{3,2,1,0:T(8,128)S(1)}, f32[16,2,8,128]{3,2,1,0:T(8,128)S(1)}, u32[]{:S(2)}, u32[]{:S(2)}) collective-permute-start(f32[16,2,8,128]{3,2,1,0:T(8,128)S(1)} %fusion.1), channel_id=1, source_target_pairs={{0,1},{31,30}} | collective-permute-start | bytes 393224 | tf_op jit(solution)/shard_map/ppermute | solution.py:310
  29.2 1.8 %main_rows.1 = (f32[16,2,2,5,8,128]{5,4,3,2,1,0:T(8,128)S(1)}, f32[6,8,128]{2,1,0:T(8,128)S(1)}, f32[4,8,128]{2,1,0:T(8,128)S(1)}) custom-call(s32[16]{0:T(128)S(4)} %get-tuple-element.20.brick_at, f32[3,8,128]{2,1,0:T(8,128)S(1)} %get-tuple-element.17.light_ref, s32[3,2,8,128]{3,2,1,0:T(8,128)S(1)} %get-tuple-element.21.word_ref, ...), custom_call_target="tpu_custom_call" | custom-call | flops 13107200 | bytes 3145728 | tf_op jit(solution)/shard_map/main_rows/pallas_call | solution.py:311
  31.0 0.0 collective-permute-done.other_ref
  31.0 0.8 %edge_rows.1 = f32[4,1,4,1024]{3,2,1,0:T(4,128)} custom-call(f32[8,128]{1,0:T(8,128)S(1)} %get-tuple-element.15.first_ref, f32[8,128]{1,0:T(8,128)S(1)} %get-tuple-element.16.last_ref, f32[3,8,128]{2,1,0:T(8,128)S(1)} %get-tuple-element.17.light_ref, f32[16,6,2,8,128]{4,3,2,1,0:T(8,128)S(1)} %bitcast.19, ...), custom_call_target="tpu_custom_call" | custom-call | flops 1310720 | bytes 3145728 | tf_op jit(solution)/shard_map/edge_rows/pallas_call | solution.py:326
  (1 shorter events, 0.0 us)
Async XLA Ops:
  27.6 3.4 %collective-permute-start = (f32[16,2,8,128]{3,2,1,0:T(8,128)S(1)}, f32[16,2,8,128]{3,2,1,0:T(8,128)S(1)}, u32[]{:S(2)}, u32[]{:S(2)}) collective-permute-start(f32[16,2,8,128]{3,2,1,0:T(8,128)S(1)} %fusion.1), channel_id=1, source_target_pairs={{0,1},{31,30}} | collective-permute-start | bytes 393224 | tf_op jit(solution)/shard_map/ppermute | solution.py:310

commit v29 on v27

--- a/solution.py
+++ b/solution.py
@@ -12,9 +12,16 @@
 COLOR_UNIT, COLOR_LEAST, OPACITY_UNIT = 2 ** 11, 204, 2 ** 18
 
 
-def exchange_order(tiles):
+def exchange_orders(tiles):
     parts = 4 if tiles % 4 == 0 else 1
-    return [(parts - 1 - i % parts) * (tiles // parts) + i // parts for i in range(tiles)]
+    size = tiles // parts
+    quarters = range(parts)[::-1]
+    return ([p * size + i for i in range(size) for p in quarters],
+            [p * size + i for p in quarters for i in range(size)])
+
+
+def of_band(even, odd):
+    return jnp.where(lax.rem(lax.axis_index("gy"), 2) == 0, even, odd)
 
 
 def pack_kernel(tiles, field_ref, order_ref, light_ref, color_ref, opacity_ref,
@@ -53,9 +60,9 @@
     spread[(rows + 1) * block:, :] = spread[block:2 * block, :]
     spread[:block, :] = spread[rows * block:(rows + 1) * block, :]
     size = (tile_rows + 2) * block
-    for place, t in enumerate(exchange_order(tiles)):
-        start = t * tile_rows * block
-        out_ref[place] = spread[start:start + size, :]
+    for place, (even, odd) in enumerate(zip(*exchange_orders(tiles))):
+        start = pl.multiple_of(of_band(even, odd) * (tile_rows * block), tile_rows * block)
+        out_ref[place] = spread[pl.ds(start, size), :]
 
 
 def prepare(order_ref, light_ref, color_ref, opacity_ref,
@@ -81,8 +88,8 @@
     here, last = lax.axis_index("gz"), order_ref.shape[0] - 1
     for ref, place in [(first_ref, here == 0), (last_ref, here == last), (later_ref, here != 0)]:
         ref[...] = jnp.full(shape, place.astype(jnp.float32), jnp.float32)
-    for place, b in enumerate(exchange_order(order_ref.shape[0])):
-        brick_at_ref[order_ref[b]] = place
+    for place, (even, odd) in enumerate(zip(*exchange_orders(order_ref.shape[0]))):
+        brick_at_ref[order_ref[of_band(even, odd)]] = place
 
 
 def table_lookup(word_ref):
@@ -213,17 +220,20 @@
 
     together = 16 if bricks % 16 == 0 else 1
 
-    def step(trip, colors):
+    even, odd = exchange_orders(bricks)
+    places = [of_band(odd.index(even[b]), even.index(odd[b])) for b in range(bricks)]
+
+    def step(b_first, colors):
         colors = list(colors)
-        for u in range(together):
-            b = trip * together + u
+        for b in range(b_first, b_first + together):
+            there = places[b]
             for i, r in enumerate(edge_rows):
                 for k in range(depth):
                     above, below = tile_ref[b, r, k], tile_ref[b, r + 2, k]
                     if r == 0:
-                        above = jnp.where(is_first, other_ref[b, k], above)
+                        above = jnp.where(is_first, other_ref[there, k], above)
                     if r == rows - 1:
-                        below = jnp.where(is_last, other_ref[b, k], below)
+                        below = jnp.where(is_last, other_ref[there, k], below)
                     dy = below - above
                     facing = part_ref[b, i, k, 3] + dy * light_rows
                     shading = shading_of(facing, part_ref[b, i, k, 4] + dy * dy)
@@ -233,7 +243,9 @@
         return tuple(colors)
 
     zero = jnp.zeros(shape, jnp.float32)
-    edge_colors = lax.fori_loop(0, bricks // together, step, (zero,) * (3 * len(edge_rows)))
+    edge_colors = (zero,) * (3 * len(edge_rows))
+    for b in range(0, bricks, together):
+        edge_colors = step(b, edge_colors)
     for r in range(rows):
         for c in range(3):
             if r in edge_rows:
@@ -290,8 +302,10 @@
         compiler_params=params,
         name="pack_rows",
     )(*[pltpu.with_memory_space_constraint(x, pltpu.HBM) for x in given])
+    orders = exchange_orders(bricks)
+    groups = [[t * bands + g for t in orders[g % 2]] for g in range(bands)]
     arrived = lax.all_to_all(
-        sent, "gz", split_axis=0, concat_axis=0, tiled=True, axis_index_groups=[exchange_order(bricks)])
+        sent, ("gz", "gy"), split_axis=0, concat_axis=0, tiled=True, axis_index_groups=groups)
     tiles = arrived.reshape(bricks, tile_rows + 2, depth, chunks, LANES)
 
     last = bricks - 1

time: 31.9 us -> 32.9 us (1.031)
  starting transfers between devices: 1.6 us -> 2.28 us
    ppermute x1, starting transfers between devices: 1.6 us -> 2.28 us  [shards(): other = lax.ppermute(wrapped, ('gz', 'gy'), pairs)]
  transfers between devices with their start and end apart: 1 -> 1, of which waited for: 0 -> 0; matrix products, arithmetic and copies ran while one was open for 0% -> 0% of each run, Pallas kernels for 6% -> 5%
where the time goes in v29:
time: 32.9 us; the launch traced here: 32.7 us
  blocking collectives  26.4 us (80%)
  Pallas kernels  3.98 us (12%)
  starting transfers between devices  2.28 us (7%)
    all_to_all x1, blocking collectives, shards(): lax.all_to_all(sent, ('gz', 'gy'), split_axis=0, concat_axis=0, tiled=Tru...  26.4 us
    ppermute x1, starting transfers between devices, shards(): other = lax.ppermute(wrapped, ('gz', 'gy'), pairs)  2.28 us
    pallas_call x1, Pallas kernels, shards(): pl.pallas_call(functools.partial(main_kernel, edge_rows), out_shape=[jax....  1.78 us
    pallas_call x1, Pallas kernels, shards(): pl.pallas_call(functools.partial(pack_kernel, bricks), out_shape=[pltpu.V...  1.38 us
    pallas_call x1, Pallas kernels, shards(): pl.pallas_call(functools.partial(finish_kernel, edge_rows), out_shape=jax...  0.82 us
  transfers between devices with their start and end apart: 1, of which 0 were waited for; matrix products, arithmetic and copies ran while one was open for 0% of the time, Pallas kernels for 5%

profile of v29, /device:TPU:0, one launch (start us, length us, event | category | flops | bytes accessed | tf_op | source)
XLA Modules:
  0.0 32.7 jit_solution(13738165850280791098)
XLA Ops:
  0.0 1.4 %pack_rows.1 = (f32[16,96,128]{2,1,0:T(8,128)S(1)}, s32[16]{0:T(128)S(4)}, s32[3,2,8,128]{3,2,1,0:T(8,128)S(1)}, f32[3,8,128]{2,1,0:T(8,128)S(1)}, f32[8,128]{1,...) custom-call(f32[2,64,1024]{2,1,0:T(8,128)} %field_ref.1, s32[16]{0:T(128)} %order_ref.1, f32[3]{0:T(128)} %light_ref.1, ...), custom_call_target="tpu_custom_call" | custom-call | tf_op jit(solution)/shard_map/pack_rows/pallas_call | solution.py:282
  1.4 26.4 %all_to_all.5 = f32[16,96,128]{2,1,0:T(8,128)S(1)} all-to-all(f32[16,96,128]{2,1,0:T(8,128)S(1)} %get-tuple-element.18), channel_id=1, replica_groups={{24,16,8,0,26,18,10,2,28,20,12,4,30,22,14,6},{25,27,29,31,17,19,21,23,9..., dimensions={0} | all-to-all | bytes 1572864 | tf_op jit(solution)/shard_map/all_to_all | solution.py:307
  27.8 2.3 %collective-permute-start = (f32[16,2,8,128]{3,2,1,0:T(8,128)S(1)}, f32[16,2,8,128]{3,2,1,0:T(8,128)S(1)}, u32[]{:S(2)}, u32[]{:S(2)}) collective-permute-start(f32[16,2,8,128]{3,2,1,0:T(8,128)S(1)} %fusion.1), channel_id=1, source_target_pairs={{0,1},{31,30}} | collective-permute-start | bytes 393224 | tf_op jit(solution)/shard_map/ppermute | solution.py:315
  30.1 1.8 %main_rows.1 = (f32[16,2,2,5,8,128]{5,4,3,2,1,0:T(8,128)S(1)}, f32[6,8,128]{2,1,0:T(8,128)S(1)}, f32[4,8,128]{2,1,0:T(8,128)S(1)}) custom-call(s32[16]{0:T(128)S(4)} %get-tuple-element.20.brick_at, f32[3,8,128]{2,1,0:T(8,128)S(1)} %get-tuple-element.17.light_ref, s32[3,2,8,128]{3,2,1,0:T(8,128)S(1)} %get-tuple-element.21.word_ref, ...), custom_call_target="tpu_custom_call" | custom-call | flops 13107200 | bytes 3145728 | tf_op jit(solution)/shard_map/main_rows/pallas_call | solution.py:316
  31.8 0.0 collective-permute-done.other_ref
  31.9 0.8 %edge_rows.1 = f32[4,1,4,1024]{3,2,1,0:T(4,128)} custom-call(f32[8,128]{1,0:T(8,128)S(1)} %get-tuple-element.15.first_ref, f32[8,128]{1,0:T(8,128)S(1)} %get-tuple-element.16.last_ref, f32[3,8,128]{2,1,0:T(8,128)S(1)} %get-tuple-element.17.light_ref, f32[16,6,2,8,128]{4,3,2,1,0:T(8,128)S(1)} %bitcast.19, ...), custom_call_target="tpu_custom_call" | custom-call | flops 1310720 | bytes 3145728 | tf_op jit(solution)/shard_map/edge_rows/pallas_call | solution.py:331
  (1 shorter events, 0.0 us)
Async XLA Ops:
  27.8 4.1 %collective-permute-start = (f32[16,2,8,128]{3,2,1,0:T(8,128)S(1)}, f32[16,2,8,128]{3,2,1,0:T(8,128)S(1)}, u32[]{:S(2)}, u32[]{:S(2)}) collective-permute-start(f32[16,2,8,128]{3,2,1,0:T(8,128)S(1)} %fusion.1), channel_id=1, source_target_pairs={{0,1},{31,30}} | collective-permute-start | bytes 393224 | tf_op jit(solution)/shard_map/ppermute | solution.py:315

commit v30 on v27

--- a/solution.py
+++ b/solution.py
@@ -9,6 +9,7 @@
 from jax.sharding import PartitionSpec as P
 
 SUB, LANES = 8, 128
+ROW_STEP = 3
 COLOR_UNIT, COLOR_LEAST, OPACITY_UNIT = 2 ** 11, 204, 2 ** 18
 
 
@@ -22,7 +23,7 @@
                 field, spread, order, light, color, opacity, sems, table_sems):
     depth, rows, cols = field_ref.shape
     chunks = cols // LANES
-    block = depth * chunks
+    pitch = rows * ROW_STEP + 1
     tile_rows = rows // tiles
     pieces = sems.shape[0]
     piece_rows = rows // pieces
@@ -49,13 +50,14 @@
             for row in range(p * piece_rows, (p + 1) * piece_rows, SUB):
                 lines = [field[k, row:row + SUB, c * LANES:(c + 1) * LANES] for c in range(chunks)]
                 for c, value in enumerate(lines):
-                    spread[pl.ds((row + 1) * block + k * chunks + c, SUB, stride=block), :] = value
-    spread[(rows + 1) * block:, :] = spread[block:2 * block, :]
-    spread[:block, :] = spread[rows * block:(rows + 1) * block, :]
-    size = (tile_rows + 2) * block
+                    spread[pl.ds((k * chunks + c) * pitch + row * ROW_STEP, SUB, stride=ROW_STEP), :] = value
     for place, t in enumerate(exchange_order(tiles)):
-        start = t * tile_rows * block
-        out_ref[place] = spread[start:start + size, :]
+        for i in range(tile_rows + 2):
+            row = (t * tile_rows + i - 1) % rows
+            for k in range(depth):
+                at = (i * depth + k) * chunks
+                line = spread[pl.ds(k * chunks * pitch + row * ROW_STEP, chunks, stride=pitch), :]
+                out_ref[place, at:at + chunks, :] = line
 
 
 def prepare(order_ref, light_ref, color_ref, opacity_ref,
@@ -233,6 +235,7 @@
         return tuple(colors)
 
     zero = jnp.zeros(shape, jnp.float32)
+    pitch = 4 * rows * ROW_STEP + 1
     edge_colors = lax.fori_loop(0, bricks // together, step, (zero,) * (3 * len(edge_rows)))
     for r in range(rows):
         for c in range(3):
@@ -240,13 +243,12 @@
                 value = edge_colors[c * len(edge_rows) + edge_rows.index(r)]
             else:
                 value = color_sum_ref[c * len(inner_rows) + inner_rows.index(r)]
-            at = (c * rows + r) * chunks
-            staged[at:at + chunks, :] = value * (1.0 / COLOR_UNIT)
-        at = (3 * rows + r) * chunks
-        staged[at:at + chunks, :] = 1.0 - keep_ref[r]
+            staged[pl.ds((c * rows + r) * ROW_STEP, chunks, stride=pitch), :] = value * (1.0 / COLOR_UNIT)
+        staged[pl.ds((3 * rows + r) * ROW_STEP, chunks, stride=pitch), :] = 1.0 - keep_ref[r]
     for c in range(4):
         for q in range(chunks):
-            source = pl.ds(c * rows * chunks + q, rows, stride=chunks) if rows > 1 else pl.ds(c * chunks + q, 1)
+            start = q * pitch + c * rows * ROW_STEP
+            source = pl.ds(start, rows, stride=ROW_STEP) if rows > 1 else pl.ds(start, 1)
             out_ref[c, 0, :, q * LANES:(q + 1) * LANES] = staged[source, :]
 
 
@@ -279,7 +281,7 @@
         out_specs=[vmem, smem] + [vmem] * 5,
         scratch_shapes=[
             pltpu.VMEM(scalar.shape, scalar.dtype),
-            pltpu.VMEM(((rows + 2) * depth * chunks, LANES), scalar.dtype),
+            pltpu.VMEM((depth * chunks * (rows * ROW_STEP + 1), LANES), scalar.dtype),
             pltpu.SMEM(view_order.shape, view_order.dtype),
             pltpu.SMEM(light_dir.shape, light_dir.dtype),
             pltpu.VMEM(color_table.shape, color_table.dtype),
@@ -319,7 +321,7 @@
         out_shape=jax.ShapeDtypeStruct((4, 1, tile_rows, cols), jnp.float32),
         in_specs=[vmem] * 8,
         out_specs=vmem,
-        scratch_shapes=[pltpu.VMEM((4 * tile_rows * chunks, LANES), jnp.float32)],
+        scratch_shapes=[pltpu.VMEM((chunks * (4 * tile_rows * ROW_STEP + 1), LANES), jnp.float32)],
         compiler_params=params,
         cost_estimate=pl.CostEstimate(
             flops=10 * cells * tile_rows, bytes_accessed=24 * cells * tile_rows, transcendentals=0),

time: 31.9 us -> 31.8 us (level)
  no operation moved by 1% of the time
where the time goes in v30:
time: 31.8 us; the launch traced here: 31.6 us
  blocking collectives  26.1 us (82%)
  Pallas kernels  3.86 us (12%)
  starting transfers between devices  1.6 us (5%)
    all_to_all x1, blocking collectives, shards(): lax.all_to_all(sent, 'gz', split_axis=0, concat_axis=0, tiled=True, axis_...  26.1 us
    pallas_call x1, Pallas kernels, shards(): pl.pallas_call(functools.partial(main_kernel, edge_rows), out_shape=[jax....  1.78 us
    ppermute x1, starting transfers between devices, shards(): other = lax.ppermute(wrapped, ('gz', 'gy'), pairs)  1.6 us
    pallas_call x1, Pallas kernels, shards(): pl.pallas_call(functools.partial(pack_kernel, bricks), out_shape=[pltpu.V...  1.26 us
    pallas_call x1, Pallas kernels, shards(): pl.pallas_call(functools.partial(finish_kernel, edge_rows), out_shape=jax...  0.82 us
  transfers between devices with their start and end apart: 1, of which 0 were waited for; matrix products, arithmetic and copies ran while one was open for 0% of the time, Pallas kernels for 6%

profile of v30, /device:TPU:0, one launch (start us, length us, event | category | flops | bytes accessed | tf_op | source)
XLA Modules:
  0.0 31.6 jit_solution(7869867756666809481)
XLA Ops:
  0.0 1.3 %pack_rows.1 = (f32[16,96,128]{2,1,0:T(8,128)S(1)}, s32[16]{0:T(128)S(4)}, s32[3,2,8,128]{3,2,1,0:T(8,128)S(1)}, f32[3,8,128]{2,1,0:T(8,128)S(1)}, f32[8,128]{1,...) custom-call(f32[2,64,1024]{2,1,0:T(8,128)} %field_ref.1, s32[16]{0:T(128)} %order_ref.1, f32[3]{0:T(128)} %light_ref.1, ...), custom_call_target="tpu_custom_call" | custom-call | tf_op jit(solution)/shard_map/pack_rows/pallas_call | solution.py:272
  1.3 26.1 %all_to_all.5 = f32[16,96,128]{2,1,0:T(8,128)S(1)} all-to-all(f32[16,96,128]{2,1,0:T(8,128)S(1)} %get-tuple-element.18), channel_id=1, replica_groups={{24,16,8,0,26,18,10,2,28,20,12,4,30,22,14,6},{25,17,9,1,27,19,11,3,29,2..., dimensions={0} | all-to-all | bytes 1572864 | tf_op jit(solution)/shard_map/all_to_all | solution.py:295
  27.4 1.6 %collective-permute-start = (f32[16,2,8,128]{3,2,1,0:T(8,128)S(1)}, f32[16,2,8,128]{3,2,1,0:T(8,128)S(1)}, u32[]{:S(2)}, u32[]{:S(2)}) collective-permute-start(f32[16,2,8,128]{3,2,1,0:T(8,128)S(1)} %fusion.1), channel_id=1, source_target_pairs={{0,1},{31,30}} | collective-permute-start | bytes 393224 | tf_op jit(solution)/shard_map/ppermute | solution.py:303
  29.0 1.8 %main_rows.1 = (f32[16,2,2,5,8,128]{5,4,3,2,1,0:T(8,128)S(1)}, f32[6,8,128]{2,1,0:T(8,128)S(1)}, f32[4,8,128]{2,1,0:T(8,128)S(1)}) custom-call(s32[16]{0:T(128)S(4)} %get-tuple-element.20.brick_at, f32[3,8,128]{2,1,0:T(8,128)S(1)} %get-tuple-element.17.light_ref, s32[3,2,8,128]{3,2,1,0:T(8,128)S(1)} %get-tuple-element.21.word_ref, ...), custom_call_target="tpu_custom_call" | custom-call | flops 13107200 | bytes 3145728 | tf_op jit(solution)/shard_map/main_rows/pallas_call | solution.py:304
  30.8 0.0 collective-permute-done.other_ref
  30.8 0.8 %edge_rows.1 = f32[4,1,4,1024]{3,2,1,0:T(4,128)} custom-call(f32[8,128]{1,0:T(8,128)S(1)} %get-tuple-element.15.first_ref, f32[8,128]{1,0:T(8,128)S(1)} %get-tuple-element.16.last_ref, f32[3,8,128]{2,1,0:T(8,128)S(1)} %get-tuple-element.17.light_ref, f32[16,6,2,8,128]{4,3,2,1,0:T(8,128)S(1)} %bitcast.19, ...), custom_call_target="tpu_custom_call" | custom-call | flops 1310720 | bytes 3145728 | tf_op jit(solution)/shard_map/edge_rows/pallas_call | solution.py:319
  (1 shorter events, 0.0 us)
Async XLA Ops:
  27.4 3.4 %collective-permute-start = (f32[16,2,8,128]{3,2,1,0:T(8,128)S(1)}, f32[16,2,8,128]{3,2,1,0:T(8,128)S(1)}, u32[]{:S(2)}, u32[]{:S(2)}) collective-permute-start(f32[16,2,8,128]{3,2,1,0:T(8,128)S(1)} %fusion.1), channel_id=1, source_target_pairs={{0,1},{31,30}} | collective-permute-start | bytes 393224 | tf_op jit(solution)/shard_map/ppermute | solution.py:303

commit v31 on v30

--- a/solution.py
+++ b/solution.py
@@ -15,7 +15,8 @@
 
 def exchange_order(tiles):
     parts = 4 if tiles % 4 == 0 else 1
-    return [(parts - 1 - i % parts) * (tiles // parts) + i // parts for i in range(tiles)]
+    size = tiles // parts
+    return [p * size + -i % size for i in range(size) for p in range(parts)[::-1]]
 
 
 def pack_kernel(tiles, field_ref, order_ref, light_ref, color_ref, opacity_ref,

time: 31.8 us -> 32.2 us (1.013)
  blocking collectives: 26.1 us -> 26.8 us
    all_to_all x1, blocking collectives: 26.1 us -> 26.8 us  [shards(): lax.all_to_all(sent, 'gz', split_axis=0, concat_axis=0, tiled=True, axis_...]
where the time goes in v31:
time: 32.2 us; the launch traced here: 32 us
  blocking collectives  26.8 us (83%)
  Pallas kernels  3.86 us (12%)
  starting transfers between devices  1.3 us (4%)
    all_to_all x1, blocking collectives, shards(): lax.all_to_all(sent, 'gz', split_axis=0, concat_axis=0, tiled=True, axis_...  26.8 us
    pallas_call x1, Pallas kernels, shards(): pl.pallas_call(functools.partial(main_kernel, edge_rows), out_shape=[jax....  1.78 us
    ppermute x1, starting transfers between devices, shards(): other = lax.ppermute(wrapped, ('gz', 'gy'), pairs)  1.3 us
    pallas_call x1, Pallas kernels, shards(): pl.pallas_call(functools.partial(pack_kernel, bricks), out_shape=[pltpu.V...  1.26 us
    pallas_call x1, Pallas kernels, shards(): pl.pallas_call(functools.partial(finish_kernel, edge_rows), out_shape=jax...  0.82 us
  transfers between devices with their start and end apart: 1, of which 0 were waited for; matrix products, arithmetic and copies ran while one was open for 0% of the time, Pallas kernels for 6%

profile of v31, /device:TPU:0, one launch (start us, length us, event | category | flops | bytes accessed | tf_op | source)
XLA Modules:
  0.0 32.0 jit_solution(14132006778198270019)
XLA Ops:
  0.0 1.3 %pack_rows.1 = (f32[16,96,128]{2,1,0:T(8,128)S(1)}, s32[16]{0:T(128)S(4)}, s32[3,2,8,128]{3,2,1,0:T(8,128)S(1)}, f32[3,8,128]{2,1,0:T(8,128)S(1)}, f32[8,128]{1,...) custom-call(f32[2,64,1024]{2,1,0:T(8,128)} %field_ref.1, s32[16]{0:T(128)} %order_ref.1, f32[3]{0:T(128)} %light_ref.1, ...), custom_call_target="tpu_custom_call" | custom-call | tf_op jit(solution)/shard_map/pack_rows/pallas_call | solution.py:273
  1.3 26.8 %all_to_all.5 = f32[16,96,128]{2,1,0:T(8,128)S(1)} all-to-all(f32[16,96,128]{2,1,0:T(8,128)S(1)} %get-tuple-element.18), channel_id=1, replica_groups={{24,16,8,0,30,22,14,6,28,20,12,4,26,18,10,2},{25,17,9,1,31,23,15,7,29,2..., dimensions={0} | all-to-all | bytes 1572864 | tf_op jit(solution)/shard_map/all_to_all | solution.py:296
  28.1 1.3 %collective-permute-start = (f32[16,2,8,128]{3,2,1,0:T(8,128)S(1)}, f32[16,2,8,128]{3,2,1,0:T(8,128)S(1)}, u32[]{:S(2)}, u32[]{:S(2)}) collective-permute-start(f32[16,2,8,128]{3,2,1,0:T(8,128)S(1)} %fusion.1), channel_id=1, source_target_pairs={{0,1},{31,30}} | collective-permute-start | bytes 393224 | tf_op jit(solution)/shard_map/ppermute | solution.py:304
  29.4 1.8 %main_rows.1 = (f32[16,2,2,5,8,128]{5,4,3,2,1,0:T(8,128)S(1)}, f32[6,8,128]{2,1,0:T(8,128)S(1)}, f32[4,8,128]{2,1,0:T(8,128)S(1)}) custom-call(s32[16]{0:T(128)S(4)} %get-tuple-element.20.brick_at, f32[3,8,128]{2,1,0:T(8,128)S(1)} %get-tuple-element.17.light_ref, s32[3,2,8,128]{3,2,1,0:T(8,128)S(1)} %get-tuple-element.21.word_ref, ...), custom_call_target="tpu_custom_call" | custom-call | flops 13107200 | bytes 3145728 | tf_op jit(solution)/shard_map/main_rows/pallas_call | solution.py:305
  31.1 0.0 collective-permute-done.other_ref
  31.2 0.8 %edge_rows.1 = f32[4,1,4,1024]{3,2,1,0:T(4,128)} custom-call(f32[8,128]{1,0:T(8,128)S(1)} %get-tuple-element.15.first_ref, f32[8,128]{1,0:T(8,128)S(1)} %get-tuple-element.16.last_ref, f32[3,8,128]{2,1,0:T(8,128)S(1)} %get-tuple-element.17.light_ref, f32[16,6,2,8,128]{4,3,2,1,0:T(8,128)S(1)} %bitcast.19, ...), custom_call_target="tpu_custom_call" | custom-call | flops 1310720 | bytes 3145728 | tf_op jit(solution)/shard_map/edge_rows/pallas_call | solution.py:320
  (1 shorter events, 0.0 us)
Async XLA Ops:
  28.1 3.1 %collective-permute-start = (f32[16,2,8,128]{3,2,1,0:T(8,128)S(1)}, f32[16,2,8,128]{3,2,1,0:T(8,128)S(1)}, u32[]{:S(2)}, u32[]{:S(2)}) collective-permute-start(f32[16,2,8,128]{3,2,1,0:T(8,128)S(1)} %fusion.1), channel_id=1, source_target_pairs={{0,1},{31,30}} | collective-permute-start | bytes 393224 | tf_op jit(solution)/shard_map/ppermute | solution.py:304

commit v32 on v30

--- a/solution.py
+++ b/solution.py
@@ -265,7 +265,7 @@
     cells = bricks * depth * cols
     lines = (chunks, LANES)
     halves = (color_table.shape[1] - 1) // LANES
-    together = 8 if bricks % 8 == 0 else 1
+    together = 16 if bricks % 16 == 0 else 1
     pieces = 4 if rows % (4 * SUB) == 0 else 1
     hbm = pl.BlockSpec(memory_space=pltpu.HBM)
     given = [scalar, view_order, light_dir, color_table, opacity_table]

time: 31.8 us -> 31.7 us (level)
  transfers between devices with their start and end apart: 1 -> 1, of which waited for: 0 -> 0; matrix products, arithmetic and copies ran while one was open for 0% -> 0% of each run, Pallas kernels for 6% -> 5%
where the time goes in v32:
time: 31.7 us; the launch traced here: 31.5 us
  blocking collectives  26.1 us (82%)
  Pallas kernels  3.76 us (12%)
  starting transfers between devices  1.6 us (5%)
    all_to_all x1, blocking collectives, shards(): lax.all_to_all(sent, 'gz', split_axis=0, concat_axis=0, tiled=True, axis_...  26.1 us
    pallas_call x1, Pallas kernels, shards(): pl.pallas_call(functools.partial(main_kernel, edge_rows), out_shape=[jax....  1.68 us
    ppermute x1, starting transfers between devices, shards(): other = lax.ppermute(wrapped, ('gz', 'gy'), pairs)  1.6 us
    pallas_call x1, Pallas kernels, shards(): pl.pallas_call(functools.partial(pack_kernel, bricks), out_shape=[pltpu.V...  1.26 us
    pallas_call x1, Pallas kernels, shards(): pl.pallas_call(functools.partial(finish_kernel, edge_rows), out_shape=jax...  0.82 us
  transfers between devices with their start and end apart: 1, of which 0 were waited for; matrix products, arithmetic and copies ran while one was open for 0% of the time, Pallas kernels for 5%

profile of v32, /device:TPU:0, one launch (start us, length us, event | category | flops | bytes accessed | tf_op | source)
XLA Modules:
  0.0 31.5 jit_solution(13971828765801455849)
XLA Ops:
  0.0 1.3 %pack_rows.1 = (f32[16,96,128]{2,1,0:T(8,128)S(1)}, s32[16]{0:T(128)S(4)}, s32[3,2,8,128]{3,2,1,0:T(8,128)S(1)}, f32[3,8,128]{2,1,0:T(8,128)S(1)}, f32[8,128]{1,...) custom-call(f32[2,64,1024]{2,1,0:T(8,128)} %field_ref.1, s32[16]{0:T(128)} %order_ref.1, f32[3]{0:T(128)} %light_ref.1, ...), custom_call_target="tpu_custom_call" | custom-call | tf_op jit(solution)/shard_map/pack_rows/pallas_call | solution.py:272
  1.3 26.1 %all_to_all.5 = f32[16,96,128]{2,1,0:T(8,128)S(1)} all-to-all(f32[16,96,128]{2,1,0:T(8,128)S(1)} %get-tuple-element.18), channel_id=1, replica_groups={{24,16,8,0,26,18,10,2,28,20,12,4,30,22,14,6},{25,17,9,1,27,19,11,3,29,2..., dimensions={0} | all-to-all | bytes 1572864 | tf_op jit(solution)/shard_map/all_to_all | solution.py:295
  27.4 1.6 %collective-permute-start = (f32[16,2,8,128]{3,2,1,0:T(8,128)S(1)}, f32[16,2,8,128]{3,2,1,0:T(8,128)S(1)}, u32[]{:S(2)}, u32[]{:S(2)}) collective-permute-start(f32[16,2,8,128]{3,2,1,0:T(8,128)S(1)} %fusion.1), channel_id=1, source_target_pairs={{0,1},{31,30}} | collective-permute-start | bytes 393224 | tf_op jit(solution)/shard_map/ppermute | solution.py:303
  29.0 1.7 %main_rows.1 = (f32[16,2,2,5,8,128]{5,4,3,2,1,0:T(8,128)S(1)}, f32[6,8,128]{2,1,0:T(8,128)S(1)}, f32[4,8,128]{2,1,0:T(8,128)S(1)}) custom-call(s32[16]{0:T(128)S(4)} %get-tuple-element.20.brick_at, f32[3,8,128]{2,1,0:T(8,128)S(1)} %get-tuple-element.17.light_ref, s32[3,2,8,128]{3,2,1,0:T(8,128)S(1)} %get-tuple-element.21.word_ref, ...), custom_call_target="tpu_custom_call" | custom-call | flops 13107200 | bytes 3145728 | tf_op jit(solution)/shard_map/main_rows/pallas_call | solution.py:304
  30.7 0.0 collective-permute-done.other_ref
  30.7 0.8 %edge_rows.1 = f32[4,1,4,1024]{3,2,1,0:T(4,128)} custom-call(f32[8,128]{1,0:T(8,128)S(1)} %get-tuple-element.15.first_ref, f32[8,128]{1,0:T(8,128)S(1)} %get-tuple-element.16.last_ref, f32[3,8,128]{2,1,0:T(8,128)S(1)} %get-tuple-element.17.light_ref, f32[16,6,2,8,128]{4,3,2,1,0:T(8,128)S(1)} %bitcast.19, ...), custom_call_target="tpu_custom_call" | custom-call | flops 1310720 | bytes 3145728 | tf_op jit(solution)/shard_map/edge_rows/pallas_call | solution.py:319
  (1 shorter events, 0.0 us)
Async XLA Ops:
  27.4 3.3 %collective-permute-start = (f32[16,2,8,128]{3,2,1,0:T(8,128)S(1)}, f32[16,2,8,128]{3,2,1,0:T(8,128)S(1)}, u32[]{:S(2)}, u32[]{:S(2)}) collective-permute-start(f32[16,2,8,128]{3,2,1,0:T(8,128)S(1)} %fusion.1), channel_id=1, source_target_pairs={{0,1},{31,30}} | collective-permute-start | bytes 393224 | tf_op jit(solution)/shard_map/ppermute | solution.py:303

commit v33 on v32

--- a/solution.py
+++ b/solution.py
@@ -15,7 +15,9 @@
 
 def exchange_order(tiles):
     parts = 4 if tiles % 4 == 0 else 1
-    return [(parts - 1 - i % parts) * (tiles // parts) + i // parts for i in range(tiles)]
+    size = tiles // parts
+    chips = sorted(range(size), key=lambda i: i % 2)
+    return [p * size + i for i in chips for p in range(parts)[::-1]]
 
 
 def pack_kernel(tiles, field_ref, order_ref, light_ref, color_ref, opacity_ref,

time: 31.7 us -> 31.7 us (level)
  no operation moved by 1% of the time
where the time goes in v33:
time: 31.7 us; the launch traced here: 31.5 us
  blocking collectives  26.1 us (82%)
  Pallas kernels  3.76 us (12%)
  starting transfers between devices  1.6 us (5%)
    all_to_all x1, blocking collectives, shards(): lax.all_to_all(sent, 'gz', split_axis=0, concat_axis=0, tiled=True, axis_...  26.1 us
    pallas_call x1, Pallas kernels, shards(): pl.pallas_call(functools.partial(main_kernel, edge_rows), out_shape=[jax....  1.68 us
    ppermute x1, starting transfers between devices, shards(): other = lax.ppermute(wrapped, ('gz', 'gy'), pairs)  1.6 us
    pallas_call x1, Pallas kernels, shards(): pl.pallas_call(functools.partial(pack_kernel, bricks), out_shape=[pltpu.V...  1.26 us
    pallas_call x1, Pallas kernels, shards(): pl.pallas_call(functools.partial(finish_kernel, edge_rows), out_shape=jax...  0.82 us
  transfers between devices with their start and end apart: 1, of which 0 were waited for; matrix products, arithmetic and copies ran while one was open for 0% of the time, Pallas kernels for 5%

profile of v33, /device:TPU:0, one launch (start us, length us, event | category | flops | bytes accessed | tf_op | source)
XLA Modules:
  0.0 31.5 jit_solution(17879649881341078562)
XLA Ops:
  0.0 1.3 %pack_rows.1 = (f32[16,96,128]{2,1,0:T(8,128)S(1)}, s32[16]{0:T(128)S(4)}, s32[3,2,8,128]{3,2,1,0:T(8,128)S(1)}, f32[3,8,128]{2,1,0:T(8,128)S(1)}, f32[8,128]{1,...) custom-call(f32[2,64,1024]{2,1,0:T(8,128)} %field_ref.1, s32[16]{0:T(128)} %order_ref.1, f32[3]{0:T(128)} %light_ref.1, ...), custom_call_target="tpu_custom_call" | custom-call | tf_op jit(solution)/shard_map/pack_rows/pallas_call | solution.py:274
  1.3 26.1 %all_to_all.5 = f32[16,96,128]{2,1,0:T(8,128)S(1)} all-to-all(f32[16,96,128]{2,1,0:T(8,128)S(1)} %get-tuple-element.18), channel_id=1, replica_groups={{24,16,8,0,28,20,12,4,26,18,10,2,30,22,14,6},{25,17,9,1,29,21,13,5,27,1..., dimensions={0} | all-to-all | bytes 1572864 | tf_op jit(solution)/shard_map/all_to_all | solution.py:297
  27.4 1.6 %collective-permute-start = (f32[16,2,8,128]{3,2,1,0:T(8,128)S(1)}, f32[16,2,8,128]{3,2,1,0:T(8,128)S(1)}, u32[]{:S(2)}, u32[]{:S(2)}) collective-permute-start(f32[16,2,8,128]{3,2,1,0:T(8,128)S(1)} %fusion.1), channel_id=1, source_target_pairs={{0,1},{31,30}} | collective-permute-start | bytes 393224 | tf_op jit(solution)/shard_map/ppermute | solution.py:305
  29.0 1.7 %main_rows.1 = (f32[16,2,2,5,8,128]{5,4,3,2,1,0:T(8,128)S(1)}, f32[6,8,128]{2,1,0:T(8,128)S(1)}, f32[4,8,128]{2,1,0:T(8,128)S(1)}) custom-call(s32[16]{0:T(128)S(4)} %get-tuple-element.20.brick_at, f32[3,8,128]{2,1,0:T(8,128)S(1)} %get-tuple-element.17.light_ref, s32[3,2,8,128]{3,2,1,0:T(8,128)S(1)} %get-tuple-element.21.word_ref, ...), custom_call_target="tpu_custom_call" | custom-call | flops 13107200 | bytes 3145728 | tf_op jit(solution)/shard_map/main_rows/pallas_call | solution.py:306
  30.7 0.0 collective-permute-done.other_ref
  30.7 0.8 %edge_rows.1 = f32[4,1,4,1024]{3,2,1,0:T(4,128)} custom-call(f32[8,128]{1,0:T(8,128)S(1)} %get-tuple-element.15.first_ref, f32[8,128]{1,0:T(8,128)S(1)} %get-tuple-element.16.last_ref, f32[3,8,128]{2,1,0:T(8,128)S(1)} %get-tuple-element.17.light_ref, f32[16,6,2,8,128]{4,3,2,1,0:T(8,128)S(1)} %bitcast.19, ...), custom_call_target="tpu_custom_call" | custom-call | flops 1310720 | bytes 3145728 | tf_op jit(solution)/shard_map/edge_rows/pallas_call | solution.py:321
  (1 shorter events, 0.0 us)
Async XLA Ops:
  27.4 3.3 %collective-permute-start = (f32[16,2,8,128]{3,2,1,0:T(8,128)S(1)}, f32[16,2,8,128]{3,2,1,0:T(8,128)S(1)}, u32[]{:S(2)}, u32[]{:S(2)}) collective-permute-start(f32[16,2,8,128]{3,2,1,0:T(8,128)S(1)} %fusion.1), channel_id=1, source_target_pairs={{0,1},{31,30}} | collective-permute-start | bytes 393224 | tf_op jit(solution)/shard_map/ppermute | solution.py:305

commit v34 on v33

--- a/solution.py
+++ b/solution.py
@@ -13,11 +13,17 @@
 COLOR_UNIT, COLOR_LEAST, OPACITY_UNIT = 2 ** 11, 204, 2 ** 18
 
 
-def exchange_order(tiles):
+def exchange_orders(tiles):
     parts = 4 if tiles % 4 == 0 else 1
     size = tiles // parts
-    chips = sorted(range(size), key=lambda i: i % 2)
-    return [p * size + i for i in chips for p in range(parts)[::-1]]
+    return [
+        [p * size + i for i in chips for p in range(parts)[::-1]]
+        for chips in (sorted(range(size), key=lambda i: i % 2), range(size))
+    ]
+
+
+def of_band(even, odd):
+    return jnp.where(lax.rem(lax.axis_index("gy"), 2) == 0, even, odd)
 
 
 def pack_kernel(tiles, field_ref, order_ref, light_ref, color_ref, opacity_ref,
@@ -53,7 +59,9 @@
                 lines = [field[k, row:row + SUB, c * LANES:(c + 1) * LANES] for c in range(chunks)]
                 for c, value in enumerate(lines):
                     spread[pl.ds((k * chunks + c) * pitch + row * ROW_STEP, SUB, stride=ROW_STEP), :] = value
-    for place, t in enumerate(exchange_order(tiles)):
+    even, odd = exchange_orders(tiles)
+    for t in range(tiles):
+        place = of_band(even.index(t), odd.index(t))
         for i in range(tile_rows + 2):
             row = (t * tile_rows + i - 1) % rows
             for k in range(depth):
@@ -85,8 +93,9 @@
     here, last = lax.axis_index("gz"), order_ref.shape[0] - 1
     for ref, place in [(first_ref, here == 0), (last_ref, here == last), (later_ref, here != 0)]:
         ref[...] = jnp.full(shape, place.astype(jnp.float32), jnp.float32)
-    for place, b in enumerate(exchange_order(order_ref.shape[0])):
-        brick_at_ref[order_ref[b]] = place
+    even, odd = exchange_orders(order_ref.shape[0])
+    for b in range(order_ref.shape[0]):
+        brick_at_ref[order_ref[b]] = of_band(even.index(b), odd.index(b))
 
 
 def table_lookup(word_ref):
@@ -215,19 +224,19 @@
     light_rows = light_ref[1]
     is_first, is_last = first_ref[...] == 1.0, last_ref[...] == 1.0
 
-    together = 16 if bricks % 16 == 0 else 1
-
-    def step(trip, colors):
+    even, odd = exchange_orders(bricks)
+    places = [of_band(odd.index(even[b]), even.index(odd[b])) for b in range(bricks)]
+
+    def step(colors):
         colors = list(colors)
-        for u in range(together):
-            b = trip * together + u
+        for b, there in enumerate(places):
             for i, r in enumerate(edge_rows):
                 for k in range(depth):
                     above, below = tile_ref[b, r, k], tile_ref[b, r + 2, k]
                     if r == 0:
-                        above = jnp.where(is_first, other_ref[b, k], above)
+                        above = jnp.where(is_first, other_ref[there, k], above)
                     if r == rows - 1:
-                        below = jnp.where(is_last, other_ref[b, k], below)
+                        below = jnp.where(is_last, other_ref[there, k], below)
                     dy = below - above
                     facing = part_ref[b, i, k, 3] + dy * light_rows
                     shading = shading_of(facing, part_ref[b, i, k, 4] + dy * dy)
@@ -238,7 +247,7 @@
 
     zero = jnp.zeros(shape, jnp.float32)
     pitch = 4 * rows * ROW_STEP + 1
-    edge_colors = lax.fori_loop(0, bricks // together, step, (zero,) * (3 * len(edge_rows)))
+    edge_colors = step((zero,) * (3 * len(edge_rows)))
     for r in range(rows):
         for c in range(3):
             if r in edge_rows:
@@ -294,8 +303,10 @@
         compiler_params=params,
         name="pack_rows",
     )(*[pltpu.with_memory_space_constraint(x, pltpu.HBM) for x in given])
+    orders = exchange_orders(bricks)
+    groups = [[t * bands + g for t in orders[g % 2]] for g in range(bands)]
     arrived = lax.all_to_all(
-        sent, "gz", split_axis=0, concat_axis=0, tiled=True, axis_index_groups=[exchange_order(bricks)])
+        sent, ("gz", "gy"), split_axis=0, concat_axis=0, tiled=True, axis_index_groups=groups)
     tiles = arrived.reshape(bricks, tile_rows + 2, depth, chunks, LANES)
 
     last = bricks - 1

time: 31.7 us -> 31.7 us (level)
  no operation moved by 1% of the time
where the time goes in v34:
time: 31.7 us; the launch traced here: 31.5 us
  blocking collectives  26.1 us (82%)
  Pallas kernels  3.76 us (12%)
  starting transfers between devices  1.6 us (5%)
    all_to_all x1, blocking collectives, shards(): lax.all_to_all(sent, ('gz', 'gy'), split_axis=0, concat_axis=0, tiled=Tru...  26.1 us
    pallas_call x1, Pallas kernels, shards(): pl.pallas_call(functools.partial(main_kernel, edge_rows), out_shape=[jax....  1.68 us
    ppermute x1, starting transfers between devices, shards(): other = lax.ppermute(wrapped, ('gz', 'gy'), pairs)  1.6 us
    pallas_call x1, Pallas kernels, shards(): pl.pallas_call(functools.partial(pack_kernel, bricks), out_shape=[pltpu.V...  1.26 us
    pallas_call x1, Pallas kernels, shards(): pl.pallas_call(functools.partial(finish_kernel, edge_rows), out_shape=jax...  0.82 us
  transfers between devices with their start and end apart: 1, of which 0 were waited for; matrix products, arithmetic and copies ran while one was open for 0% of the time, Pallas kernels for 5%

profile of v34, /device:TPU:0, one launch (start us, length us, event | category | flops | bytes accessed | tf_op | source)
XLA Modules:
  0.0 31.5 jit_solution(8946763275897755774)
XLA Ops:
  0.0 1.3 %pack_rows.1 = (f32[16,96,128]{2,1,0:T(8,128)S(1)}, s32[16]{0:T(128)S(4)}, s32[3,2,8,128]{3,2,1,0:T(8,128)S(1)}, f32[3,8,128]{2,1,0:T(8,128)S(1)}, f32[8,128]{1,...) custom-call(f32[2,64,1024]{2,1,0:T(8,128)} %field_ref.1, s32[16]{0:T(128)} %order_ref.1, f32[3]{0:T(128)} %light_ref.1, ...), custom_call_target="tpu_custom_call" | custom-call | tf_op jit(solution)/shard_map/pack_rows/pallas_call | solution.py:283
  1.3 26.1 %all_to_all.5 = f32[16,96,128]{2,1,0:T(8,128)S(1)} all-to-all(f32[16,96,128]{2,1,0:T(8,128)S(1)} %get-tuple-element.18), channel_id=1, replica_groups={{24,16,8,0,28,20,12,4,26,18,10,2,30,22,14,6},{25,17,9,1,27,19,11,3,29,2..., dimensions={0} | all-to-all | bytes 1572864 | tf_op jit(solution)/shard_map/all_to_all | solution.py:308
  27.4 1.6 %collective-permute-start = (f32[16,2,8,128]{3,2,1,0:T(8,128)S(1)}, f32[16,2,8,128]{3,2,1,0:T(8,128)S(1)}, u32[]{:S(2)}, u32[]{:S(2)}) collective-permute-start(f32[16,2,8,128]{3,2,1,0:T(8,128)S(1)} %fusion.1), channel_id=1, source_target_pairs={{0,1},{31,30}} | collective-permute-start | bytes 393224 | tf_op jit(solution)/shard_map/ppermute | solution.py:316
  29.0 1.7 %main_rows.1 = (f32[16,2,2,5,8,128]{5,4,3,2,1,0:T(8,128)S(1)}, f32[6,8,128]{2,1,0:T(8,128)S(1)}, f32[4,8,128]{2,1,0:T(8,128)S(1)}) custom-call(s32[16]{0:T(128)S(4)} %get-tuple-element.20.brick_at, f32[3,8,128]{2,1,0:T(8,128)S(1)} %get-tuple-element.17.light_ref, s32[3,2,8,128]{3,2,1,0:T(8,128)S(1)} %get-tuple-element.21.word_ref, ...), custom_call_target="tpu_custom_call" | custom-call | flops 13107200 | bytes 3145728 | tf_op jit(solution)/shard_map/main_rows/pallas_call | solution.py:317
  30.7 0.0 collective-permute-done.other_ref
  30.7 0.8 %edge_rows.1 = f32[4,1,4,1024]{3,2,1,0:T(4,128)} custom-call(f32[8,128]{1,0:T(8,128)S(1)} %get-tuple-element.15.first_ref, f32[8,128]{1,0:T(8,128)S(1)} %get-tuple-element.16.last_ref, f32[3,8,128]{2,1,0:T(8,128)S(1)} %get-tuple-element.17.light_ref, f32[16,6,2,8,128]{4,3,2,1,0:T(8,128)S(1)} %bitcast.19, ...), custom_call_target="tpu_custom_call" | custom-call | flops 1310720 | bytes 3145728 | tf_op jit(solution)/shard_map/edge_rows/pallas_call | solution.py:332
  (1 shorter events, 0.0 us)
Async XLA Ops:
  27.4 3.3 %collective-permute-start = (f32[16,2,8,128]{3,2,1,0:T(8,128)S(1)}, f32[16,2,8,128]{3,2,1,0:T(8,128)S(1)}, u32[]{:S(2)}, u32[]{:S(2)}) collective-permute-start(f32[16,2,8,128]{3,2,1,0:T(8,128)S(1)} %fusion.1), channel_id=1, source_target_pairs={{0,1},{31,30}} | collective-permute-start | bytes 393224 | tf_op jit(solution)/shard_map/ppermute | solution.py:316

commit v35 on v33

--- a/solution.py
+++ b/solution.py
@@ -39,13 +39,10 @@
         for i, (source, target) in enumerate(
             [(color_ref, color), (opacity_ref, opacity), (order_ref, order), (light_ref, light)])
     ]
-    for copy in table_copies:
-        copy.start()
     for p in range(pieces):
         copy_in(p).start()
     for copy in table_copies:
-        copy.wait()
-    prepare(order, light, color, opacity, brick_at_ref, word_ref, light_rows_ref, first_ref, last_ref, later_ref)
+        copy.start()
     for p in range(pieces):
         copy_in(p).wait()
         for k in range(depth):
@@ -53,6 +50,10 @@
                 lines = [field[k, row:row + SUB, c * LANES:(c + 1) * LANES] for c in range(chunks)]
                 for c, value in enumerate(lines):
                     spread[pl.ds((k * chunks + c) * pitch + row * ROW_STEP, SUB, stride=ROW_STEP), :] = value
+        if p == 0:
+            for copy in table_copies:
+                copy.wait()
+            prepare(order, light, color, opacity, brick_at_ref, word_ref, light_rows_ref, first_ref, last_ref, later_ref)
     for place, t in enumerate(exchange_order(tiles)):
         for i in range(tile_rows + 2):
             row = (t * tile_rows + i - 1) % rows

time: 31.7 us -> 31.8 us (level)
  no operation moved by 1% of the time
where the time goes in v35:
time: 31.8 us; the launch traced here: 31.6 us
  blocking collectives  26.1 us (82%)
  Pallas kernels  3.88 us (12%)
  starting transfers between devices  1.6 us (5%)
    all_to_all x1, blocking collectives, shards(): lax.all_to_all(sent, 'gz', split_axis=0, concat_axis=0, tiled=True, axis_...  26.1 us
    pallas_call x1, Pallas kernels, shards(): pl.pallas_call(functools.partial(main_kernel, edge_rows), out_shape=[jax....  1.68 us
    ppermute x1, starting transfers between devices, shards(): other = lax.ppermute(wrapped, ('gz', 'gy'), pairs)  1.6 us
    pallas_call x1, Pallas kernels, shards(): pl.pallas_call(functools.partial(pack_kernel, bricks), out_shape=[pltpu.V...  1.38 us
    pallas_call x1, Pallas kernels, shards(): pl.pallas_call(functools.partial(finish_kernel, edge_rows), out_shape=jax...  0.82 us
  transfers between devices with their start and end apart: 1, of which 0 were waited for; matrix products, arithmetic and copies ran while one was open for 0% of the time, Pallas kernels for 5%

profile of v35, /device:TPU:0, one launch (start us, length us, event | category | flops | bytes accessed | tf_op | source)
XLA Modules:
  0.0 31.6 jit_solution(3909441626583071822)
XLA Ops:
  0.0 1.4 %pack_rows.1 = (f32[16,96,128]{2,1,0:T(8,128)S(1)}, s32[16]{0:T(128)S(4)}, s32[3,2,8,128]{3,2,1,0:T(8,128)S(1)}, f32[3,8,128]{2,1,0:T(8,128)S(1)}, f32[8,128]{1,...) custom-call(f32[2,64,1024]{2,1,0:T(8,128)} %field_ref.1, s32[16]{0:T(128)} %order_ref.1, f32[3]{0:T(128)} %light_ref.1, ...), custom_call_target="tpu_custom_call" | custom-call | tf_op jit(solution)/shard_map/pack_rows/pallas_call | solution.py:275
  1.4 26.1 %all_to_all.5 = f32[16,96,128]{2,1,0:T(8,128)S(1)} all-to-all(f32[16,96,128]{2,1,0:T(8,128)S(1)} %get-tuple-element.18), channel_id=1, replica_groups={{24,16,8,0,28,20,12,4,26,18,10,2,30,22,14,6},{25,17,9,1,29,21,13,5,27,1..., dimensions={0} | all-to-all | bytes 1572864 | tf_op jit(solution)/shard_map/all_to_all | solution.py:298
  27.5 1.6 %collective-permute-start = (f32[16,2,8,128]{3,2,1,0:T(8,128)S(1)}, f32[16,2,8,128]{3,2,1,0:T(8,128)S(1)}, u32[]{:S(2)}, u32[]{:S(2)}) collective-permute-start(f32[16,2,8,128]{3,2,1,0:T(8,128)S(1)} %fusion.1), channel_id=1, source_target_pairs={{0,1},{31,30}} | collective-permute-start | bytes 393224 | tf_op jit(solution)/shard_map/ppermute | solution.py:306
  29.1 1.7 %main_rows.1 = (f32[16,2,2,5,8,128]{5,4,3,2,1,0:T(8,128)S(1)}, f32[6,8,128]{2,1,0:T(8,128)S(1)}, f32[4,8,128]{2,1,0:T(8,128)S(1)}) custom-call(s32[16]{0:T(128)S(4)} %get-tuple-element.20.brick_at, f32[3,8,128]{2,1,0:T(8,128)S(1)} %get-tuple-element.17.light_ref, s32[3,2,8,128]{3,2,1,0:T(8,128)S(1)} %get-tuple-element.21.word_ref, ...), custom_call_target="tpu_custom_call" | custom-call | flops 13107200 | bytes 3145728 | tf_op jit(solution)/shard_map/main_rows/pallas_call | solution.py:307
  30.8 0.0 collective-permute-done.other_ref
  30.8 0.8 %edge_rows.1 = f32[4,1,4,1024]{3,2,1,0:T(4,128)} custom-call(f32[8,128]{1,0:T(8,128)S(1)} %get-tuple-element.15.first_ref, f32[8,128]{1,0:T(8,128)S(1)} %get-tuple-element.16.last_ref, f32[3,8,128]{2,1,0:T(8,128)S(1)} %get-tuple-element.17.light_ref, f32[16,6,2,8,128]{4,3,2,1,0:T(8,128)S(1)} %bitcast.19, ...), custom_call_target="tpu_custom_call" | custom-call | flops 1310720 | bytes 3145728 | tf_op jit(solution)/shard_map/edge_rows/pallas_call | solution.py:322
  (1 shorter events, 0.0 us)
Async XLA Ops:
  27.5 3.3 %collective-permute-start = (f32[16,2,8,128]{3,2,1,0:T(8,128)S(1)}, f32[16,2,8,128]{3,2,1,0:T(8,128)S(1)}, u32[]{:S(2)}, u32[]{:S(2)}) collective-permute-start(f32[16,2,8,128]{3,2,1,0:T(8,128)S(1)} %fusion.1), channel_id=1, source_target_pairs={{0,1},{31,30}} | collective-permute-start | bytes 393224 | tf_op jit(solution)/shard_map/ppermute | solution.py:306

commit v36 on v33

--- a/solution.py
+++ b/solution.py
@@ -20,8 +20,8 @@
     return [p * size + i for i in chips for p in range(parts)[::-1]]
 
 
-def pack_kernel(tiles, field_ref, order_ref, light_ref, color_ref, opacity_ref,
-                out_ref, brick_at_ref, word_ref, light_rows_ref, first_ref, last_ref, later_ref,
+def pack_kernel(tiles, bands, field_ref, order_ref, light_ref, color_ref, opacity_ref,
+                out_ref, brick_at_ref, word_ref, light_rows_ref, first_ref, last_ref, later_ref, inside_ref,
                 field, spread, order, light, color, opacity, sems, table_sems):
     depth, rows, cols = field_ref.shape
     chunks = cols // LANES
@@ -45,7 +45,8 @@
         copy_in(p).start()
     for copy in table_copies:
         copy.wait()
-    prepare(order, light, color, opacity, brick_at_ref, word_ref, light_rows_ref, first_ref, last_ref, later_ref)
+    prepare(bands, order, light, color, opacity, brick_at_ref, word_ref, light_rows_ref,
+            first_ref, last_ref, later_ref, inside_ref)
     for p in range(pieces):
         copy_in(p).wait()
         for k in range(depth):
@@ -62,8 +63,8 @@
                 out_ref[place, at:at + chunks, :] = line
 
 
-def prepare(order_ref, light_ref, color_ref, opacity_ref,
-            brick_at_ref, word_ref, light_rows_ref, first_ref, last_ref, later_ref):
+def prepare(bands, order_ref, light_ref, color_ref, opacity_ref,
+            brick_at_ref, word_ref, light_rows_ref, first_ref, last_ref, later_ref, inside_ref):
     bins = color_ref.shape[1] - 1
     _, halves, chunks, lanes = word_ref.shape
     shape = (chunks, lanes)
@@ -83,7 +84,10 @@
     for i in range(3):
         light_rows_ref[i] = jnp.full(shape, light_ref[i], jnp.float32) * math.sqrt(0.75)
     here, last = lax.axis_index("gz"), order_ref.shape[0] - 1
-    for ref, place in [(first_ref, here == 0), (last_ref, here == last), (later_ref, here != 0)]:
+    band = lax.axis_index("gy")
+    inside = jnp.where(here == 0, band > 0, band < bands - 1)
+    for ref, place in [
+        (first_ref, here == 0), (last_ref, here == last), (later_ref, here != 0), (inside_ref, inside)]:
         ref[...] = jnp.full(shape, place.astype(jnp.float32), jnp.float32)
     for place, b in enumerate(exchange_order(order_ref.shape[0])):
         brick_at_ref[order_ref[b]] = place
@@ -206,7 +210,7 @@
         keep_ref[r] = value
 
 
-def finish_kernel(edge_rows, first_ref, last_ref, light_ref, tile_ref, other_ref, part_ref, color_sum_ref, keep_ref,
+def finish_kernel(edge_rows, first_ref, last_ref, inside_ref, light_ref, tile_ref, other_ref, part_ref, color_sum_ref, keep_ref,
                   out_ref, staged):
     bricks, padded_rows, depth, chunks, lanes = tile_ref.shape
     rows = padded_rows - 2
@@ -214,6 +218,7 @@
     shape = (chunks, lanes)
     light_rows = light_ref[1]
     is_first, is_last = first_ref[...] == 1.0, last_ref[...] == 1.0
+    inside = inside_ref[...]
 
     together = 16 if bricks % 16 == 0 else 1
 
@@ -225,9 +230,9 @@
                 for k in range(depth):
                     above, below = tile_ref[b, r, k], tile_ref[b, r + 2, k]
                     if r == 0:
-                        above = jnp.where(is_first, other_ref[b, k], above)
+                        above = jnp.where(is_first, other_ref[b, k] * inside, above)
                     if r == rows - 1:
-                        below = jnp.where(is_last, other_ref[b, k], below)
+                        below = jnp.where(is_last, other_ref[b, k] * inside, below)
                     dy = below - above
                     facing = part_ref[b, i, k, 3] + dy * light_rows
                     shading = shading_of(facing, part_ref[b, i, k, 4] + dy * dy)
@@ -271,16 +276,16 @@
     pieces = 4 if rows % (4 * SUB) == 0 else 1
     hbm = pl.BlockSpec(memory_space=pltpu.HBM)
     given = [scalar, view_order, light_dir, color_table, opacity_table]
-    sent, brick_at, words, light_rows, first, final, later = pl.pallas_call(
-        functools.partial(pack_kernel, bricks),
+    sent, brick_at, words, light_rows, first, final, later, inside = pl.pallas_call(
+        functools.partial(pack_kernel, bricks, bands),
         out_shape=[
             pltpu.VMEM((bricks, (tile_rows + 2) * depth * chunks, LANES), jnp.float32),
             pltpu.SMEM((bricks,), jnp.int32),
             jax.ShapeDtypeStruct((3, halves) + lines, jnp.int32),
             jax.ShapeDtypeStruct((3,) + lines, jnp.float32),
-        ] + [jax.ShapeDtypeStruct(lines, jnp.float32)] * 3,
+        ] + [jax.ShapeDtypeStruct(lines, jnp.float32)] * 4,
         in_specs=[hbm] * 5,
-        out_specs=[vmem, smem] + [vmem] * 5,
+        out_specs=[vmem, smem] + [vmem] * 6,
         scratch_shapes=[
             pltpu.VMEM(scalar.shape, scalar.dtype),
             pltpu.VMEM((depth * chunks * (rows * ROW_STEP + 1), LANES), scalar.dtype),
@@ -301,6 +306,8 @@
     last = bricks - 1
     pairs = [(g, g + 1) for g in range(bands - 1)]
     pairs += [(last * bands + g + 1, last * bands + g) for g in range(bands - 1)]
+    if bands == 2:
+        pairs += [(j, i) for i, j in pairs]
     wrapped = tiles[:, 0] * first + tiles[:, -1] * later
     other = lax.ppermute(wrapped, ("gz", "gy"), pairs)
     parts, color_sums, keeps = pl.pallas_call(
@@ -321,14 +328,14 @@
     return pl.pallas_call(
         functools.partial(finish_kernel, edge_rows),
         out_shape=jax.ShapeDtypeStruct((4, 1, tile_rows, cols), jnp.float32),
-        in_specs=[vmem] * 8,
+        in_specs=[vmem] * 9,
         out_specs=vmem,
         scratch_shapes=[pltpu.VMEM((chunks * (4 * tile_rows * ROW_STEP + 1), LANES), jnp.float32)],
         compiler_params=params,
         cost_estimate=pl.CostEstimate(
             flops=10 * cells * tile_rows, bytes_accessed=24 * cells * tile_rows, transcendentals=0),
         name="edge_rows",
-    )(first, final, light_rows, tiles, other, parts, color_sums, keeps)
+    )(first, final, inside, light_rows, tiles, other, parts, color_sums, keeps)
 
 
 def solution(mesh):

time: 31.7 us -> 32 us (level)
    ppermute x1, starting transfers between devices: 1.6 us -> 1.92 us  [shards(): other = lax.ppermute(wrapped, ('gz', 'gy'), pairs)]
where the time goes in v36:
time: 32 us; the launch traced here: 31.8 us
  blocking collectives  26.1 us (82%)
  Pallas kernels  3.75 us (12%)
  starting transfers between devices  1.92 us (6%)
    all_to_all x1, blocking collectives, shards(): lax.all_to_all(sent, 'gz', split_axis=0, concat_axis=0, tiled=True, axis_...  26.1 us
    ppermute x1, starting transfers between devices, shards(): other = lax.ppermute(wrapped, ('gz', 'gy'), pairs)  1.92 us
    pallas_call x1, Pallas kernels, shards(): pl.pallas_call(functools.partial(main_kernel, edge_rows), out_shape=[jax....  1.67 us
    pallas_call x1, Pallas kernels, shards(): pl.pallas_call(functools.partial(pack_kernel, bricks, bands), out_shape=[...  1.26 us
    pallas_call x1, Pallas kernels, shards(): pl.pallas_call(functools.partial(finish_kernel, edge_rows), out_shape=jax...  0.82 us
  transfers between devices with their start and end apart: 1, of which 0 were waited for; matrix products, arithmetic and copies ran while one was open for 0% of the time, Pallas kernels for 5%

profile of v36, /device:TPU:0, one launch (start us, length us, event | category | flops | bytes accessed | tf_op | source)
XLA Modules:
  0.0 31.8 jit_solution(14813630511317977402)
XLA Ops:
  0.0 1.3 %pack_rows.1 = (f32[16,96,128]{2,1,0:T(8,128)S(1)}, s32[16]{0:T(128)S(4)}, s32[3,2,8,128]{3,2,1,0:T(8,128)S(1)}, f32[3,8,128]{2,1,0:T(8,128)S(1)}, f32[8,128]{1,...) custom-call(f32[2,64,1024]{2,1,0:T(8,128)} %field_ref.1, s32[16]{0:T(128)} %order_ref.1, ...), custom_call_target="tpu_custom_call" | custom-call | tf_op jit(solution)/shard_map/pack_rows/pallas_call | solution.py:279
  1.3 26.1 %all_to_all.5 = f32[16,96,128]{2,1,0:T(8,128)S(1)} all-to-all(f32[16,96,128]{2,1,0:T(8,128)S(1)} %get-tuple-element.20), channel_id=1, replica_groups={{24,16,8,0,28,20,12,4,26,18,10,2,30,22,14,6},{25,17,9,1,29,21,13,5,27,1..., dimensions={0} | all-to-all | bytes 1572864 | tf_op jit(solution)/shard_map/all_to_all | solution.py:302
  27.4 1.9 %collective-permute-start = (f32[16,2,8,128]{3,2,1,0:T(8,128)S(1)}, f32[16,2,8,128]{3,2,1,0:T(8,128)S(1)}, u32[]{:S(2)}, u32[]{:S(2)}) collective-permute-start(f32[16,2,8,128]{3,2,1,0:T(8,128)S(1)} %fusion.1), channel_id=1, source_target_pairs={{0,1},{31,30},{1,0},{30,31}} | collective-permute-start | bytes 393224 | tf_op jit(solution)/shard_map/ppermute | solution.py:312
  29.3 1.7 %main_rows.1 = (f32[16,2,2,5,8,128]{5,4,3,2,1,0:T(8,128)S(1)}, f32[6,8,128]{2,1,0:T(8,128)S(1)}, f32[4,8,128]{2,1,0:T(8,128)S(1)}) custom-call(s32[16]{0:T(128)S(4)} %get-tuple-element.22.brick_at, f32[3,8,128]{2,1,0:T(8,128)S(1)} %get-tuple-element.19.light_ref, s32[3,2,8,128]{3,2,1,0:T(8,128)S(1)} %get-tuple-element.23.word_ref, ...), custom_call_target="tpu_custom_call" | custom-call | flops 13107200 | bytes 3145728 | tf_op jit(solution)/shard_map/main_rows/pallas_call | solution.py:313
  31.0 0.0 collective-permute-done.other_ref
  31.0 0.8 %edge_rows.1 = f32[4,1,4,1024]{3,2,1,0:T(4,128)} custom-call(f32[8,128]{1,0:T(8,128)S(1)} %get-tuple-element.16.first_ref, f32[8,128]{1,0:T(8,128)S(1)} %get-tuple-element.17.last_ref, f32[8,128]{1,0:T(8,128)S(1)} %get-tuple-element.18.inside_ref, f32[3,8,128]{2,1,0:T(8,128)S(1)} %get-tuple-element.19.light_ref, f32[16,6,2,8,128]{4,3,2,1,0:T(8,128)S(1)} %bitcast.19, ...), custom_call_target="tpu_custom_call" | custom-call | flops 1310720 | bytes 3145728 | tf_op jit(solution)/shard_map/edge_rows/pallas_call | solution.py:328
  (1 shorter events, 0.0 us)
Async XLA Ops:
  27.4 3.6 %collective-permute-start = (f32[16,2,8,128]{3,2,1,0:T(8,128)S(1)}, f32[16,2,8,128]{3,2,1,0:T(8,128)S(1)}, u32[]{:S(2)}, u32[]{:S(2)}) collective-permute-start(f32[16,2,8,128]{3,2,1,0:T(8,128)S(1)} %fusion.1), channel_id=1, source_target_pairs={{0,1},{31,30},{1,0},{30,31}} | collective-permute-start | bytes 393224 | tf_op jit(solution)/shard_map/ppermute | solution.py:312

commit v37 on v33

--- a/solution.py
+++ b/solution.py
@@ -168,9 +168,14 @@
     def step(trip, carry):
         colors, keeps = list(carry[0]), list(carry[1])
         at = [brick_at[trip * together + u] for u in range(together)]
-        fields = [[[tile_ref[b, r, k] for k in range(depth)] for r in range(padded_rows)] for b in at]
-        kept = []
-        for u, (b, field) in enumerate(zip(at, fields)):
+
+        def loaded(b):
+            return [[tile_ref[b, r, k] for k in range(depth)] for r in range(padded_rows)]
+
+        following = loaded(at[0])
+        for u, b in enumerate(at):
+            field, kept = following, []
+            following = loaded(at[u + 1]) if u + 1 < together else None
             cells = [x for line in field[1:-1] for x in line]
             column = column_differences(cells, carried, u * len(cells))
             for r in range(rows):
@@ -183,7 +188,7 @@
                     squared = (dz * dz + 1.0) + dx * dx
                     if r in edge_rows:
                         values = [weight * color[c] for c in range(3)] + [facing, squared]
-                        kept.append((b, edge_rows.index(r), k, values))
+                        kept.append((edge_rows.index(r), k, values))
                     else:
                         i = inner_rows.index(r)
                         dy = field[r + 2][k] - field[r][k]
@@ -192,9 +197,9 @@
                             slot = c * len(inner_rows) + i
                             colors[slot] = colors[slot] + shaded * color[c]
                     keeps[r] = keeps[r] - weight
-        for b, i, k, values in kept:
-            for v, value in enumerate(values):
-                part_ref[b, i, k, v] = value
+            for i, k, values in kept:
+                for v, value in enumerate(values):
+                    part_ref[b, i, k, v] = value
         return tuple(colors), tuple(keeps)
 
     zero, one = jnp.zeros(shape, jnp.float32), jnp.ones(shape, jnp.float32)

time: 31.7 us -> 31.7 us (level)
  no operation moved by 1% of the time
where the time goes in v37:
time: 31.7 us; the launch traced here: 31.5 us
  blocking collectives  26.1 us (82%)
  Pallas kernels  3.76 us (12%)
  starting transfers between devices  1.6 us (5%)
    all_to_all x1, blocking collectives, shards(): lax.all_to_all(sent, 'gz', split_axis=0, concat_axis=0, tiled=True, axis_...  26.1 us
    pallas_call x1, Pallas kernels, shards(): pl.pallas_call(functools.partial(main_kernel, edge_rows), out_shape=[jax....  1.68 us
    ppermute x1, starting transfers between devices, shards(): other = lax.ppermute(wrapped, ('gz', 'gy'), pairs)  1.6 us
    pallas_call x1, Pallas kernels, shards(): pl.pallas_call(functools.partial(pack_kernel, bricks), out_shape=[pltpu.V...  1.26 us
    pallas_call x1, Pallas kernels, shards(): pl.pallas_call(functools.partial(finish_kernel, edge_rows), out_shape=jax...  0.82 us
  transfers between devices with their start and end apart: 1, of which 0 were waited for; matrix products, arithmetic and copies ran while one was open for 0% of the time, Pallas kernels for 5%

profile of v37, /device:TPU:0, one launch (start us, length us, event | category | flops | bytes accessed | tf_op | source)
XLA Modules:
  0.0 31.5 jit_solution(17879649881341078562)
XLA Ops:
  0.0 1.3 %pack_rows.1 = (f32[16,96,128]{2,1,0:T(8,128)S(1)}, s32[16]{0:T(128)S(4)}, s32[3,2,8,128]{3,2,1,0:T(8,128)S(1)}, f32[3,8,128]{2,1,0:T(8,128)S(1)}, f32[8,128]{1,...) custom-call(f32[2,64,1024]{2,1,0:T(8,128)} %field_ref.1, s32[16]{0:T(128)} %order_ref.1, f32[3]{0:T(128)} %light_ref.1, ...), custom_call_target="tpu_custom_call" | custom-call | tf_op jit(solution)/shard_map/pack_rows/pallas_call | solution.py:279
  1.3 26.1 %all_to_all.5 = f32[16,96,128]{2,1,0:T(8,128)S(1)} all-to-all(f32[16,96,128]{2,1,0:T(8,128)S(1)} %get-tuple-element.18), channel_id=1, replica_groups={{24,16,8,0,28,20,12,4,26,18,10,2,30,22,14,6},{25,17,9,1,29,21,13,5,27,1..., dimensions={0} | all-to-all | bytes 1572864 | tf_op jit(solution)/shard_map/all_to_all | solution.py:302
  27.4 1.6 %collective-permute-start = (f32[16,2,8,128]{3,2,1,0:T(8,128)S(1)}, f32[16,2,8,128]{3,2,1,0:T(8,128)S(1)}, u32[]{:S(2)}, u32[]{:S(2)}) collective-permute-start(f32[16,2,8,128]{3,2,1,0:T(8,128)S(1)} %fusion.1), channel_id=1, source_target_pairs={{0,1},{31,30}} | collective-permute-start | bytes 393224 | tf_op jit(solution)/shard_map/ppermute | solution.py:310
  29.0 1.7 %main_rows.1 = (f32[16,2,2,5,8,128]{5,4,3,2,1,0:T(8,128)S(1)}, f32[6,8,128]{2,1,0:T(8,128)S(1)}, f32[4,8,128]{2,1,0:T(8,128)S(1)}) custom-call(s32[16]{0:T(128)S(4)} %get-tuple-element.20.brick_at, f32[3,8,128]{2,1,0:T(8,128)S(1)} %get-tuple-element.17.light_ref, s32[3,2,8,128]{3,2,1,0:T(8,128)S(1)} %get-tuple-element.21.word_ref, ...), custom_call_target="tpu_custom_call" | custom-call | flops 13107200 | bytes 3145728 | tf_op jit(solution)/shard_map/main_rows/pallas_call | solution.py:311
  30.7 0.0 collective-permute-done.other_ref
  30.7 0.8 %edge_rows.1 = f32[4,1,4,1024]{3,2,1,0:T(4,128)} custom-call(f32[8,128]{1,0:T(8,128)S(1)} %get-tuple-element.15.first_ref, f32[8,128]{1,0:T(8,128)S(1)} %get-tuple-element.16.last_ref, f32[3,8,128]{2,1,0:T(8,128)S(1)} %get-tuple-element.17.light_ref, f32[16,6,2,8,128]{4,3,2,1,0:T(8,128)S(1)} %bitcast.19, ...), custom_call_target="tpu_custom_call" | custom-call | flops 1310720 | bytes 3145728 | tf_op jit(solution)/shard_map/edge_rows/pallas_call | solution.py:326
  (1 shorter events, 0.0 us)
Async XLA Ops:
  27.4 3.3 %collective-permute-start = (f32[16,2,8,128]{3,2,1,0:T(8,128)S(1)}, f32[16,2,8,128]{3,2,1,0:T(8,128)S(1)}, u32[]{:S(2)}, u32[]{:S(2)}) collective-permute-start(f32[16,2,8,128]{3,2,1,0:T(8,128)S(1)} %fusion.1), channel_id=1, source_target_pairs={{0,1},{31,30}} | collective-permute-start | bytes 393224 | tf_op jit(solution)/shard_map/ppermute | solution.py:310

commit v38 on v33

--- a/solution.py
+++ b/solution.py
@@ -43,10 +43,11 @@
         copy.start()
     for p in range(pieces):
         copy_in(p).start()
-    for copy in table_copies:
-        copy.wait()
-    prepare(order, light, color, opacity, brick_at_ref, word_ref, light_rows_ref, first_ref, last_ref, later_ref)
     for p in range(pieces):
+        if p == pieces - 1:
+            for copy in table_copies:
+                copy.wait()
+            prepare(order, light, color, opacity, brick_at_ref, word_ref, light_rows_ref, first_ref, last_ref, later_ref)
         copy_in(p).wait()
         for k in range(depth):
             for row in range(p * piece_rows, (p + 1) * piece_rows, SUB):

time: 31.7 us -> 31.9 us (level)
  no operation moved by 1% of the time
where the time goes in v38:
time: 31.9 us; the launch traced here: 31.7 us
  blocking collectives  26.1 us (82%)
  Pallas kernels  4.02 us (13%)
  starting transfers between devices  1.6 us (5%)
    all_to_all x1, blocking collectives, shards(): lax.all_to_all(sent, 'gz', split_axis=0, concat_axis=0, tiled=True, axis_...  26.1 us
    pallas_call x1, Pallas kernels, shards(): pl.pallas_call(functools.partial(main_kernel, edge_rows), out_shape=[jax....  1.68 us
    ppermute x1, starting transfers between devices, shards(): other = lax.ppermute(wrapped, ('gz', 'gy'), pairs)  1.6 us
    pallas_call x1, Pallas kernels, shards(): pl.pallas_call(functools.partial(pack_kernel, bricks), out_shape=[pltpu.V...  1.52 us
    pallas_call x1, Pallas kernels, shards(): pl.pallas_call(functools.partial(finish_kernel, edge_rows), out_shape=jax...  0.82 us
  transfers between devices with their start and end apart: 1, of which 0 were waited for; matrix products, arithmetic and copies ran while one was open for 0% of the time, Pallas kernels for 5%

profile of v38, /device:TPU:0, one launch (start us, length us, event | category | flops | bytes accessed | tf_op | source)
XLA Modules:
  0.0 31.7 jit_solution(4568747403536017507)
XLA Ops:
  0.0 1.5 %pack_rows.1 = (f32[16,96,128]{2,1,0:T(8,128)S(1)}, s32[16]{0:T(128)S(4)}, s32[3,2,8,128]{3,2,1,0:T(8,128)S(1)}, f32[3,8,128]{2,1,0:T(8,128)S(1)}, f32[8,128]{1,...) custom-call(f32[2,64,1024]{2,1,0:T(8,128)} %field_ref.1, s32[16]{0:T(128)} %order_ref.1, f32[3]{0:T(128)} %light_ref.1, ...), custom_call_target="tpu_custom_call" | custom-call | tf_op jit(solution)/shard_map/pack_rows/pallas_call | solution.py:275
  1.5 26.1 %all_to_all.5 = f32[16,96,128]{2,1,0:T(8,128)S(1)} all-to-all(f32[16,96,128]{2,1,0:T(8,128)S(1)} %get-tuple-element.18), channel_id=1, replica_groups={{24,16,8,0,28,20,12,4,26,18,10,2,30,22,14,6},{25,17,9,1,29,21,13,5,27,1..., dimensions={0} | all-to-all | bytes 1572864 | tf_op jit(solution)/shard_map/all_to_all | solution.py:298
  27.6 1.6 %collective-permute-start = (f32[16,2,8,128]{3,2,1,0:T(8,128)S(1)}, f32[16,2,8,128]{3,2,1,0:T(8,128)S(1)}, u32[]{:S(2)}, u32[]{:S(2)}) collective-permute-start(f32[16,2,8,128]{3,2,1,0:T(8,128)S(1)} %fusion.1), channel_id=1, source_target_pairs={{0,1},{31,30}} | collective-permute-start | bytes 393224 | tf_op jit(solution)/shard_map/ppermute | solution.py:306
  29.2 1.7 %main_rows.1 = (f32[16,2,2,5,8,128]{5,4,3,2,1,0:T(8,128)S(1)}, f32[6,8,128]{2,1,0:T(8,128)S(1)}, f32[4,8,128]{2,1,0:T(8,128)S(1)}) custom-call(s32[16]{0:T(128)S(4)} %get-tuple-element.20.brick_at, f32[3,8,128]{2,1,0:T(8,128)S(1)} %get-tuple-element.17.light_ref, s32[3,2,8,128]{3,2,1,0:T(8,128)S(1)} %get-tuple-element.21.word_ref, ...), custom_call_target="tpu_custom_call" | custom-call | flops 13107200 | bytes 3145728 | tf_op jit(solution)/shard_map/main_rows/pallas_call | solution.py:307
  30.9 0.0 collective-permute-done.other_ref
  30.9 0.8 %edge_rows.1 = f32[4,1,4,1024]{3,2,1,0:T(4,128)} custom-call(f32[8,128]{1,0:T(8,128)S(1)} %get-tuple-element.15.first_ref, f32[8,128]{1,0:T(8,128)S(1)} %get-tuple-element.16.last_ref, f32[3,8,128]{2,1,0:T(8,128)S(1)} %get-tuple-element.17.light_ref, f32[16,6,2,8,128]{4,3,2,1,0:T(8,128)S(1)} %bitcast.19, ...), custom_call_target="tpu_custom_call" | custom-call | flops 1310720 | bytes 3145728 | tf_op jit(solution)/shard_map/edge_rows/pallas_call | solution.py:322
  (1 shorter events, 0.0 us)
Async XLA Ops:
  27.6 3.3 %collective-permute-start = (f32[16,2,8,128]{3,2,1,0:T(8,128)S(1)}, f32[16,2,8,128]{3,2,1,0:T(8,128)S(1)}, u32[]{:S(2)}, u32[]{:S(2)}) collective-permute-start(f32[16,2,8,128]{3,2,1,0:T(8,128)S(1)} %fusion.1), channel_id=1, source_target_pairs={{0,1},{31,30}} | collective-permute-start | bytes 393224 | tf_op jit(solution)/shard_map/ppermute | solution.py:306

commit v39 on v33

--- a/solution.py
+++ b/solution.py
@@ -268,7 +268,7 @@
     lines = (chunks, LANES)
     halves = (color_table.shape[1] - 1) // LANES
     together = 16 if bricks % 16 == 0 else 1
-    pieces = 4 if rows % (4 * SUB) == 0 else 1
+    pieces = 2 if rows % (2 * SUB) == 0 else 1
     hbm = pl.BlockSpec(memory_space=pltpu.HBM)
     given = [scalar, view_order, light_dir, color_table, opacity_table]
     sent, brick_at, words, light_rows, first, final, later = pl.pallas_call(

time: 31.7 us -> 31.7 us (level)
  no operation moved by 1% of the time
where the time goes in v39:
time: 31.7 us; the launch traced here: 31.5 us
  blocking collectives  26.1 us (82%)
  Pallas kernels  3.74 us (12%)
  starting transfers between devices  1.6 us (5%)
    all_to_all x1, blocking collectives, shards(): lax.all_to_all(sent, 'gz', split_axis=0, concat_axis=0, tiled=True, axis_...  26.1 us
    pallas_call x1, Pallas kernels, shards(): pl.pallas_call(functools.partial(main_kernel, edge_rows), out_shape=[jax....  1.68 us
    ppermute x1, starting transfers between devices, shards(): other = lax.ppermute(wrapped, ('gz', 'gy'), pairs)  1.6 us
    pallas_call x1, Pallas kernels, shards(): pl.pallas_call(functools.partial(pack_kernel, bricks), out_shape=[pltpu.V...  1.24 us
    pallas_call x1, Pallas kernels, shards(): pl.pallas_call(functools.partial(finish_kernel, edge_rows), out_shape=jax...  0.82 us
  transfers between devices with their start and end apart: 1, of which 0 were waited for; matrix products, arithmetic and copies ran while one was open for 0% of the time, Pallas kernels for 5%

profile of v39, /device:TPU:0, one launch (start us, length us, event | category | flops | bytes accessed | tf_op | source)
XLA Modules:
  0.0 31.5 jit_solution(1091831002178582160)
XLA Ops:
  0.0 1.2 %pack_rows.1 = (f32[16,96,128]{2,1,0:T(8,128)S(1)}, s32[16]{0:T(128)S(4)}, s32[3,2,8,128]{3,2,1,0:T(8,128)S(1)}, f32[3,8,128]{2,1,0:T(8,128)S(1)}, f32[8,128]{1,...) custom-call(f32[2,64,1024]{2,1,0:T(8,128)} %field_ref.1, s32[16]{0:T(128)} %order_ref.1, f32[3]{0:T(128)} %light_ref.1, ...), custom_call_target="tpu_custom_call" | custom-call | tf_op jit(solution)/shard_map/pack_rows/pallas_call | solution.py:274
  1.2 26.1 %all_to_all.5 = f32[16,96,128]{2,1,0:T(8,128)S(1)} all-to-all(f32[16,96,128]{2,1,0:T(8,128)S(1)} %get-tuple-element.18), channel_id=1, replica_groups={{24,16,8,0,28,20,12,4,26,18,10,2,30,22,14,6},{25,17,9,1,29,21,13,5,27,1..., dimensions={0} | all-to-all | bytes 1572864 | tf_op jit(solution)/shard_map/all_to_all | solution.py:297
  27.3 1.6 %collective-permute-start = (f32[16,2,8,128]{3,2,1,0:T(8,128)S(1)}, f32[16,2,8,128]{3,2,1,0:T(8,128)S(1)}, u32[]{:S(2)}, u32[]{:S(2)}) collective-permute-start(f32[16,2,8,128]{3,2,1,0:T(8,128)S(1)} %fusion.1), channel_id=1, source_target_pairs={{0,1},{31,30}} | collective-permute-start | bytes 393224 | tf_op jit(solution)/shard_map/ppermute | solution.py:305
  28.9 1.7 %main_rows.1 = (f32[16,2,2,5,8,128]{5,4,3,2,1,0:T(8,128)S(1)}, f32[6,8,128]{2,1,0:T(8,128)S(1)}, f32[4,8,128]{2,1,0:T(8,128)S(1)}) custom-call(s32[16]{0:T(128)S(4)} %get-tuple-element.20.brick_at, f32[3,8,128]{2,1,0:T(8,128)S(1)} %get-tuple-element.17.light_ref, s32[3,2,8,128]{3,2,1,0:T(8,128)S(1)} %get-tuple-element.21.word_ref, ...), custom_call_target="tpu_custom_call" | custom-call | flops 13107200 | bytes 3145728 | tf_op jit(solution)/shard_map/main_rows/pallas_call | solution.py:306
  30.6 0.0 collective-permute-done.other_ref
  30.6 0.8 %edge_rows.1 = f32[4,1,4,1024]{3,2,1,0:T(4,128)} custom-call(f32[8,128]{1,0:T(8,128)S(1)} %get-tuple-element.15.first_ref, f32[8,128]{1,0:T(8,128)S(1)} %get-tuple-element.16.last_ref, f32[3,8,128]{2,1,0:T(8,128)S(1)} %get-tuple-element.17.light_ref, f32[16,6,2,8,128]{4,3,2,1,0:T(8,128)S(1)} %bitcast.19, ...), custom_call_target="tpu_custom_call" | custom-call | flops 1310720 | bytes 3145728 | tf_op jit(solution)/shard_map/edge_rows/pallas_call | solution.py:321
  (1 shorter events, 0.0 us)
Async XLA Ops:
  27.3 3.3 %collective-permute-start = (f32[16,2,8,128]{3,2,1,0:T(8,128)S(1)}, f32[16,2,8,128]{3,2,1,0:T(8,128)S(1)}, u32[]{:S(2)}, u32[]{:S(2)}) collective-permute-start(f32[16,2,8,128]{3,2,1,0:T(8,128)S(1)} %fusion.1), channel_id=1, source_target_pairs={{0,1},{31,30}} | collective-permute-start | bytes 393224 | tf_op jit(solution)/shard_map/ppermute | solution.py:305
